TPU v7x, 32 devices: a whole 2x2x4 slice. The times are simulated.
32 devices in a mesh: rep: 4 (over z), fsdp: 8 (over y, x, core).
Axes of the slice: x: 2, y: 2, z: 4, core: 2. Of those that a mesh axis runs over, the one named last changes fastest.
Arguments:
- tokens: bfloat16 [16384, 1536], P(('rep', 'fsdp')), may hold values from -6 to 6
- cotangent: bfloat16 [16384, 1536], P(('rep', 'fsdp')), may hold values from -6 to 6
- lengths: int32 [4, 8, 2], P('rep', 'fsdp'), may hold values from 128 to 384, as said below
- dealing: int32 [4, 8, 8], P('rep', 'fsdp'), may hold values from 0 to 7, each once within a row
- norm_gain: bfloat16 [1536], P('fsdp'), may hold values from 0.5 to 1.5
- in_weight: bfloat16 [1536, 6448], P('fsdp'), may hold values from -0.15625 to 0.15625
- conv_weight: bfloat16 [4, 3328], P(None, 'fsdp'), may hold values from -3 to 3
- conv_bias: bfloat16 [3328], P('fsdp'), may hold values from -3 to 3
- dt_bias: bfloat16 [48], P('fsdp'), may hold values from -6 to -1
- a_log: bfloat16 [48], P('fsdp'), may hold values from 0 to 2.6875
- d_skip: bfloat16 [48], P('fsdp'), may hold values from 0.5 to 1.5
- gated_gain: bfloat16 [3072], P('fsdp'), may hold values from 0.5 to 1.5
- out_weight: bfloat16 [3072, 1536], P('fsdp'), may hold values from -0.109375 to 0.109375
Outputs:
- output: bfloat16 [16384, 1536], P(('rep', 'fsdp'))
- input_grad: bfloat16 [16384, 1536], P(('rep', 'fsdp'))
- norm_gain_grad: float32 [1536], P('fsdp')
- in_weight_grad: float32 [1536, 6448], P('fsdp')
- conv_weight_grad: float32 [4, 3328], P(None, 'fsdp')
- conv_bias_grad: float32 [3328], P('fsdp')
- dt_bias_grad: float32 [48], P('fsdp')
- a_log_grad: float32 [48], P('fsdp')
- d_skip_grad: float32 [48], P('fsdp')
- gated_gain_grad: float32 [3072], P('fsdp')
- out_weight_grad: float32 [3072, 1536], P('fsdp')
Inputs may be any that keep to these rules, and one draw needn't show every extreme that they name: Each device's 2 lengths sum to 512. Each row dealing[r, f, :] is a permutation, so every device of a group receives exactly one block from every device of it.
All inputs are finite; a program needn't handle non-finite values.
Results may differ from a plain program's by a relative error of at most 0.0066.
Values may be sent and summed in bfloat16 or wider, within the bound.
No kernel may reach another device: no remote copies, remote signals or barrier semaphores. Data moves between devices by JAX's collectives and lax.ppermute only.
A program may use at most 320 MiB of HBM per device.

v0:
```python
import jax
import jax.numpy as jnp
from jax import lax
from jax.sharding import PartitionSpec as P

DI = 3072
HEAD_DIM = 64
NSTATE = 128
KW = 4
SPAN = 256
HEADS = 48


epsilon = 1e-05


def segment_ids(seq_lengths, rows):
    ends = jnp.cumsum(seq_lengths)
    places = jnp.arange(rows, dtype=jnp.int32)
    return jnp.sum((places[:, None] >= ends[None, :]).astype(jnp.int32), axis=1)


def block_step(state, inputs):
    inner, step_size, log_decay, b_input, c_output, segment, carry_mask, last_mask = inputs
    cumulative = jnp.cumsum(log_decay, axis=0)
    places = jnp.arange(SPAN, dtype=jnp.int32)
    causal = (places[:, None] >= places[None, :]) & (segment[:, None] == segment[None, :])
    mask = causal.astype(jnp.float32)[:, :, None]
    spread = cumulative[:, None, :] - cumulative[None, :, :]
    decay = jnp.exp(jnp.where(mask > 0, spread, 0.0)) * mask
    scores = jnp.dot(c_output, b_input.T, precision=lax.Precision.HIGHEST)
    weighted = inner * step_size[:, :, None]
    mixing = scores[:, :, None] * decay
    local_out = jnp.einsum("tsh,shp->thp", mixing, weighted, precision=lax.Precision.HIGHEST)
    carried = jnp.einsum("tn,hnp->thp", c_output, state, precision=lax.Precision.HIGHEST)
    result = local_out + carried * (jnp.exp(cumulative) * carry_mask[:, None])[:, :, None]
    end_weight = jnp.exp(cumulative[-1][None, :] - cumulative) * last_mask[:, None]
    new_state = jnp.exp(cumulative[-1])[:, None, None] * state * carry_mask[-1]
    new_state = new_state + jnp.einsum(
        "sn,shp->hnp", b_input, weighted * end_weight[:, :, None], precision=lax.Precision.HIGHEST
    )
    return (new_state, result)


def mixer_core(projected, segment, conv_weight, conv_bias, dt_bias, a_log, d_skip, gated_gain):
    length = projected.shape[0]
    gate_part = projected[:, :DI]
    conv_input = projected[:, DI : 2 * DI + 2 * NSTATE]
    step_raw = projected[:, 2 * DI + 2 * NSTATE :]
    mixed = conv_bias + conv_weight[KW - 1] * conv_input
    for offset in range(1, KW):
        shifted = jnp.concatenate(
            [jnp.zeros((offset, conv_input.shape[1]), jnp.float32), conv_input[:-offset]], axis=0
        )
        earlier = jnp.concatenate([jnp.full((offset,), -1, jnp.int32), segment[:-offset]])
        keep_mask = (earlier == segment).astype(jnp.float32)[:, None]
        mixed = mixed + conv_weight[KW - 1 - offset] * shifted * keep_mask
    activated = jax.nn.silu(mixed)
    inner = activated[:, :DI].reshape(length, HEADS, HEAD_DIM)
    b_input = activated[:, DI : DI + NSTATE]
    c_output = activated[:, DI + NSTATE :]
    step_size = jax.nn.softplus(step_raw + dt_bias)
    log_decay = -jnp.exp(a_log) * step_size
    blocks = length // SPAN
    seg_blocks = segment.reshape(blocks, SPAN)
    before = jnp.concatenate([jnp.full((1,), -1, jnp.int32), seg_blocks[:-1, -1]])
    carry_mask = (seg_blocks == before[:, None]).astype(jnp.float32)
    last_mask = (seg_blocks == seg_blocks[:, -1:]).astype(jnp.float32)
    scanned = (
        inner.reshape(blocks, SPAN, HEADS, HEAD_DIM),
        step_size.reshape(blocks, SPAN, HEADS),
        log_decay.reshape(blocks, SPAN, HEADS),
        b_input.reshape(blocks, SPAN, NSTATE),
        c_output.reshape(blocks, SPAN, NSTATE),
        seg_blocks,
        carry_mask,
        last_mask,
    )
    start_state = jnp.zeros((HEADS, NSTATE, HEAD_DIM), jnp.float32)
    final_state, outputs = lax.scan(jax.checkpoint(block_step), start_state, scanned)
    ssm_out = outputs.reshape(length, HEADS, HEAD_DIM) + d_skip[None, :, None] * inner
    gated = ssm_out.reshape(length, DI) * jax.nn.silu(gate_part)
    return gated * lax.rsqrt(jnp.mean(gated * gated, axis=-1, keepdims=True) + epsilon) * gated_gain


def norm_input(hidden, gain):
    return hidden * lax.rsqrt(jnp.mean(hidden * hidden, axis=-1, keepdims=True) + epsilon) * gain


def contract_rows(left, right):
    return lax.dot_general(
        left, right, (((0,), (0,)), ((), ())), preferred_element_type=jnp.float32
    )


def contract_cols(left, right):
    return lax.dot_general(
        left, right, (((1,), (1,)), ((), ())), preferred_element_type=jnp.float32
    )


def per_device(
    tokens,
    cotangent,
    lengths,
    dealing,
    norm_gain,
    in_weight,
    conv_weight,
    conv_bias,
    dt_bias,
    a_log,
    d_skip,
    gated_gain,
    out_weight,
):
    groups = lax.axis_size("fsdp")
    tok_rows = tokens.shape[0]
    width = tokens.shape[1]
    block_rows = tok_rows // groups
    targets = dealing.reshape(groups)
    inverse = jnp.argsort(targets)
    tok_blocks = tokens.reshape(groups, block_rows, width)[inverse]
    cot_blocks = cotangent.reshape(groups, block_rows, width)[inverse]
    dealt_tokens, dealt_cot = (
        lax.all_to_all(tok_blocks, "fsdp", split_axis=0, concat_axis=0, tiled=True),
        lax.all_to_all(cot_blocks, "fsdp", split_axis=0, concat_axis=0, tiled=True),
    )
    hidden = dealt_tokens.reshape(tok_rows, width).astype(jnp.float32)
    cot_rows = dealt_cot.reshape(tok_rows, width)
    segment = segment_ids(lengths.reshape(-1), tok_rows)
    gain_full, in_full, conv_full, cbias_full, dtb_full, alog_full, dskip_full = (
        lax.all_gather(norm_gain, "fsdp", axis=0, tiled=True),
        lax.all_gather(in_weight, "fsdp", axis=0, tiled=True),
        lax.all_gather(conv_weight, "fsdp", axis=1, tiled=True),
        lax.all_gather(conv_bias, "fsdp", axis=0, tiled=True),
        lax.all_gather(dt_bias, "fsdp", axis=0, tiled=True),
        lax.all_gather(a_log, "fsdp", axis=0, tiled=True),
        lax.all_gather(d_skip, "fsdp", axis=0, tiled=True),
    )
    ggain_full, out_full = (
        lax.all_gather(gated_gain, "fsdp", axis=0, tiled=True),
        lax.all_gather(out_weight, "fsdp", axis=0, tiled=True),
    )
    normed, norm_backward = jax.vjp(norm_input, hidden, gain_full.astype(jnp.float32))
    normed_low = normed.astype(jnp.bfloat16)
    projected = jnp.dot(normed_low, in_full, preferred_element_type=jnp.float32)

    def mixer_local(proj_values, conv_taps, conv_shift, step_bias, decay_log, skip_coef, gate_gain):
        return mixer_core(
            proj_values, segment, conv_taps, conv_shift, step_bias, decay_log, skip_coef, gate_gain
        )

    gated, mixer_backward = jax.vjp(
        mixer_local,
        projected,
        conv_full.astype(jnp.float32),
        cbias_full.astype(jnp.float32),
        dtb_full.astype(jnp.float32),
        alog_full.astype(jnp.float32),
        dskip_full.astype(jnp.float32),
        ggain_full.astype(jnp.float32),
    )
    gated_low = gated.astype(jnp.bfloat16)
    branch = jnp.dot(gated_low, out_full, preferred_element_type=jnp.float32)
    result = (hidden + branch).astype(jnp.bfloat16)
    out_back = lax.all_gather(out_weight, "fsdp", axis=0, tiled=True)
    d_gated = contract_cols(cot_rows, out_back)
    d_proj, g_conv, g_cbias, g_dtb, g_alog, g_dskip, g_ggain = mixer_backward(d_gated)
    d_proj_low = d_proj.astype(jnp.bfloat16)
    in_back = lax.all_gather(in_weight, "fsdp", axis=0, tiled=True)
    d_normed = contract_cols(d_proj_low, in_back)
    d_hidden, g_gain = norm_backward(d_normed)
    d_input = (cot_rows.astype(jnp.float32) + d_hidden).astype(jnp.bfloat16)
    out_term = contract_rows(gated_low, cot_rows)
    in_term = contract_rows(normed_low, d_proj_low)
    s_gain, s_in, s_conv, s_cbias, s_dtb, s_alog, s_dskip, s_ggain, s_out = (
        lax.psum_scatter(g_gain, "fsdp", scatter_dimension=0, tiled=True),
        lax.psum_scatter(in_term, "fsdp", scatter_dimension=0, tiled=True),
        lax.psum_scatter(g_conv, "fsdp", scatter_dimension=1, tiled=True),
        lax.psum_scatter(g_cbias, "fsdp", scatter_dimension=0, tiled=True),
        lax.psum_scatter(g_dtb, "fsdp", scatter_dimension=0, tiled=True),
        lax.psum_scatter(g_alog, "fsdp", scatter_dimension=0, tiled=True),
        lax.psum_scatter(g_dskip, "fsdp", scatter_dimension=0, tiled=True),
        lax.psum_scatter(g_ggain, "fsdp", scatter_dimension=0, tiled=True),
        lax.psum_scatter(out_term, "fsdp", scatter_dimension=0, tiled=True),
    )
    r_gain, r_in, r_conv, r_cbias, r_dtb, r_alog, r_dskip, r_ggain, r_out = lax.psum(
        (s_gain, s_in, s_conv, s_cbias, s_dtb, s_alog, s_dskip, s_ggain, s_out), "rep"
    )
    sent_result = result.reshape(groups, block_rows, width)
    sent_grad = d_input.reshape(groups, block_rows, width)
    got_result, got_grad = (
        lax.all_to_all(sent_result, "fsdp", split_axis=0, concat_axis=0, tiled=True),
        lax.all_to_all(sent_grad, "fsdp", split_axis=0, concat_axis=0, tiled=True),
    )
    output = got_result[targets].reshape(tok_rows, width)
    input_grad = got_grad[targets].reshape(tok_rows, width)
    return (
        output,
        input_grad,
        r_gain,
        r_in,
        r_conv,
        r_cbias,
        r_dtb,
        r_alog,
        r_dskip,
        r_ggain,
        r_out,
    )


def solution(mesh):
    placed = (
        P(("rep", "fsdp"), None),
        P(("rep", "fsdp"), None),
        P("rep", "fsdp", None),
        P("rep", "fsdp", None),
        P("fsdp"),
        P("fsdp", None),
        P(None, "fsdp"),
        P("fsdp"),
        P("fsdp"),
        P("fsdp"),
        P("fsdp"),
        P("fsdp"),
        P("fsdp", None),
    )
    return jax.shard_map(
        per_device,
        mesh=mesh,
        in_specs=placed,
        out_specs=(
            P(("rep", "fsdp"), None),
            P(("rep", "fsdp"), None),
            P("fsdp"),
            P("fsdp", None),
            P(None, "fsdp"),
            P("fsdp"),
            P("fsdp"),
            P("fsdp"),
            P("fsdp"),
            P("fsdp"),
            P("fsdp", None),
        ),
        check_vma=False,
    )
```

profile of v0, /device:TPU:0, one launch (start us, length us, event | category | flops | bytes accessed | tf_op | source)
XLA Modules:
  0.0 1515.4 jit_solution(3715169556668521389)
XLA Ops:
  22.3 45.1 %all-reduce.34 = (bf16[1536]{0:T(1024)(128)(2,1)S(1)}, bf16[48]{0:T(256)(128)(2,1)S(1)}, bf16[48]{0:T(256)(128)(2,1)S(1)}, bf16[3328]{0:T(1024)(128)(2,1)S(1)}, bf16[48]{0:T(256)(128)(2,1)S(1)}) all-reduce(bf16[1536]{0:T(1024)(128)(2,1)S(1)} %dynamic-update-slice.1, ...), channel_id=1, replica_groups=mesh['rep'=4,'fsdp'=8] {'fsdp'}, use_global_device_ids=true, to_apply=%add.21 | all-reduce | flops 5008 | bytes 20032
  67.5 9.3 all-gather.1
  77.5 8.0 all-gather
  94.0 51.8 %all-gather.5.cloned.1.call-done = bf16[1536,6448]{1,0:T(8,128)(2,1)} async-done(((bf16[192,6448]{1,0:T(8,128)(2,1)}), bf16[1536,6448]{1,0:T(8,128)(2,1)}) %all-gather.5.cloned.1.call-update) | async-done | bytes 19808272 | tf_op jit(solution)/shard_map/all_gather | solution.py:134
  145.8 18.0 %fusion.164 = f32[512,6448]{0,1:T(8,128)} fusion(bf16[512,1536]{1,0:T(8,128)(2,1)S(1)} %fusion.130, bf16[1536,6448]{1,0:T(8,128)(2,1)} %all-gather.5.cloned.1.call-done), kind=kOutput, calls=%fused_computation.249 | convolution fusion | flops 10141827072 | bytes 34586624 | tf_op jit(solution)/shard_map/dot_general | solution.py:147
  163.8 7.4 slice.184
  179.6 11.3 fusion.121
  196.7 8.3 reshape.582
  204.9 6.5 copy.214
  213.7 5.6 broadcast.339.clone2
  219.4 207.9 %while.41 = (s32[]{:T(128)}, f32[48,128,64]{1,2,0:T(8,128)}, f32[2,256,48,64]{1,0,3,2:T(2,128)}, f32[2,48,128,64]{2,3,1,0:T(8,128)}, f32[2,256,48]{1,2,0:T(8,128...) while((s32[]{:T(128)}, f32[48,128,64]{1,2,0:T(8,128)}, ...), condition=%wide.region_7.8_spmd.clone, body=%wide.region_4.7_spmd.clone.sunk | while | flops 4952539136 | bytes 59179096 | solution.py:80
  239.7 6.9 bitcast_add_fusion.6
  249.2 14.2 fusion.233
  266.6 63.3 %dynamic_update_slice.77 = f32[2,256,48,64]{1,0,3,2:T(2,128)} dynamic-update-slice(f32[2,256,48,64]{1,0,3,2:T(2,128)} %get-tuple-element.1210, f32[1,256,48,64]{1,0,3,2:T(1,128)S(1)} %copy.325, s32[]{:T(128)S(6)} %copy.357, s32[]{:T(128)} %constant.136.clone.1..sunk, s32[]{:T(128)} %constant.136.clone.1..sunk, s32[]{:T(128)} %constant.136.clone.1..sunk) | dynamic-update-slice | bytes 6291460 | tf_op jit(solution)/shard_map/jvp()/while/body/jit(dynamic_update_index_in_dim)/dynamic_update_slice | solution.py:80
  336.7 6.9 bitcast_add_fusion.6
  346.2 14.2 fusion.233
  363.7 63.3 %dynamic_update_slice.77 = f32[2,256,48,64]{1,0,3,2:T(2,128)} dynamic-update-slice(f32[2,256,48,64]{1,0,3,2:T(2,128)} %get-tuple-element.1210, f32[1,256,48,64]{1,0,3,2:T(1,128)S(1)} %copy.325, s32[]{:T(128)S(6)} %copy.357, s32[]{:T(128)} %constant.136.clone.1..sunk, s32[]{:T(128)} %constant.136.clone.1..sunk, s32[]{:T(128)} %constant.136.clone.1..sunk) | dynamic-update-slice | bytes 6291460 | tf_op jit(solution)/shard_map/jvp()/while/body/jit(dynamic_update_index_in_dim)/dynamic_update_slice | solution.py:80
  430.8 9.9 multiply_reduce_fusion.11
  440.8 11.8 fusion.148
  452.6 11.1 multiply_reduce_fusion.8
  463.7 15.7 %multiply_reduce_fusion.9 = (f32[3072]{0:T(1024)}, f32[512,3072]{0,1:T(8,128)}, f32[512,3072]{0,1:T(8,128)}) fusion(f32[512,3328]{0,1:T(8,128)} %copy-done.6, f32[512,6448]{0,1:T(8,128)} %fusion.164, f32[512,3072]{0,1:T(8,128)} %get-tuple-element.894, f32[512]{0:T(512)S(1)} %multiply_multiply_fusion.2, f32[512]{0:T(512)S(1)} %fusion.143, ...), kind=kLoop, calls=%fused_computation.169 | loop fusion | flops 33027072 | bytes 44081152 | tf_op jit(solution)/shard_map/transpose(jvp())/reduce_sum | solution.py:81
  479.4 8.2 reshape.592
  490.4 5.9 broadcast.339.clone
  496.3 374.1 %while.42 = (s32[]{:T(128)}, f32[48,128,64]{1,2,0:T(8,128)}, f32[2,256,48,64]{1,0,3,2:T(2,128)}, f32[2,256,48]{1,0,2:T(2,128)}, f32[2,256,48]{1,0,2:T(2,128)}, /...) while((s32[]{:T(128)}, f32[48,128,64]{1,2,0:T(8,128)}, ...), condition=%wide.region_23.24_spmd.clone, body=%wide.region_10.23_spmd.clone.sunk | while | flops 11239006208 | bytes 151892112 | solution.py:80
  522.1 22.7 %fusion.254 = (f32[256,48]{0,1:T(8,128)}, f32[256,48]{0,1:T(8,128)}, f32[256,256]{1,0:T(8,128)}) fusion(f32[256,256]{1,0:T(8,128)S(1)} %get-tuple-element.1171, f32[256,48]{0,1:T(8,128)} %copy.330, f32[256,256]{1,0:T(8,128)S(1)} %fusion.253, pred[256,256]{1,0:T(8,128)(4,1)S(1)} %get-tuple-element.1175, f32[256,48,64]{0,2,1:T(8,128)} %get-tuple-element.1176, ...), kind=kOutput, calls=%fused_computation.74.clone.1 | convolution fusion | flops 2451218432 | bytes 7340032 | tf_op jit(solution)/shard_map/transpose(jvp())/while/body/eval_jaxpr/checkpoint/tsh,shp->thp/dot_general | solution.py:34
  549.6 8.5 fusion.261
  567.9 14.8 multiply_reduce_fusion.18
  591.7 6.6 fusion.262
  598.3 5.9 bitcast_add_fusion.7
  611.5 5.2 copy.337
  616.6 63.3 %dynamic_update_slice.80 = f32[2,256,48,64]{1,0,3,2:T(2,128)} dynamic-update-slice(f32[2,256,48,64]{1,0,3,2:T(2,128)} %get-tuple-element.1262, f32[1,256,48,64]{1,0,3,2:T(1,128)S(1)} %copy.337, s32[]{:T(128)S(6)} %sub.240, s32[]{:T(128)} %constant.136.clone.1..sunk.1, s32[]{:T(128)} %constant.136.clone.1..sunk.1, s32[]{:T(128)} %constant.136.clone.1..sunk.1) | dynamic-update-slice | bytes 6291460 | tf_op jit(solution)/shard_map/transpose(jvp())/while/body/jit(dynamic_update_index_in_dim)/dynamic_update_slice | solution.py:80
  704.9 22.9 %fusion.254 = (f32[256,48]{0,1:T(8,128)}, f32[256,48]{0,1:T(8,128)}, f32[256,256]{1,0:T(8,128)}) fusion(f32[256,256]{1,0:T(8,128)S(1)} %get-tuple-element.1171, f32[256,48]{0,1:T(8,128)} %copy.330, f32[256,256]{1,0:T(8,128)S(1)} %fusion.253, pred[256,256]{1,0:T(8,128)(4,1)S(1)} %get-tuple-element.1175, f32[256,48,64]{0,2,1:T(8,128)} %get-tuple-element.1176, ...), kind=kOutput, calls=%fused_computation.74.clone.1 | convolution fusion | flops 2451218432 | bytes 7340032 | tf_op jit(solution)/shard_map/transpose(jvp())/while/body/eval_jaxpr/checkpoint/tsh,shp->thp/dot_general | solution.py:34
  732.7 8.2 fusion.261
  750.5 14.5 multiply_reduce_fusion.18
  774.1 6.5 fusion.262
  780.6 5.9 bitcast_add_fusion.7
  799.0 63.3 %dynamic_update_slice.80 = f32[2,256,48,64]{1,0,3,2:T(2,128)} dynamic-update-slice(f32[2,256,48,64]{1,0,3,2:T(2,128)} %get-tuple-element.1262, f32[1,256,48,64]{1,0,3,2:T(1,128)S(1)} %copy.337, s32[]{:T(128)S(6)} %sub.240, s32[]{:T(128)} %constant.136.clone.1..sunk.1, s32[]{:T(128)} %constant.136.clone.1..sunk.1, s32[]{:T(128)} %constant.136.clone.1..sunk.1) | dynamic-update-slice | bytes 6291460 | tf_op jit(solution)/shard_map/transpose(jvp())/while/body/jit(dynamic_update_index_in_dim)/dynamic_update_slice | solution.py:80
  881.7 11.5 multiply_reduce_fusion.7
  893.2 10.0 multiply_reduce_fusion.6
  918.2 13.3 fusion.149
  931.5 21.9 %fusion.146 = f32[1536,6448]{1,0:T(8,128)} fusion(bf16[512,1536]{1,0:T(8,128)(2,1)S(1)} %copy-done.24, f32[512,3072]{0,1:T(8,128)} %get-tuple-element.920, f32[512,3328]{0,1:T(8,128)} %get-tuple-element.921, f32[512,48]{0,1:T(8,128)S(1)} %get-tuple-element.892), kind=kOutput, calls=%fused_computation.239 | convolution fusion | flops 10151731200 | bytes 54394880 | tf_op jit(solution)/shard_map/dot_general | solution.py:91
  955.5 233.8 %reduce-scatter.6.cloned.1.call-done = f32[192,6448]{1,0:T(8,128)} async-done(((f32[1536,6448]{1,0:T(8,128)}), f32[192,6448]{1,0:T(8,128)}) %reduce-scatter.6.cloned.1.call-update) | async-done | bytes 4952080 | tf_op jit(solution)/shard_map/reduce_scatter | solution.py:179
  1189.5 11.0 fusion.134
  1204.3 24.0 %fusion.131 = (f32[1536]{0:T(1024)S(1)}, f32[512]{0:T(512)S(1)}, f32[512,1536]{1,0:T(8,128)}) fusion(bf16[8,64,1536]{2,1,0:T(8,128)(2,1)S(1)} %copy-done.12, f32[512]{0:T(512)S(1)} %copy-done.55, f32[1536]{0:T(1024)S(1)} %copy-done.46, bf16[1536,6448]{1,0:T(8,128)(2,1)} %all-gather.5.cloned.1.call-done, f32[512,3072]{0,1:T(8,128)} %get-tuple-element.920, ...), kind=kOutput, calls=%fused_computation.192 | convolution fusion | flops 10157234176 | bytes 37748736 | tf_op jit(solution)/shard_map/dot_general | solution.py:97
  1239.9 37.0 %all-reduce.31 = (f32[1536]{0:T(1024)S(1)}, f32[3328]{0:T(1024)S(1)}, f32[48]{0:T(128)S(1)}, f32[48]{0:T(128)S(1)}, f32[48]{0:T(128)S(1)}, /*index=5*/f32[3072]{0:T(1024)S(1)}) all-reduce(f32[1536]{0:T(1024)S(1)} %get-tuple-element.796, f32[3328]{0:T(1024)S(1)} %get-tuple-element.794, ...), channel_id=2, replica_groups=mesh['rep'=4,'fsdp'=8] {'fsdp'}, use_global_device_ids=true, to_apply=%region_26.27.clone | all-reduce | flops 8080 | bytes 64640
  1278.4 20.4 %all-reduce.32 = (f32[192]{0:T(256)}, f32[4,416]{1,0:T(4,128)}, f32[416]{0:T(512)}, f32[6]{0:T(128)}, f32[6]{0:T(128)}, /*index=5*/f32[6]{0:T(128)}, f32[384]{0:T(512)}) all-reduce(f32[192]{0:T(256)S(1)} %dynamic-slice.6, f32[4,416]{1,0:T(4,128)S(1)} %copy.238, f32[416]{0:T(512)S(1)} %dynamic-slice.8, ...), channel_id=1, replica_groups=mesh['rep'=4,'fsdp'=8] {'rep'}, use_global_device_ids=true, to_apply=%region_27.28 | all-reduce | flops 2674 | bytes 21392 | tf_op jit(solution)/shard_map/psum | solution.py:188
  1302.4 199.4 %all-reduce.37.cloned.1.call-done = (f32[192,6448]{1,0:T(8,128)}, f32[384,1536]{1,0:T(8,128)}) async-done(((f32[192,6448]{1,0:T(8,128)}, f32[384,1536]{1,0:T(8,128)}), (f32[192,6448]{1,0:T(8,128)}, f32[384,1536]{1,0:T(8,128)})) %all-reduce.37.cloned.1.call-update) | async-done | bytes 7311376 | tf_op jit(solution)/shard_map/psum | solution.py:188
  1501.7 5.2 copy.391
  (469 shorter events, 232.9 us)
Async XLA Ops:
  7.3 70.3 %copy-start.63 = (bf16[4,416]{1,0:T(4,128)(2,1)S(1)}, bf16[4,416]{1,0:T(4,128)(2,1)}, u32[]{:S(2)}) copy-start(bf16[4,416]{1,0:T(4,128)(2,1)} %param.23) | copy-start | bytes 9988
  7.3 78.3 %copy-start.22 = (bf16[512,1536]{1,0:T(8,128)(2,1)S(1)}, bf16[512,1536]{1,0:T(8,128)(2,1)}, u32[]{:S(2)}) copy-start(bf16[512,1536]{1,0:T(8,128)(2,1)} %param.18) | copy-start | bytes 4718596
  7.3 138.5 %all-gather.5.cloned.1.call-start = ((), (), s32[]{:S(2)}) async-start(), calls=%async_computation.7 | async-start | bytes 22560768 | tf_op jit(solution)/shard_map/all_gather | solution.py:134
  11.7 77.0 %all-to-all-start = ((bf16[8,64,1536]{2,1,0:T(8,128)(2,1)}), bf16[8,64,1536]{2,1,0:T(8,128)(2,1)S(1)}, u32[]{:S(2)}, u32[]{:S(2)}) async-start(bf16[8,64,1536]{2,1,0:T(8,128)(2,1)} %gather_fusion), calls=%async_computation | async-start | bytes 3145728 | tf_op jit(solution)/shard_map/all_to_all | solution.py:126
  16.8 435.7 %all-gather.7.cloned.1.call-start = ((), (), s32[]{:S(2)}) async-start(), calls=%async_computation.8 | async-start | bytes 10616832 | tf_op jit(solution)/shard_map/all_gather | solution.py:143
  67.5 96.3 %copy-start.77 = (bf16[48]{0:T(256)(128)(2,1)}, bf16[48]{0:T(256)(128)(2,1)S(1)}, u32[]{:S(2)}) copy-start(bf16[48]{0:T(256)(128)(2,1)S(1)} %get-tuple-element.877) | copy-start | bytes 292
  67.5 143.9 %copy-start.65 = (f32[48]{0:T(128)}, f32[48]{0:T(128)S(1)}, u32[]{:S(2)}) copy-start(f32[48]{0:T(128)S(1)} %convert_element_type.109) | copy-start | bytes 580
  67.5 96.3 %copy-start.45 = (f32[1536]{0:T(1024)}, f32[1536]{0:T(1024)S(1)}, u32[]{:S(2)}) copy-start(f32[1536]{0:T(1024)S(1)} %convert_element_type.107) | copy-start | bytes 18436
  77.5 386.1 %copy-start.29 = (f32[3072]{0:T(1024)}, f32[3072]{0:T(1024)S(1)}, u32[]{:S(2)}) copy-start(f32[3072]{0:T(1024)S(1)} %mul.813) | copy-start | bytes 36868
  88.5 89.2 %copy-start.31 = (f32[3328]{0:T(1024)}, f32[3328]{0:T(1024)S(1)}, u32[]{:S(2)}) copy-start(f32[3328]{0:T(1024)S(1)} %get-tuple-element.798) | copy-start | bytes 39940
  88.5 89.2 %copy-start.33 = (f32[3328]{0:T(1024)}, f32[3328]{0:T(1024)S(1)}, u32[]{:S(2)}) copy-start(f32[3328]{0:T(1024)S(1)} %get-tuple-element.799) | copy-start | bytes 39940
  88.5 89.2 %copy-start.35 = (f32[3328]{0:T(1024)}, f32[3328]{0:T(1024)S(1)}, u32[]{:S(2)}) copy-start(f32[3328]{0:T(1024)S(1)} %get-tuple-element.801) | copy-start | bytes 39940
  88.5 89.2 %copy-start.37 = (f32[3328]{0:T(1024)}, f32[3328]{0:T(1024)S(1)}, u32[]{:S(2)}) copy-start(f32[3328]{0:T(1024)S(1)} %get-tuple-element.800) | copy-start | bytes 39940
  88.5 122.9 %copy-start.67 = (f32[48]{0:T(128)}, f32[48]{0:T(128)S(1)}, u32[]{:S(2)}) copy-start(f32[48]{0:T(128)S(1)} %fusion.145) | copy-start | bytes 580
  88.7 89.0 %copy-start.50 = (f32[512]{0:T(512)}, f32[512]{0:T(512)S(1)}, u32[]{:S(2)}) copy-start(f32[512]{0:T(512)S(1)} %get-tuple-element.930) | copy-start | bytes 6148
  88.7 89.0 %copy-start.56 = (f32[512]{0:T(512)}, f32[512]{0:T(512)S(1)}, u32[]{:S(2)}) copy-start(f32[512]{0:T(512)S(1)} %get-tuple-element.929) | copy-start | bytes 6148
  88.7 89.0 %copy-start.58 = (f32[512]{0:T(512)}, f32[512]{0:T(512)S(1)}, u32[]{:S(2)}) copy-start(f32[512]{0:T(512)S(1)} %get-tuple-element.931) | copy-start | bytes 6148
  88.7 75.1 %copy-start.11 = (bf16[8,64,1536]{2,1,0:T(8,128)(2,1)}, bf16[8,64,1536]{2,1,0:T(8,128)(2,1)S(1)}, u32[]{:S(2)}) copy-start(bf16[8,64,1536]{2,1,0:T(8,128)(2,1)S(1)} %all-to-all-done) | copy-start | bytes 4718596
  88.7 352.1 %all-to-all-start.2 = ((bf16[8,64,1536]{2,1,0:T(8,128)(2,1)}), bf16[8,64,1536]{2,1,0:T(8,128)(2,1)}, u32[]{:S(2)}, u32[]{:S(2)}) async-start(bf16[8,64,1536]{2,1,0:T(8,128)(2,1)} %gather_fusion.2), calls=%async_computation.2 | async-start | bytes 3145728 | tf_op jit(solution)/shard_map/all_to_all | solution.py:127
  93.0 862.5 %reduce-scatter.8.cloned.1.call-start = ((), (), s32[]{:S(2)}) async-start(), calls=%async_computation.10 | async-start | bytes 21233664 | tf_op jit(solution)/shard_map/reduce_scatter | solution.py:186
  93.6 70.2 %copy-start.52 = (f32[512]{0:T(512)}, f32[512]{0:T(512)S(1)}, u32[]{:S(2)}) copy-start(f32[512]{0:T(512)S(1)} %add.194) | copy-start | bytes 6148
  93.6 70.2 %copy-start.54 = (f32[512]{0:T(512)}, f32[512]{0:T(512)S(1)}, u32[]{:S(2)}) copy-start(f32[512]{0:T(512)S(1)} %rsqrt.20) | copy-start | bytes 6148
  94.0 69.8 %copy-start.23 = (bf16[512,1536]{1,0:T(8,128)(2,1)}, bf16[512,1536]{1,0:T(8,128)(2,1)S(1)}, u32[]{:S(2)}) copy-start(bf16[512,1536]{1,0:T(8,128)(2,1)S(1)} %fusion.130) | copy-start | bytes 4718596
  440.8 22.9 %copy-start.61 = (f32[512]{0:T(512)}, f32[512]{0:T(512)S(1)}, u32[]{:S(2)}) copy-start(f32[512]{0:T(512)S(1)} %fusion.143) | copy-start | bytes 6148
  487.6 701.8 %reduce-scatter.6.cloned.1.call-start = ((), (), s32[]{:S(2)}) async-start(), calls=%async_computation.9 | async-start | bytes 45121536 | tf_op jit(solution)/shard_map/reduce_scatter | solution.py:179
  521.9 22.9 %copy-start.16 = (f32[256,256]{1,0:T(8,128)}, f32[256,256]{1,0:T(8,128)S(1)}, u32[]{:S(2)}) copy-start(f32[256,256]{1,0:T(8,128)S(1)} %fusion.253) | copy-start | bytes 786436 | tf_op jit(solution)/shard_map/transpose(jvp())/while
  522.0 22.8 %copy-start.15 = (f32[256,256]{1,0:T(8,128)}, f32[256,256]{1,0:T(8,128)S(1)}, u32[]{:S(2)}) copy-start(f32[256,256]{1,0:T(8,128)S(1)} %get-tuple-element.1171) | copy-start | bytes 786436 | tf_op jit(solution)/shard_map/transpose(jvp())/while
  522.1 22.8 %copy-start.21 = (pred[256,256]{1,0:T(8,128)(4,1)}, pred[256,256]{1,0:T(8,128)(4,1)S(1)}, u32[]{:S(2)}) copy-start(pred[256,256]{1,0:T(8,128)(4,1)S(1)} %get-tuple-element.1175) | copy-start | bytes 196612 | tf_op jit(solution)/shard_map/transpose(jvp())/while
  567.8 20.2 %copy-start.40 = (f32[1,256]{1,0:T(1,128)S(1)}, f32[1,256]{1,0:T(1,128)}, u32[]{:S(2)}) copy-start(f32[1,256]{1,0:T(1,128)} %copy-done.39) | copy-start | bytes 3076 | tf_op jit(solution)/shard_map/transpose(jvp())/while
  611.5 68.4 %copy-start.14 = (f32[2,256,128]{2,1,0:T(8,128)S(1)}, f32[2,256,128]{2,1,0:T(8,128)}, u32[]{:S(2)}) copy-start(f32[2,256,128]{2,1,0:T(8,128)} %copy-done.13) | copy-start | bytes 786436 | tf_op jit(solution)/shard_map/transpose(jvp())/while
  611.5 68.4 %copy-start.19 = (f32[2,256,48]{1,2,0:T(8,128)S(1)}, f32[2,256,48]{1,2,0:T(8,128)}, u32[]{:S(2)}) copy-start(f32[2,256,48]{1,2,0:T(8,128)} %copy-done.18) | copy-start | bytes 294916 | tf_op jit(solution)/shard_map/transpose(jvp())/while
  611.5 68.4 %copy-start.42 = (s32[2,256]{1,0:T(2,128)S(1)}, s32[2,256]{1,0:T(2,128)}, u32[]{:S(2)}) copy-start(s32[2,256]{1,0:T(2,128)} %copy-done.41) | copy-start | bytes 6148 | tf_op jit(solution)/shard_map/transpose(jvp())/while
  611.5 68.5 %copy-start.44 = (f32[2,256]{1,0:T(2,128)S(1)}, f32[2,256]{1,0:T(2,128)}, u32[]{:S(2)}) copy-start(f32[2,256]{1,0:T(2,128)} %copy-done.43) | copy-start | bytes 6148 | tf_op jit(solution)/shard_map/transpose(jvp())/while
  704.8 23.1 %copy-start.16 = (f32[256,256]{1,0:T(8,128)}, f32[256,256]{1,0:T(8,128)S(1)}, u32[]{:S(2)}) copy-start(f32[256,256]{1,0:T(8,128)S(1)} %fusion.253) | copy-start | bytes 786436 | tf_op jit(solution)/shard_map/transpose(jvp())/while
  704.9 23.0 %copy-start.15 = (f32[256,256]{1,0:T(8,128)}, f32[256,256]{1,0:T(8,128)S(1)}, u32[]{:S(2)}) copy-start(f32[256,256]{1,0:T(8,128)S(1)} %get-tuple-element.1171) | copy-start | bytes 786436 | tf_op jit(solution)/shard_map/transpose(jvp())/while
  704.9 23.0 %copy-start.21 = (pred[256,256]{1,0:T(8,128)(4,1)}, pred[256,256]{1,0:T(8,128)(4,1)S(1)}, u32[]{:S(2)}) copy-start(pred[256,256]{1,0:T(8,128)(4,1)S(1)} %get-tuple-element.1175) | copy-start | bytes 196612 | tf_op jit(solution)/shard_map/transpose(jvp())/while
  793.8 68.4 %copy-start.14 = (f32[2,256,128]{2,1,0:T(8,128)S(1)}, f32[2,256,128]{2,1,0:T(8,128)}, u32[]{:S(2)}) copy-start(f32[2,256,128]{2,1,0:T(8,128)} %copy-done.13) | copy-start | bytes 786436 | tf_op jit(solution)/shard_map/transpose(jvp())/while
  793.8 68.4 %copy-start.19 = (f32[2,256,48]{1,2,0:T(8,128)S(1)}, f32[2,256,48]{1,2,0:T(8,128)}, u32[]{:S(2)}) copy-start(f32[2,256,48]{1,2,0:T(8,128)} %copy-done.18) | copy-start | bytes 294916 | tf_op jit(solution)/shard_map/transpose(jvp())/while
  793.8 68.4 %copy-start.42 = (s32[2,256]{1,0:T(2,128)S(1)}, s32[2,256]{1,0:T(2,128)}, u32[]{:S(2)}) copy-start(s32[2,256]{1,0:T(2,128)} %copy-done.41) | copy-start | bytes 6148 | tf_op jit(solution)/shard_map/transpose(jvp())/while
  793.8 68.5 %copy-start.44 = (f32[2,256]{1,0:T(2,128)S(1)}, f32[2,256]{1,0:T(2,128)}, u32[]{:S(2)}) copy-start(f32[2,256]{1,0:T(2,128)} %copy-done.43) | copy-start | bytes 6148 | tf_op jit(solution)/shard_map/transpose(jvp())/while
  953.5 235.9 %copy-start.12 = (bf16[8,64,1536]{2,1,0:T(8,128)(2,1)S(1)}, bf16[8,64,1536]{2,1,0:T(8,128)(2,1)}, u32[]{:S(2)}) copy-start(bf16[8,64,1536]{2,1,0:T(8,128)(2,1)} %copy-done.11) | copy-start | bytes 4718596
  953.5 235.9 %copy-start.48 = (f32[8,1,384]{2,1,0:T(1,128)S(1)}, f32[8,1,384]{2,1,0:T(1,128)}, u32[]{:S(2)}) copy-start(f32[8,1,384]{2,1,0:T(1,128)} %convert_element_type.127) | copy-start | bytes 36868
  953.5 235.9 %copy-start.62 = (f32[512]{0:T(512)S(1)}, f32[512]{0:T(512)}, u32[]{:S(2)}) copy-start(f32[512]{0:T(512)} %copy-done.61) | copy-start | bytes 6148
  953.5 323.9 %reduce-scatter.10.cloned.1.call-start = ((), (), s32[]{:S(2)}) async-start(), calls=%async_computation.11 | async-start | bytes 1916928
  955.5 546.3 %all-reduce.37.cloned.1.call-start = ((), (), s32[]{:S(2)}) async-start(), calls=%async_computation.12 | async-start | bytes 14745600 | tf_op jit(solution)/shard_map/psum | solution.py:188
  1200.4 32.5 %all-to-all-start.1 = ((bf16[8,64,1536]{2,1,0:T(8,128)(2,1)}), bf16[8,64,1536]{2,1,0:T(8,128)(2,1)S(1)}, u32[]{:S(2)}, u32[]{:S(2)}) async-start(bf16[8,64,1536]{2,1,0:T(8,128)(2,1)} %bitcast.460), calls=%async_computation.1 | async-start | bytes 3145728 | tf_op jit(solution)/shard_map/all_to_all | solution.py:194
  1204.3 24.1 %copy-start.53 = (f32[512]{0:T(512)S(1)}, f32[512]{0:T(512)}, u32[]{:S(2)}) copy-start(f32[512]{0:T(512)} %copy-done.52) | copy-start | bytes 6148
  1232.9 67.7 %all-to-all-start.3 = ((bf16[8,64,1536]{2,1,0:T(8,128)(2,1)}), bf16[8,64,1536]{2,1,0:T(8,128)(2,1)S(1)}, u32[]{:S(2)}, u32[]{:S(2)}) async-start(bf16[8,64,1536]{2,1,0:T(8,128)(2,1)} %bitcast.459), calls=%async_computation.3 | async-start | bytes 3145728 | tf_op jit(solution)/shard_map/all_to_all | solution.py:195
  (72 other events, 604.3 us)
Sparse Core Ops, SparseCore 0:
  10.0 135.7 all-gather.4
  147.7 58.8 all-gather.6
  487.7 126.1 reduce-scatter.7
  953.6 235.7 reduce-scatter.5
  1193.1 47.4 reduce-scatter.9
  1243.0 258.6 all-reduce.36
where the time goes:
time: 1530 us; the launch traced here: 1520 us
  waiting for transfers between devices  486 us (32%)
  local copies, waits for them, and re-layouts  433 us (28%)
  matrix products  282 us (18%)
  other arithmetic  132 us (9%)
  blocking collectives  120 us (8%)
  loops' own time  24.5 us (2%)
  between operations  19.9 us (1%)
  starting transfers between devices  17.7 us (1%)
    dynamic_update_slice x16, local copies, waits for them, and re-layouts, mixer_core(): lax.scan(jax.checkpoint(block_step), start_state, scanned)  280 us
    reduce_scatter x1, waiting for transfers between devices, per_device(): lax.psum_scatter(in_term, 'fsdp', scatter_dimension=0, tiled=True)  234 us
    psum x1, waiting for transfers between devices, per_device(): lax.psum((s_gain, s_in, s_conv, s_cbias, s_dtb, s_alog, s_dskip, s_ggain,...  199 us
    dot_general x6, matrix products, block_step(): jnp.einsum('tsh,shp->thp', mixing, weighted, precision=lax.Precision.HIGH...  103 us
    unnamed x2, blocking collectives  82.1 us
    all_gather x1, waiting for transfers between devices, per_device(): lax.all_gather(in_weight, 'fsdp', axis=0, tiled=True)  51.8 us
    dot_general x6, matrix products, block_step(): jnp.einsum('sn,shp->hnp', b_input, weighted * end_weight[:, :, None], pre...  38.5 us
    dot_general x2, matrix products, contract_cols(): lax.dot_general(left, right, (((1,), (1,)), ((), ())), preferred_element_...  35.1 us
  transfers between devices with their start and end apart: 10, of which 3 were waited for; matrix products, arithmetic and copies ran while one was open for 53% of the time, Pallas kernels for 0%

commit v1 on v0

v1 whole, which is shorter than its diff:
```python
import functools

import jax
import jax.numpy as jnp
from jax import lax
from jax.experimental import pallas as pl
from jax.experimental.pallas import tpu as pltpu
from jax.sharding import PartitionSpec as P

DI = 3072
HEAD_DIM = 64
NSTATE = 128
KW = 4
HEADS = 48
BCD = 384

epsilon = 1e-05


Q = 128
GROUP = 8
LANES = GROUP * HEAD_DIM
NEG = -1e30
VMEM = 56 * 1024 * 1024


def dot32(a, b, dims=(((1,), (0,)), ((), ())), precision=None):
    return lax.dot_general(a, b, dims, preferred_element_type=jnp.float32, precision=precision)


NT = (((1,), (1,)), ((), ()))


def row_ids(start, rows, cols):
    return lax.broadcasted_iota(jnp.int32, (rows, cols), 0) + start


def shifted_down(ref, cols, c, first, width):
    if c == 0:
        tall = jnp.concatenate([jnp.zeros((8, width), jnp.float32), ref[0:Q, cols]], axis=0)
    else:
        tall = ref[c * Q - 8 : c * Q + Q, cols]
    place = row_ids(c * Q, Q, width)
    outs = [tall[8:]]
    for j in range(1, KW):
        moved = pltpu.roll(tall, j, 0)[8:]
        keep = (place >= j) & ((place < first) | (place >= first + j))
        outs.append(jnp.where(keep, moved, 0.0))
    return outs


def conv_back(ref, cols, c, first, width, taps):
    tall = ref[c * Q : c * Q + Q + 8, cols]
    place = row_ids(c * Q, Q, width)
    total = taps[KW - 1] * tall[:Q]
    for j in range(1, KW):
        moved = pltpu.roll(tall, Q + 8 - j, 0)[:Q]
        keep = (place < first - j) | (place >= first)
        total = total + taps[KW - 1 - j] * jnp.where(keep, moved, 0.0)
    return total


def sum_rows(v):
    return jnp.sum(v, axis=0, keepdims=True)


def prep_kernel(first_ref, bcd_ref, conv_ref, head_ref, bn_ref, cn_ref, bt_ref, ct_ref, s_ref, st_ref, cum_ref, cp_ref, cumt_ref, cpt_ref):
    first = first_ref[0]
    tri = (row_ids(0, Q, Q) >= lax.broadcasted_iota(jnp.int32, (Q, Q), 1)).astype(jnp.float32)
    rate = -jnp.exp(head_ref[1:2, :])
    lane = lax.broadcasted_iota(jnp.int32, (Q, 128), 1)
    for c in range(bcd_ref.shape[0] // Q):
        rows = slice(c * Q, c * Q + Q)
        moved = shifted_down(bcd_ref, slice(0, 2 * NSTATE), c, first, 2 * NSTATE)
        mixed = conv_ref[4:5, :] + conv_ref[3:4, :] * moved[0]
        for j in range(1, KW):
            mixed = mixed + conv_ref[KW - 1 - j : KW - j, :] * moved[j]
        act = mixed * jax.nn.sigmoid(mixed)
        b32, c32 = act[:, :NSTATE], act[:, NSTATE:]
        b16, c16 = b32.astype(jnp.bfloat16), c32.astype(jnp.bfloat16)
        bn_ref[rows, :] = b16
        cn_ref[rows, :] = c16
        bt_ref[:, rows] = b32.T.astype(jnp.bfloat16)
        ct_ref[:, rows] = c32.T.astype(jnp.bfloat16)
        s_ref[rows, :] = dot32(c16, b16, NT)
        st_ref[rows, :] = dot32(b16, c16, NT)
        raw = jnp.where(lane < HEADS, bcd_ref[rows, 2 * NSTATE :] + head_ref[0:1, :], 0.0)
        step = jax.nn.softplus(raw)
        cum = dot32(tri, rate * step, precision=lax.Precision.HIGHEST)
        cp = cum - jnp.log(jnp.maximum(step, 1e-37))
        cum_ref[rows, :] = cum
        cp_ref[rows, :] = cp
        cumt_ref[:, rows] = cum.T
        cpt_ref[:, rows] = cp.T


def chunk_masks(first, c, transposed):
    base = c * Q
    row = row_ids(base, Q, Q)
    col = lax.broadcasted_iota(jnp.int32, (Q, Q), 1) + base
    ordered = (col >= row) if transposed else (row >= col)
    inside = ordered & ((row >= first) == (col >= first))
    carry = ((row >= first) == (base - 1 >= first)) & (base > 0)
    last = (row >= first) == (base + Q - 1 >= first)
    through = (base > 0) & ((base + Q - 1 >= first) == (base - 1 >= first))
    return inside, carry, last, through


def lane_column(values, k):
    return jnp.broadcast_to(values[:, k : k + 1], (Q, Q))


def forward_kernel(base, first_ref, z_ref, x_ref, conv_ref, gain_ref, bn_ref, cn_ref, bt_ref, s_ref, cum_ref, cp_ref, cpt_ref, y_ref, g_ref, sq_ref, states_ref, state):
    first = first_ref[0]
    group = base + pl.program_id(0)
    half = lax.broadcasted_iota(jnp.int32, (Q, Q), 1) < HEAD_DIM
    state[...] = jnp.zeros_like(state)

    @pl.when(pl.program_id(0) == 0)
    def _():
        sq_ref[...] = jnp.zeros_like(sq_ref)

    shift = (Q - GROUP * group) % Q
    for c in range(x_ref.shape[0] // Q):
        rows = slice(c * Q, c * Q + Q)
        inside, carry, last, through = chunk_masks(first, c, False)
        cum = pltpu.roll(cum_ref[rows, :], shift, 1)
        cp = pltpu.roll(cp_ref[rows, :], shift, 1)
        cpt = cpt_ref[pl.ds(pl.multiple_of(group * GROUP, GROUP), GROUP), rows]
        scores = s_ref[rows, :]
        c16 = cn_ref[rows, :]
        squares = jnp.zeros((Q, Q), jnp.float32)
        for p in range(GROUP // 2):
            cols = slice(p * Q, p * Q + Q)
            moved = shifted_down(x_ref, cols, c, first, Q)
            mixed = conv_ref[4:5, cols] + conv_ref[3:4, cols] * moved[0]
            for j in range(1, KW):
                mixed = mixed + conv_ref[KW - 1 - j : KW - j, cols] * moved[j]
            xs = mixed * jax.nn.sigmoid(mixed)
            x16 = xs.astype(jnp.bfloat16)
            locals_, cums, cps = [], [], []
            for e in range(2):
                k = 2 * p + e
                cum_b = lane_column(cum, k)
                decay = jnp.exp(jnp.where(inside, cum_b - cpt[k : k + 1, :], NEG))
                locals_.append(dot32((scores * decay).astype(jnp.bfloat16), x16))
                cums.append(cum_b)
                cps.append(lane_column(cp, k))
            cum_pair = jnp.where(half, cums[0], cums[1])
            cp_pair = jnp.where(half, cps[0], cps[1])
            y = jnp.where(half, locals_[0], locals_[1])
            old = state[:, cols]
            old16 = old.astype(jnp.bfloat16)
            states_ref[c * NSTATE : (c + 1) * NSTATE, cols] = old16
            if c > 0:
                y = y + jnp.where(carry, jnp.exp(cum_pair), 0.0) * dot32(c16, old16)
            y_ref[rows, cols] = y
            end = cum_pair[Q - 1 : Q, :]
            weight = jnp.where(last, jnp.exp(end - cp_pair), 0.0)
            fresh = dot32(bt_ref[:, rows], (weight * xs).astype(jnp.bfloat16))
            keep = jnp.where(through, jnp.exp(end), 0.0)
            state[:, cols] = fresh if c == 0 else keep * old + fresh
            zv = z_ref[rows, cols]
            g = (y + gain_ref[0:1, cols] * xs) * (zv * jax.nn.sigmoid(zv))
            g_ref[rows, cols] = g
            squares = squares + g * g
        sq_ref[rows, :] += squares


def split_dot(values, right):
    high = values.astype(jnp.bfloat16)
    low = (values - high.astype(jnp.float32)).astype(jnp.bfloat16)
    return dot32(high, right) + dot32(low, right)


def backward_kernel(base, first_ref, z_ref, x_ref, y_ref, dg_ref, rk_ref, conv_ref, gain_ref, bn_ref, cn_ref, ct_ref, st_ref, cum_ref, cp_ref, cumt_ref, states_ref, dz_ref, dx_ref, grads_ref, dst_ref, db_ref, dc_ref, u_ref, v_ref, w_ref, flow_ref, dstate, dconv):
    first = first_ref[0]
    group = base + pl.program_id(0)
    lane = lax.broadcasted_iota(jnp.int32, (Q, Q), 1)
    half = lane < HEAD_DIM
    dstate[...] = jnp.zeros_like(dstate)
    rows_all = x_ref.shape[0]
    dconv[rows_all : rows_all + 8, :] = jnp.zeros((8, dconv.shape[1]), jnp.float32)
    grads_ref[...] = jnp.zeros_like(grads_ref)
    flow_ref[...] = jnp.zeros_like(flow_ref)

    @pl.when(pl.program_id(0) == 0)
    def _():
        for ref in (dst_ref, db_ref, dc_ref, u_ref, v_ref, w_ref):
            ref[...] = jnp.zeros_like(ref)

    shift = (Q - GROUP * group) % Q
    chunks = rows_all // Q
    for c in range(chunks - 1, -1, -1):
        rows = slice(c * Q, c * Q + Q)
        inside, carry, last, through = chunk_masks(first, c, True)
        cum = pltpu.roll(cum_ref[rows, :], shift, 1)
        cp = pltpu.roll(cp_ref[rows, :], shift, 1)
        cumt = cumt_ref[pl.ds(pl.multiple_of(group * GROUP, GROUP), GROUP), rows]
        scores_t = st_ref[rows, :]
        b16, c16t = bn_ref[rows, :], ct_ref[:, rows]
        scale = lane_column(rk_ref[rows, :], 0)
        pull = lane_column(rk_ref[rows, :], 1)
        dst = jnp.zeros((Q, Q), jnp.float32)
        db = jnp.zeros((Q, NSTATE), jnp.float32)
        dc = jnp.zeros((Q, NSTATE), jnp.float32)
        us, vs, ws = (jnp.zeros((Q, Q), jnp.float32) for _ in range(3))
        for p in range(GROUP // 2):
            cols = slice(p * Q, p * Q + Q)
            moved = shifted_down(x_ref, cols, c, first, Q)
            mixed = conv_ref[4:5, cols] + conv_ref[3:4, cols] * moved[0]
            for j in range(1, KW):
                mixed = mixed + conv_ref[KW - 1 - j : KW - j, cols] * moved[j]
            sx = jax.nn.sigmoid(mixed)
            xs = mixed * sx
            x16 = xs.astype(jnp.bfloat16)
            zv = z_ref[rows, cols]
            sz = jax.nn.sigmoid(zv)
            silu_z = zv * sz
            skip, gain = gain_ref[0:1, cols], gain_ref[1:2, cols]
            y = y_ref[rows, cols]
            ssm = y + skip * xs
            g = ssm * silu_z
            gs = dg_ref[rows, cols] * scale
            grads_ref[6:7, cols] += sum_rows(gs * g)
            d_g = gain * gs - g * pull
            dz_ref[rows, cols] = (d_g * ssm * (sz + silu_z * (1.0 - sz))).astype(dz_ref.dtype)
            d_ssm = d_g * silu_z
            grads_ref[5:6, cols] += sum_rows(d_ssm * xs)
            dy16 = d_ssm.astype(jnp.bfloat16)
            locals_, cums, cps = [], [], []
            for e in range(2):
                k = 2 * p + e
                cp_b = lane_column(cp, k)
                decay = jnp.exp(jnp.where(inside, cumt[k : k + 1, :] - cp_b, NEG))
                locals_.append(dot32((scores_t * decay).astype(jnp.bfloat16), dy16))
                x_half = jnp.where(half == (e == 0), x16, jnp.zeros_like(x16))
                dst = dst + decay * dot32(x_half, dy16, NT)
                cums.append(lane_column(cum, k))
                cps.append(cp_b)
            cum_pair = jnp.where(half, cums[0], cums[1])
            cp_pair = jnp.where(half, cps[0], cps[1])
            dx = jnp.where(half, locals_[0], locals_[1])
            dy32, x32 = dy16.astype(jnp.float32), x16.astype(jnp.float32)
            pick = (lane == GROUP * group + 2 * p + (row_ids(0, Q, Q) >= HEAD_DIM).astype(jnp.int32)).astype(jnp.bfloat16)
            in_dot = x32 * dx
            us = us + split_dot(dy32 * y - in_dot, pick)
            vs = vs + split_dot(in_dot, pick)
            end = cum_pair[Q - 1 : Q, :]
            keep = jnp.where(through, jnp.exp(end), 0.0)
            if c < chunks - 1:
                later = dstate[:, cols]
                later16 = later.astype(jnp.bfloat16)
                weight = jnp.where(last, jnp.exp(end - cp_pair), 0.0)
                carried = weight * dot32(b16, later16)
                dx = dx + carried
                ws = ws + split_dot(xs * carried, pick)
                db = db + dot32((weight * xs).astype(jnp.bfloat16), later16, NT)
            if c > 0:
                ey16 = (jnp.where(carry, jnp.exp(cum_pair), 0.0) * d_ssm).astype(jnp.bfloat16)
                old16 = states_ref[c * NSTATE : (c + 1) * NSTATE, cols]
                dc = dc + dot32(ey16, old16, NT)
                fresh = dot32(c16t, ey16)
                if c < chunks - 1:
                    flow_ref[c : c + 1, cols] = keep * sum_rows(later * old16.astype(jnp.float32))
                    fresh = keep * later + fresh
                dstate[:, cols] = fresh
            d_mixed = (dx + skip * d_ssm) * (sx + xs * (1.0 - sx))
            dconv[rows, cols] = d_mixed
            grads_ref[4:5, cols] += sum_rows(d_mixed)
            for j in range(KW):
                grads_ref[KW - 1 - j : KW - j, cols] += sum_rows(d_mixed * moved[j])
            taps = [conv_ref[i : i + 1, cols] for i in range(KW)]
            dx_ref[rows, cols] = conv_back(dconv, cols, c, first, Q, taps).astype(dx_ref.dtype)
        dst_ref[rows, :] += dst
        db_ref[rows, :] += db
        dc_ref[rows, :] += dc
        u_ref[rows, :] += us
        v_ref[rows, :] += vs
        w_ref[rows, :] += ws


def post_kernel(first_ref, bcd_ref, conv_ref, head_ref, bn_ref, cn_ref, dst_ref, db_ref, dc_ref, u_ref, v_ref, w_ref, flow_ref, d_ref, grads_ref, hgrads_ref, dconv):
    first = first_ref[0]
    rows_all = bcd_ref.shape[0]
    wide = 2 * NSTATE
    dconv[rows_all : rows_all + 8, :] = jnp.zeros((8, wide), jnp.float32)
    grads_ref[...] = jnp.zeros_like(grads_ref)
    hgrads_ref[...] = jnp.zeros_like(hgrads_ref)
    lane = lax.broadcasted_iota(jnp.int32, (Q, 128), 1)
    rate = -jnp.exp(head_ref[1:2, :])
    spread = (lax.broadcasted_iota(jnp.int32, (DI, 128), 0) // HEAD_DIM == lax.broadcasted_iota(jnp.int32, (DI, 128), 1)).astype(jnp.float32)
    flow = dot32(flow_ref[...], spread, precision=lax.Precision.HIGHEST)
    row, col = row_ids(0, Q, Q), lax.broadcasted_iota(jnp.int32, (Q, Q), 1)
    earlier_sum = (col < row).astype(jnp.float32)
    for c in range(rows_all // Q - 1, -1, -1):
        rows = slice(c * Q, c * Q + Q)
        moved = shifted_down(bcd_ref, slice(0, wide), c, first, wide)
        mixed = conv_ref[4:5, :] + conv_ref[3:4, :] * moved[0]
        for j in range(1, KW):
            mixed = mixed + conv_ref[KW - 1 - j : KW - j, :] * moved[j]
        sx = jax.nn.sigmoid(mixed)
        dst = jnp.sum(dst_ref[:, rows, :], axis=0)
        d_b = jnp.sum(db_ref[:, rows, :], axis=0) + dot32(dst.astype(jnp.bfloat16), cn_ref[rows, :])
        d_c = jnp.sum(dc_ref[:, rows, :], axis=0) + dot32(dst.T.astype(jnp.bfloat16), bn_ref[rows, :])
        d_mixed = jnp.concatenate([d_b, d_c], axis=1) * (sx + mixed * sx * (1.0 - sx))
        dconv[rows, :] = d_mixed
        grads_ref[4:5, :] += sum_rows(d_mixed)
        for j in range(KW):
            grads_ref[KW - 1 - j : KW - j, :] += sum_rows(d_mixed * moved[j])
        taps = [conv_ref[i : i + 1, :] for i in range(KW)]
        d_ref[rows, :wide] = conv_back(dconv, slice(0, wide), c, first, wide, taps).astype(d_ref.dtype)
        carried = jnp.sum(w_ref[:, rows, :], axis=0)
        later_sum = ((col >= row) & ((row + c * Q >= first) == (col + c * Q >= first))).astype(jnp.float32)
        d_la = dot32(later_sum, jnp.sum(u_ref[:, rows, :], axis=0), precision=lax.Precision.HIGHEST)
        d_la = d_la + dot32(earlier_sum, carried, precision=lax.Precision.HIGHEST) + flow[c : c + 1, :]
        d_log = jnp.sum(v_ref[:, rows, :], axis=0) + carried
        raw = bcd_ref[rows, wide:] + head_ref[0:1, :]
        step = jax.nn.softplus(raw)
        sig = jax.nn.sigmoid(raw)
        ratio = jnp.where(raw < -17.0, 1.0, sig / jnp.maximum(step, 1e-37))
        d_raw = jnp.where(lane < HEADS, d_log * ratio + d_la * rate * sig, 0.0)
        d_ref[rows, wide:] = d_raw.astype(d_ref.dtype)
        hgrads_ref[0:1, :] += sum_rows(d_raw)
        hgrads_ref[1:2, :] += sum_rows(jnp.where(lane < HEADS, d_la * rate * step, 0.0))


def smem():
    return pl.BlockSpec(memory_space=pltpu.SMEM)


def whole(shape):
    return pl.BlockSpec(shape, lambda g: (0,) * len(shape))


def run_prep(first, bcd, conv, heads):
    rows = bcd.shape[0]
    f32, b16 = jnp.float32, jnp.bfloat16
    shapes = [((rows, 128), b16), ((rows, 128), b16), ((128, rows), b16), ((128, rows), b16), ((rows, Q), f32), ((rows, Q), f32), ((rows, 128), f32), ((rows, 128), f32), ((128, rows), f32), ((128, rows), f32)]
    return pl.pallas_call(
        prep_kernel,
        grid=(1,),
        in_specs=[smem(), whole((rows, BCD)), whole((8, 2 * NSTATE)), whole((8, 128))],
        out_specs=[whole(s) for s, _ in shapes],
        out_shape=[jax.ShapeDtypeStruct(s, d) for s, d in shapes],
        compiler_params=pltpu.CompilerParams(vmem_limit_bytes=VMEM),
    )(first, bcd, conv, heads)


def run_forward(base, count, first, z, x, conv, gains, prep):
    rows = x.shape[0]
    bn, cn, bt, ct, s, st, cum, cp, cumt, cpt = prep
    f32, b16 = jnp.float32, jnp.bfloat16
    chunks = rows // Q
    at = lambda g: (0, g + base)
    here = lambda g: (0, g)
    return pl.pallas_call(
        functools.partial(forward_kernel, base),
        grid=(count,),
        in_specs=[smem(), pl.BlockSpec((rows, LANES), at), pl.BlockSpec((rows, LANES), at), pl.BlockSpec((8, LANES), at), pl.BlockSpec((8, LANES), at)]
        + [whole(v.shape) for v in (bn, cn, bt, s, cum, cp, cpt)],
        out_specs=[pl.BlockSpec((rows, LANES), here), pl.BlockSpec((rows, LANES), here), whole((rows, Q)), pl.BlockSpec((chunks * NSTATE, LANES), here)],
        out_shape=[jax.ShapeDtypeStruct((rows, count * LANES), f32), jax.ShapeDtypeStruct((rows, count * LANES), f32), jax.ShapeDtypeStruct((rows, Q), f32), jax.ShapeDtypeStruct((chunks * NSTATE, count * LANES), b16)],
        scratch_shapes=[pltpu.VMEM((NSTATE, LANES), f32)],
        compiler_params=pltpu.CompilerParams(vmem_limit_bytes=VMEM),
        cost_estimate=pl.CostEstimate(flops=count * 1200000000, bytes_accessed=count * 6000000, transcendentals=0),
    )(first, z, x, conv, gains, bn, cn, bt, s, cum, cp, cpt)


def run_backward(base, count, first, z, x, y, dg, rk, conv, gains, prep, states):
    rows = x.shape[0]
    bn, cn, bt, ct, s, st, cum, cp, cumt, cpt = prep
    f32, b16 = jnp.float32, jnp.bfloat16
    chunks = rows // Q
    at = lambda g: (0, g + base)
    here = lambda g: (0, g)
    block = pl.BlockSpec((rows, LANES), at)
    local = pl.BlockSpec((rows, LANES), here)
    sums = [(rows, Q), (rows, NSTATE), (rows, NSTATE), (rows, 128), (rows, 128), (rows, 128)]
    return pl.pallas_call(
        functools.partial(backward_kernel, base),
        grid=(count,),
        in_specs=[smem(), block, block, block, block, whole(rk.shape), pl.BlockSpec((8, LANES), at), pl.BlockSpec((8, LANES), at)]
        + [whole(v.shape) for v in (bn, cn, ct, st, cum, cp, cumt)]
        + [pl.BlockSpec((chunks * NSTATE, LANES), at)],
        out_specs=[local, local, pl.BlockSpec((8, LANES), here)] + [whole(v) for v in sums] + [pl.BlockSpec((8, LANES), here)],
        out_shape=[jax.ShapeDtypeStruct((rows, count * LANES), b16)] * 2 + [jax.ShapeDtypeStruct((8, count * LANES), f32)] + [jax.ShapeDtypeStruct(v, f32) for v in sums] + [jax.ShapeDtypeStruct((8, count * LANES), f32)],
        scratch_shapes=[pltpu.VMEM((NSTATE, LANES), f32), pltpu.VMEM((rows + 8, LANES), f32)],
        compiler_params=pltpu.CompilerParams(vmem_limit_bytes=VMEM),
        cost_estimate=pl.CostEstimate(flops=count * 4000000000, bytes_accessed=count * 8000000, transcendentals=0),
    )(first, z, x, y, dg, rk, conv, gains, bn, cn, ct, st, cum, cp, cumt, states)


def run_post(first, bcd, conv, heads, prep, *sums):
    rows = bcd.shape[0]
    bn, cn = prep[0], prep[1]
    f32 = jnp.float32
    return pl.pallas_call(
        post_kernel,
        grid=(1,),
        in_specs=[smem(), whole((rows, BCD)), whole((8, 2 * NSTATE)), whole((8, 128)), whole(bn.shape), whole(cn.shape)] + [whole(t.shape) for t in sums],
        out_specs=[whole((rows, BCD)), whole((8, 2 * NSTATE)), whole((8, 128))],
        out_shape=[jax.ShapeDtypeStruct((rows, BCD), jnp.bfloat16), jax.ShapeDtypeStruct((8, 2 * NSTATE), f32), jax.ShapeDtypeStruct((8, 128), f32)],
        scratch_shapes=[pltpu.VMEM((rows + 8, 2 * NSTATE), f32)],
        compiler_params=pltpu.CompilerParams(vmem_limit_bytes=VMEM),
    )(first, bcd, conv, heads, bn, cn, *sums)


def contract_rows(left, right, kind=jnp.float32):
    return lax.dot_general(left, right, (((0,), (0,)), ((), ())), preferred_element_type=kind)


def contract_cols(left, right):
    return lax.dot_general(left, right, NT, preferred_element_type=jnp.float32)


def pad_lanes(v, width):
    return jnp.pad(v, ((0, 0), (0, width - v.shape[1])))


def per_device(tokens, cotangent, lengths, dealing, norm_gain, in_weight, conv_weight, conv_bias, dt_bias, a_log, d_skip, gated_gain, out_weight):
    f32, b16 = jnp.float32, jnp.bfloat16
    groups = lax.axis_size("fsdp")
    tok_rows, width = tokens.shape
    block_rows = tok_rows // groups
    targets = dealing.reshape(groups)
    inverse = jnp.argsort(targets)
    first = lengths.reshape(-1)[:1]

    small = jnp.concatenate([norm_gain, conv_weight.reshape(-1), conv_bias, dt_bias, a_log, d_skip, gated_gain])
    sizes = [v.size for v in (norm_gain, conv_weight, conv_bias, dt_bias, a_log, d_skip, gated_gain)]
    small_all = lax.all_gather(jnp.pad(small, (0, -small.size % 128)), "fsdp", axis=0, tiled=False).astype(f32)
    in_full = lax.all_gather(in_weight, "fsdp", axis=0, tiled=True)
    out_full = lax.all_gather(out_weight, "fsdp", axis=0, tiled=True)

    def deal(values):
        blocks = values.reshape(groups, block_rows, width)[inverse]
        return lax.all_to_all(blocks, "fsdp", split_axis=0, concat_axis=0, tiled=True).reshape(tok_rows, width)

    def undeal(values):
        blocks = lax.all_to_all(values.reshape(groups, block_rows, width), "fsdp", split_axis=0, concat_axis=0, tiled=True)
        return blocks[targets].reshape(tok_rows, width)

    hidden = deal(tokens).astype(f32)
    cot = deal(cotangent)

    ends, parts = 0, []
    for size in sizes:
        parts.append(small_all[:, ends : ends + size])
        ends += size
    gain = parts[0].reshape(1, -1)
    taps = parts[1].reshape(groups, KW, -1).transpose(1, 0, 2).reshape(KW, -1)
    bias, step_bias, rate, skip, ggain = (v.reshape(1, -1) for v in parts[2:])
    conv = jnp.concatenate([taps, bias, jnp.zeros((3, bias.shape[1]), f32)])
    heads = pad_lanes(jnp.concatenate([step_bias, rate, jnp.zeros((6, HEADS), f32)]), 128)
    gains = jnp.concatenate([jnp.repeat(skip, HEAD_DIM, axis=1), ggain, jnp.zeros((6, DI), f32)])
    conv_x, conv_bc = conv[:, :DI], conv[:, DI:]

    rn = lax.rsqrt(jnp.mean(hidden * hidden, axis=-1, keepdims=True) + epsilon)
    normed = (hidden * rn * gain).astype(b16)
    w_z, w_x, w_b = in_full[:, :DI], in_full[:, DI : 2 * DI], pad_lanes(in_full[:, 2 * DI :], BCD)
    z, x, bcd = (jnp.dot(normed, w, preferred_element_type=f32) for w in (w_z, w_x, w_b))

    prep = run_prep(first, bcd, conv_bc, heads)
    y, g, sq, states = run_forward(0, HEADS // GROUP, first, z, x, conv_x, gains, prep)
    r = lax.rsqrt(jnp.sum(sq, axis=-1, keepdims=True) / DI + epsilon)
    gated = (g * r * ggain).astype(b16)
    branch = jnp.dot(gated, out_full, preferred_element_type=f32)
    result = (hidden + branch).astype(b16)
    output = undeal(result)
    cot32 = cot.astype(f32)
    pull = r * r * (jnp.sum(cot32 * branch, axis=-1, keepdims=True) / DI)
    rk = pad_lanes(jnp.concatenate([r, pull], axis=1), 128)
    d_gated = contract_cols(cot, out_full)
    out_term = contract_rows(gated, cot, b16)
    s_out = lax.psum_scatter(out_term, "fsdp", scatter_dimension=0, tiled=True)

    d_z, d_x, xgrads, *sums, flow = run_backward(0, HEADS // GROUP, first, z, x, y, d_gated, rk, conv_x, gains, prep, states)
    d_b, bgrads, hgrads = run_post(first, bcd, conv_bc, heads, prep, *[t[None] for t in sums], flow)
    in_term = jnp.concatenate([contract_rows(normed, d_z, b16), contract_rows(normed, d_x, b16), contract_rows(normed, d_b, b16)[:, : in_weight.shape[1] - 2 * DI]], axis=1)
    s_in = lax.psum_scatter(in_term, "fsdp", scatter_dimension=0, tiled=True)
    d_normed = contract_cols(d_z, w_z) + contract_cols(d_x, w_x) + contract_cols(d_b, w_b)
    g_gain = jnp.sum(d_normed * hidden * rn, axis=0)
    d_scaled = d_normed * gain
    d_hidden = rn * d_scaled - hidden * (rn * rn * rn * jnp.mean(hidden * d_scaled, axis=-1, keepdims=True))
    input_grad = undeal((cot32 + d_hidden).astype(b16))

    g_conv = jnp.concatenate([xgrads[:KW], bgrads[:KW]], axis=1)
    g_cbias = jnp.concatenate([xgrads[KW], bgrads[KW]])
    g_dskip = jnp.sum(xgrads[5].reshape(HEADS, HEAD_DIM), axis=1)
    spread = [
        g_gain.reshape(groups, -1),
        g_conv.reshape(KW, groups, -1).transpose(1, 0, 2).reshape(groups, -1),
        g_cbias.reshape(groups, -1),
        hgrads[0, :HEADS].reshape(groups, -1),
        hgrads[1, :HEADS].reshape(groups, -1),
        g_dskip.reshape(groups, -1),
        xgrads[6].reshape(groups, -1),
    ]
    packed = pad_lanes(jnp.concatenate(spread, axis=1), small_all.shape[1])
    s_small = jnp.sum(lax.all_to_all(packed, "fsdp", split_axis=0, concat_axis=0, tiled=True), axis=0)
    r_small = jnp.sum(lax.all_gather(s_small, "rep", axis=0, tiled=False), axis=0)
    r_in = lax.psum(s_in, "rep").astype(f32)
    r_out = lax.psum(s_out, "rep").astype(f32)
    ends, outs = 0, []
    for size in sizes:
        outs.append(r_small[ends : ends + size])
        ends += size
    return (output, input_grad, outs[0], r_in, outs[1].reshape(conv_weight.shape), outs[2], outs[3], outs[4], outs[5], outs[6], r_out)


def solution(mesh):
    placed = (
        P(("rep", "fsdp"), None),
        P(("rep", "fsdp"), None),
        P("rep", "fsdp", None),
        P("rep", "fsdp", None),
        P("fsdp"),
        P("fsdp", None),
        P(None, "fsdp"),
        P("fsdp"),
        P("fsdp"),
        P("fsdp"),
        P("fsdp"),
        P("fsdp"),
        P("fsdp", None),
    )
    return jax.shard_map(
        per_device,
        mesh=mesh,
        in_specs=placed,
        out_specs=(
            P(("rep", "fsdp"), None),
            P(("rep", "fsdp"), None),
            P("fsdp"),
            P("fsdp", None),
            P(None, "fsdp"),
            P("fsdp"),
            P("fsdp"),
            P("fsdp"),
            P("fsdp"),
            P("fsdp"),
            P("fsdp", None),
        ),
        check_vma=False,
    )
```

time: 1530 us -> 612 us (0.40)
  local copies, waits for them, and re-layouts: 433 us -> 32.1 us
  waiting for transfers between devices: 486 us -> 273 us
  matrix products: 282 us -> 91.9 us
  other arithmetic: 132 us -> 36.1 us
  Pallas kernels: 0 us -> 85.1 us
  blocking collectives: 120 us -> 58.1 us
  loops' own time: 24.5 us -> 0 us
    dynamic_update_slice x16 -> x0, local copies, waits for them, and re-layouts: 280 us -> none  [mixer_core(): lax.scan(jax.checkpoint(block_step), start_state, scanned)]
    dot_general x28 -> x8, matrix products: 238 us -> 63.9 us  [the longest x4 33.5 us: contract_cols(): return lax.dot_general(left, right, NT, preferred_element_type=jnp.float32)]
    reduce_scatter x2, waiting for transfers between devices: 234 us -> 97.8 us  [the longest x1 97.8 us: per_device(): s_in = lax.psum_scatter(in_term, 'fsdp', scatter_dimension=0, tiled=True)]
    psum x1, waiting for transfers between devices: 199 us -> 81.8 us  [per_device(): r_in = lax.psum(s_in, 'rep').astype(f32)]
    pallas_call x0 -> x4, Pallas kernels: none -> 85.1 us  [the longest x1 51.2 us: run_backward(): pl.pallas_call(functools.partial(backward_kernel, base), grid=(count,), i...]
    unnamed x2 -> x0, blocking collectives: 82.1 us -> none
    reduce_sum x15 -> x5, other arithmetic: 70.3 us -> 1.7 us  [the longest x1 1.1 us: per_device(): r = lax.rsqrt(jnp.sum(sq, axis=-1, keepdims=True) / DI + epsilon)]
    all_gather x2, blocking collectives: 17.3 us -> 50.5 us  [the longest x1 36.5 us: per_device(): lax.all_gather(jnp.pad(small, (0, -small.size % 128)), 'fsdp', axis=0, ti...]
  transfers between devices with their start and end apart: 10 -> 9, of which waited for: 3 -> 5; matrix products, arithmetic and copies ran while one was open for 53% -> 25% of each run, Pallas kernels for 0% -> 14%
where the time goes in v1:
time: 612 us; the launch traced here: 608 us
  waiting for transfers between devices  273 us (45%)
  matrix products  91.9 us (15%)
  Pallas kernels  85.1 us (14%)
  blocking collectives  58.1 us (9%)
  other arithmetic  36.1 us (6%)
  local copies, waits for them, and re-layouts  32.1 us (5%)
  starting transfers between devices  17.2 us (3%)
  between operations  14.6 us (2%)
    reduce_scatter x1, waiting for transfers between devices, per_device(): s_in = lax.psum_scatter(in_term, 'fsdp', scatter_dimension=0, tiled=True)  97.8 us
    psum x1, waiting for transfers between devices, per_device(): r_in = lax.psum(s_in, 'rep').astype(f32)  81.8 us
    all_gather x1, waiting for transfers between devices, per_device(): in_full = lax.all_gather(in_weight, 'fsdp', axis=0, tiled=True)  74.2 us
    pallas_call x1, Pallas kernels, run_backward(): pl.pallas_call(functools.partial(backward_kernel, base), grid=(count,), i...  51.2 us
    all_gather x1, blocking collectives, per_device(): lax.all_gather(jnp.pad(small, (0, -small.size % 128)), 'fsdp', axis=0, ti...  36.5 us
    dot_general x4, matrix products, contract_cols(): return lax.dot_general(left, right, NT, preferred_element_type=jnp.float32)  33.5 us
    dot_general x4, matrix products, contract_rows(): lax.dot_general(left, right, (((0,), (0,)), ((), ())), preferred_element_...  28 us
    pallas_call x1, Pallas kernels, run_forward(): pl.pallas_call(functools.partial(forward_kernel, base), grid=(count,), in...  24.1 us
  transfers between devices with their start and end apart: 9, of which 5 were waited for; matrix products, arithmetic and copies ran while one was open for 25% of the time, Pallas kernels for 14%

profile of v1, /device:TPU:0, one launch (start us, length us, event | category | flops | bytes accessed | tf_op | source)
XLA Modules:
  0.0 608.0 jit_solution(15773709301684928493)
XLA Ops:
  8.7 1.0 sort.17
  9.8 1.8 gather_fusion
  11.6 5.2 all-to-all-start
  17.0 36.5 %all-gather.2 = bf16[8,1,2688]{2,1,0:T(2,128)(2,1)S(1)} all-gather(bf16[1,1,2688]{2,1,0:T(2,128)(2,1)S(1)} %reshape.269), channel_id=2, replica_groups=mesh['rep'=4,'fsdp'=8] {'fsdp'}, dimensions={0}, use_global_device_ids=true | all-gather | bytes 48384 | tf_op jit(solution)/shard_map/all_gather | solution.py:432
  56.8 1.8 gather_fusion.2
  59.4 3.6 all-to-all-start.2
  63.6 1.6 fusion.18
  65.2 74.2 %all-gather.7.cloned.1.call-done = bf16[1536,6448]{1,0:T(8,128)(2,1)} async-done(((bf16[192,6448]{1,0:T(8,128)(2,1)}), bf16[1536,6448]{1,0:T(8,128)(2,1)}) %all-gather.7.cloned.1.call-update) | async-done | bytes 19808272 | tf_op jit(solution)/shard_map/all_gather | solution.py:433
  139.5 11.0 %fusion.2.x_ref = f32[512,3072]{1,0:T(8,128)} fusion(bf16[512,1536]{1,0:T(8,128)(2,1)} %fusion.18, bf16[1536,6448]{1,0:T(8,128)(2,1)} %all-gather.7.cloned.1.call-done), kind=kOutput, calls=%fused_computation.7 | convolution fusion | flops 4831838208 | bytes 17301504 | tf_op jit(solution)/shard_map/dot_general | solution.py:462
  150.4 2.5 copy-done.9
  152.9 6.9 %fusion.6.z_ref = f32[512,3072]{1,0:T(8,128)} fusion(bf16[512,1536]{1,0:T(8,128)(2,1)S(1)} %copy-done.5, bf16[1536,6448]{1,0:T(8,128)(2,1)S(1)} %copy-done.9), kind=kOutput, calls=%fused_computation.11 | convolution fusion | flops 4831838208 | bytes 17301504 | tf_op jit(solution)/shard_map/dot_general | solution.py:462
  160.0 1.0 copy-done.2
  161.0 1.9 fusion.26.bcd_ref
  162.9 4.0 shard_map.212
  166.9 24.1 %shard_map.213 = (f32[512,3072]{1,0:T(8,128)}, f32[512,3072]{1,0:T(8,128)}, f32[512,128]{1,0:T(8,128)}, bf16[512,3072]{1,0:T(8,128)(2,1)}) custom-call(s32[1]{0:T(128)} %bitcast.106, f32[512,3072]{1,0:T(8,128)} %fusion.6.z_ref, f32[512,3072]{1,0:T(8,128)} %fusion.2.x_ref, f32[8,3072]{1,0:T(8,128)} %slice.134.conv_ref, ...), custom_call_target="tpu_custom_call" | custom-call | flops 7200000000 | bytes 36000000 | tf_op jit(solution)/shard_map/pallas_call | solution.py:357
  191.0 1.1 reduce_sum.73
  192.1 10.7 %fusion.34 = bf16[3072,1536]{1,0:T(8,128)(2,1)} fusion(bf16[512,1536]{1,0:T(8,128)(2,1)S(1)} %bitcast.79, f32[512,3072]{1,0:T(8,128)} %get-tuple-element.47, f32[3072]{0:T(1024)S(1)} %mul.129, f32[512]{0:T(512)S(1)} %add_rsqrt_fusion.1), kind=kOutput, calls=%fused_computation.68 | convolution fusion | flops 4836556800 | bytes 17315840 | tf_op jit(solution)/shard_map/dot_general | solution.py:410
  203.1 11.0 %fusion.39.dg_ref = f32[512,3072]{1,0:T(8,128)} fusion(bf16[512,1536]{1,0:T(8,128)(2,1)S(1)} %bitcast.80, bf16[3072,1536]{1,0:T(8,128)(2,1)} %all-gather.9.cloned.1.call-done), kind=kOutput, calls=%fused_computation.73 | convolution fusion | flops 4831838208 | bytes 17301504 | tf_op jit(solution)/shard_map/dot_general | solution.py:414
  214.1 10.7 %fusion.14 = (f32[512]{0:T(512)S(1)}, bf16[512,1536]{1,0:T(8,128)(2,1)}) fusion(bf16[8,64,1536]{2,1,0:T(8,128)(2,1)S(1)} %all-to-all-done.2, bf16[8,64,1536]{2,1,0:T(8,128)(2,1)S(1)} %all-to-all-done, bf16[3072,1536]{1,0:T(8,128)(2,1)S(1)} %copy-done.23, f32[512,3072]{1,0:T(8,128)} %get-tuple-element.47, f32[3072]{0:T(1024)S(1)} %mul.129, ...), kind=kOutput, calls=%fused_computation.18 | convolution fusion | flops 4841274880 | bytes 20463616 | tf_op jit(solution)/shard_map/dot_general | solution.py:468
  225.7 51.2 %shard_map.214 = (bf16[512,3072]{1,0:T(8,128)(2,1)}, bf16[512,3072]{1,0:T(8,128)(2,1)}, f32[8,3072]{1,0:T(8,128)}, f32[512,128]{1,0:T(8,128)}, f32[512,128]{1,0:...) custom-call(s32[1]{0:T(128)} %bitcast.107, ...), custom_call_target="tpu_custom_call" | custom-call | flops 24000000000 | bytes 48000000 | tf_op jit(solution)/shard_map/pallas_call | solution.py:380
  276.9 5.8 shard_map.215
  282.7 2.2 fusion.28
  284.9 7.6 %fusion.40 = bf16[1536,3072]{1,0:T(8,128)(2,1)} fusion(bf16[512,1536]{1,0:T(8,128)(2,1)S(1)} %copy-done.6, bf16[512,3072]{1,0:T(8,128)(2,1)S(1)} %copy-done.26), kind=kOutput, calls=%fused_computation.74 | convolution fusion | flops 4831838208 | bytes 14155776 | tf_op jit(solution)/shard_map/dot_general | solution.py:410
  292.5 7.5 %fusion.41 = bf16[1536,3072]{1,0:T(8,128)(2,1)} fusion(bf16[512,1536]{1,0:T(8,128)(2,1)S(1)} %copy-done.6, bf16[512,3072]{1,0:T(8,128)(2,1)S(1)} %copy-done.28), kind=kOutput, calls=%fused_computation.75 | convolution fusion | flops 4831838208 | bytes 14155776 | tf_op jit(solution)/shard_map/dot_general | solution.py:410
  300.1 21.4 %pad_maximum_fusion = bf16[1536,6448]{1,0:T(8,128)(2,1)} fusion(bf16[1536,304]{1,0:T(8,128)(2,1)S(1)} %fusion.28, bf16[1536,3072]{1,0:T(8,128)(2,1)} %fusion.41, bf16[1536,3072]{1,0:T(8,128)(2,1)} %fusion.40), kind=kLoop, calls=%fused_computation.4 | loop fusion | flops 59424768 | bytes 39616512 | tf_op jit(solution)/shard_map/concatenate | solution.py:480
  321.5 1.3 slice.107
  322.8 1.3 slice.105
  324.1 1.3 slice_reduce_fusion.2
  325.4 0.7 reshape_squeeze.13
  326.1 1.3 reshape_squeeze.12
  327.5 1.5 slice.104
  329.0 2.3 slice_reduce_fusion
  331.3 1.3 reshape_squeeze.15
  332.6 2.7 fusion.24
  335.8 9.1 %fusion = f32[512,1536]{1,0:T(8,128)S(1)} fusion(bf16[512,3072]{1,0:T(8,128)(2,1)S(1)} %copy-done.29, bf16[1536,6448]{1,0:T(8,128)(2,1)} %all-gather.7.cloned.1.call-done), kind=kOutput, calls=%fused_computation.5 | convolution fusion | flops 4831838208 | bytes 15728640 | tf_op jit(solution)/shard_map/dot_general | solution.py:414
  344.9 10.6 %fusion.23 = (f32[1536]{0:T(1024)S(1)}, f32[512]{0:T(512)S(1)}, f32[512,1536]{1,0:T(8,128)}) fusion(bf16[8,64,1536]{2,1,0:T(8,128)(2,1)S(1)} %all-to-all-done, f32[512]{0:T(512)S(1)} %rsqrt.34, f32[1536]{0:T(1024)S(1)} %mul.124, f32[512,1536]{1,0:T(8,128)S(1)} %fusion.24, f32[512,1536]{1,0:T(8,128)S(1)} %fusion, bf16[512,3072]{1,0:T(8,128)(2,1)S(1)} %copy-done.27, ...), kind=kOutput, calls=%fused_computation.33 | convolution fusion | flops 4838914048 | bytes 23609344 | tf_op jit(solution)/shard_map/dot_general | solution.py:414
  355.6 97.8 %reduce-scatter.3.cloned.1.call-done = bf16[192,6448]{1,0:T(8,128)(2,1)} async-done(((bf16[1536,6448]{1,0:T(8,128)(2,1)}), bf16[192,6448]{1,0:T(8,128)(2,1)}) %reduce-scatter.3.cloned.1.call-update) | async-done | bytes 2476048 | tf_op jit(solution)/shard_map/reduce_scatter | solution.py:481
  454.4 7.6 %all_to_all.29 = f32[8,1,2688]{2,1,0:T(1,128)S(1)} all-to-all(f32[8,1,2688]{2,1,0:T(1,128)S(1)} %copy.36), channel_id=1, replica_groups=mesh['rep'=4,'fsdp'=8] {'fsdp'}, dimensions={0} | all-to-all | bytes 172032 | tf_op jit(solution)/shard_map/all_to_all | solution.py:501
  462.1 4.3 all-to-all-start.1
  466.4 3.9 fusion.15
  470.3 17.2 %all-to-all-done.1 = bf16[8,64,1536]{2,1,0:T(8,128)(2,1)} async-done(((bf16[8,64,1536]{2,1,0:T(8,128)(2,1)}), bf16[8,64,1536]{2,1,0:T(8,128)(2,1)}, u32[]{:S(2)}, u32[]{:S(2)}) %all-to-all-start.1) | async-done | bytes 1572896 | tf_op jit(solution)/shard_map/all_to_all | solution.py:441
  487.4 3.6 all-to-all-start.3
  491.1 14.0 %all-gather.3 = f32[4,1,2688]{2,1,0:T(1,128)S(1)} all-gather(f32[1,1,2688]{2,1,0:T(1,128)S(1)} %reshape.271), channel_id=3, replica_groups=mesh['rep'=4,'fsdp'=8] {'rep'}, dimensions={0}, use_global_device_ids=true | all-gather | bytes 53760 | tf_op jit(solution)/shard_map/all_gather | solution.py:502
  508.4 3.2 gather_fusion.1
  512.0 1.8 gather_fusion.3
  513.8 81.8 %all-reduce.8.cloned.1.call-done = (bf16[192,6448]{1,0:T(8,128)(2,1)}, bf16[384,1536]{1,0:T(8,128)(2,1)}) async-done(((bf16[192,6448]{1,0:T(8,128)(2,1)}, bf16[384,1536]{1,0:T(8,128)(2,1)}), (bf16[192,6448]{1,0:T(8,128)(2,1)}, bf16[384,1536]{1,0:T(8,128)(2,1)})) %all-reduce.8.cloned.1.call-update) | async-done | bytes 3655696 | tf_op jit(solution)/shard_map/psum | solution.py:503
  595.6 3.1 convert_element_type.53
  598.7 2.6 convert_element_type.52
  (143 shorter events, 13.0 us)
Async XLA Ops:
  7.2 2.5 copy-start
  7.2 1.5 copy-start.24
  7.2 132.3 %all-gather.7.cloned.1.call-start = ((), (), s32[]{:S(2)}) async-start(), calls=%async_computation.7 | async-start | bytes 22560768 | tf_op jit(solution)/shard_map/all_gather | solution.py:433
  7.9 195.2 %all-gather.9.cloned.1.call-start = ((), (), s32[]{:S(2)}) async-start(), calls=%async_computation.8 | async-start | bytes 10616832 | tf_op jit(solution)/shard_map/all_gather | solution.py:434
  9.7 7.1 %copy-start.15 = (bf16[4,416]{1,0:T(4,128)(2,1)S(1)}, bf16[4,416]{1,0:T(4,128)(2,1)}, u32[]{:S(2)}) copy-start(bf16[4,416]{1,0:T(4,128)(2,1)} %param.19) | copy-start | bytes 9988
  9.7 7.1 %copy-start.17 = (bf16[416]{0:T(512)(128)(2,1)S(1)}, bf16[416]{0:T(512)(128)(2,1)}, u32[]{:S(2)}) copy-start(bf16[416]{0:T(512)(128)(2,1)} %param.20) | copy-start | bytes 2500
  9.7 7.1 %copy-start.18 = (bf16[384]{0:T(512)(128)(2,1)S(1)}, bf16[384]{0:T(512)(128)(2,1)}, u32[]{:S(2)}) copy-start(bf16[384]{0:T(512)(128)(2,1)} %param.24) | copy-start | bytes 2308
  9.7 7.1 %copy-start.19 = (bf16[192]{0:T(256)(128)(2,1)S(1)}, bf16[192]{0:T(256)(128)(2,1)}, u32[]{:S(2)}) copy-start(bf16[192]{0:T(256)(128)(2,1)} %param.17) | copy-start | bytes 1156
  9.7 7.1 %copy-start.20 = (bf16[6]{0:T(256)(128)(2,1)S(1)}, bf16[6]{0:T(256)(128)(2,1)}, u32[]{:S(2)}) copy-start(bf16[6]{0:T(256)(128)(2,1)} %param.21) | copy-start | bytes 40
  9.8 7.1 %copy-start.21 = (bf16[6]{0:T(256)(128)(2,1)S(1)}, bf16[6]{0:T(256)(128)(2,1)}, u32[]{:S(2)}) copy-start(bf16[6]{0:T(256)(128)(2,1)} %param.22) | copy-start | bytes 40
  9.8 7.1 %copy-start.22 = (bf16[6]{0:T(256)(128)(2,1)S(1)}, bf16[6]{0:T(256)(128)(2,1)}, u32[]{:S(2)}) copy-start(bf16[6]{0:T(256)(128)(2,1)} %param.23) | copy-start | bytes 40
  9.8 47.1 %copy-start.4 = (bf16[512,1536]{1,0:T(8,128)(2,1)S(1)}, bf16[512,1536]{1,0:T(8,128)(2,1)}, u32[]{:S(2)}) copy-start(bf16[512,1536]{1,0:T(8,128)(2,1)} %param.14) | copy-start | bytes 4718596
  11.6 47.8 %all-to-all-start = ((bf16[8,64,1536]{2,1,0:T(8,128)(2,1)}), bf16[8,64,1536]{2,1,0:T(8,128)(2,1)S(1)}, u32[]{:S(2)}, u32[]{:S(2)}) async-start(bf16[8,64,1536]{2,1,0:T(8,128)(2,1)} %gather_fusion), calls=%async_computation | async-start | bytes 3145728 | tf_op jit(solution)/shard_map/all_to_all | solution.py:438
  59.4 132.7 %all-to-all-start.2 = ((bf16[8,64,1536]{2,1,0:T(8,128)(2,1)}), bf16[8,64,1536]{2,1,0:T(8,128)(2,1)S(1)}, u32[]{:S(2)}, u32[]{:S(2)}) async-start(bf16[8,64,1536]{2,1,0:T(8,128)(2,1)} %gather_fusion.2), calls=%async_computation.2 | async-start | bytes 3145728 | tf_op jit(solution)/shard_map/all_to_all | solution.py:438
  63.0 292.7 %reduce-scatter.5.cloned.1.call-start = ((), (), s32[]{:S(2)}) async-start(), calls=%async_computation.10 | async-start | bytes 10616832 | tf_op jit(solution)/shard_map/reduce_scatter | solution.py:476
  139.5 11.0 %copy-start.5 = (bf16[512,1536]{1,0:T(8,128)(2,1)S(1)}, bf16[512,1536]{1,0:T(8,128)(2,1)}, u32[]{:S(2)}) copy-start(bf16[512,1536]{1,0:T(8,128)(2,1)} %fusion.18) | copy-start | bytes 4718596
  139.5 13.5 %copy-start.9 = (bf16[1536,6448]{1,0:T(8,128)(2,1)S(1)}, bf16[1536,6448]{1,0:T(8,128)(2,1)}, u32[]{:S(2)}) copy-start(bf16[1536,6448]{1,0:T(8,128)(2,1)} %all-gather.7.cloned.1.call-done) | copy-start | bytes 59424772
  160.0 1.0 copy-start.2
  202.8 250.6 %reduce-scatter.3.cloned.1.call-start = ((), (), s32[]{:S(2)}) async-start(), calls=%async_computation.9 | async-start | bytes 22560768 | tf_op jit(solution)/shard_map/reduce_scatter | solution.py:481
  203.1 11.0 %copy-start.23 = (bf16[3072,1536]{1,0:T(8,128)(2,1)S(1)}, bf16[3072,1536]{1,0:T(8,128)(2,1)}, u32[]{:S(2)}) copy-start(bf16[3072,1536]{1,0:T(8,128)(2,1)} %all-gather.9.cloned.1.call-done) | copy-start | bytes 28311556
  225.7 57.0 %copy-start.6 = (bf16[512,1536]{1,0:T(8,128)(2,1)S(1)}, bf16[512,1536]{1,0:T(8,128)(2,1)}, u32[]{:S(2)}) copy-start(bf16[512,1536]{1,0:T(8,128)(2,1)} %fusion.18) | copy-start | bytes 4718596
  282.7 2.2 copy-start.26
  284.9 7.6 %copy-start.28 = (bf16[512,3072]{1,0:T(8,128)(2,1)S(1)}, bf16[512,3072]{1,0:T(8,128)(2,1)}, u32[]{:S(2)}) copy-start(bf16[512,3072]{1,0:T(8,128)(2,1)} %get-tuple-element.55) | copy-start | bytes 9437188
  321.4 11.1 %copy-start.7 = (bf16[512,384]{1,0:T(8,128)(2,1)S(1)}, bf16[512,384]{1,0:T(8,128)(2,1)}, u32[]{:S(2)}) copy-start(bf16[512,384]{1,0:T(8,128)(2,1)} %get-tuple-element.63) | copy-start | bytes 1179652
  321.5 274.1 %all-reduce.8.cloned.1.call-start = ((), (), s32[]{:S(2)}) async-start(), calls=%async_computation.11 | async-start | bytes 7372800 | tf_op jit(solution)/shard_map/psum | solution.py:503
  332.6 3.2 copy-start.29
  335.8 9.1 %copy-start.27 = (bf16[512,3072]{1,0:T(8,128)(2,1)S(1)}, bf16[512,3072]{1,0:T(8,128)(2,1)}, u32[]{:S(2)}) copy-start(bf16[512,3072]{1,0:T(8,128)(2,1)} %get-tuple-element.54) | copy-start | bytes 9437188
  355.6 97.9 %copy-start.8 = (f32[4,3072]{1,0:T(4,128)S(1)}, f32[4,3072]{1,0:T(4,128)}, u32[]{:S(2)}) copy-start(f32[4,3072]{1,0:T(4,128)} %slice.104) | copy-start | bytes 147460
  355.6 97.9 %copy-start.14 = (f32[4,256]{1,0:T(4,128)S(1)}, f32[4,256]{1,0:T(4,128)}, u32[]{:S(2)}) copy-start(f32[4,256]{1,0:T(4,128)} %slice.105) | copy-start | bytes 12292
  355.6 98.2 %copy-start.12 = (f32[1,3072]{1,0:T(1,128)S(1)}, f32[1,3072]{1,0:T(1,128)}, u32[]{:S(2)}) copy-start(f32[1,3072]{1,0:T(1,128)} %get-tuple-element.77) | copy-start | bytes 36868
  355.6 98.2 %copy-start.16 = (f32[1,256]{1,0:T(1,128)S(1)}, f32[1,256]{1,0:T(1,128)}, u32[]{:S(2)}) copy-start(f32[1,256]{1,0:T(1,128)} %slice.107) | copy-start | bytes 3076
  355.6 98.3 %copy-start.11 = (f32[3072]{0:T(1024)S(1)}, f32[3072]{0:T(1024)}, u32[]{:S(2)}) copy-start(f32[3072]{0:T(1024)} %get-tuple-element.70) | copy-start | bytes 36868
  355.6 98.6 %copy-start.10 = (f32[8,384]{1,0:T(8,128)S(1)}, f32[8,384]{1,0:T(8,128)}, u32[]{:S(2)}) copy-start(f32[8,384]{1,0:T(8,128)} %reshape_squeeze.15) | copy-start | bytes 36868
  355.6 98.6 %copy-start.13 = (f32[8,6]{1,0:T(8,128)S(1)}, f32[8,6]{1,0:T(8,128)}, u32[]{:S(2)}) copy-start(f32[8,6]{1,0:T(8,128)} %reshape_squeeze.12) | copy-start | bytes 580
  462.1 25.3 %all-to-all-start.1 = ((bf16[8,64,1536]{2,1,0:T(8,128)(2,1)}), bf16[8,64,1536]{2,1,0:T(8,128)(2,1)}, u32[]{:S(2)}, u32[]{:S(2)}) async-start(bf16[8,64,1536]{2,1,0:T(8,128)(2,1)} %bitcast.82), calls=%async_computation.1 | async-start | bytes 3145728 | tf_op jit(solution)/shard_map/all_to_all | solution.py:441
  470.3 20.8 %copy-start.25 = (s32[1,1,8]{2,1,0:T(1,128)S(1)}, s32[1,1,8]{2,1,0:T(1,128)}, u32[]{:S(2)}) copy-start(s32[1,1,8]{2,1,0:T(1,128)} %param.16) | copy-start | bytes 100
  487.4 24.5 %all-to-all-start.3 = ((bf16[8,64,1536]{2,1,0:T(8,128)(2,1)}), bf16[8,64,1536]{2,1,0:T(8,128)(2,1)S(1)}, u32[]{:S(2)}, u32[]{:S(2)}) async-start(bf16[8,64,1536]{2,1,0:T(8,128)(2,1)} %bitcast.81), calls=%async_computation.3 | async-start | bytes 3145728 | tf_op jit(solution)/shard_map/all_to_all | solution.py:441
  595.6 3.1 copy-start.3
  598.7 2.6 copy-start.1
Sparse Core Ops, SparseCore 0:
  9.9 129.4 all-gather.6
  141.3 59.3 all-gather.8
  204.3 76.4 reduce-scatter.4
  321.6 131.7 reduce-scatter.2
  455.8 139.6 all-reduce.7

commit v2 on v1

--- a/solution.py
+++ b/solution.py
@@ -173,7 +173,7 @@
     return dot32(high, right) + dot32(low, right)
 
 
-def backward_kernel(base, first_ref, z_ref, x_ref, y_ref, dg_ref, rk_ref, conv_ref, gain_ref, bn_ref, cn_ref, ct_ref, st_ref, cum_ref, cp_ref, cumt_ref, states_ref, dz_ref, dx_ref, grads_ref, dst_ref, db_ref, dc_ref, u_ref, v_ref, w_ref, flow_ref, dstate, dconv):
+def backward_kernel(base, count, first_ref, z_ref, x_ref, y_ref, dg_ref, rk_ref, conv_ref, gain_ref, bn_ref, cn_ref, ct_ref, st_ref, cum_ref, cp_ref, cumt_ref, states_ref, d_ref, grads_ref, dst_ref, db_ref, dc_ref, u_ref, v_ref, w_ref, flow_ref, dstate, dconv):
     first = first_ref[0]
     group = base + pl.program_id(0)
     lane = lax.broadcasted_iota(jnp.int32, (Q, Q), 1)
@@ -224,7 +224,8 @@
             gs = dg_ref[rows, cols] * scale
             grads_ref[6:7, cols] += sum_rows(gs * g)
             d_g = gain * gs - g * pull
-            dz_ref[rows, cols] = (d_g * ssm * (sz + silu_z * (1.0 - sz))).astype(dz_ref.dtype)
+            z_cols = pl.ds(pl.multiple_of(pl.program_id(0) * LANES + p * Q, Q), Q)
+            d_ref[rows, z_cols] = (d_g * ssm * (sz + silu_z * (1.0 - sz))).astype(d_ref.dtype)
             d_ssm = d_g * silu_z
             grads_ref[5:6, cols] += sum_rows(d_ssm * xs)
             dy16 = d_ssm.astype(jnp.bfloat16)
@@ -271,7 +272,8 @@
             for j in range(KW):
                 grads_ref[KW - 1 - j : KW - j, cols] += sum_rows(d_mixed * moved[j])
             taps = [conv_ref[i : i + 1, cols] for i in range(KW)]
-            dx_ref[rows, cols] = conv_back(dconv, cols, c, first, Q, taps).astype(dx_ref.dtype)
+            x_cols = pl.ds(pl.multiple_of((pl.program_id(0) + count) * LANES + p * Q, Q), Q)
+            d_ref[rows, x_cols] = conv_back(dconv, cols, c, first, Q, taps).astype(d_ref.dtype)
         dst_ref[rows, :] += dst
         db_ref[rows, :] += db
         dc_ref[rows, :] += dc
@@ -347,8 +349,8 @@
     )(first, bcd, conv, heads)
 
 
-def run_forward(base, count, first, z, x, conv, gains, prep):
-    rows = x.shape[0]
+def run_forward(base, count, first, zx, conv, gains, prep):
+    rows = zx.shape[0]
     bn, cn, bt, ct, s, st, cum, cp, cumt, cpt = prep
     f32, b16 = jnp.float32, jnp.bfloat16
     chunks = rows // Q
@@ -357,38 +359,37 @@
     return pl.pallas_call(
         functools.partial(forward_kernel, base),
         grid=(count,),
-        in_specs=[smem(), pl.BlockSpec((rows, LANES), at), pl.BlockSpec((rows, LANES), at), pl.BlockSpec((8, LANES), at), pl.BlockSpec((8, LANES), at)]
+        in_specs=[smem(), pl.BlockSpec((rows, LANES), here), pl.BlockSpec((rows, LANES), lambda g: (0, g + count)), pl.BlockSpec((8, LANES), at), pl.BlockSpec((8, LANES), at)]
         + [whole(v.shape) for v in (bn, cn, bt, s, cum, cp, cpt)],
         out_specs=[pl.BlockSpec((rows, LANES), here), pl.BlockSpec((rows, LANES), here), whole((rows, Q)), pl.BlockSpec((chunks * NSTATE, LANES), here)],
         out_shape=[jax.ShapeDtypeStruct((rows, count * LANES), f32), jax.ShapeDtypeStruct((rows, count * LANES), f32), jax.ShapeDtypeStruct((rows, Q), f32), jax.ShapeDtypeStruct((chunks * NSTATE, count * LANES), b16)],
         scratch_shapes=[pltpu.VMEM((NSTATE, LANES), f32)],
         compiler_params=pltpu.CompilerParams(vmem_limit_bytes=VMEM),
         cost_estimate=pl.CostEstimate(flops=count * 1200000000, bytes_accessed=count * 6000000, transcendentals=0),
-    )(first, z, x, conv, gains, bn, cn, bt, s, cum, cp, cpt)
-
-
-def run_backward(base, count, first, z, x, y, dg, rk, conv, gains, prep, states):
-    rows = x.shape[0]
+    )(first, zx, zx, conv, gains, bn, cn, bt, s, cum, cp, cpt)
+
+
+def run_backward(base, count, first, zx, y, dg, rk, conv, gains, prep, states):
+    rows = zx.shape[0]
     bn, cn, bt, ct, s, st, cum, cp, cumt, cpt = prep
     f32, b16 = jnp.float32, jnp.bfloat16
     chunks = rows // Q
     at = lambda g: (0, g + base)
     here = lambda g: (0, g)
-    block = pl.BlockSpec((rows, LANES), at)
     local = pl.BlockSpec((rows, LANES), here)
     sums = [(rows, Q), (rows, NSTATE), (rows, NSTATE), (rows, 128), (rows, 128), (rows, 128)]
     return pl.pallas_call(
-        functools.partial(backward_kernel, base),
+        functools.partial(backward_kernel, base, count),
         grid=(count,),
-        in_specs=[smem(), block, block, block, block, whole(rk.shape), pl.BlockSpec((8, LANES), at), pl.BlockSpec((8, LANES), at)]
+        in_specs=[smem(), local, pl.BlockSpec((rows, LANES), lambda g: (0, g + count)), local, local, whole(rk.shape), pl.BlockSpec((8, LANES), at), pl.BlockSpec((8, LANES), at)]
         + [whole(v.shape) for v in (bn, cn, ct, st, cum, cp, cumt)]
-        + [pl.BlockSpec((chunks * NSTATE, LANES), at)],
-        out_specs=[local, local, pl.BlockSpec((8, LANES), here)] + [whole(v) for v in sums] + [pl.BlockSpec((8, LANES), here)],
-        out_shape=[jax.ShapeDtypeStruct((rows, count * LANES), b16)] * 2 + [jax.ShapeDtypeStruct((8, count * LANES), f32)] + [jax.ShapeDtypeStruct(v, f32) for v in sums] + [jax.ShapeDtypeStruct((8, count * LANES), f32)],
+        + [pl.BlockSpec((chunks * NSTATE, LANES), here)],
+        out_specs=[whole((rows, 2 * count * LANES)), pl.BlockSpec((8, LANES), here)] + [whole(v) for v in sums] + [pl.BlockSpec((8, LANES), here)],
+        out_shape=[jax.ShapeDtypeStruct((rows, 2 * count * LANES), b16)] + [jax.ShapeDtypeStruct((8, count * LANES), f32)] + [jax.ShapeDtypeStruct(v, f32) for v in sums] + [jax.ShapeDtypeStruct((8, count * LANES), f32)],
         scratch_shapes=[pltpu.VMEM((NSTATE, LANES), f32), pltpu.VMEM((rows + 8, LANES), f32)],
         compiler_params=pltpu.CompilerParams(vmem_limit_bytes=VMEM),
         cost_estimate=pl.CostEstimate(flops=count * 4000000000, bytes_accessed=count * 8000000, transcendentals=0),
-    )(first, z, x, y, dg, rk, conv, gains, bn, cn, ct, st, cum, cp, cumt, states)
+    )(first, zx, zx, y, dg, rk, conv, gains, bn, cn, ct, st, cum, cp, cumt, states)
 
 
 def run_post(first, bcd, conv, heads, prep, *sums):
@@ -418,6 +419,75 @@
     return jnp.pad(v, ((0, 0), (0, width - v.shape[1])))
 
 
+PARTS = 3
+ORDER = (1, 3, 5, 7, 6, 2, 4, 0)
+
+
+def swap(v, bit):
+    return lax.ppermute(v, "fsdp", [(i, i ^ bit) for i in range(lax.axis_size("fsdp"))])
+
+
+def across(v, pairs):
+    return lax.ppermute(v, "rep", pairs)
+
+
+def gather_rows(w):
+    groups = lax.axis_size("fsdp")
+    if groups != 8:
+        return lax.all_gather(w, "fsdp", axis=0, tiled=True)
+    rows = w.shape[0]
+    one, two, four = swap(w, 1), swap(w, 2), swap(w, 4)
+    six = jnp.concatenate([swap(two[: rows // 2], 4), swap(four[rows // 2 :], 2)])
+    three, five, seven = swap(two, 1), swap(four, 1), swap(six, 1)
+    me = lax.axis_index("fsdp")
+    full = jnp.zeros((groups * rows, w.shape[1]), w.dtype)
+    for j, piece in enumerate((w, one, two, three, four, five, six, seven)):
+        full = lax.dynamic_update_slice(full, piece, ((me ^ j) * rows, 0))
+    return full
+
+
+def send_order(v, blocks):
+    if blocks != 8:
+        return v
+    me = lax.axis_index("fsdp")
+    step = v.shape[1] // blocks
+    return jnp.concatenate([lax.dynamic_slice(v, (0, (me ^ j) * step), (v.shape[0], step)) for j in ORDER], axis=1)
+
+
+def scatter_term(left, right):
+    groups = lax.axis_size("fsdp")
+    b16 = jnp.bfloat16
+    if groups != 8:
+        return lax.psum_scatter(contract_rows(left, right, b16), "fsdp", scatter_dimension=0, tiled=True).astype(jnp.float32)
+    rows = left.shape[1] // groups
+    half = rows // 2
+    got = swap(contract_rows(left[:, : 4 * rows], right).astype(b16), 1).astype(jnp.float32)
+    diag = (contract_rows(left[:, 4 * rows : 5 * rows], right) + got[3 * rows :]).astype(b16)
+    from_x, from_y = swap(diag[:half], 2), swap(diag[half:], 4)
+    low = jnp.pad(from_y.astype(jnp.float32), ((half, 0), (0, 0)))
+    high = jnp.pad(from_x.astype(jnp.float32), ((0, half), (0, 0)))
+    to_x = (contract_rows(left[:, 5 * rows : 6 * rows], right) + got[rows : 2 * rows] + low).astype(b16)
+    to_y = (contract_rows(left[:, 6 * rows : 7 * rows], right) + got[2 * rows : 3 * rows] + high).astype(b16)
+    got_x, got_y = swap(to_x, 2), swap(to_y, 4)
+    return contract_rows(left[:, 7 * rows :], right) + got[:rows] + got_x.astype(jnp.float32) + got_y.astype(jnp.float32)
+
+
+def sum_rep(own):
+    b16 = jnp.bfloat16
+    if lax.axis_size("rep") != 4:
+        return lax.psum(own.astype(b16), "rep")
+    place = lax.axis_index("rep")
+    inner = (place == 1) | (place == 2)
+    half = own.shape[0] // 2
+    pair = own + across(own.astype(b16), [(0, 1), (3, 2)]).astype(jnp.float32)
+    top, bottom = pair[:half], pair[half:]
+    got = across(jnp.where(place == 1, bottom, top).astype(b16), [(1, 2), (2, 1)])
+    mine = (jnp.where(place == 1, top, bottom) + got.astype(jnp.float32)).astype(b16)
+    other = across(mine, [(1, 2), (2, 1)])
+    full = jnp.where(place == 1, jnp.concatenate([mine, other]), jnp.concatenate([other, mine]))
+    return jnp.where(inner, full, across(full, [(1, 0), (2, 3)]))
+
+
 def per_device(tokens, cotangent, lengths, dealing, norm_gain, in_weight, conv_weight, conv_bias, dt_bias, a_log, d_skip, gated_gain, out_weight):
     f32, b16 = jnp.float32, jnp.bfloat16
     groups = lax.axis_size("fsdp")
@@ -426,23 +496,25 @@
     targets = dealing.reshape(groups)
     inverse = jnp.argsort(targets)
     first = lengths.reshape(-1)[:1]
+    count = HEADS // GROUP // PARTS
+    lanes = count * LANES
+
+    def deal(values):
+        blocks = values.reshape(groups, block_rows, width)[inverse]
+        return lax.all_to_all(blocks, "fsdp", split_axis=0, concat_axis=0, tiled=True).reshape(tok_rows, width)
+
+    def undeal(values):
+        blocks = lax.all_to_all(values.reshape(groups, block_rows, width), "fsdp", split_axis=0, concat_axis=0, tiled=True)
+        return blocks[targets].reshape(tok_rows, width)
 
     small = jnp.concatenate([norm_gain, conv_weight.reshape(-1), conv_bias, dt_bias, a_log, d_skip, gated_gain])
     sizes = [v.size for v in (norm_gain, conv_weight, conv_bias, dt_bias, a_log, d_skip, gated_gain)]
     small_all = lax.all_gather(jnp.pad(small, (0, -small.size % 128)), "fsdp", axis=0, tiled=False).astype(f32)
-    in_full = lax.all_gather(in_weight, "fsdp", axis=0, tiled=True)
-    out_full = lax.all_gather(out_weight, "fsdp", axis=0, tiled=True)
-
-    def deal(values):
-        blocks = values.reshape(groups, block_rows, width)[inverse]
-        return lax.all_to_all(blocks, "fsdp", split_axis=0, concat_axis=0, tiled=True).reshape(tok_rows, width)
-
-    def undeal(values):
-        blocks = lax.all_to_all(values.reshape(groups, block_rows, width), "fsdp", split_axis=0, concat_axis=0, tiled=True)
-        return blocks[targets].reshape(tok_rows, width)
-
     hidden = deal(tokens).astype(f32)
+    w_b = gather_rows(pad_lanes(in_weight[:, 2 * DI :], BCD))
+    w_zx = [gather_rows(jnp.concatenate([in_weight[:, k * lanes : (k + 1) * lanes], in_weight[:, DI + k * lanes : DI + (k + 1) * lanes]], axis=1)) for k in range(PARTS)]
     cot = deal(cotangent)
+    out_full = gather_rows(out_weight)
 
     ends, parts = 0, []
     for size in sizes:
@@ -458,28 +530,41 @@
 
     rn = lax.rsqrt(jnp.mean(hidden * hidden, axis=-1, keepdims=True) + epsilon)
     normed = (hidden * rn * gain).astype(b16)
-    w_z, w_x, w_b = in_full[:, :DI], in_full[:, DI : 2 * DI], pad_lanes(in_full[:, 2 * DI :], BCD)
-    z, x, bcd = (jnp.dot(normed, w, preferred_element_type=f32) for w in (w_z, w_x, w_b))
-
+    normed_sent = send_order(normed, groups)
+    bcd = jnp.dot(normed, w_b, preferred_element_type=f32)
     prep = run_prep(first, bcd, conv_bc, heads)
-    y, g, sq, states = run_forward(0, HEADS // GROUP, first, z, x, conv_x, gains, prep)
-    r = lax.rsqrt(jnp.sum(sq, axis=-1, keepdims=True) / DI + epsilon)
-    gated = (g * r * ggain).astype(b16)
+    zx, ys, gs, sqs, states = [], [], [], [], []
+    for k in range(PARTS):
+        zx.append(jnp.dot(normed, w_zx[k], preferred_element_type=f32))
+        y, g, sq, state = run_forward(k * count, count, first, zx[k], conv_x, gains, prep)
+        ys.append(y)
+        gs.append(g)
+        sqs.append(sq)
+        states.append(state)
+    r = lax.rsqrt(jnp.sum(sum(sqs), axis=-1, keepdims=True) / DI + epsilon)
+    gated = (jnp.concatenate(gs, axis=1) * r * ggain).astype(b16)
     branch = jnp.dot(gated, out_full, preferred_element_type=f32)
-    result = (hidden + branch).astype(b16)
-    output = undeal(result)
+    output = undeal((hidden + branch).astype(b16))
     cot32 = cot.astype(f32)
     pull = r * r * (jnp.sum(cot32 * branch, axis=-1, keepdims=True) / DI)
     rk = pad_lanes(jnp.concatenate([r, pull], axis=1), 128)
-    d_gated = contract_cols(cot, out_full)
-    out_term = contract_rows(gated, cot, b16)
-    s_out = lax.psum_scatter(out_term, "fsdp", scatter_dimension=0, tiled=True)
-
-    d_z, d_x, xgrads, *sums, flow = run_backward(0, HEADS // GROUP, first, z, x, y, d_gated, rk, conv_x, gains, prep, states)
-    d_b, bgrads, hgrads = run_post(first, bcd, conv_bc, heads, prep, *[t[None] for t in sums], flow)
-    in_term = jnp.concatenate([contract_rows(normed, d_z, b16), contract_rows(normed, d_x, b16), contract_rows(normed, d_b, b16)[:, : in_weight.shape[1] - 2 * DI]], axis=1)
-    s_in = lax.psum_scatter(in_term, "fsdp", scatter_dimension=0, tiled=True)
-    d_normed = contract_cols(d_z, w_z) + contract_cols(d_x, w_x) + contract_cols(d_b, w_b)
+    r_out = sum_rep(scatter_term(send_order(gated, groups), cot)).astype(f32)
+
+    d_zx, xgrads, sums, flows, r_in = [], [], [], [], []
+    for k in range(PARTS):
+        d_gated = contract_cols(cot, out_full[k * lanes : (k + 1) * lanes])
+        d, grads, *more, flow = run_backward(k * count, count, first, zx[k], ys[k], d_gated, rk, conv_x, gains, prep, states[k])
+        d_zx.append(d)
+        xgrads.append(grads)
+        sums.append(more)
+        flows.append(flow)
+        r_in.append(sum_rep(scatter_term(normed_sent, d)))
+    d_b, bgrads, hgrads = run_post(first, bcd, conv_bc, heads, prep, *[jnp.stack(t) for t in zip(*sums)], jnp.concatenate(flows, axis=1))
+    r_b = sum_rep(scatter_term(normed_sent, d_b))
+    d_normed = contract_cols(d_b, w_b)
+    for k in range(PARTS):
+        d_normed = d_normed + contract_cols(d_zx[k], w_zx[k])
+    xgrads = jnp.concatenate(xgrads, axis=1)
     g_gain = jnp.sum(d_normed * hidden * rn, axis=0)
     d_scaled = d_normed * gain
     d_hidden = rn * d_scaled - hidden * (rn * rn * rn * jnp.mean(hidden * d_scaled, axis=-1, keepdims=True))
@@ -500,8 +585,8 @@
     packed = pad_lanes(jnp.concatenate(spread, axis=1), small_all.shape[1])
     s_small = jnp.sum(lax.all_to_all(packed, "fsdp", split_axis=0, concat_axis=0, tiled=True), axis=0)
     r_small = jnp.sum(lax.all_gather(s_small, "rep", axis=0, tiled=False), axis=0)
-    r_in = lax.psum(s_in, "rep").astype(f32)
-    r_out = lax.psum(s_out, "rep").astype(f32)
+    pieces = [v[:, :lanes] for v in r_in] + [v[:, lanes:] for v in r_in] + [r_b[:, : in_weight.shape[1] - 2 * DI]]
+    r_in = jnp.concatenate(pieces, axis=1).astype(f32)
     ends, outs = 0, []
     for size in sizes:
         outs.append(r_small[ends : ends + size])

time: 612 us -> 831 us (1.36)
  local copies, waits for them, and re-layouts: 32.1 us -> 132 us
  starting transfers between devices: 17.2 us -> 114 us
  waiting for transfers between devices: 273 us -> 232 us
  matrix products: 91.9 us -> 127 us
  Pallas kernels: 85.1 us -> 108 us
  other arithmetic: 36.1 us -> 58.5 us
  blocking collectives: 58.1 us -> 46.2 us
  between operations: 14.6 us -> 2.88 us
    ppermute x0 -> x85, waiting for transfers between devices: none -> 232 us  [the longest x65 141 us: swap(): lax.ppermute(v, 'fsdp', [(i, i ^ bit) for i in range(lax.axis_size('fsdp'...]
    reduce_scatter x2 -> x0, waiting for transfers between devices: 97.8 us -> none  [the longest x1 97.8 us: per_device(): s_in = lax.psum_scatter(in_term, 'fsdp', scatter_dimension=0, tiled=True)]
    ppermute x0 -> x85, starting transfers between devices: none -> 94.7 us  [the longest x65 53.5 us: swap(): lax.ppermute(v, 'fsdp', [(i, i ^ bit) for i in range(lax.axis_size('fsdp'...]
    psum x1 -> x0, waiting for transfers between devices: 81.8 us -> none  [per_device(): r_in = lax.psum(s_in, 'rep').astype(f32)]
    all_gather x2 -> x0, waiting for transfers between devices: 74.3 us -> none  [the longest x1 74.2 us: per_device(): in_full = lax.all_gather(in_weight, 'fsdp', axis=0, tiled=True)]
    dynamic_update_slice x0 -> x36, local copies, waits for them, and re-layouts: none -> 53.3 us  [gather_rows(): full = lax.dynamic_update_slice(full, piece, ((me ^ j) * rows, 0))]
    dot_general x4 -> x25, matrix products: 28 us -> 55.3 us  [contract_rows(): lax.dot_general(left, right, (((0,), (0,)), ((), ())), preferred_element_...]
    convert_element_type x2 -> x18, other arithmetic: 5.72 us -> 24.6 us  [the longest x5 14.1 us: scatter_term(): swap(contract_rows(left[:, :4 * rows], right).astype(b16), 1)]
  transfers between devices with their start and end apart: 9 -> 90, of which waited for: 5 -> 26; matrix products, arithmetic and copies ran while one was open for 25% -> 27% of each run, Pallas kernels for 14% -> 5%
where the time goes in v2:
time: 831 us; the launch traced here: 821 us
  waiting for transfers between devices  232 us (28%)
  local copies, waits for them, and re-layouts  132 us (16%)
  matrix products  127 us (15%)
  starting transfers between devices  114 us (14%)
  Pallas kernels  108 us (13%)
  other arithmetic  58.5 us (7%)
  blocking collectives  46.2 us (6%)
    ppermute x65, waiting for transfers between devices, swap(): lax.ppermute(v, 'fsdp', [(i, i ^ bit) for i in range(lax.axis_size('fsdp'...  141 us
    ppermute x20, waiting for transfers between devices, across(): return lax.ppermute(v, 'rep', pairs)  90.9 us
    pallas_call x3, Pallas kernels, run_backward(): pl.pallas_call(functools.partial(backward_kernel, base, count), grid=(cou...  63.8 us
    dot_general x25, matrix products, contract_rows(): lax.dot_general(left, right, (((0,), (0,)), ((), ())), preferred_element_...  55.3 us
    ppermute x65, starting transfers between devices, swap(): lax.ppermute(v, 'fsdp', [(i, i ^ bit) for i in range(lax.axis_size('fsdp'...  53.5 us
    dynamic_update_slice x36, local copies, waits for them, and re-layouts, gather_rows(): full = lax.dynamic_update_slice(full, piece, ((me ^ j) * rows, 0))  53.3 us
    ppermute x20, starting transfers between devices, across(): return lax.ppermute(v, 'rep', pairs)  41.2 us
    dot_general x7, matrix products, contract_cols(): return lax.dot_general(left, right, NT, preferred_element_type=jnp.float32)  36.8 us
  transfers between devices with their start and end apart: 90, of which 26 were waited for; matrix products, arithmetic and copies ran while one was open for 27% of the time, Pallas kernels for 5%

profile of v2, /device:TPU:0, one launch (start us, length us, event | category | flops | bytes accessed | tf_op | source)
XLA Modules:
  0.0 820.8 jit_solution(10449258612076256006)
XLA Ops:
  21.2 33.1 %all-gather.2 = bf16[8,1,2688]{2,1,0:T(2,128)(2,1)S(1)} all-gather(bf16[1,1,2688]{2,1,0:T(2,128)(2,1)S(1)} %reshape.269), channel_id=2, replica_groups=mesh['rep'=4,'fsdp'=8] {'fsdp'}, dimensions={0}, use_global_device_ids=true | all-gather | bytes 48384 | tf_op jit(solution)/shard_map/all_gather | solution.py:512
  65.7 4.2 broadcast_in_dim.37
  83.0 9.7 %collective-permute-done.13 = bf16[96,384]{1,0:T(8,128)(2,1)S(1)} collective-permute-done((bf16[96,384]{1,0:T(8,128)(2,1)S(1)}, bf16[96,384]{1,0:T(8,128)(2,1)S(1)}, u32[]{:S(2)}, u32[]{:S(2)}) %collective-permute-start.13) | collective-permute-done | bytes 73760 | tf_op jit(solution)/shard_map/ppermute | solution.py:427
  101.5 13.5 %collective-permute-done.17 = bf16[192,2048]{1,0:T(8,128)(2,1)} collective-permute-done((bf16[192,2048]{1,0:T(8,128)(2,1)}, bf16[192,2048]{1,0:T(8,128)(2,1)}, u32[]{:S(2)}, u32[]{:S(2)}) %collective-permute-start.17) | collective-permute-done | bytes 786464 | tf_op jit(solution)/shard_map/ppermute | solution.py:427
  121.9 9.2 %collective-permute-done.1 = bf16[192,2048]{1,0:T(8,128)(2,1)} collective-permute-done((bf16[192,2048]{1,0:T(8,128)(2,1)}, bf16[192,2048]{1,0:T(8,128)(2,1)}, u32[]{:S(2)}, u32[]{:S(2)}) %collective-permute-start.1) | collective-permute-done | bytes 786464 | tf_op jit(solution)/shard_map/ppermute | solution.py:427
  145.6 26.5 %collective-permute-done.29 = bf16[96,2048]{1,0:T(8,128)(2,1)S(1)} collective-permute-done((bf16[96,2048]{1,0:T(8,128)(2,1)S(1)}, bf16[96,2048]{1,0:T(8,128)(2,1)S(1)}, u32[]{:S(2)}, u32[]{:S(2)}) %collective-permute-start.29) | collective-permute-done | bytes 393248 | tf_op jit(solution)/shard_map/ppermute | solution.py:427
  176.5 4.1 collective-permute-done.21
  181.8 5.8 collective-permute-done.5
  189.0 4.2 collective-permute-done.22
  240.7 6.1 collective-permute-done.37
  246.9 4.6 collective-permute-done.38
  253.1 7.7 fusion.174.z_ref.x_ref
  260.7 11.0 %shard_map.215 = (f32[512,1024]{1,0:T(8,128)}, f32[512,1024]{1,0:T(8,128)}, f32[512,128]{1,0:T(8,128)}, bf16[512,1024]{1,0:T(8,128)(2,1)}) custom-call(s32[1]{0:T(128)} %bitcast.169, f32[512,2048]{1,0:T(8,128)} %fusion.174.z_ref.x_ref, f32[512,2048]{1,0:T(8,128)} %fusion.174.z_ref.x_ref, f32[8,3072]{1,0:T(8,128)} %slice.390.conv_ref, ...), custom_call_target="tpu_custom_call" | custom-call | flops 2400000000 | bytes 12000000 | tf_op jit(solution)/shard_map/pallas_call | solution.py:359
  273.9 7.7 fusion.173.z_ref.x_ref
  281.6 11.4 %shard_map.214 = (f32[512,1024]{1,0:T(8,128)}, f32[512,1024]{1,0:T(8,128)}, f32[512,128]{1,0:T(8,128)}, bf16[512,1024]{1,0:T(8,128)(2,1)}) custom-call(s32[1]{0:T(128)} %bitcast.170, f32[512,2048]{1,0:T(8,128)} %fusion.173.z_ref.x_ref, f32[512,2048]{1,0:T(8,128)} %fusion.173.z_ref.x_ref, f32[8,3072]{1,0:T(8,128)} %slice.390.conv_ref, ...), custom_call_target="tpu_custom_call" | custom-call | flops 2400000000 | bytes 12000000 | tf_op jit(solution)/shard_map/pallas_call | solution.py:359
  295.1 7.7 fusion.171.z_ref.x_ref
  302.8 11.2 %shard_map.213 = (f32[512,1024]{1,0:T(8,128)}, f32[512,1024]{1,0:T(8,128)}, f32[512,128]{1,0:T(8,128)}, bf16[512,1024]{1,0:T(8,128)(2,1)}) custom-call(s32[1]{0:T(128)} %bitcast.171, f32[512,2048]{1,0:T(8,128)} %fusion.171.z_ref.x_ref, f32[512,2048]{1,0:T(8,128)} %fusion.171.z_ref.x_ref, f32[8,3072]{1,0:T(8,128)} %slice.390.conv_ref, ...), custom_call_target="tpu_custom_call" | custom-call | flops 2400000000 | bytes 12000000 | tf_op jit(solution)/shard_map/pallas_call | solution.py:359
  329.8 5.0 fusion.6.dg_ref
  334.9 5.0 fusion.8.dg_ref
  339.9 5.2 fusion.10.dg_ref
  345.0 10.1 %fusion.4 = (f32[512]{0:T(512)S(1)}, bf16[512,1536]{1,0:T(8,128)(2,1)}) fusion(bf16[8,64,1536]{2,1,0:T(8,128)(2,1)S(1)} %all-to-all-done.2, bf16[8,64,1536]{2,1,0:T(8,128)(2,1)S(1)} %all-to-all-done, bf16[512,3072]{1,0:T(8,128)(2,1)S(1)} %copy-done.13, bf16[3072,1536]{1,0:T(8,128)(2,1)} %constant_dynamic-update-slice_fusion.13), kind=kOutput, calls=%fused_computation.16 | convolution fusion | flops 4836556288 | bytes 17303552 | tf_op jit(solution)/shard_map/dot_general | solution.py:546
  356.1 21.2 %shard_map.218 = (bf16[512,2048]{1,0:T(8,128)(2,1)}, f32[8,1024]{1,0:T(8,128)}, f32[512,128]{1,0:T(8,128)}, f32[512,128]{1,0:T(8,128)}, f32[512,128]{1,0:T(8,128...) custom-call(s32[1]{0:T(128)} %bitcast.172, ...), custom_call_target="tpu_custom_call" | custom-call | flops 8000000000 | bytes 16000000 | tf_op jit(solution)/shard_map/pallas_call | solution.py:381
  377.3 21.2 %shard_map.217 = (bf16[512,2048]{1,0:T(8,128)(2,1)}, f32[8,1024]{1,0:T(8,128)}, f32[512,128]{1,0:T(8,128)}, f32[512,128]{1,0:T(8,128)}, f32[512,128]{1,0:T(8,128...) custom-call(s32[1]{0:T(128)} %bitcast.173, ...), custom_call_target="tpu_custom_call" | custom-call | flops 8000000000 | bytes 16000000 | tf_op jit(solution)/shard_map/pallas_call | solution.py:381
  398.6 21.4 %shard_map.216 = (bf16[512,2048]{1,0:T(8,128)(2,1)}, f32[8,1024]{1,0:T(8,128)}, f32[512,128]{1,0:T(8,128)}, f32[512,128]{1,0:T(8,128)}, f32[512,128]{1,0:T(8,128...) custom-call(s32[1]{0:T(128)} %bitcast.174, ...), custom_call_target="tpu_custom_call" | custom-call | flops 8000000000 | bytes 16000000 | tf_op jit(solution)/shard_map/pallas_call | solution.py:381
  427.1 7.0 shard_map.219
  438.0 6.2 fusion.176
  444.2 5.7 fusion.175
  457.3 5.6 fusion.177
  490.9 4.1 all-to-all-start.4
  495.0 5.7 convolution_convert_fusion.1
  509.0 4.3 all-to-all-start.1
  523.9 12.6 %collective-permute-done.71 = bf16[192,384]{1,0:T(8,128)(2,1)S(1)} collective-permute-done((bf16[192,384]{1,0:T(8,128)(2,1)S(1)}, bf16[192,384]{1,0:T(8,128)(2,1)S(1)}, u32[]{:S(2)}, u32[]{:S(2)}) %collective-permute-start.71) | collective-permute-done | bytes 147488 | tf_op jit(solution)/shard_map/ppermute | solution.py:427
  546.1 5.7 convolution_convert_fusion
  556.9 13.1 %all-gather.3 = f32[4,1,2688]{2,1,0:T(1,128)S(1)} all-gather(f32[1,1,2688]{2,1,0:T(1,128)S(1)} %reshape.271), channel_id=3, replica_groups=mesh['rep'=4,'fsdp'=8] {'rep'}, dimensions={0}, use_global_device_ids=true | all-gather | bytes 53760 | tf_op jit(solution)/shard_map/all_gather | solution.py:587
  622.1 16.6 %collective-permute-done.79 = bf16[192,1536]{1,0:T(8,128)(2,1)S(1)} collective-permute-done((bf16[192,1536]{1,0:T(8,128)(2,1)S(1)}, bf16[192,1536]{1,0:T(8,128)(2,1)S(1)}, u32[]{:S(2)}, u32[]{:S(2)}) %collective-permute-start.79) | collective-permute-done | bytes 589856 | tf_op jit(solution)/shard_map/ppermute | solution.py:427
  642.7 14.3 %collective-permute-done.77 = bf16[192,1536]{1,0:T(8,128)(2,1)S(1)} collective-permute-done((bf16[192,1536]{1,0:T(8,128)(2,1)S(1)}, bf16[192,1536]{1,0:T(8,128)(2,1)S(1)}, u32[]{:S(2)}, u32[]{:S(2)}) %collective-permute-start.77) | collective-permute-done | bytes 589856 | tf_op jit(solution)/shard_map/ppermute | solution.py:427
  666.1 4.9 collective-permute-start.45
  673.9 7.0 collective-permute-done.62
  681.3 5.4 collective-permute-start.54
  689.2 4.3 collective-permute-start.63
  695.9 10.2 %collective-permute-done.54 = bf16[192,2048]{1,0:T(8,128)(2,1)} collective-permute-done((bf16[192,2048]{1,0:T(8,128)(2,1)}, bf16[192,2048]{1,0:T(8,128)(2,1)}, u32[]{:S(2)}, u32[]{:S(2)}) %collective-permute-start.54) | collective-permute-done | bytes 786464 | tf_op jit(solution)/shard_map/ppermute | solution.py:431
  709.0 9.4 %collective-permute-done.63 = bf16[192,2048]{1,0:T(8,128)(2,1)S(1)} collective-permute-done((bf16[192,2048]{1,0:T(8,128)(2,1)}, bf16[192,2048]{1,0:T(8,128)(2,1)S(1)}, u32[]{:S(2)}, u32[]{:S(2)}) %collective-permute-start.63) | collective-permute-done | bytes 786464 | tf_op jit(solution)/shard_map/ppermute | solution.py:431
  723.1 8.8 %collective-permute-start.81 = (bf16[384,1536]{1,0:T(8,128)(2,1)S(1)}, bf16[384,1536]{1,0:T(8,128)(2,1)S(1)}, u32[]{:S(2)}, u32[]{:S(2)}) collective-permute-start(bf16[384,1536]{1,0:T(8,128)(2,1)S(1)} %get-tuple-element.175), channel_id=1, source_target_pairs={{0,8},{24,16},{1,9},{25,17},{2,10},{26,18},{3,11},{27,19},{4,12},{... | collective-permute-start | bytes 3538952 | tf_op jit(solution)/shard_map/ppermute | solution.py:431
  739.0 13.3 %collective-permute-done.81 = bf16[384,1536]{1,0:T(8,128)(2,1)S(1)} collective-permute-done((bf16[384,1536]{1,0:T(8,128)(2,1)S(1)}, bf16[384,1536]{1,0:T(8,128)(2,1)S(1)}, u32[]{:S(2)}, u32[]{:S(2)}) %collective-permute-start.81) | collective-permute-done | bytes 1179680 | tf_op jit(solution)/shard_map/ppermute | solution.py:431
  755.6 15.8 %collective-permute-done.48 = bf16[192,2048]{1,0:T(8,128)(2,1)S(1)} collective-permute-done((bf16[192,2048]{1,0:T(8,128)(2,1)S(1)}, bf16[192,2048]{1,0:T(8,128)(2,1)S(1)}, u32[]{:S(2)}, u32[]{:S(2)}) %collective-permute-start.48) | collective-permute-done | bytes 786464 | tf_op jit(solution)/shard_map/ppermute | solution.py:431
  771.5 13.6 %collective-permute-done.57 = bf16[192,2048]{1,0:T(8,128)(2,1)S(1)} collective-permute-done((bf16[192,2048]{1,0:T(8,128)(2,1)S(1)}, bf16[192,2048]{1,0:T(8,128)(2,1)S(1)}, u32[]{:S(2)}, u32[]{:S(2)}) %collective-permute-start.57) | collective-permute-done | bytes 786464 | tf_op jit(solution)/shard_map/ppermute | solution.py:431
  786.3 13.2 %collective-permute-done.66 = bf16[192,2048]{1,0:T(8,128)(2,1)S(1)} collective-permute-done((bf16[192,2048]{1,0:T(8,128)(2,1)S(1)}, bf16[192,2048]{1,0:T(8,128)(2,1)S(1)}, u32[]{:S(2)}, u32[]{:S(2)}) %collective-permute-start.66) | collective-permute-done | bytes 786464 | tf_op jit(solution)/shard_map/ppermute | solution.py:431
  804.0 14.8 %collective-permute-done.84 = bf16[384,1536]{1,0:T(8,128)(2,1)S(1)} collective-permute-done((bf16[384,1536]{1,0:T(8,128)(2,1)S(1)}, bf16[384,1536]{1,0:T(8,128)(2,1)S(1)}, u32[]{:S(2)}, u32[]{:S(2)}) %collective-permute-start.84) | collective-permute-done | bytes 1179680 | tf_op jit(solution)/shard_map/ppermute | solution.py:431
  (576 shorter events, 329.5 us)
Async XLA Ops:
  8.4 89.9 %collective-permute-start.24 = (bf16[192,2048]{1,0:T(8,128)(2,1)}, bf16[192,2048]{1,0:T(8,128)(2,1)}, u32[]{:S(2)}, u32[]{:S(2)}) collective-permute-start(bf16[192,2048]{1,0:T(8,128)(2,1)} %get-tuple-element.151), channel_id=1, source_target_pairs={{0,1},{1,0},{2,3},{3,2},{4,5},{5,4},{6,7},{7,6},{8,9},{9,8},{10,11... | collective-permute-start | bytes 2359304 | tf_op jit(solution)/shard_map/ppermute | solution.py:427
  8.8 91.0 %collective-permute-start.25 = (bf16[192,2048]{1,0:T(8,128)(2,1)}, bf16[192,2048]{1,0:T(8,128)(2,1)}, u32[]{:S(2)}, u32[]{:S(2)}) collective-permute-start(bf16[192,2048]{1,0:T(8,128)(2,1)} %get-tuple-element.151), channel_id=1, source_target_pairs={{0,2},{1,3},{2,0},{3,1},{4,6},{5,7},{6,4},{7,5},{8,10},{9,11},{10,... | collective-permute-start | bytes 2359304 | tf_op jit(solution)/shard_map/ppermute | solution.py:427
  12.1 62.9 %collective-permute-start.8 = (bf16[192,384]{1,0:T(8,128)(2,1)}, bf16[192,384]{1,0:T(8,128)(2,1)}, u32[]{:S(2)}, u32[]{:S(2)}) collective-permute-start(bf16[192,384]{1,0:T(8,128)(2,1)} %get-tuple-element.155), channel_id=1, source_target_pairs={{0,1},{1,0},{2,3},{3,2},{4,5},{5,4},{6,7},{7,6},{8,9},{9,8},{10,11... | collective-permute-start | bytes 442376 | tf_op jit(solution)/shard_map/ppermute | solution.py:427
  12.3 58.8 %collective-permute-start.9 = (bf16[192,384]{1,0:T(8,128)(2,1)}, bf16[192,384]{1,0:T(8,128)(2,1)}, u32[]{:S(2)}, u32[]{:S(2)}) collective-permute-start(bf16[192,384]{1,0:T(8,128)(2,1)} %get-tuple-element.155), channel_id=1, source_target_pairs={{0,2},{1,3},{2,0},{3,1},{4,6},{5,7},{6,4},{7,5},{8,10},{9,11},{10,... | collective-permute-start | bytes 442376 | tf_op jit(solution)/shard_map/ppermute | solution.py:427
  12.6 61.1 %collective-permute-start.11 = (bf16[192,384]{1,0:T(8,128)(2,1)}, bf16[192,384]{1,0:T(8,128)(2,1)}, u32[]{:S(2)}, u32[]{:S(2)}) collective-permute-start(bf16[192,384]{1,0:T(8,128)(2,1)} %get-tuple-element.155), channel_id=1, source_target_pairs={{0,4},{1,5},{2,6},{3,7},{4,0},{5,1},{6,2},{7,3},{8,12},{9,13},{10,... | collective-permute-start | bytes 442376 | tf_op jit(solution)/shard_map/ppermute | solution.py:427
  17.2 184.1 %all-to-all-start = ((bf16[8,64,1536]{2,1,0:T(8,128)(2,1)}), bf16[8,64,1536]{2,1,0:T(8,128)(2,1)S(1)}, u32[]{:S(2)}, u32[]{:S(2)}) async-start(bf16[8,64,1536]{2,1,0:T(8,128)(2,1)} %gather_fusion), calls=%async_computation | async-start | bytes 3145728 | tf_op jit(solution)/shard_map/all_to_all | solution.py:504
  71.1 30.2 %collective-permute-start.27 = (bf16[192,2048]{1,0:T(8,128)(2,1)}, bf16[192,2048]{1,0:T(8,128)(2,1)}, u32[]{:S(2)}, u32[]{:S(2)}) collective-permute-start(bf16[192,2048]{1,0:T(8,128)(2,1)} %get-tuple-element.151), channel_id=1, source_target_pairs={{0,4},{1,5},{2,6},{3,7},{4,0},{5,1},{6,2},{7,3},{8,12},{9,13},{10,... | collective-permute-start | bytes 2359304 | tf_op jit(solution)/shard_map/ppermute | solution.py:427
  98.3 32.7 %collective-permute-start.1 = (bf16[192,2048]{1,0:T(8,128)(2,1)}, bf16[192,2048]{1,0:T(8,128)(2,1)}, u32[]{:S(2)}, u32[]{:S(2)}) collective-permute-start(bf16[192,2048]{1,0:T(8,128)(2,1)} %get-tuple-element.147), channel_id=1, source_target_pairs={{0,2},{1,3},{2,0},{3,1},{4,6},{5,7},{6,4},{7,5},{8,10},{9,11},{10,... | collective-permute-start | bytes 2359304 | tf_op jit(solution)/shard_map/ppermute | solution.py:427
  99.9 34.9 %collective-permute-start.3 = (bf16[192,2048]{1,0:T(8,128)(2,1)}, bf16[192,2048]{1,0:T(8,128)(2,1)S(1)}, u32[]{:S(2)}, u32[]{:S(2)}) collective-permute-start(bf16[192,2048]{1,0:T(8,128)(2,1)} %get-tuple-element.147), channel_id=1, source_target_pairs={{0,4},{1,5},{2,6},{3,7},{4,0},{5,1},{6,2},{7,3},{8,12},{9,13},{10,... | collective-permute-start | bytes 2359304 | tf_op jit(solution)/shard_map/ppermute | solution.py:427
  101.3 36.1 %collective-permute-start.16 = (bf16[192,2048]{1,0:T(8,128)(2,1)}, bf16[192,2048]{1,0:T(8,128)(2,1)S(1)}, u32[]{:S(2)}, u32[]{:S(2)}) collective-permute-start(bf16[192,2048]{1,0:T(8,128)(2,1)} %get-tuple-element.149), channel_id=1, source_target_pairs={{0,1},{1,0},{2,3},{3,2},{4,5},{5,4},{6,7},{7,6},{8,9},{9,8},{10,11... | collective-permute-start | bytes 2359304 | tf_op jit(solution)/shard_map/ppermute | solution.py:427
  115.0 27.1 %collective-permute-start = (bf16[192,2048]{1,0:T(8,128)(2,1)}, bf16[192,2048]{1,0:T(8,128)(2,1)S(1)}, u32[]{:S(2)}, u32[]{:S(2)}) collective-permute-start(bf16[192,2048]{1,0:T(8,128)(2,1)} %get-tuple-element.147), channel_id=1, source_target_pairs={{0,1},{1,0},{2,3},{3,2},{4,5},{5,4},{6,7},{7,6},{8,9},{9,8},{10,11... | collective-permute-start | bytes 2359304 | tf_op jit(solution)/shard_map/ppermute | solution.py:427
  120.3 78.3 %collective-permute-start.32 = (bf16[384,1536]{1,0:T(8,128)(2,1)S(1)}, bf16[384,1536]{1,0:T(8,128)(2,1)S(1)}, u32[]{:S(2)}, u32[]{:S(2)}) collective-permute-start(bf16[384,1536]{1,0:T(8,128)(2,1)S(1)} %copy-done.39), channel_id=1, source_target_pairs={{0,1},{1,0},{2,3},{3,2},{4,5},{5,4},{6,7},{7,6},{8,9},{9,8},{10,11... | collective-permute-start | bytes 3538952 | tf_op jit(solution)/shard_map/ppermute | solution.py:427
  131.1 41.6 %collective-permute-start.33 = (bf16[384,1536]{1,0:T(8,128)(2,1)S(1)}, bf16[384,1536]{1,0:T(8,128)(2,1)S(1)}, u32[]{:S(2)}, u32[]{:S(2)}) collective-permute-start(bf16[384,1536]{1,0:T(8,128)(2,1)S(1)} %copy-done.39), channel_id=1, source_target_pairs={{0,2},{1,3},{2,0},{3,1},{4,6},{5,7},{6,4},{7,5},{8,10},{9,11},{10,... | collective-permute-start | bytes 3538952 | tf_op jit(solution)/shard_map/ppermute | solution.py:427
  134.8 40.4 %collective-permute-start.35 = (bf16[384,1536]{1,0:T(8,128)(2,1)S(1)}, bf16[384,1536]{1,0:T(8,128)(2,1)S(1)}, u32[]{:S(2)}, u32[]{:S(2)}) collective-permute-start(bf16[384,1536]{1,0:T(8,128)(2,1)S(1)} %copy-done.39), channel_id=1, source_target_pairs={{0,4},{1,5},{2,6},{3,7},{4,0},{5,1},{6,2},{7,3},{8,12},{9,13},{10,... | collective-permute-start | bytes 3538952 | tf_op jit(solution)/shard_map/ppermute | solution.py:427
  137.4 34.7 %collective-permute-start.29 = (bf16[96,2048]{1,0:T(8,128)(2,1)S(1)}, bf16[96,2048]{1,0:T(8,128)(2,1)S(1)}, u32[]{:S(2)}, u32[]{:S(2)}) collective-permute-start(bf16[96,2048]{1,0:T(8,128)(2,1)S(1)} %slice.400), channel_id=1, source_target_pairs={{0,4},{1,5},{2,6},{3,7},{4,0},{5,1},{6,2},{7,3},{8,12},{9,13},{10,... | collective-permute-start | bytes 1179656 | tf_op jit(solution)/shard_map/ppermute | solution.py:427
  142.1 38.4 %collective-permute-start.21 = (bf16[96,2048]{1,0:T(8,128)(2,1)S(1)}, bf16[96,2048]{1,0:T(8,128)(2,1)S(1)}, u32[]{:S(2)}, u32[]{:S(2)}) collective-permute-start(bf16[96,2048]{1,0:T(8,128)(2,1)S(1)} %slice.398), channel_id=1, source_target_pairs={{0,4},{1,5},{2,6},{3,7},{4,0},{5,1},{6,2},{7,3},{8,12},{9,13},{10,... | collective-permute-start | bytes 1179656 | tf_op jit(solution)/shard_map/ppermute | solution.py:427
  187.7 26.4 %collective-permute-start.26 = (bf16[192,2048]{1,0:T(8,128)(2,1)}, bf16[192,2048]{1,0:T(8,128)(2,1)}, u32[]{:S(2)}, u32[]{:S(2)}) collective-permute-start(bf16[192,2048]{1,0:T(8,128)(2,1)} %collective-permute-done.25), channel_id=1, source_target_pairs={{0,1},{1,0},{2,3},{3,2},{4,5},{5,4},{6,7},{7,6},{8,9},{9,8},{10,11... | collective-permute-start | bytes 2359304 | tf_op jit(solution)/shard_map/ppermute | solution.py:427
  188.5 30.3 %collective-permute-start.28 = (bf16[192,2048]{1,0:T(8,128)(2,1)}, bf16[192,2048]{1,0:T(8,128)(2,1)}, u32[]{:S(2)}, u32[]{:S(2)}) collective-permute-start(bf16[192,2048]{1,0:T(8,128)(2,1)} %collective-permute-done.27), channel_id=1, source_target_pairs={{0,1},{1,0},{2,3},{3,2},{4,5},{5,4},{6,7},{7,6},{8,9},{9,8},{10,11... | collective-permute-start | bytes 2359304 | tf_op jit(solution)/shard_map/ppermute | solution.py:427
  193.2 28.9 %collective-permute-start.18 = (bf16[192,2048]{1,0:T(8,128)(2,1)}, bf16[192,2048]{1,0:T(8,128)(2,1)}, u32[]{:S(2)}, u32[]{:S(2)}) collective-permute-start(bf16[192,2048]{1,0:T(8,128)(2,1)} %collective-permute-done.17), channel_id=1, source_target_pairs={{0,1},{1,0},{2,3},{3,2},{4,5},{5,4},{6,7},{7,6},{8,9},{9,8},{10,11... | collective-permute-start | bytes 2359304 | tf_op jit(solution)/shard_map/ppermute | solution.py:427
  197.7 28.9 %collective-permute-start.20 = (bf16[192,2048]{1,0:T(8,128)(2,1)}, bf16[192,2048]{1,0:T(8,128)(2,1)}, u32[]{:S(2)}, u32[]{:S(2)}) collective-permute-start(bf16[192,2048]{1,0:T(8,128)(2,1)} %collective-permute-done.19), channel_id=1, source_target_pairs={{0,1},{1,0},{2,3},{3,2},{4,5},{5,4},{6,7},{7,6},{8,9},{9,8},{10,11... | collective-permute-start | bytes 2359304 | tf_op jit(solution)/shard_map/ppermute | solution.py:427
  198.5 32.6 %collective-permute-start.2 = (bf16[192,2048]{1,0:T(8,128)(2,1)}, bf16[192,2048]{1,0:T(8,128)(2,1)}, u32[]{:S(2)}, u32[]{:S(2)}) collective-permute-start(bf16[192,2048]{1,0:T(8,128)(2,1)} %collective-permute-done.1), channel_id=1, source_target_pairs={{0,1},{1,0},{2,3},{3,2},{4,5},{5,4},{6,7},{7,6},{8,9},{9,8},{10,11... | collective-permute-start | bytes 2359304 | tf_op jit(solution)/shard_map/ppermute | solution.py:427
  201.3 128.6 %all-to-all-start.2 = ((bf16[8,64,1536]{2,1,0:T(8,128)(2,1)}), bf16[8,64,1536]{2,1,0:T(8,128)(2,1)S(1)}, u32[]{:S(2)}, u32[]{:S(2)}) async-start(bf16[8,64,1536]{2,1,0:T(8,128)(2,1)} %gather_fusion.2), calls=%async_computation.2 | async-start | bytes 3145728 | tf_op jit(solution)/shard_map/all_to_all | solution.py:504
  218.8 32.7 %collective-permute-start.31 = (bf16[192,2048]{1,0:T(8,128)(2,1)S(1)}, bf16[192,2048]{1,0:T(8,128)(2,1)S(1)}, u32[]{:S(2)}, u32[]{:S(2)}) collective-permute-start(bf16[192,2048]{1,0:T(8,128)(2,1)S(1)} %copy-done.34), channel_id=1, source_target_pairs={{0,1},{1,0},{2,3},{3,2},{4,5},{5,4},{6,7},{7,6},{8,9},{9,8},{10,11... | collective-permute-start | bytes 2359304 | tf_op jit(solution)/shard_map/ppermute | solution.py:427
  222.1 49.7 %collective-permute-start.23 = (bf16[192,2048]{1,0:T(8,128)(2,1)}, bf16[192,2048]{1,0:T(8,128)(2,1)}, u32[]{:S(2)}, u32[]{:S(2)}) collective-permute-start(bf16[192,2048]{1,0:T(8,128)(2,1)} %constant_dynamic-update-slice_fusion.4), channel_id=1, source_target_pairs={{0,1},{1,0},{2,3},{3,2},{4,5},{5,4},{6,7},{7,6},{8,9},{9,8},{10,11... | collective-permute-start | bytes 2359304 | tf_op jit(solution)/shard_map/ppermute | solution.py:427
  226.6 66.4 %collective-permute-start.7 = (bf16[192,2048]{1,0:T(8,128)(2,1)}, bf16[192,2048]{1,0:T(8,128)(2,1)}, u32[]{:S(2)}, u32[]{:S(2)}) collective-permute-start(bf16[192,2048]{1,0:T(8,128)(2,1)} %constant_dynamic-update-slice_fusion), channel_id=1, source_target_pairs={{0,1},{1,0},{2,3},{3,2},{4,5},{5,4},{6,7},{7,6},{8,9},{9,8},{10,11... | collective-permute-start | bytes 2359304 | tf_op jit(solution)/shard_map/ppermute | solution.py:427
  246.8 73.5 %collective-permute-start.34 = (bf16[384,1536]{1,0:T(8,128)(2,1)S(1)}, bf16[384,1536]{1,0:T(8,128)(2,1)}, u32[]{:S(2)}, u32[]{:S(2)}) collective-permute-start(bf16[384,1536]{1,0:T(8,128)(2,1)S(1)} %copy-done.30), channel_id=1, source_target_pairs={{0,1},{1,0},{2,3},{3,2},{4,5},{5,4},{6,7},{7,6},{8,9},{9,8},{10,11... | collective-permute-start | bytes 3538952 | tf_op jit(solution)/shard_map/ppermute | solution.py:427
  251.4 72.6 %collective-permute-start.36 = (bf16[384,1536]{1,0:T(8,128)(2,1)S(1)}, bf16[384,1536]{1,0:T(8,128)(2,1)}, u32[]{:S(2)}, u32[]{:S(2)}) collective-permute-start(bf16[384,1536]{1,0:T(8,128)(2,1)S(1)} %copy-done.28), channel_id=1, source_target_pairs={{0,1},{1,0},{2,3},{3,2},{4,5},{5,4},{6,7},{7,6},{8,9},{9,8},{10,11... | collective-permute-start | bytes 3538952 | tf_op jit(solution)/shard_map/ppermute | solution.py:427
  251.5 76.0 %collective-permute-start.39 = (bf16[384,1536]{1,0:T(8,128)(2,1)S(1)}, bf16[384,1536]{1,0:T(8,128)(2,1)}, u32[]{:S(2)}, u32[]{:S(2)}) collective-permute-start(bf16[384,1536]{1,0:T(8,128)(2,1)S(1)} %constant_dynamic-update-slice_fusion.8), channel_id=1, source_target_pairs={{0,1},{1,0},{2,3},{3,2},{4,5},{5,4},{6,7},{7,6},{8,9},{9,8},{10,11... | collective-permute-start | bytes 3538952 | tf_op jit(solution)/shard_map/ppermute | solution.py:427
  507.0 73.2 %collective-permute-start.40 = (bf16[768,2048]{1,0:T(8,128)(2,1)}, bf16[768,2048]{1,0:T(8,128)(2,1)}, u32[]{:S(2)}, u32[]{:S(2)}) collective-permute-start(bf16[768,2048]{1,0:T(8,128)(2,1)} %convolution_convert_fusion.3), channel_id=1, source_target_pairs={{0,1},{1,0},{2,3},{3,2},{4,5},{5,4},{6,7},{7,6},{8,9},{9,8},{10,11... | collective-permute-start | bytes 9437192 | tf_op jit(solution)/shard_map/ppermute | solution.py:427
  507.0 80.1 %collective-permute-start.49 = (bf16[768,2048]{1,0:T(8,128)(2,1)}, bf16[768,2048]{1,0:T(8,128)(2,1)}, u32[]{:S(2)}, u32[]{:S(2)}) collective-permute-start(bf16[768,2048]{1,0:T(8,128)(2,1)} %convolution_convert_fusion.2), channel_id=1, source_target_pairs={{0,1},{1,0},{2,3},{3,2},{4,5},{5,4},{6,7},{7,6},{8,9},{9,8},{10,11... | collective-permute-start | bytes 9437192 | tf_op jit(solution)/shard_map/ppermute | solution.py:427
  507.5 83.8 %collective-permute-start.58 = (bf16[768,2048]{1,0:T(8,128)(2,1)}, bf16[768,2048]{1,0:T(8,128)(2,1)}, u32[]{:S(2)}, u32[]{:S(2)}) collective-permute-start(bf16[768,2048]{1,0:T(8,128)(2,1)} %convolution_convert_fusion.1), channel_id=1, source_target_pairs={{0,1},{1,0},{2,3},{3,2},{4,5},{5,4},{6,7},{7,6},{8,9},{9,8},{10,11... | collective-permute-start | bytes 9437192 | tf_op jit(solution)/shard_map/ppermute | solution.py:427
  509.0 33.4 %all-to-all-start.1 = ((bf16[8,64,1536]{2,1,0:T(8,128)(2,1)}), bf16[8,64,1536]{2,1,0:T(8,128)(2,1)}, u32[]{:S(2)}, u32[]{:S(2)}) async-start(bf16[8,64,1536]{2,1,0:T(8,128)(2,1)} %bitcast.135), calls=%async_computation.1 | async-start | bytes 3145728 | tf_op jit(solution)/shard_map/all_to_all | solution.py:507
  542.4 35.9 %all-to-all-start.3 = ((bf16[8,64,1536]{2,1,0:T(8,128)(2,1)}), bf16[8,64,1536]{2,1,0:T(8,128)(2,1)S(1)}, u32[]{:S(2)}, u32[]{:S(2)}) async-start(bf16[8,64,1536]{2,1,0:T(8,128)(2,1)} %bitcast.134), calls=%async_computation.3 | async-start | bytes 3145728 | tf_op jit(solution)/shard_map/all_to_all | solution.py:507
  551.8 59.0 %collective-permute-start.76 = (bf16[1536,1536]{1,0:T(8,128)(2,1)}, bf16[1536,1536]{1,0:T(8,128)(2,1)}, u32[]{:S(2)}, u32[]{:S(2)}) collective-permute-start(bf16[1536,1536]{1,0:T(8,128)(2,1)} %convolution_convert_fusion), channel_id=1, source_target_pairs={{0,1},{1,0},{2,3},{3,2},{4,5},{5,4},{6,7},{7,6},{8,9},{9,8},{10,11... | collective-permute-start | bytes 14155784 | tf_op jit(solution)/shard_map/ppermute | solution.py:427
  603.3 57.1 %collective-permute-start.44 = (bf16[192,2048]{1,0:T(8,128)(2,1)}, bf16[192,2048]{1,0:T(8,128)(2,1)}, u32[]{:S(2)}, u32[]{:S(2)}) collective-permute-start(bf16[192,2048]{1,0:T(8,128)(2,1)} %fusion.42), channel_id=1, source_target_pairs={{0,4},{1,5},{2,6},{3,7},{4,0},{5,1},{6,2},{7,3},{8,12},{9,13},{10,... | collective-permute-start | bytes 2359304 | tf_op jit(solution)/shard_map/ppermute | solution.py:427
  607.3 54.6 %collective-permute-start.42 = (bf16[192,2048]{1,0:T(8,128)(2,1)}, bf16[192,2048]{1,0:T(8,128)(2,1)}, u32[]{:S(2)}, u32[]{:S(2)}) collective-permute-start(bf16[192,2048]{1,0:T(8,128)(2,1)} %fusion.45), channel_id=1, source_target_pairs={{0,2},{1,3},{2,0},{3,1},{4,6},{5,7},{6,4},{7,5},{8,10},{9,11},{10,... | collective-permute-start | bytes 2359304 | tf_op jit(solution)/shard_map/ppermute | solution.py:427
  610.8 55.0 %collective-permute-start.53 = (bf16[192,2048]{1,0:T(8,128)(2,1)}, bf16[192,2048]{1,0:T(8,128)(2,1)}, u32[]{:S(2)}, u32[]{:S(2)}) collective-permute-start(bf16[192,2048]{1,0:T(8,128)(2,1)} %fusion.35), channel_id=1, source_target_pairs={{0,4},{1,5},{2,6},{3,7},{4,0},{5,1},{6,2},{7,3},{8,12},{9,13},{10,... | collective-permute-start | bytes 2359304 | tf_op jit(solution)/shard_map/ppermute | solution.py:427
  618.0 39.0 %collective-permute-start.77 = (bf16[192,1536]{1,0:T(8,128)(2,1)S(1)}, bf16[192,1536]{1,0:T(8,128)(2,1)S(1)}, u32[]{:S(2)}, u32[]{:S(2)}) collective-permute-start(bf16[192,1536]{1,0:T(8,128)(2,1)S(1)} %get-tuple-element.139), channel_id=1, source_target_pairs={{0,4},{1,5},{2,6},{3,7},{4,0},{5,1},{6,2},{7,3},{8,12},{9,13},{10,... | collective-permute-start | bytes 1769480 | tf_op jit(solution)/shard_map/ppermute | solution.py:427
  638.7 27.4 %collective-permute-start.51 = (bf16[192,2048]{1,0:T(8,128)(2,1)S(1)}, bf16[192,2048]{1,0:T(8,128)(2,1)S(1)}, u32[]{:S(2)}, u32[]{:S(2)}) collective-permute-start(bf16[192,2048]{1,0:T(8,128)(2,1)S(1)} %copy-done.42), channel_id=1, source_target_pairs={{0,2},{1,3},{2,0},{3,1},{4,6},{5,7},{6,4},{7,5},{8,10},{9,11},{10,... | collective-permute-start | bytes 2359304 | tf_op jit(solution)/shard_map/ppermute | solution.py:427
  657.0 144.4 %collective-permute-start.75 = (bf16[192,384]{1,0:T(8,128)(2,1)S(1)}, bf16[192,384]{1,0:T(8,128)(2,1)S(1)}, u32[]{:S(2)}, u32[]{:S(2)}) collective-permute-start(bf16[192,384]{1,0:T(8,128)(2,1)S(1)} %maximum_select_fusion.4), channel_id=1, source_target_pairs={{8,0},{16,24},{9,1},{17,25},{10,2},{18,26},{11,3},{19,27},{12,4},{... | collective-permute-start | bytes 442376 | tf_op jit(solution)/shard_map/ppermute | solution.py:431
  665.8 54.0 %collective-permute-start.80 = (bf16[384,1536]{1,0:T(8,128)(2,1)}, bf16[384,1536]{1,0:T(8,128)(2,1)}, u32[]{:S(2)}, u32[]{:S(2)}) collective-permute-start(bf16[384,1536]{1,0:T(8,128)(2,1)} %fusion.21), channel_id=1, source_target_pairs={{0,4},{1,5},{2,6},{3,7},{4,0},{5,1},{6,2},{7,3},{8,12},{9,13},{10,... | collective-permute-start | bytes 3538952 | tf_op jit(solution)/shard_map/ppermute | solution.py:427
  680.9 39.5 %collective-permute-start.78 = (bf16[384,1536]{1,0:T(8,128)(2,1)}, bf16[384,1536]{1,0:T(8,128)(2,1)}, u32[]{:S(2)}, u32[]{:S(2)}) collective-permute-start(bf16[384,1536]{1,0:T(8,128)(2,1)} %fusion.24), channel_id=1, source_target_pairs={{0,2},{1,3},{2,0},{3,1},{4,6},{5,7},{6,4},{7,5},{8,10},{9,11},{10,... | collective-permute-start | bytes 3538952 | tf_op jit(solution)/shard_map/ppermute | solution.py:427
  689.2 29.1 %collective-permute-start.63 = (bf16[192,2048]{1,0:T(8,128)(2,1)}, bf16[192,2048]{1,0:T(8,128)(2,1)S(1)}, u32[]{:S(2)}, u32[]{:S(2)}) collective-permute-start(bf16[192,2048]{1,0:T(8,128)(2,1)} %get-tuple-element.171), channel_id=1, source_target_pairs={{0,8},{24,16},{1,9},{25,17},{2,10},{26,18},{3,11},{27,19},{4,12},{... | collective-permute-start | bytes 2359304 | tf_op jit(solution)/shard_map/ppermute | solution.py:431
  723.1 29.1 %collective-permute-start.81 = (bf16[384,1536]{1,0:T(8,128)(2,1)S(1)}, bf16[384,1536]{1,0:T(8,128)(2,1)S(1)}, u32[]{:S(2)}, u32[]{:S(2)}) collective-permute-start(bf16[384,1536]{1,0:T(8,128)(2,1)S(1)} %get-tuple-element.175), channel_id=1, source_target_pairs={{0,8},{24,16},{1,9},{25,17},{2,10},{26,18},{3,11},{27,19},{4,12},{... | collective-permute-start | bytes 3538952 | tf_op jit(solution)/shard_map/ppermute | solution.py:431
  734.7 36.8 %collective-permute-start.48 = (bf16[192,2048]{1,0:T(8,128)(2,1)S(1)}, bf16[192,2048]{1,0:T(8,128)(2,1)S(1)}, u32[]{:S(2)}, u32[]{:S(2)}) collective-permute-start(bf16[192,2048]{1,0:T(8,128)(2,1)S(1)} %maximum_select_fusion.1), channel_id=1, source_target_pairs={{8,0},{16,24},{9,1},{17,25},{10,2},{18,26},{11,3},{19,27},{12,4},{... | collective-permute-start | bytes 2359304 | tf_op jit(solution)/shard_map/ppermute | solution.py:431
  736.2 48.9 %collective-permute-start.57 = (bf16[192,2048]{1,0:T(8,128)(2,1)S(1)}, bf16[192,2048]{1,0:T(8,128)(2,1)S(1)}, u32[]{:S(2)}, u32[]{:S(2)}) collective-permute-start(bf16[192,2048]{1,0:T(8,128)(2,1)S(1)} %maximum_select_fusion.2), channel_id=1, source_target_pairs={{8,0},{16,24},{9,1},{17,25},{10,2},{18,26},{11,3},{19,27},{12,4},{... | collective-permute-start | bytes 2359304 | tf_op jit(solution)/shard_map/ppermute | solution.py:431
  737.7 61.8 %collective-permute-start.66 = (bf16[192,2048]{1,0:T(8,128)(2,1)S(1)}, bf16[192,2048]{1,0:T(8,128)(2,1)S(1)}, u32[]{:S(2)}, u32[]{:S(2)}) collective-permute-start(bf16[192,2048]{1,0:T(8,128)(2,1)S(1)} %maximum_select_fusion.3), channel_id=1, source_target_pairs={{8,0},{16,24},{9,1},{17,25},{10,2},{18,26},{11,3},{19,27},{12,4},{... | collective-permute-start | bytes 2359304 | tf_op jit(solution)/shard_map/ppermute | solution.py:431
  754.9 30.3 %collective-permute-start.82 = (bf16[192,1536]{1,0:T(8,128)(2,1)S(1)}, bf16[192,1536]{1,0:T(8,128)(2,1)S(1)}, u32[]{:S(2)}, u32[]{:S(2)}) collective-permute-start(bf16[192,1536]{1,0:T(8,128)(2,1)S(1)} %select_convert_fusion.1), channel_id=1, source_target_pairs={{8,16},{16,8},{9,17},{17,9},{10,18},{18,10},{11,19},{19,11},{12,20... | collective-permute-start | bytes 1769480 | tf_op jit(solution)/shard_map/ppermute | solution.py:431
  (138 other events, 1506.3 us)

commit v3 on v1

v3 whole, which is shorter than its diff:
```python
import functools

import jax
import jax.numpy as jnp
from jax import lax
from jax.experimental import pallas as pl
from jax.experimental.pallas import tpu as pltpu
from jax.sharding import PartitionSpec as P

DI = 3072
HEAD_DIM = 64
NSTATE = 128
KW = 4
HEADS = 48
BCD = 384

epsilon = 1e-05


Q = 128
GROUP = 8
LANES = GROUP * HEAD_DIM
NEG = -1e30
VMEM = 56 * 1024 * 1024
BIG = 56 * 1024 * 1024


def dot32(a, b, dims=(((1,), (0,)), ((), ())), precision=None):
    return lax.dot_general(a, b, dims, preferred_element_type=jnp.float32, precision=precision)


NT = (((1,), (1,)), ((), ()))


def row_ids(start, rows, cols):
    return lax.broadcasted_iota(jnp.int32, (rows, cols), 0) + start


def shifted_down(ref, cols, c, first, width):
    if c == 0:
        tall = jnp.concatenate([jnp.zeros((8, width), jnp.float32), ref[0:Q, cols]], axis=0)
    else:
        tall = ref[c * Q - 8 : c * Q + Q, cols]
    place = row_ids(c * Q, Q, width)
    outs = [tall[8:]]
    for j in range(1, KW):
        moved = pltpu.roll(tall, j, 0)[8:]
        keep = (place >= j) & ((place < first) | (place >= first + j))
        outs.append(jnp.where(keep, moved, 0.0))
    return outs


def conv_back(ref, cols, c, first, width, taps):
    tall = ref[c * Q : c * Q + Q + 8, cols]
    place = row_ids(c * Q, Q, width)
    total = taps[KW - 1] * tall[:Q]
    for j in range(1, KW):
        moved = pltpu.roll(tall, Q + 8 - j, 0)[:Q]
        keep = (place < first - j) | (place >= first)
        total = total + taps[KW - 1 - j] * jnp.where(keep, moved, 0.0)
    return total


def sigmoid(v):
    return 0.5 * jnp.tanh(0.5 * v) + 0.5


def sum_rows(v):
    return jnp.sum(v, axis=0, keepdims=True)


def prep_kernel(first_ref, bcd_ref, conv_ref, head_ref, wide_ref, tall_ref, bc_ref, bct_ref):
    first = first_ref[0]
    tri = (row_ids(0, Q, Q) >= lax.broadcasted_iota(jnp.int32, (Q, Q), 1)).astype(jnp.float32)
    rate = -jnp.exp(head_ref[1:2, :])
    lane = lax.broadcasted_iota(jnp.int32, (Q, 128), 1)
    for c in range(bcd_ref.shape[0] // Q):
        rows = slice(c * Q, c * Q + Q)
        moved = shifted_down(bcd_ref, slice(0, 2 * NSTATE), c, first, 2 * NSTATE)
        mixed = conv_ref[4:5, :] + conv_ref[3:4, :] * moved[0]
        for j in range(1, KW):
            mixed = mixed + conv_ref[KW - 1 - j : KW - j, :] * moved[j]
        act = mixed * sigmoid(mixed)
        b32, c32 = act[:, :NSTATE], act[:, NSTATE:]
        b16, c16 = b32.astype(jnp.bfloat16), c32.astype(jnp.bfloat16)
        bc_ref[rows, :] = act.astype(jnp.bfloat16)
        bct_ref[:NSTATE, rows] = b32.T.astype(jnp.bfloat16)
        bct_ref[NSTATE:, rows] = c32.T.astype(jnp.bfloat16)
        wide_ref[rows, :Q] = dot32(c16, b16, NT)
        wide_ref[rows, Q : 2 * Q] = dot32(b16, c16, NT)
        raw = jnp.where(lane < HEADS, bcd_ref[rows, 2 * NSTATE :] + head_ref[0:1, :], 0.0)
        step = jax.nn.softplus(raw)
        cum = dot32(tri, rate * step, precision=lax.Precision.HIGHEST)
        cp = cum - jnp.log(jnp.maximum(step, 1e-37))
        wide_ref[rows, 2 * Q : 3 * Q] = cum
        wide_ref[rows, 3 * Q :] = cp
        tall_ref[:128, rows] = cum.T
        tall_ref[128:, rows] = cp.T


def chunk_masks(first, c, transposed):
    base = c * Q
    row = row_ids(base, Q, Q)
    col = lax.broadcasted_iota(jnp.int32, (Q, Q), 1) + base
    ordered = (col >= row) if transposed else (row >= col)
    inside = ordered & ((row >= first) == (col >= first))
    carry = ((row >= first) == (base - 1 >= first)) & (base > 0)
    last = (row >= first) == (base + Q - 1 >= first)
    through = (base > 0) & ((base + Q - 1 >= first) == (base - 1 >= first))
    return inside, carry, last, through


def lane_column(values, k):
    return jnp.broadcast_to(values[:, k : k + 1], (Q, Q))


def forward_kernel(first_ref, x_ref, conv_ref, gain_ref, wide_ref, tall_ref, bc_ref, bct_ref, ssm_ref, states_ref, state):
    first = first_ref[0]
    group = pl.program_id(0)
    half = lax.broadcasted_iota(jnp.int32, (Q, Q), 1) < HEAD_DIM
    state[...] = jnp.zeros_like(state)

    shift = (Q - GROUP * group) % Q
    for c in range(x_ref.shape[0] // Q):
        rows = slice(c * Q, c * Q + Q)
        inside, carry, last, through = chunk_masks(first, c, False)
        cum = pltpu.roll(wide_ref[rows, 2 * Q : 3 * Q], shift, 1)
        cp = pltpu.roll(wide_ref[rows, 3 * Q :], shift, 1)
        cpt = tall_ref[pl.ds(pl.multiple_of(128 + group * GROUP, GROUP), GROUP), rows]
        scores = wide_ref[rows, :Q]
        c16 = bc_ref[rows, NSTATE:]
        for p in range(GROUP // 2):
            cols = slice(p * Q, p * Q + Q)
            moved = shifted_down(x_ref, cols, c, first, Q)
            mixed = conv_ref[4:5, cols] + conv_ref[3:4, cols] * moved[0]
            for j in range(1, KW):
                mixed = mixed + conv_ref[KW - 1 - j : KW - j, cols] * moved[j]
            xs = mixed * sigmoid(mixed)
            x16 = xs.astype(jnp.bfloat16)
            locals_, cums, cps = [], [], []
            for e in range(2):
                k = 2 * p + e
                cum_b = lane_column(cum, k)
                decay = jnp.exp(jnp.where(inside, cum_b - cpt[k : k + 1, :], NEG))
                locals_.append(dot32((scores * decay).astype(jnp.bfloat16), x16))
                cums.append(cum_b)
                cps.append(lane_column(cp, k))
            cum_pair = jnp.where(half, cums[0], cums[1])
            cp_pair = jnp.where(half, cps[0], cps[1])
            y = jnp.where(half, locals_[0], locals_[1])
            old = state[:, cols]
            old16 = old.astype(jnp.bfloat16)
            states_ref[c * NSTATE : (c + 1) * NSTATE, cols] = old16
            if c > 0:
                y = y + jnp.where(carry, jnp.exp(cum_pair), 0.0) * dot32(c16, old16)
            ssm_ref[rows, cols] = y + gain_ref[0:1, cols] * xs
            end = cum_pair[Q - 1 : Q, :]
            weight = jnp.where(last, jnp.exp(end - cp_pair), 0.0)
            fresh = dot32(bct_ref[:NSTATE, rows], (weight * xs).astype(jnp.bfloat16))
            keep = jnp.where(through, jnp.exp(end), 0.0)
            state[:, cols] = fresh if c == 0 else keep * old + fresh


def gated_kernel(z_ref, ssm_ref, gain_ref, gated_ref, r_ref):
    squares = jnp.zeros((Q, Q), jnp.float32)
    for p in range(z_ref.shape[1] // Q):
        cols = slice(p * Q, p * Q + Q)
        zv = z_ref[:, cols]
        g = ssm_ref[:, cols] * (zv * sigmoid(zv))
        squares = squares + g * g
    r = lax.rsqrt(jnp.sum(squares, axis=-1, keepdims=True) / DI + epsilon)
    wide = jnp.broadcast_to(r, (Q, Q))
    r_ref[...] = wide
    for p in range(z_ref.shape[1] // Q):
        cols = slice(p * Q, p * Q + Q)
        zv = z_ref[:, cols]
        g = ssm_ref[:, cols] * (zv * sigmoid(zv))
        gated_ref[:, cols] = (g * wide * gain_ref[1:2, cols]).astype(gated_ref.dtype)


def gate_kernel(z_ref, ssm_ref, cot_ref, weight_ref, rk_ref, gain_ref, dz_ref, ds_ref, grads_ref):
    grads_ref[...] = jnp.zeros_like(grads_ref)
    for c in range(z_ref.shape[0] // Q):
        rows = slice(c * Q, c * Q + Q)
        scale = lane_column(rk_ref[rows, :], 0)
        pull = lane_column(rk_ref[rows, :], 1)
        d_gated = dot32(cot_ref[rows, :], weight_ref[...], NT)
        for p in range(z_ref.shape[1] // Q):
            cols = slice(p * Q, p * Q + Q)
            zv = z_ref[rows, cols]
            sz = sigmoid(zv)
            silu_z = zv * sz
            ssm = ssm_ref[rows, cols]
            g = ssm * silu_z
            gs = d_gated[:, cols] * scale
            grads_ref[0:1, cols] += sum_rows(gs * g)
            d_g = gain_ref[1:2, cols] * gs - g * pull
            dz_ref[rows, cols] = (d_g * ssm * (sz + silu_z * (1.0 - sz))).astype(dz_ref.dtype)
            ds_ref[rows, cols] = (d_g * silu_z).astype(ds_ref.dtype)


def split_dot(values, right):
    high = values.astype(jnp.bfloat16)
    low = (values - high.astype(jnp.float32)).astype(jnp.bfloat16)
    return dot32(high, right) + dot32(low, right)


def backward_kernel(base, first_ref, x_ref, ssm_ref, ds_ref, conv_ref, gain_ref, wide_ref, tall_ref, bc_ref, bct_ref, states_ref, d_ref, grads_ref, sums_ref, flow_ref, dstate, dconv):
    first = first_ref[0]
    group = base + pl.program_id(0)
    lane = lax.broadcasted_iota(jnp.int32, (Q, Q), 1)
    half = lane < HEAD_DIM
    dstate[...] = jnp.zeros_like(dstate)
    rows_all = x_ref.shape[0]
    dconv[rows_all : rows_all + 8, :] = jnp.zeros((8, dconv.shape[1]), jnp.float32)
    grads_ref[...] = jnp.zeros_like(grads_ref)
    flow_ref[...] = jnp.zeros_like(flow_ref)

    @pl.when(pl.program_id(0) == 0)
    def _():
        sums_ref[...] = jnp.zeros_like(sums_ref)

    shift = (Q - GROUP * group) % Q
    chunks = rows_all // Q
    for c in range(chunks - 1, -1, -1):
        rows = slice(c * Q, c * Q + Q)
        inside, carry, last, through = chunk_masks(first, c, True)
        cum = pltpu.roll(wide_ref[rows, 2 * Q : 3 * Q], shift, 1)
        cp = pltpu.roll(wide_ref[rows, 3 * Q :], shift, 1)
        cumt = tall_ref[pl.ds(pl.multiple_of(group * GROUP, GROUP), GROUP), rows]
        scores_t = wide_ref[rows, Q : 2 * Q]
        b16, c16t = bc_ref[rows, :NSTATE], bct_ref[NSTATE:, rows]
        dst = jnp.zeros((Q, Q), jnp.float32)
        db = jnp.zeros((Q, NSTATE), jnp.float32)
        dc = jnp.zeros((Q, NSTATE), jnp.float32)
        us, vs, ws = (jnp.zeros((Q, Q), jnp.float32) for _ in range(3))
        for p in range(GROUP // 2):
            cols = slice(p * Q, p * Q + Q)
            moved = shifted_down(x_ref, cols, c, first, Q)
            mixed = conv_ref[4:5, cols] + conv_ref[3:4, cols] * moved[0]
            for j in range(1, KW):
                mixed = mixed + conv_ref[KW - 1 - j : KW - j, cols] * moved[j]
            sx = sigmoid(mixed)
            xs = mixed * sx
            x16 = xs.astype(jnp.bfloat16)
            skip = gain_ref[0:1, cols]
            y = ssm_ref[rows, cols] - skip * xs
            dy16 = ds_ref[rows, cols]
            d_ssm = dy16.astype(jnp.float32)
            grads_ref[5:6, cols] += sum_rows(d_ssm * xs)
            locals_, cums, cps = [], [], []
            for e in range(2):
                k = 2 * p + e
                cp_b = lane_column(cp, k)
                decay = jnp.exp(jnp.where(inside, cumt[k : k + 1, :] - cp_b, NEG))
                locals_.append(dot32((scores_t * decay).astype(jnp.bfloat16), dy16))
                x_half = jnp.where(half == (e == 0), x16, jnp.zeros_like(x16))
                dst = dst + decay * dot32(x_half, dy16, NT)
                cums.append(lane_column(cum, k))
                cps.append(cp_b)
            cum_pair = jnp.where(half, cums[0], cums[1])
            cp_pair = jnp.where(half, cps[0], cps[1])
            dx = jnp.where(half, locals_[0], locals_[1])
            x32 = x16.astype(jnp.float32)
            pick = (lane == GROUP * group + 2 * p + (row_ids(0, Q, Q) >= HEAD_DIM).astype(jnp.int32)).astype(jnp.bfloat16)
            in_dot = x32 * dx
            us = us + split_dot(d_ssm * y - in_dot, pick)
            vs = vs + split_dot(in_dot, pick)
            end = cum_pair[Q - 1 : Q, :]
            keep = jnp.where(through, jnp.exp(end), 0.0)
            if c < chunks - 1:
                later = dstate[:, cols]
                later16 = later.astype(jnp.bfloat16)
                weight = jnp.where(last, jnp.exp(end - cp_pair), 0.0)
                carried = weight * dot32(b16, later16)
                dx = dx + carried
                ws = ws + split_dot(xs * carried, pick)
                db = db + dot32((weight * xs).astype(jnp.bfloat16), later16, NT)
            if c > 0:
                ey16 = (jnp.where(carry, jnp.exp(cum_pair), 0.0) * d_ssm).astype(jnp.bfloat16)
                old16 = states_ref[c * NSTATE : (c + 1) * NSTATE, cols]
                dc = dc + dot32(ey16, old16, NT)
                fresh = dot32(c16t, ey16)
                if c < chunks - 1:
                    flow_ref[c : c + 1, cols] = keep * sum_rows(later * old16.astype(jnp.float32))
                    fresh = keep * later + fresh
                dstate[:, cols] = fresh
            d_mixed = (dx + skip * d_ssm) * (sx + xs * (1.0 - sx))
            dconv[rows, cols] = d_mixed
            grads_ref[4:5, cols] += sum_rows(d_mixed)
            for j in range(KW):
                grads_ref[KW - 1 - j : KW - j, cols] += sum_rows(d_mixed * moved[j])
            taps = [conv_ref[i : i + 1, cols] for i in range(KW)]
            d_ref[rows, cols] = conv_back(dconv, cols, c, first, Q, taps).astype(d_ref.dtype)
        for i, term in enumerate((dst, db, dc, us, vs, ws)):
            sums_ref[rows, i * Q : (i + 1) * Q] += term


def post_kernel(calls, first_ref, bcd_ref, conv_ref, head_ref, bc_ref, *refs):
    sums_refs, flow_refs, (d_ref, grads_ref, hgrads_ref, dconv) = refs[:calls], refs[calls:-4], refs[-4:]
    first = first_ref[0]
    rows_all = bcd_ref.shape[0]
    wide = 2 * NSTATE
    dconv[rows_all : rows_all + 8, :] = jnp.zeros((8, wide), jnp.float32)
    grads_ref[...] = jnp.zeros_like(grads_ref)
    hgrads_ref[...] = jnp.zeros_like(hgrads_ref)
    lane = lax.broadcasted_iota(jnp.int32, (Q, 128), 1)
    rate = -jnp.exp(head_ref[1:2, :])
    flow = jnp.zeros((8, 128), jnp.float32)
    start = 0
    for ref in flow_refs:
        width = ref.shape[1]
        spread = (row_ids(start, width, 128) // HEAD_DIM == lax.broadcasted_iota(jnp.int32, (width, 128), 1)).astype(jnp.float32)
        flow = flow + dot32(ref[...], spread, precision=lax.Precision.HIGHEST)
        start += width
    row, col = row_ids(0, Q, Q), lax.broadcasted_iota(jnp.int32, (Q, Q), 1)
    earlier_sum = (col < row).astype(jnp.float32)
    for c in range(rows_all // Q - 1, -1, -1):
        rows = slice(c * Q, c * Q + Q)
        moved = shifted_down(bcd_ref, slice(0, wide), c, first, wide)
        mixed = conv_ref[4:5, :] + conv_ref[3:4, :] * moved[0]
        for j in range(1, KW):
            mixed = mixed + conv_ref[KW - 1 - j : KW - j, :] * moved[j]
        sx = sigmoid(mixed)
        dst, db, dc, us, vs, carried = (functools.reduce(jnp.add, [ref[rows, i * Q : (i + 1) * Q] for ref in sums_refs]) for i in range(6))
        d_b = db + dot32(dst.astype(jnp.bfloat16), bc_ref[rows, NSTATE:])
        d_c = dc + dot32(dst.T.astype(jnp.bfloat16), bc_ref[rows, :NSTATE])
        d_mixed = jnp.concatenate([d_b, d_c], axis=1) * (sx + mixed * sx * (1.0 - sx))
        dconv[rows, :] = d_mixed
        grads_ref[4:5, :] += sum_rows(d_mixed)
        for j in range(KW):
            grads_ref[KW - 1 - j : KW - j, :] += sum_rows(d_mixed * moved[j])
        taps = [conv_ref[i : i + 1, :] for i in range(KW)]
        d_ref[rows, :wide] = conv_back(dconv, slice(0, wide), c, first, wide, taps).astype(d_ref.dtype)
        later_sum = ((col >= row) & ((row + c * Q >= first) == (col + c * Q >= first))).astype(jnp.float32)
        d_la = dot32(later_sum, us, precision=lax.Precision.HIGHEST)
        d_la = d_la + dot32(earlier_sum, carried, precision=lax.Precision.HIGHEST) + flow[c : c + 1, :]
        d_log = vs + carried
        raw = bcd_ref[rows, wide:] + head_ref[0:1, :]
        step = jax.nn.softplus(raw)
        sig = sigmoid(raw)
        ratio = jnp.where(raw < -17.0, 1.0, sig / jnp.maximum(step, 1e-37))
        d_raw = jnp.where(lane < HEADS, d_log * ratio + d_la * rate * sig, 0.0)
        d_ref[rows, wide:] = d_raw.astype(d_ref.dtype)
        hgrads_ref[0:1, :] += sum_rows(d_raw)
        hgrads_ref[1:2, :] += sum_rows(jnp.where(lane < HEADS, d_la * rate * step, 0.0))


def smem():
    return pl.BlockSpec(memory_space=pltpu.SMEM)


def whole(shape):
    return pl.BlockSpec(shape, lambda g: (0,) * len(shape))


def shaped(shape, kind):
    return jax.ShapeDtypeStruct(shape, kind)


def params(limit=VMEM):
    return pltpu.CompilerParams(vmem_limit_bytes=limit)


def cost(flops, size):
    return pl.CostEstimate(flops=flops // 3, bytes_accessed=size // 3, transcendentals=0)


def run_prep(first, bcd, conv, heads):
    rows = bcd.shape[0]
    f32, b16 = jnp.float32, jnp.bfloat16
    shapes = [((rows, 4 * Q), f32), ((256, rows), f32), ((rows, 2 * NSTATE), b16), ((2 * NSTATE, rows), b16)]
    return pl.pallas_call(
        prep_kernel,
        grid=(1,),
        in_specs=[smem(), whole((rows, BCD)), whole((8, 2 * NSTATE)), whole((8, 128))],
        out_specs=[whole(s) for s, _ in shapes],
        out_shape=[shaped(s, d) for s, d in shapes],
        compiler_params=params(),
        cost_estimate=cost(2000000000, 4000000),
    )(first, bcd, conv, heads)


def run_forward(first, x, conv, gains, prep):
    rows, width = x.shape
    chunks = rows // Q
    here = lambda g: (0, g)
    block, eight = pl.BlockSpec((rows, LANES), here), pl.BlockSpec((8, LANES), here)
    return pl.pallas_call(
        forward_kernel,
        grid=(width // LANES,),
        in_specs=[smem(), block, eight, eight] + [whole(v.shape) for v in prep],
        out_specs=[block, pl.BlockSpec((chunks * NSTATE, LANES), here)],
        out_shape=[shaped((rows, width), jnp.float32), shaped((chunks * NSTATE, width), jnp.bfloat16)],
        scratch_shapes=[pltpu.VMEM((NSTATE, LANES), jnp.float32)],
        compiler_params=params(),
        cost_estimate=cost(20000000000, 20000000),
    )(first, x, conv, gains, *prep)


def run_gated(z, ssm, gains):
    rows, width = z.shape
    block = pl.BlockSpec((Q, width), lambda g: (g, 0))
    thin = pl.BlockSpec((Q, Q), lambda g: (g, 0))
    return pl.pallas_call(
        gated_kernel,
        grid=(rows // Q,),
        in_specs=[block, block, whole(gains.shape)],
        out_specs=[block, thin],
        out_shape=[shaped((rows, width), jnp.bfloat16), shaped((rows, Q), jnp.float32)],
        compiler_params=params(),
        cost_estimate=cost(4000000000, 16000000),
    )(z, ssm, gains)


def run_gate(z, ssm, cot, weight, rk, gains):
    rows, width = cot.shape
    b16 = jnp.bfloat16
    here = lambda g: (0, g)
    block, eight = pl.BlockSpec((rows, LANES), here), pl.BlockSpec((8, LANES), here)
    return pl.pallas_call(
        gate_kernel,
        grid=(DI // LANES,),
        in_specs=[block, block, whole(cot.shape), pl.BlockSpec((LANES, width), lambda g: (g, 0)), whole(rk.shape), eight],
        out_specs=[block, block, eight],
        out_shape=[shaped((rows, DI), b16)] * 2 + [shaped((8, DI), jnp.float32)],
        compiler_params=params(),
        cost_estimate=cost(12000000000, 36000000),
    )(z, ssm, cot, weight, rk, gains)


def run_backward(base, count, first, x, ssm, ds, conv, gains, prep, states):
    rows = x.shape[0]
    f32, b16 = jnp.float32, jnp.bfloat16
    chunks = rows // Q
    at = lambda g: (0, g + base)
    here = lambda g: (0, g)
    block, eight = pl.BlockSpec((rows, LANES), at), pl.BlockSpec((8, LANES), at)
    own = pl.BlockSpec((8, LANES), here)
    return pl.pallas_call(
        functools.partial(backward_kernel, base),
        grid=(count,),
        in_specs=[smem(), block, block, block, eight, eight] + [whole(v.shape) for v in prep] + [pl.BlockSpec((chunks * NSTATE, LANES), at)],
        out_specs=[pl.BlockSpec((rows, LANES), here), own, whole((rows, 6 * Q)), own],
        out_shape=[shaped((rows, count * LANES), b16), shaped((8, count * LANES), f32), shaped((rows, 6 * Q), f32), shaped((8, count * LANES), f32)],
        scratch_shapes=[pltpu.VMEM((NSTATE, LANES), f32), pltpu.VMEM((rows + 8, LANES), f32)],
        compiler_params=params(),
        cost_estimate=cost(count * 7000000000, count * 8000000),
    )(first, x, ssm, ds, conv, gains, *prep, states)


def run_post(first, bcd, conv, heads, prep, backs):
    rows = bcd.shape[0]
    bc = prep[2]
    f32 = jnp.float32
    sums = [t for some in zip(*backs) for t in some]
    return pl.pallas_call(
        functools.partial(post_kernel, len(backs)),
        grid=(1,),
        in_specs=[smem(), whole((rows, BCD)), whole((8, 2 * NSTATE)), whole((8, 128)), whole(bc.shape)] + [whole(t.shape) for t in sums],
        out_specs=[whole((rows, BCD)), whole((8, 2 * NSTATE)), whole((8, 128))],
        out_shape=[shaped((rows, BCD), jnp.bfloat16), shaped((8, 2 * NSTATE), f32), shaped((8, 128), f32)],
        scratch_shapes=[pltpu.VMEM((rows + 8, 2 * NSTATE), f32)],
        compiler_params=params(),
        cost_estimate=cost(4000000000, 8000000),
    )(first, bcd, conv, heads, bc, *sums)


def contract_rows(left, right, kind=jnp.float32):
    return lax.dot_general(left, right, (((0,), (0,)), ((), ())), preferred_element_type=kind)


def pad_lanes(v, width):
    return jnp.pad(v, ((0, 0), (0, width - v.shape[1])))


ORDER = (7, 3, 5, 1, 6, 2, 4, 0)
WIDE = 512


def project_kernel(places, me_ref, left_ref, *refs):
    pieces, (out_ref, full_ref) = refs[:-2], refs[-2:]
    part = full_ref.shape[0] // 8
    for (j, skip, rows), ref in zip(places, pieces):
        full_ref[pl.ds(pl.multiple_of((me_ref[0] ^ j) * part + skip, 16), rows), :] = ref[:rows, :]
    out_ref[...] = dot32(left_ref[...], full_ref[...])


def run_project(me, left, pieces, skip, cols):
    rows, inner = left.shape
    step = min(WIDE, cols)
    here = lambda g: (0, g)
    places = tuple((j, start, min(v.shape[0], inner // 8 - start)) for v, j, start in pieces)
    return pl.pallas_call(
        functools.partial(project_kernel, places),
        grid=(cols // step,),
        in_specs=[smem(), whole(left.shape)] + [pl.BlockSpec((v.shape[0], step), lambda g: (0, g + skip // step)) for v, _, _ in pieces],
        out_specs=[pl.BlockSpec((rows, step), here), pl.BlockSpec((inner, step), here)],
        out_shape=[shaped((rows, cols), jnp.float32), shaped((inner, cols), left.dtype)],
        compiler_params=params(),
        cost_estimate=cost(2 * rows * inner * cols, 4 * inner * (rows + cols) + 4 * rows * cols),
    )(me, left, *[v for v, _, _ in pieces])


def unpack_kernel(places, widths, me_ref, *refs):
    pieces, (gain_ref, conv_ref, heads_ref, gains_ref, found) = refs[:-5], refs[-5:]
    span = found.shape[2]
    for j, ref in zip(places, pieces):
        found[me_ref[0] ^ j] = ref[:, :span].astype(jnp.float32)
    for ref in (gain_ref, conv_ref, heads_ref, gains_ref):
        ref[...] = jnp.zeros_like(ref)
    wide, taps, few, long = widths
    for i in range(8):
        gain_ref[:, i * wide : (i + 1) * wide] = found[i, 0:1, :wide]
        conv_ref[0:5, i * taps : (i + 1) * taps] = found[i, 1:6, :taps]
        heads_ref[0:3, i * few : (i + 1) * few] = found[i, 6:9, :few]
        gains_ref[1:2, i * long : (i + 1) * long] = found[i, 9:10, :long]
    spread = (row_ids(0, 128, DI) == lax.broadcasted_iota(jnp.int32, (128, DI), 1) // HEAD_DIM).astype(jnp.float32)
    gains_ref[0:1, :] = dot32(heads_ref[...], spread, precision=lax.Precision.HIGHEST)[2:3, :]


def run_unpack(me, pieces, rows, widths):
    f32 = jnp.float32
    wide, taps, few, long = widths
    shapes = [(1, 8 * wide), (8, 8 * taps), (8, 128), (8, 8 * long)]
    return pl.pallas_call(
        functools.partial(unpack_kernel, tuple(j for _, j, _ in pieces), widths),
        grid=(1,),
        in_specs=[smem()] + [pl.BlockSpec((SMALL, 512), lambda g, at=(rows - start) // SMALL: (at, 0)) for _, _, start in pieces],
        out_specs=[whole(s) for s in shapes],
        out_shape=[shaped(s, f32) for s in shapes],
        scratch_shapes=[pltpu.VMEM((8, SMALL, 512), f32)],
        compiler_params=params(),
        cost_estimate=cost(1000000, 1000000),
    )(me, *[v for v, _, _ in pieces])


def out_kernel(gated_ref, weight_ref, x_ref, cot_ref, r_ref, result_ref, rk_ref, acc):
    weight = weight_ref[...]
    branch = dot32(gated_ref[...], weight)
    result_ref[...] = (x_ref[...].astype(jnp.float32) + branch).astype(result_ref.dtype)
    product = cot_ref[...].astype(jnp.float32) * branch
    part = product[:, :Q]
    for p in range(1, product.shape[1] // Q):
        part = part + product[:, p * Q : (p + 1) * Q]

    @pl.when(pl.program_id(0) == 0)
    def _():
        acc[...] = part

    @pl.when(pl.program_id(0) > 0)
    def _():
        acc[...] += part

    @pl.when(pl.program_id(0) == pl.num_programs(0) - 1)
    def _():
        r = r_ref[...]
        pull = r * r * (jnp.sum(acc[...], axis=-1, keepdims=True) / DI)
        lane = lax.broadcasted_iota(jnp.int32, rk_ref.shape, 1)
        rk_ref[...] = jnp.where(lane == 0, r, jnp.where(lane == 1, pull, 0.0))


def run_out(gated, weight, x, cot, r):
    rows, inner = gated.shape
    width = x.shape[1]
    step = width // 3
    here = lambda g: (0, g)
    return pl.pallas_call(
        out_kernel,
        grid=(3,),
        in_specs=[whole(gated.shape)] + [pl.BlockSpec((v.shape[0], step), here) for v in (weight, x, cot)] + [whole(r.shape)],
        out_specs=[pl.BlockSpec((rows, step), here), whole((rows, 128))],
        out_shape=[shaped((rows, width), x.dtype), shaped((rows, 128), jnp.float32)],
        scratch_shapes=[pltpu.VMEM((rows, Q), jnp.float32)],
        compiler_params=params(),
        cost_estimate=cost(4 * rows * inner * width, 4 * inner * width + 8 * rows * width),
    )(gated, weight, x, cot, r)


def pack_kernel(calls, widths, *refs):
    x_refs, (b_ref, h_ref, g_ref, n_ref, out_ref, conv) = refs[:calls], refs[calls:]
    wide, taps, few, long = widths
    start = 0
    for ref in (*x_refs, b_ref):
        conv[:, start : start + ref.shape[1]] = ref[...]
        start += ref.shape[1]
    inner = 8 * long
    spread = (row_ids(0, inner, 128) // HEAD_DIM == lax.broadcasted_iota(jnp.int32, (inner, 128), 1)).astype(jnp.float32)
    skips = dot32(conv[:, :inner], spread, precision=lax.Precision.HIGHEST)
    out_ref[...] = jnp.zeros_like(out_ref)
    for i in range(8):
        fields = [n_ref[0:1, i * wide : (i + 1) * wide]]
        fields += [conv[k : k + 1, i * taps : (i + 1) * taps] for k in range(KW + 1)]
        fields += [h_ref[k : k + 1, i * few : (i + 1) * few] for k in range(2)] + [skips[5:6, i * few : (i + 1) * few]]
        fields += [g_ref[0:1, i * long : (i + 1) * long]]
        start = 0
        for field in fields:
            out_ref[i : i + 1, start : start + field.shape[1]] = field
            start += field.shape[1]


def run_pack(widths, x_grads, b_grads, h_grads, g_grads, n_grads):
    wide, taps, few, long = widths
    width = wide + (KW + 1) * taps + 3 * few + long
    width += -width % 128
    args = (*x_grads, b_grads, h_grads, g_grads, n_grads)
    return pl.pallas_call(
        functools.partial(pack_kernel, len(x_grads), widths),
        grid=(1,),
        in_specs=[whole(v.shape) for v in args],
        out_specs=whole((8, width)),
        out_shape=shaped((8, width), jnp.float32),
        scratch_shapes=[pltpu.VMEM((8, 8 * taps), jnp.float32)],
        compiler_params=params(),
        cost_estimate=cost(1000000, 1000000),
    )(*args)


def back_kernel(spans, based, *refs):
    out_ref = refs[-1]
    grid = pl.program_id(0)

    @pl.when(grid == 0)
    def _():
        out_ref[...] = refs[0][...] if based else jnp.zeros_like(out_ref)

    refs = refs[based:-1]
    for i, (start, stop) in enumerate(spans):

        @pl.when((grid >= start) & (grid < stop))
        def _():
            out_ref[...] += dot32(refs[2 * i][...], refs[2 * i + 1][...], NT)


def run_back(pairs, base=None):
    rows, inner = pairs[0][0].shape[0], pairs[0][2].shape[0]
    spans, specs, args, start = [], [], [], 0
    if base is not None:
        specs, args = [whole((rows, inner))], [base]
    for grad, left_skip, weight, right_skip, width in pairs:
        step = min(WIDE, width)
        steps = width // step
        spans.append((start, start + steps))

        def at(skip, g, start=start, steps=steps):
            return (0, jnp.clip(g - start, 0, steps - 1) + skip)

        specs += [pl.BlockSpec((rows, step), functools.partial(at, left_skip // step)), pl.BlockSpec((inner, step), functools.partial(at, right_skip // step))]
        args += [grad, weight]
        start += steps
    return pl.pallas_call(
        functools.partial(back_kernel, tuple(spans), int(base is not None)),
        grid=(start,),
        in_specs=specs,
        out_specs=whole((rows, inner)),
        out_shape=shaped((rows, inner), jnp.float32),
        input_output_aliases={0: 0} if base is not None else {},
        compiler_params=params(),
        cost_estimate=cost(3000, 3000),
    )(*args)


def norm_kernel(order, me_ref, x_ref, gain_ref, out_ref, sent_ref, turned):
    rows, width = x_ref.shape
    for c in range(rows // Q):
        place = slice(c * Q, c * Q + Q)
        v = x_ref[place, :].astype(jnp.float32)
        normed = v * lax.rsqrt(jnp.mean(v * v, axis=-1, keepdims=True) + epsilon) * gain_ref[...]
        out_ref[place, :] = normed.astype(out_ref.dtype)
        for p in range(width // Q):
            turned[p * Q : p * Q + Q, place] = normed[:, p * Q : p * Q + Q].T.astype(turned.dtype)
    part = width // len(order)
    for k, j in enumerate(order):
        sent_ref[k * part : (k + 1) * part, :] = turned[pl.ds(pl.multiple_of((me_ref[0] ^ j) * part, 16), part), :]


def run_norm(order, me, x, gain):
    rows, width = x.shape
    b16 = jnp.bfloat16
    return pl.pallas_call(
        functools.partial(norm_kernel, order),
        grid=(1,),
        in_specs=[smem(), whole(x.shape), whole((1, width))],
        out_specs=[whole(x.shape), whole((width, rows))],
        out_shape=[shaped(x.shape, b16), shaped((width, rows), b16)],
        scratch_shapes=[pltpu.VMEM((width, rows), b16)],
        compiler_params=params(),
        cost_estimate=cost(2000000000, 6 * rows * width),
    )(me, x, gain)


def norm_back_kernel(d_ref, x_ref, cot_ref, gain_ref, out_ref, grad_ref):
    @pl.when(pl.program_id(0) == 0)
    def _():
        grad_ref[...] = jnp.zeros_like(grad_ref)

    v = x_ref[...].astype(jnp.float32)
    rn = lax.rsqrt(jnp.mean(v * v, axis=-1, keepdims=True) + epsilon)
    d = d_ref[...]
    grad_ref[0:1, :] += sum_rows(d * v * rn)
    scaled = d * gain_ref[...]
    pull = rn * rn * rn * jnp.mean(v * scaled, axis=-1, keepdims=True)
    out_ref[...] = (cot_ref[...].astype(jnp.float32) + rn * scaled - v * pull).astype(out_ref.dtype)


def run_norm_back(d, x, cot, gain):
    rows, width = x.shape
    block = pl.BlockSpec((Q, width), lambda g: (g, 0))
    return pl.pallas_call(
        norm_back_kernel,
        grid=(rows // Q,),
        in_specs=[block, block, block, whole((1, width))],
        out_specs=[block, whole((8, width))],
        out_shape=[shaped(x.shape, x.dtype), shaped((8, width), jnp.float32)],
        compiler_params=params(),
        cost_estimate=cost(3000, 3000),
    )(d, x, cot, gain)


SMALL = 16
CALLS = ((0, 4), (4, 2))


def partners(bit):
    return [(i, i ^ bit) for i in range(8)]


def rotated(step):
    return [(i, (i + step) % 4) for i in range(4)]


def tie(*values):
    return lax.optimization_barrier(values)


def custom():
    return lax.axis_size("fsdp") == 8 and lax.axis_size("rep") == 4


def gathered_rows(w):
    half = w.shape[0] // 32 * 16
    two, four = yield [(w, "fsdp", partners(j)) for j in (2, 4)], 1
    top, bottom, one = yield [(two[:half], "fsdp", partners(4)), (four[half:], "fsdp", partners(2)), (w, "fsdp", partners(1))], 1
    three, five, other_top, other_bottom = yield [(v, "fsdp", partners(1)) for v in (two, four, top, bottom)], 1
    near = [(w, 0, 0), (one, 1, 0), (two, 2, 0), (three, 3, 0), (four, 4, 0), (five, 5, 0)]
    return near + [(top, 6, 0), (bottom, 6, half), (other_top, 7, 0), (other_bottom, 7, half)]


def dealt(v, turns):
    (got,) = yield [(v, "fsdp", None)], turns
    return got


def widen(v):
    return v.astype(jnp.float32)


def group_sum(product, rows):
    b16 = jnp.bfloat16
    (got,) = yield [(product(0, 4).astype(b16), "fsdp", partners(1))], 1
    terms = [product(4 + i, 5 + i) + widen(got[i * rows : (i + 1) * rows]) for i in range(4)]
    others = yield [(v.astype(b16), "fsdp", partners(j)) for v, j in zip(terms, ORDER[4:7])], 1
    return terms[3] + widen(others[0]) + widen(others[1]) + widen(others[2])


def left_rows(left, right):
    rows = left.shape[0] // 8
    return lambda i, j: jnp.dot(left[i * rows : j * rows], right, preferred_element_type=jnp.float32)


def half_sum(own):
    b16 = jnp.bfloat16
    place = lax.axis_index("rep")
    odd, late = place % 2 == 1, place >= 2
    across = [(0, 2), (1, 3), (2, 0), (3, 1)]
    beside = [(0, 1), (1, 0), (2, 3), (3, 2)]

    def halves(v, second):
        top, bottom = jnp.split(v, 2)
        return jnp.where(second, bottom, top), jnp.where(second, top, bottom)

    def joined(mine, other, second):
        return jnp.where(second, jnp.concatenate([other, mine]), jnp.concatenate([mine, other]))

    keep, send = halves(own, odd)
    (got,) = yield [(send.astype(b16), "rep", beside)], 1
    keep, send = halves(widen(keep) + widen(got), late)
    (got,) = yield [(send.astype(b16), "rep", across)], 1
    mine = (keep + widen(got)).astype(b16)
    (got,) = yield [(mine, "rep", across)], 1
    mine = joined(mine, got, late)
    (got,) = yield [(mine, "rep", beside)], 1
    return joined(mine, got, odd)


def small_sum(rows):
    place = lax.axis_index("rep")
    (got,) = yield [(rows, "fsdp", None)], 1
    row = jnp.sum(got, axis=0, keepdims=True)
    got = yield [(row, "rep", rotated(k)) for k in (1, 2, 3)], 1
    stack = jnp.concatenate([row, *got])
    return jnp.sum(stack[(place - jnp.arange(4)) % 4], axis=0)


def transfer(v, axis, pairs):
    if pairs is None:
        return lax.all_to_all(v, axis, split_axis=0, concat_axis=0, tiled=True)
    return lax.ppermute(v, axis, pairs)


def slice_sum(left, right):
    own = yield from group_sum(left_rows(left, right), left.shape[0] // 8)
    return (yield from half_sum(own))


class Moves:
    def __init__(self):
        self.active = []

    def add(self, generator):
        want, turns = next(generator)
        entry = {"gen": generator, "want": want, "turns": turns, "got": None, "value": None}
        self.active.append(entry)
        return entry

    def turn(self, work=None, *values):
        fresh = [e for e in self.active if e["got"] is None]
        arrays, values = tie([[item[0] for item in e["want"]] for e in fresh], values)
        for e, some in zip(fresh, arrays):
            e["got"] = [transfer(v, *item[1:]) for v, item in zip(some, e["want"])]
        results = work(*values) if work else ()
        for e in self.active:
            e["turns"] -= 1
        due = [e for e in self.active if e["turns"] == 0]
        arrived, results = tie([e["got"] for e in due], results)
        for e, got in zip(due, arrived):
            try:
                e["want"], e["turns"] = e["gen"].send(got)
                e["got"] = None
            except StopIteration as stop:
                e["value"] = stop.value
                self.active.remove(e)
        return results

    def after(self, value):
        want = self.active[0]["want"]
        array, *rest = want[-1]
        value, array = tie(value, array)
        want[-1] = (array, *rest)
        return value

    def finish(self):
        while self.active:
            self.turn()


def per_device(tokens, cotangent, lengths, dealing, norm_gain, in_weight, conv_weight, conv_bias, dt_bias, a_log, d_skip, gated_gain, out_weight):
    f32, b16 = jnp.float32, jnp.bfloat16
    groups = lax.axis_size("fsdp")
    tok_rows, width = tokens.shape
    block_rows = tok_rows // groups
    targets = dealing.reshape(groups)
    inverse = jnp.argsort(targets)
    first = lengths.reshape(-1)[:1]
    me = lax.axis_index("fsdp").reshape(1)
    moves = Moves()

    def blocks(values):
        return values.reshape(groups, block_rows, width)[inverse]

    def deal(values):
        return lax.all_to_all(blocks(values), "fsdp", split_axis=0, concat_axis=0, tiled=True).reshape(tok_rows, width)

    def undeal(values):
        blocks = lax.all_to_all(values.reshape(groups, block_rows, width), "fsdp", split_axis=0, concat_axis=0, tiled=True)
        return blocks[targets].reshape(tok_rows, width)

    own_small = [norm_gain[None], conv_weight, conv_bias[None], dt_bias[None], a_log[None], d_skip[None], gated_gain[None]]
    longest = max(v.shape[1] for v in own_small)
    small = jnp.concatenate([pad_lanes(v, longest) for v in own_small])
    small = jnp.pad(small, ((0, SMALL - small.shape[0]), (0, 0)))
    if custom():
        rows, span = in_weight.shape[0], DI + BCD
        w_xb = jnp.pad(in_weight[:, DI:], ((0, SMALL), (0, span + DI - in_weight.shape[1])))
        e_xb = moves.add(gathered_rows(w_xb + jnp.pad(small, ((rows, 0), (0, span - small.shape[1])))))
        moves.turn()
        e_x = moves.add(dealt(blocks(tokens), 1))
        moves.turn()
        out_weight = moves.after(out_weight)
        w_out = lax.all_gather(out_weight, "fsdp", axis=0, tiled=True)
        moves.turn()
        pieces = e_xb["value"]
        x = e_x["value"].reshape(tok_rows, width)
        behind = [[p for p in pieces if p[1] == j][-1] for j in range(8)]
        widths = (norm_gain.size, conv_bias.size, dt_bias.size, gated_gain.size)
        gain, conv, heads, gains = run_unpack(me, behind, rows, widths)
    else:
        x = deal(tokens)
        w_z = lax.all_gather(in_weight[:, :DI], "fsdp", axis=0, tiled=True)
        w_out = lax.all_gather(out_weight, "fsdp", axis=0, tiled=True)
        small_all = lax.all_gather(small, "fsdp", axis=0, tiled=False).astype(f32)
        w_xb = lax.all_gather(pad_lanes(in_weight[:, DI:], DI + BCD), "fsdp", axis=0, tiled=True)
        parts, row = [], 0
        for v in own_small:
            parts.append(small_all[:, row : row + v.shape[0], : v.shape[1]].transpose(1, 0, 2).reshape(v.shape[0], -1))
            row += v.shape[0]
        gain, taps, bias, step_bias, rate, skip, ggain = parts
        conv = jnp.concatenate([taps, bias, jnp.zeros((3, bias.shape[1]), f32)])
        heads = pad_lanes(jnp.concatenate([step_bias, rate, jnp.zeros((6, HEADS), f32)]), 128)
        gains = jnp.concatenate([jnp.repeat(skip, HEAD_DIM, axis=1), ggain, jnp.zeros((6, DI), f32)])
    conv_x, conv_bc = conv[:, :DI], conv[:, DI:]

    if custom():

        def open_up(x):
            normed, sent = run_norm(ORDER, me, x, gain)
            bcd, w_b = run_project(me, normed, pieces, DI, BCD)
            xr, w_x = run_project(me, normed, pieces, 0, DI)
            return normed, sent, bcd, w_b, xr, w_x, run_prep(first, bcd, conv_bc, heads)

        e_z = moves.add(gathered_rows(in_weight[:, :DI]))
        normed, sent, bcd, w_b, xr, w_x, prep = moves.turn(open_up, x)
        e_cot = moves.add(dealt(blocks(cotangent), 1))
        ssm, states = moves.turn(lambda v: run_forward(first, v, conv_x, gains, prep), xr)
        moves.turn()
        z, w_z = run_project(me, normed, e_z["value"], 0, DI)
        gated, r = run_gated(z, ssm, gains)
        cot = e_cot["value"].reshape(tok_rows, width)
        out_term, gated = tie(contract_rows(gated, cot, b16), gated)
        result, rk = run_out(gated, w_out, x, cot, r)
    else:
        normed, sent = run_norm((0,), me * 0, x, gain)
        w_x, w_b = w_xb[:, :DI], w_xb[:, DI:]
        bcd = jnp.dot(normed, w_b, preferred_element_type=f32)
        xr = jnp.dot(normed, w_x, preferred_element_type=f32)
        cot = deal(cotangent)
        prep = run_prep(first, bcd, conv_bc, heads)
        ssm, states = run_forward(first, xr, conv_x, gains, prep)
        z = jnp.dot(normed, w_z, preferred_element_type=f32)
        gated, r = run_gated(z, ssm, gains)
        result, rk = run_out(gated, w_out, x, cot, r)
        out_term = contract_rows(gated, cot, b16)
    s_out = lax.psum_scatter(out_term, "fsdp", scatter_dimension=0, tiled=True)
    dz, ds, ggrads = run_gate(z, ssm, cot, w_out, rk, gains)
    z_term, ds = tie(contract_rows(normed, dz, b16), ds)
    s_z = lax.psum_scatter(z_term, "fsdp", scatter_dimension=0, tiled=True)

    def backward(base, count, ds):
        return run_backward(base, count, first, xr, ssm, ds, conv_x, gains, prep, states)

    def close(backs):
        return run_post(first, bcd, conv_bc, heads, prep, [b[2:] for b in backs])

    def back(backs, d_b):
        pairs = [(dz, 0, w_z, 0, DI)] + [(b[0], 0, w_x, base * LANES, count * LANES) for b, (base, count) in zip(backs, CALLS)]
        return run_back(pairs + [(d_b, 0, w_b, 0, BCD)])

    if custom():
        backs = [backward(*CALLS[0], ds)]
        e_first = moves.add(slice_sum(sent, backs[0][0]))
        e_output = moves.add(dealt(result.reshape(groups, block_rows, width), 1))

        def middle(ds):
            both = backs + [backward(*CALLS[1], ds)]
            return both[1], *close(both)

        s_out, ds = tie(s_out, ds)
        e_rows = moves.add(half_sum(s_out))
        last, d_b, bgrads, hgrads = moves.turn(middle, ds)
        backs.append(last)
        e_last = moves.add(slice_sum(sent, jnp.concatenate([last[0], d_b], axis=1)))
        (d_normed,) = moves.turn(lambda d: (back(backs, d),), d_b)
        s_z, d_normed = tie(s_z, d_normed)
        e_z = moves.add(half_sum(s_z))

        def finish(d_normed):
            d_input, ngrads = run_norm_back(d_normed, x, cot, gain)
            return d_input, run_pack(widths, [b[1] for b in backs], bgrads, hgrads, ggrads, ngrads)

        d_input, packed = moves.turn(finish, d_normed)
    else:
        backs = [backward(*call, ds) for call in CALLS]
        d_b, bgrads, hgrads = close(backs)
        d_normed = back(backs, d_b)
        d_input, ngrads = run_norm_back(d_normed, x, cot, gain)
        s_in = [lax.psum_scatter(contract_rows(normed, d, b16), "fsdp", scatter_dimension=0, tiled=True) for d in [b[0] for b in backs] + [d_b]]
        output, input_grad = undeal(result), undeal(d_input)

    if not custom():
        xgrads = jnp.concatenate([b[1] for b in backs], axis=1)
        g_ggain = ggrads[0]
        g_conv = jnp.concatenate([xgrads[:KW], bgrads[:KW]], axis=1)
        g_cbias = jnp.concatenate([xgrads[KW], bgrads[KW]])
        g_dskip = jnp.sum(xgrads[5].reshape(HEADS, HEAD_DIM), axis=1)
        spread = [
            ngrads[0].reshape(groups, -1),
            g_conv.reshape(KW, groups, -1).transpose(1, 0, 2).reshape(groups, -1),
            g_cbias.reshape(groups, -1),
            hgrads[0, :HEADS].reshape(groups, -1),
            hgrads[1, :HEADS].reshape(groups, -1),
            g_dskip.reshape(groups, -1),
            g_ggain.reshape(groups, -1),
        ]
        packed = jnp.concatenate(spread, axis=1)
        packed = pad_lanes(packed, packed.shape[1] + -packed.shape[1] % 128)
    sizes = [v.size for v in own_small]
    tail = in_weight.shape[1] - 2 * DI
    if custom():
        e_small = moves.add(small_sum(packed))
        e_input = moves.add(dealt(d_input.reshape(groups, block_rows, width), 1))
        moves.finish()
        output, input_grad = (e["value"][targets].reshape(tok_rows, width) for e in (e_output, e_input))
        r_small, r_out = e_small["value"], e_rows["value"]
        r_in = jnp.concatenate([e_z["value"], e_first["value"], e_last["value"][:, : CALLS[-1][1] * LANES + tail]], axis=1)
    else:
        s_small = jnp.sum(lax.all_to_all(packed, "fsdp", split_axis=0, concat_axis=0, tiled=True), axis=0)
        r_small = jnp.sum(lax.all_gather(s_small, "rep", axis=0, tiled=False), axis=0)
        *r_in, r_out = lax.psum((s_z, *s_in, s_out), "rep")
        r_in = jnp.concatenate(r_in, axis=1)[:, : in_weight.shape[1]]
    ends, outs = 0, []
    for size in sizes:
        outs.append(r_small[ends : ends + size])
        ends += size
    return (output, input_grad, outs[0], r_in.astype(f32), outs[1].reshape(conv_weight.shape), outs[2], outs[3], outs[4], outs[5], outs[6], r_out.astype(f32))


def solution(mesh):
    placed = (
        P(("rep", "fsdp"), None),
        P(("rep", "fsdp"), None),
        P("rep", "fsdp", None),
        P("rep", "fsdp", None),
        P("fsdp"),
        P("fsdp", None),
        P(None, "fsdp"),
        P("fsdp"),
        P("fsdp"),
        P("fsdp"),
        P("fsdp"),
        P("fsdp"),
        P("fsdp", None),
    )
    return jax.shard_map(
        per_device,
        mesh=mesh,
        in_specs=placed,
        out_specs=(
            P(("rep", "fsdp"), None),
            P(("rep", "fsdp"), None),
            P("fsdp"),
            P("fsdp", None),
            P(None, "fsdp"),
            P("fsdp"),
            P("fsdp"),
            P("fsdp"),
            P("fsdp"),
            P("fsdp"),
            P("fsdp", None),
        ),
        check_vma=False,
    )
```

time: 612 us -> 582 us (0.951)
  Pallas kernels: 85.1 us -> 189 us
  waiting for transfers between devices: 273 us -> 186 us
  starting transfers between devices: 17.2 us -> 72.2 us
  blocking collectives: 58.1 us -> 7.7 us
  matrix products: 91.9 us -> 45.6 us
  other arithmetic: 36.1 us -> 18.9 us
  local copies, waits for them, and re-layouts: 32.1 us -> 40.3 us
    ppermute x0 -> x45, waiting for transfers between devices: none -> 186 us  [transfer(): return lax.ppermute(v, axis, pairs)]
    pallas_call x2 -> x13, Pallas kernels: 29.9 us -> 135 us  [the longest x3 31.1 us: run_project(): pl.pallas_call(functools.partial(project_kernel, places), grid=(cols // s...]
    reduce_scatter x1, waiting for transfers between devices: 97.8 us -> 0.07 us  [per_device(): s_z = lax.psum_scatter(z_term, 'fsdp', scatter_dimension=0, tiled=True)]
    psum x1 -> x0, waiting for transfers between devices: 81.8 us -> none  [per_device(): r_in = lax.psum(s_in, 'rep').astype(f32)]
    all_gather x2 -> x1, waiting for transfers between devices: 74.3 us -> 0.02 us  [per_device(): w_out = lax.all_gather(out_weight, 'fsdp', axis=0, tiled=True)]
    ppermute x0 -> x45, starting transfers between devices: none -> 54.3 us  [transfer(): return lax.ppermute(v, axis, pairs)]
    all_gather x2 -> x0, blocking collectives: 50.5 us -> none  [the longest x1 36.5 us: per_device(): lax.all_gather(jnp.pad(small, (0, -small.size % 128)), 'fsdp', axis=0, ti...]
    dot_general x8 -> x10, matrix products: 63.9 us -> 26.8 us  [left_rows(): jnp.dot(left[i * rows:j * rows], right, preferred_element_type=jnp.float32)]
  transfers between devices with their start and end apart: 9 -> 52, of which waited for: 5 -> 22; matrix products, arithmetic and copies ran while one was open for 25% -> 13% of each run, Pallas kernels for 14% -> 33%
where the time goes in v3:
time: 582 us; the launch traced here: 575 us
  Pallas kernels  189 us (32%)
  waiting for transfers between devices  186 us (32%)
  starting transfers between devices  72.2 us (12%)
  matrix products  45.6 us (8%)
  local copies, waits for them, and re-layouts  40.3 us (7%)
  other arithmetic  18.9 us (3%)
  between operations  14.9 us (3%)
  blocking collectives  7.7 us (1%)
    ppermute x45, waiting for transfers between devices, transfer(): return lax.ppermute(v, axis, pairs)  186 us
    ppermute x45, starting transfers between devices, transfer(): return lax.ppermute(v, axis, pairs)  54.3 us
    pallas_call x2, Pallas kernels, run_backward(): pl.pallas_call(functools.partial(backward_kernel, base), grid=(count,), i...  50.3 us
    pallas_call x3, Pallas kernels, run_project(): pl.pallas_call(functools.partial(project_kernel, places), grid=(cols // s...  31.1 us
    dot_general x10, matrix products, left_rows(): jnp.dot(left[i * rows:j * rows], right, preferred_element_type=jnp.float32)  26.8 us
    pallas_call x1, Pallas kernels, run_forward(): pl.pallas_call(forward_kernel, grid=(width // LANES,), in_specs=[smem(),...  22 us
    pallas_call x1, Pallas kernels, run_back(): pl.pallas_call(functools.partial(back_kernel, tuple(spans), int(base is n...  21.8 us
    pallas_call x1, Pallas kernels, run_gate(): pl.pallas_call(gate_kernel, grid=(DI // LANES,), in_specs=[block, block,...  20.4 us
  transfers between devices with their start and end apart: 52, of which 22 were waited for; matrix products, arithmetic and copies ran while one was open for 13% of the time, Pallas kernels for 33%

profile of v3, /device:TPU:0, one launch (start us, length us, event | category | flops | bytes accessed | tf_op | source)
XLA Modules:
  0.0 575.3 jit_solution(4014077925936593976)
XLA Ops:
  11.5 3.0 collective-permute-start
  18.8 27.3 %collective-permute-done.refs_2_ = bf16[208,3456]{1,0:T(8,128)(2,1)} collective-permute-done((bf16[208,3456]{1,0:T(8,128)(2,1)S(1)}, bf16[208,3456]{1,0:T(8,128)(2,1)}, u32[]{:S(2)}, u32[]{:S(2)}) %collective-permute-start) | collective-permute-done | bytes 1437728 | tf_op jit(solution)/shard_map/ppermute | solution.py:808
  51.6 3.6 all-to-all-start
  58.6 30.8 %collective-permute-done.2.refs_6_ = bf16[96,3456]{1,0:T(8,128)(2,1)S(1)} collective-permute-done((bf16[96,3456]{1,0:T(8,128)(2,1)}, bf16[96,3456]{1,0:T(8,128)(2,1)S(1)}, u32[]{:S(2)}, u32[]{:S(2)}) %collective-permute-start.2) | collective-permute-done | bytes 663584 | tf_op jit(solution)/shard_map/ppermute | solution.py:808
  97.1 3.2 gather_fusion.1
  105.1 3.9 shard_map.213
  109.0 3.8 shard_map.214
  112.8 4.2 shard_map.216
  117.0 13.5 %shard_map.215 = (f32[512,3072]{1,0:T(8,128)}, bf16[1536,3072]{1,0:T(8,128)(2,1)}) custom-call(s32[1]{0:T(128)} %bitcast.6.me_ref, bf16[512,1536]{1,0:T(8,128)(2,1)} %get-tuple-element.238.left_ref, bf16[208,3456]{1,0:T(8,128)(2,1)} %copy-done.5, bf16[208,3456]{1,0:T(8,128)(2,1)} %collective-permute-done.4.refs_1_, ...), custom_call_target="tpu_custom_call" | custom-call | flops 1610612736 | bytes 9437184 | tf_op jit(solution)/shard_map/pallas_call | solution.py:494
  130.5 5.8 %collective-permute-done.5.refs_2_ = bf16[192,3072]{1,0:T(8,128)(2,1)} collective-permute-done((bf16[192,3072]{1,0:T(8,128)(2,1)}, bf16[192,3072]{1,0:T(8,128)(2,1)}, u32[]{:S(2)}, u32[]{:S(2)}) %collective-permute-start.5) | collective-permute-done | bytes 1179680 | tf_op jit(solution)/shard_map/ppermute | solution.py:808
  141.2 4.6 all-to-all-start.1
  150.4 22.0 %shard_map.217 = (f32[512,3072]{1,0:T(8,128)}, bf16[512,3072]{1,0:T(8,128)(2,1)}) custom-call(s32[1]{0:T(128)} %bitcast.54, f32[512,3072]{1,0:T(8,128)} %get-tuple-element.229.x_ref, f32[8,3072]{1,0:T(8,128)} %slice.108.conv_ref, f32[8,3072]{1,0:T(8,128)} %get-tuple-element.230.gain_ref, f32[512,512]{1,0:T(8,128)} %get-tuple-element.231.wide_ref, ...), custom_call_target="tpu_custom_call" | custom-call | flops 6666666496 | bytes 6666666 | tf_op jit(solution)/shard_map/pallas_call | solution.py:389
  172.4 19.0 %collective-permute-done.11.refs_6_ = bf16[96,3072]{1,0:T(8,128)(2,1)S(1)} collective-permute-done((bf16[96,3072]{1,0:T(8,128)(2,1)}, bf16[96,3072]{1,0:T(8,128)(2,1)S(1)}, u32[]{:S(2)}, u32[]{:S(2)}) %collective-permute-start.11) | collective-permute-done | bytes 589856 | tf_op jit(solution)/shard_map/ppermute | solution.py:808
  193.4 3.5 collective-permute-done.16.refs_8_
  201.1 13.8 %shard_map.218 = (f32[512,3072]{1,0:T(8,128)}, bf16[1536,3072]{1,0:T(8,128)(2,1)}) custom-call(s32[1]{0:T(128)} %bitcast.6.me_ref, bf16[512,1536]{1,0:T(8,128)(2,1)} %get-tuple-element.238.left_ref, bf16[192,3072]{1,0:T(8,128)(2,1)} %slice.98.refs_0_, bf16[192,3072]{1,0:T(8,128)(2,1)} %copy-done.21, bf16[192,3072]{1,0:T(8,128)(2,1)} %collective-permute-done.5.refs_2_, ...), custom_call_target="tpu_custom_call" | custom-call | flops 1610612736 | bytes 9437184 | tf_op jit(solution)/shard_map/pallas_call | solution.py:494
  214.9 8.3 %shard_map.219 = (bf16[512,3072]{1,0:T(8,128)(2,1)}, f32[512,128]{1,0:T(8,128)}) custom-call(f32[512,3072]{1,0:T(8,128)} %get-tuple-element.250.z_ref, f32[512,3072]{1,0:T(8,128)} %get-tuple-element.237.ssm_ref, f32[8,3072]{1,0:T(8,128)} %get-tuple-element.230.gain_ref), custom_call_target="tpu_custom_call" | custom-call | flops 1333333376 | bytes 5333333 | tf_op jit(solution)/shard_map/pallas_call | solution.py:405
  223.1 9.4 %fusion.28 = bf16[3072,1536]{1,0:T(8,128)(2,1)} fusion(bf16[512,3072]{1,0:T(8,128)(2,1)} %get-tuple-element.254.gated_ref, bf16[512,1536]{1,0:T(8,128)(2,1)S(1)} %bitcast.40), kind=kOutput, calls=%fused_computation.83 | convolution fusion | flops 4831838208 | bytes 14155776 | tf_op jit(solution)/shard_map/dot_general | solution.py:470
  233.2 10.9 %shard_map.220 = (bf16[512,1536]{1,0:T(8,128)(2,1)}, f32[512,128]{1,0:T(8,128)}) custom-call(bf16[512,3072]{1,0:T(8,128)(2,1)} %get-tuple-element.254.gated_ref, bf16[3072,1536]{1,0:T(8,128)(2,1)} %all-gather.2.cloned.1.call-done.weight_ref, bf16[512,1536]{1,0:T(8,128)(2,1)} %bitcast.45, bf16[512,1536]{1,0:T(8,128)(2,1)} %bitcast.41, ...), custom_call_target="tpu_custom_call" | custom-call | flops 3221225472 | bytes 8388608 | tf_op jit(solution)/shard_map/pallas_call | solution.py:568
  244.1 20.4 %shard_map.221 = (bf16[512,3072]{1,0:T(8,128)(2,1)}, bf16[512,3072]{1,0:T(8,128)(2,1)}, f32[8,3072]{1,0:T(8,128)}) custom-call(f32[512,3072]{1,0:T(8,128)} %get-tuple-element.250.z_ref, f32[512,3072]{1,0:T(8,128)} %get-tuple-element.237.ssm_ref, bf16[512,1536]{1,0:T(8,128)(2,1)} %bitcast.42, bf16[3072,1536]{1,0:T(8,128)(2,1)} %all-gather.2.cloned.1.call-done.weight_ref, ...), custom_call_target="tpu_custom_call" | custom-call | flops 4000000000 | bytes 12000000 | tf_op jit(solution)/shard_map/pallas_call | solution.py:421
  264.5 9.4 %fusion.29 = bf16[1536,3072]{1,0:T(8,128)(2,1)} fusion(bf16[512,1536]{1,0:T(8,128)(2,1)S(1)} %copy-done.6, bf16[512,3072]{1,0:T(8,128)(2,1)} %get-tuple-element.257.refs_0_), kind=kOutput, calls=%fused_computation.84 | convolution fusion | flops 4831838208 | bytes 14155776 | tf_op jit(solution)/shard_map/dot_general | solution.py:470
  273.9 31.7 %shard_map.222 = (bf16[512,2048]{1,0:T(8,128)(2,1)}, f32[8,2048]{1,0:T(8,128)}, f32[512,768]{1,0:T(8,128)}, f32[8,2048]{1,0:T(8,128)}) custom-call(s32[1]{0:T(128)} %bitcast.55, f32[512,3072]{1,0:T(8,128)} %get-tuple-element.229.x_ref, f32[512,3072]{1,0:T(8,128)} %get-tuple-element.237.ssm_ref, bf16[512,3072]{1,0:T(8,128)(2,1)} %get-tuple-element.269.ds_ref, ...), custom_call_target="tpu_custom_call" | custom-call | flops 9333332992 | bytes 10666666 | tf_op jit(solution)/shard_map/pallas_call | solution.py:440
  305.6 5.0 convolution_convert_fusion
  312.6 4.3 all-to-all-start.2
  318.6 18.7 %shard_map.223 = (bf16[512,1024]{1,0:T(8,128)(2,1)}, f32[8,1024]{1,0:T(8,128)}, f32[512,768]{1,0:T(8,128)}, f32[8,1024]{1,0:T(8,128)}) custom-call(s32[1]{0:T(128)} %bitcast.56, f32[512,3072]{1,0:T(8,128)} %get-tuple-element.229.x_ref, f32[512,3072]{1,0:T(8,128)} %get-tuple-element.237.ssm_ref, bf16[512,3072]{1,0:T(8,128)(2,1)} %get-tuple-element.269.ds_ref, ...), custom_call_target="tpu_custom_call" | custom-call | flops 4666666496 | bytes 5333333 | tf_op jit(solution)/shard_map/pallas_call | solution.py:440
  337.3 6.9 %shard_map.224 = (bf16[512,384]{1,0:T(8,128)(2,1)}, f32[8,256]{1,0:T(8,128)}, f32[8,128]{1,0:T(8,128)}) custom-call(s32[1]{0:T(128)} %bitcast.57, f32[512,384]{1,0:T(8,128)} %get-tuple-element.274.bcd_ref, f32[8,256]{1,0:T(8,128)} %slice.104.conv_ref, f32[8,128]{1,0:T(8,128)} %get-tuple-element.216.head_ref, bf16[512,256]{1,0:T(8,128)(2,1)} %get-tuple-element.233.bc_ref, ...), custom_call_target="tpu_custom_call" | custom-call | flops 1333333376 | bytes 2666666 | tf_op jit(solution)/shard_map/pallas_call | solution.py:457
  349.4 2.7 fusion.7
  354.8 2.7 convolution_convert_fusion.1
  357.9 3.3 collective-permute-start.20
  364.3 21.8 %shard_map.225.d_ref = f32[512,1536]{1,0:T(8,128)} custom-call(bf16[512,3072]{1,0:T(8,128)(2,1)} %get-tuple-element.257.refs_0_, bf16[1536,3072]{1,0:T(8,128)(2,1)} %get-tuple-element.290.refs_1_, bf16[512,2048]{1,0:T(8,128)(2,1)} %get-tuple-element.261.refs_2_, bf16[1536,3072]{1,0:T(8,128)(2,1)} %get-tuple-element.291.refs_3_.refs_5_, ...), custom_call_target="tpu_custom_call" | custom-call | flops 1000 | bytes 1000 | tf_op jit(solution)/shard_map/pallas_call | solution.py:651
  386.2 17.7 %collective-permute-done.21 = bf16[192,2048]{1,0:T(8,128)(2,1)S(1)} collective-permute-done((bf16[192,2048]{1,0:T(8,128)(2,1)}, bf16[192,2048]{1,0:T(8,128)(2,1)S(1)}, u32[]{:S(2)}, u32[]{:S(2)}) %collective-permute-start.21) | collective-permute-done | bytes 786464 | tf_op jit(solution)/shard_map/ppermute | solution.py:808
  411.1 2.9 fusion.5
  423.8 8.9 %collective-permute-done.26 = bf16[96,1536]{1,0:T(8,128)(2,1)S(1)} collective-permute-done((bf16[96,1536]{1,0:T(8,128)(2,1)S(1)}, bf16[96,1536]{1,0:T(8,128)(2,1)S(1)}, u32[]{:S(2)}, u32[]{:S(2)}) %collective-permute-start.26) | collective-permute-done | bytes 294944 | tf_op jit(solution)/shard_map/ppermute | solution.py:808
  433.9 5.1 shard_map.226
  441.4 6.3 %collective-permute-done.25 = bf16[96,2048]{1,0:T(8,128)(2,1)} collective-permute-done((bf16[96,2048]{1,0:T(8,128)(2,1)}, bf16[96,2048]{1,0:T(8,128)(2,1)}, u32[]{:S(2)}, u32[]{:S(2)}) %collective-permute-start.25) | collective-permute-done | bytes 393248 | tf_op jit(solution)/shard_map/ppermute | solution.py:808
  453.7 7.7 %all_to_all.32 = f32[8,1,2688]{2,1,0:T(1,128)S(1)} all-to-all(f32[8,1,2688]{2,1,0:T(1,128)S(1)} %copy.24), channel_id=1, replica_groups=mesh['rep'=4,'fsdp'=8] {'fsdp'}, dimensions={0} | all-to-all | bytes 172032 | tf_op jit(solution)/shard_map/all_to_all | solution.py:807
  461.4 4.4 all-to-all-start.4
  470.8 26.0 %collective-permute-done.31 = bf16[48,2048]{1,0:T(8,128)(2,1)S(1)} collective-permute-done((bf16[48,2048]{1,0:T(8,128)(2,1)S(1)}, bf16[48,2048]{1,0:T(8,128)(2,1)S(1)}, u32[]{:S(2)}, u32[]{:S(2)}) %collective-permute-start.31) | collective-permute-done | bytes 196640 | tf_op jit(solution)/shard_map/ppermute | solution.py:808
  500.4 2.9 collective-permute-start.37
  503.3 2.8 collective-permute-start.36
  508.2 10.4 %collective-permute-done.38 = f32[1,2688]{1,0:T(1,128)S(1)} collective-permute-done((f32[1,2688]{1,0:T(1,128)S(1)}, f32[1,2688]{1,0:T(1,128)S(1)}, u32[]{:S(2)}, u32[]{:S(2)}) %collective-permute-start.38) | collective-permute-done | bytes 10784 | tf_op jit(solution)/shard_map/ppermute | solution.py:808
  518.6 3.2 gather_fusion.2
  521.8 9.4 %collective-permute-done.39 = f32[1,2688]{1,0:T(1,128)S(1)} collective-permute-done((f32[1,2688]{1,0:T(1,128)S(1)}, f32[1,2688]{1,0:T(1,128)S(1)}, u32[]{:S(2)}, u32[]{:S(2)}) %collective-permute-start.39) | collective-permute-done | bytes 10784 | tf_op jit(solution)/shard_map/ppermute | solution.py:808
  535.2 3.0 fusion.12
  538.2 3.2 gather_fusion.3
  544.0 3.7 collective-permute-start.42
  549.0 7.9 %collective-permute-done.42 = bf16[48,1408]{1,0:T(8,128)(2,1)S(1)} collective-permute-done((bf16[48,1408]{1,0:T(8,128)(2,1)S(1)}, bf16[48,1408]{1,0:T(8,128)(2,1)S(1)}, u32[]{:S(2)}, u32[]{:S(2)}) %collective-permute-start.42) | collective-permute-done | bytes 135200 | tf_op jit(solution)/shard_map/ppermute | solution.py:808
  558.2 3.1 collective-permute-start.44
  561.7 4.0 collective-permute-done.44
  (251 shorter events, 110.3 us)
Async XLA Ops:
  11.5 34.6 %collective-permute-start = (bf16[208,3456]{1,0:T(8,128)(2,1)S(1)}, bf16[208,3456]{1,0:T(8,128)(2,1)}, u32[]{:S(2)}, u32[]{:S(2)}) collective-permute-start(bf16[208,3456]{1,0:T(8,128)(2,1)S(1)} %pad_add_fusion.refs_0_), channel_id=1, source_target_pairs={{0,2},{1,3},{2,0},{3,1},{4,6},{5,7},{6,4},{7,5},{8,10},{9,11},{10,... | collective-permute-start | bytes 4313096 | tf_op jit(solution)/shard_map/ppermute | solution.py:808
  14.5 33.1 %collective-permute-start.1 = (bf16[208,3456]{1,0:T(8,128)(2,1)S(1)}, bf16[208,3456]{1,0:T(8,128)(2,1)}, u32[]{:S(2)}, u32[]{:S(2)}) collective-permute-start(bf16[208,3456]{1,0:T(8,128)(2,1)S(1)} %pad_add_fusion.refs_0_), channel_id=1, source_target_pairs={{0,4},{1,5},{2,6},{3,7},{4,0},{5,1},{6,2},{7,3},{8,12},{9,13},{10,... | collective-permute-start | bytes 4313096 | tf_op jit(solution)/shard_map/ppermute | solution.py:808
  51.6 40.4 %collective-permute-start.4 = (bf16[208,3456]{1,0:T(8,128)(2,1)S(1)}, bf16[208,3456]{1,0:T(8,128)(2,1)}, u32[]{:S(2)}, u32[]{:S(2)}) collective-permute-start(bf16[208,3456]{1,0:T(8,128)(2,1)S(1)} %pad_add_fusion.refs_0_), channel_id=1, source_target_pairs={{0,1},{1,0},{2,3},{3,2},{4,5},{5,4},{6,7},{7,6},{8,9},{9,8},{10,11... | collective-permute-start | bytes 4313096 | tf_op jit(solution)/shard_map/ppermute | solution.py:808
  51.6 40.4 %all-to-all-start = ((bf16[8,64,1536]{2,1,0:T(8,128)(2,1)}), bf16[8,64,1536]{2,1,0:T(8,128)(2,1)S(1)}, u32[]{:S(2)}, u32[]{:S(2)}) async-start(bf16[8,64,1536]{2,1,0:T(8,128)(2,1)} %gather_fusion), calls=%async_computation | async-start | bytes 3145728 | tf_op jit(solution)/shard_map/all_to_all | solution.py:807
  55.2 178.0 %all-gather.2.cloned.1.call-start = ((), (), s32[]{:S(2)}) async-start(), calls=%async_computation.7 | async-start | bytes 10616832 | tf_op jit(solution)/shard_map/all_gather | solution.py:890
  55.2 36.7 %collective-permute-start.3 = (bf16[112,3456]{1,0:T(8,128)(2,1)}, bf16[112,3456]{1,0:T(8,128)(2,1)}, u32[]{:S(2)}, u32[]{:S(2)}) collective-permute-start(bf16[112,3456]{1,0:T(8,128)(2,1)} %slice.101), channel_id=1, source_target_pairs={{0,2},{1,3},{2,0},{3,1},{4,6},{5,7},{6,4},{7,5},{8,10},{9,11},{10,... | collective-permute-start | bytes 2322440 | tf_op jit(solution)/shard_map/ppermute | solution.py:808
  57.1 32.3 %collective-permute-start.2 = (bf16[96,3456]{1,0:T(8,128)(2,1)}, bf16[96,3456]{1,0:T(8,128)(2,1)S(1)}, u32[]{:S(2)}, u32[]{:S(2)}) collective-permute-start(bf16[96,3456]{1,0:T(8,128)(2,1)} %slice.100), channel_id=1, source_target_pairs={{0,4},{1,5},{2,6},{3,7},{4,0},{5,1},{6,2},{7,3},{8,12},{9,13},{10,... | collective-permute-start | bytes 1990664 | tf_op jit(solution)/shard_map/ppermute | solution.py:808
  92.1 8.2 %collective-permute-start.7 = (bf16[208,3456]{1,0:T(8,128)(2,1)}, bf16[208,3456]{1,0:T(8,128)(2,1)S(1)}, u32[]{:S(2)}, u32[]{:S(2)}) collective-permute-start(bf16[208,3456]{1,0:T(8,128)(2,1)} %collective-permute-done.refs_2_), channel_id=1, source_target_pairs={{0,1},{1,0},{2,3},{3,2},{4,5},{5,4},{6,7},{7,6},{8,9},{9,8},{10,11... | collective-permute-start | bytes 4313096 | tf_op jit(solution)/shard_map/ppermute | solution.py:808
  92.6 7.8 %collective-permute-start.8 = (bf16[208,3456]{1,0:T(8,128)(2,1)}, bf16[208,3456]{1,0:T(8,128)(2,1)}, u32[]{:S(2)}, u32[]{:S(2)}) collective-permute-start(bf16[208,3456]{1,0:T(8,128)(2,1)} %collective-permute-done.1.refs_4_), channel_id=1, source_target_pairs={{0,1},{1,0},{2,3},{3,2},{4,5},{5,4},{6,7},{7,6},{8,9},{9,8},{10,11... | collective-permute-start | bytes 4313096 | tf_op jit(solution)/shard_map/ppermute | solution.py:808
  95.1 41.3 %collective-permute-start.5 = (bf16[192,3072]{1,0:T(8,128)(2,1)}, bf16[192,3072]{1,0:T(8,128)(2,1)}, u32[]{:S(2)}, u32[]{:S(2)}) collective-permute-start(bf16[192,3072]{1,0:T(8,128)(2,1)} %slice.98.refs_0_), channel_id=1, source_target_pairs={{0,2},{1,3},{2,0},{3,1},{4,6},{5,7},{6,4},{7,5},{8,10},{9,11},{10,... | collective-permute-start | bytes 3538952 | tf_op jit(solution)/shard_map/ppermute | solution.py:808
  95.4 41.8 %collective-permute-start.6 = (bf16[192,3072]{1,0:T(8,128)(2,1)}, bf16[192,3072]{1,0:T(8,128)(2,1)}, u32[]{:S(2)}, u32[]{:S(2)}) collective-permute-start(bf16[192,3072]{1,0:T(8,128)(2,1)} %slice.98.refs_0_), channel_id=1, source_target_pairs={{0,4},{1,5},{2,6},{3,7},{4,0},{5,1},{6,2},{7,3},{8,12},{9,13},{10,... | collective-permute-start | bytes 3538952 | tf_op jit(solution)/shard_map/ppermute | solution.py:808
  141.2 51.2 %all-to-all-start.1 = ((bf16[8,64,1536]{2,1,0:T(8,128)(2,1)}), bf16[8,64,1536]{2,1,0:T(8,128)(2,1)S(1)}, u32[]{:S(2)}, u32[]{:S(2)}) async-start(bf16[8,64,1536]{2,1,0:T(8,128)(2,1)} %gather_fusion.1), calls=%async_computation.1 | async-start | bytes 3145728 | tf_op jit(solution)/shard_map/all_to_all | solution.py:807
  145.8 164.8 %reduce-scatter.3.cloned.1.call-start = ((), (), s32[]{:S(2)}) async-start(), calls=%async_computation.8 | async-start | bytes 10616832 | tf_op jit(solution)/shard_map/reduce_scatter | solution.py:943
  146.1 46.2 %collective-permute-start.13 = (bf16[192,3072]{1,0:T(8,128)(2,1)}, bf16[192,3072]{1,0:T(8,128)(2,1)S(1)}, u32[]{:S(2)}, u32[]{:S(2)}) collective-permute-start(bf16[192,3072]{1,0:T(8,128)(2,1)} %slice.98.refs_0_), channel_id=1, source_target_pairs={{0,1},{1,0},{2,3},{3,2},{4,5},{5,4},{6,7},{7,6},{8,9},{9,8},{10,11... | collective-permute-start | bytes 3538952 | tf_op jit(solution)/shard_map/ppermute | solution.py:808
  147.3 44.2 %collective-permute-start.11 = (bf16[96,3072]{1,0:T(8,128)(2,1)}, bf16[96,3072]{1,0:T(8,128)(2,1)S(1)}, u32[]{:S(2)}, u32[]{:S(2)}) collective-permute-start(bf16[96,3072]{1,0:T(8,128)(2,1)} %slice.106), channel_id=1, source_target_pairs={{0,4},{1,5},{2,6},{3,7},{4,0},{5,1},{6,2},{7,3},{8,12},{9,13},{10,... | collective-permute-start | bytes 1769480 | tf_op jit(solution)/shard_map/ppermute | solution.py:808
  149.0 42.5 %collective-permute-start.12 = (bf16[96,3072]{1,0:T(8,128)(2,1)}, bf16[96,3072]{1,0:T(8,128)(2,1)S(1)}, u32[]{:S(2)}, u32[]{:S(2)}) collective-permute-start(bf16[96,3072]{1,0:T(8,128)(2,1)} %slice.107), channel_id=1, source_target_pairs={{0,2},{1,3},{2,0},{3,1},{4,6},{5,7},{6,4},{7,5},{8,10},{9,11},{10,... | collective-permute-start | bytes 1769480 | tf_op jit(solution)/shard_map/ppermute | solution.py:808
  192.3 6.5 %collective-permute-start.14 = (bf16[192,3072]{1,0:T(8,128)(2,1)}, bf16[192,3072]{1,0:T(8,128)(2,1)S(1)}, u32[]{:S(2)}, u32[]{:S(2)}) collective-permute-start(bf16[192,3072]{1,0:T(8,128)(2,1)} %collective-permute-done.5.refs_2_), channel_id=1, source_target_pairs={{0,1},{1,0},{2,3},{3,2},{4,5},{5,4},{6,7},{7,6},{8,9},{9,8},{10,11... | collective-permute-start | bytes 3538952 | tf_op jit(solution)/shard_map/ppermute | solution.py:808
  192.4 6.4 %collective-permute-start.15 = (bf16[192,3072]{1,0:T(8,128)(2,1)}, bf16[192,3072]{1,0:T(8,128)(2,1)S(1)}, u32[]{:S(2)}, u32[]{:S(2)}) collective-permute-start(bf16[192,3072]{1,0:T(8,128)(2,1)} %collective-permute-done.6.refs_4_), channel_id=1, source_target_pairs={{0,1},{1,0},{2,3},{3,2},{4,5},{5,4},{6,7},{7,6},{8,9},{9,8},{10,11... | collective-permute-start | bytes 3538952 | tf_op jit(solution)/shard_map/ppermute | solution.py:808
  232.6 182.4 %reduce-scatter.5.cloned.1.call-start = ((), (), s32[]{:S(2)}) async-start(), calls=%async_computation.9 | async-start | bytes 10616832 | tf_op jit(solution)/shard_map/reduce_scatter | solution.py:946
  311.9 32.3 %collective-permute-start.18 = (bf16[768,2048]{1,0:T(8,128)(2,1)}, bf16[768,2048]{1,0:T(8,128)(2,1)}, u32[]{:S(2)}, u32[]{:S(2)}) collective-permute-start(bf16[768,2048]{1,0:T(8,128)(2,1)} %convolution_convert_fusion), channel_id=1, source_target_pairs={{0,1},{1,0},{2,3},{3,2},{4,5},{5,4},{6,7},{7,6},{8,9},{9,8},{10,11... | collective-permute-start | bytes 9437192 | tf_op jit(solution)/shard_map/ppermute | solution.py:808
  312.6 31.6 %all-to-all-start.2 = ((bf16[8,64,1536]{2,1,0:T(8,128)(2,1)}), bf16[8,64,1536]{2,1,0:T(8,128)(2,1)}, u32[]{:S(2)}, u32[]{:S(2)}) async-start(bf16[8,64,1536]{2,1,0:T(8,128)(2,1)} %bitcast.10), calls=%async_computation.3 | async-start | bytes 3145728 | tf_op jit(solution)/shard_map/all_to_all | solution.py:807
  316.9 27.3 %collective-permute-start.19 = (bf16[192,1536]{1,0:T(8,128)(2,1)S(1)}, bf16[192,1536]{1,0:T(8,128)(2,1)S(1)}, u32[]{:S(2)}, u32[]{:S(2)}) collective-permute-start(bf16[192,1536]{1,0:T(8,128)(2,1)S(1)} %broadcast_select_fusion.1), channel_id=1, source_target_pairs={{0,8},{8,0},{16,24},{24,16},{1,9},{9,1},{17,25},{25,17},{2,10},{10... | collective-permute-start | bytes 1769480 | tf_op jit(solution)/shard_map/ppermute | solution.py:808
  357.9 46.2 %collective-permute-start.24 = (bf16[768,1408]{1,0:T(8,128)(2,1)}, bf16[768,1408]{1,0:T(8,128)(2,1)S(1)}, u32[]{:S(2)}, u32[]{:S(2)}) collective-permute-start(bf16[768,1408]{1,0:T(8,128)(2,1)} %convolution_convert_fusion.1), channel_id=1, source_target_pairs={{0,1},{1,0},{2,3},{3,2},{4,5},{5,4},{6,7},{7,6},{8,9},{9,8},{10,11... | collective-permute-start | bytes 6488072 | tf_op jit(solution)/shard_map/ppermute | solution.py:808
  357.9 28.2 %collective-permute-start.20 = (bf16[192,2048]{1,0:T(8,128)(2,1)}, bf16[192,2048]{1,0:T(8,128)(2,1)S(1)}, u32[]{:S(2)}, u32[]{:S(2)}) collective-permute-start(bf16[192,2048]{1,0:T(8,128)(2,1)} %fusion.6), channel_id=1, source_target_pairs={{0,6},{1,7},{2,4},{3,5},{4,2},{5,3},{6,0},{7,1},{8,14},{9,15},{10,... | collective-permute-start | bytes 2359304 | tf_op jit(solution)/shard_map/ppermute | solution.py:808
  361.2 42.7 %collective-permute-start.21 = (bf16[192,2048]{1,0:T(8,128)(2,1)}, bf16[192,2048]{1,0:T(8,128)(2,1)S(1)}, u32[]{:S(2)}, u32[]{:S(2)}) collective-permute-start(bf16[192,2048]{1,0:T(8,128)(2,1)} %fusion.7), channel_id=1, source_target_pairs={{0,2},{1,3},{2,0},{3,1},{4,6},{5,7},{6,4},{7,5},{8,10},{9,11},{10,... | collective-permute-start | bytes 2359304 | tf_op jit(solution)/shard_map/ppermute | solution.py:808
  361.6 42.4 %collective-permute-start.22 = (bf16[192,2048]{1,0:T(8,128)(2,1)S(1)}, bf16[192,2048]{1,0:T(8,128)(2,1)}, u32[]{:S(2)}, u32[]{:S(2)}) collective-permute-start(bf16[192,2048]{1,0:T(8,128)(2,1)S(1)} %fusion.8), channel_id=1, source_target_pairs={{0,4},{1,5},{2,6},{3,7},{4,0},{5,1},{6,2},{7,3},{8,12},{9,13},{10,... | collective-permute-start | bytes 2359304 | tf_op jit(solution)/shard_map/ppermute | solution.py:808
  361.9 24.3 %collective-permute-start.23 = (bf16[96,1536]{1,0:T(8,128)(2,1)S(1)}, bf16[96,1536]{1,0:T(8,128)(2,1)S(1)}, u32[]{:S(2)}, u32[]{:S(2)}) collective-permute-start(bf16[96,1536]{1,0:T(8,128)(2,1)S(1)} %select_convert_fusion.2), channel_id=1, source_target_pairs={{0,16},{8,24},{16,0},{24,8},{1,17},{9,25},{17,1},{25,9},{2,18},{10... | collective-permute-start | bytes 884744 | tf_op jit(solution)/shard_map/ppermute | solution.py:808
  416.4 16.4 %collective-permute-start.26 = (bf16[96,1536]{1,0:T(8,128)(2,1)S(1)}, bf16[96,1536]{1,0:T(8,128)(2,1)S(1)}, u32[]{:S(2)}, u32[]{:S(2)}) collective-permute-start(bf16[96,1536]{1,0:T(8,128)(2,1)S(1)} %add_convert_fusion.1), channel_id=1, source_target_pairs={{0,16},{8,24},{16,0},{24,8},{1,17},{9,25},{17,1},{25,9},{2,18},{10... | collective-permute-start | bytes 884744 | tf_op jit(solution)/shard_map/ppermute | solution.py:808
  418.9 28.8 %collective-permute-start.30 = (bf16[96,3072]{1,0:T(8,128)(2,1)S(1)}, bf16[96,3072]{1,0:T(8,128)(2,1)S(1)}, u32[]{:S(2)}, u32[]{:S(2)}) collective-permute-start(bf16[96,3072]{1,0:T(8,128)(2,1)S(1)} %broadcast_select_fusion), channel_id=1, source_target_pairs={{0,8},{8,0},{16,24},{24,16},{1,9},{9,1},{17,25},{25,17},{2,10},{10... | collective-permute-start | bytes 1769480 | tf_op jit(solution)/shard_map/ppermute | solution.py:808
  420.3 27.4 %collective-permute-start.27 = (bf16[192,1408]{1,0:T(8,128)(2,1)}, bf16[192,1408]{1,0:T(8,128)(2,1)S(1)}, u32[]{:S(2)}, u32[]{:S(2)}) collective-permute-start(bf16[192,1408]{1,0:T(8,128)(2,1)} %fusion.9), channel_id=1, source_target_pairs={{0,6},{1,7},{2,4},{3,5},{4,2},{5,3},{6,0},{7,1},{8,14},{9,15},{10,... | collective-permute-start | bytes 1622024 | tf_op jit(solution)/shard_map/ppermute | solution.py:808
  421.8 25.9 %collective-permute-start.28 = (bf16[192,1408]{1,0:T(8,128)(2,1)}, bf16[192,1408]{1,0:T(8,128)(2,1)S(1)}, u32[]{:S(2)}, u32[]{:S(2)}) collective-permute-start(bf16[192,1408]{1,0:T(8,128)(2,1)} %fusion.10), channel_id=1, source_target_pairs={{0,2},{1,3},{2,0},{3,1},{4,6},{5,7},{6,4},{7,5},{8,10},{9,11},{10,... | collective-permute-start | bytes 1622024 | tf_op jit(solution)/shard_map/ppermute | solution.py:808
  423.1 24.6 %collective-permute-start.29 = (bf16[192,1408]{1,0:T(8,128)(2,1)S(1)}, bf16[192,1408]{1,0:T(8,128)(2,1)S(1)}, u32[]{:S(2)}, u32[]{:S(2)}) collective-permute-start(bf16[192,1408]{1,0:T(8,128)(2,1)S(1)} %copy-done.32), channel_id=1, source_target_pairs={{0,4},{1,5},{2,6},{3,7},{4,0},{5,1},{6,2},{7,3},{8,12},{9,13},{10,... | collective-permute-start | bytes 1622024 | tf_op jit(solution)/shard_map/ppermute | solution.py:808
  433.5 14.2 %collective-permute-start.25 = (bf16[96,2048]{1,0:T(8,128)(2,1)}, bf16[96,2048]{1,0:T(8,128)(2,1)}, u32[]{:S(2)}, u32[]{:S(2)}) collective-permute-start(bf16[96,2048]{1,0:T(8,128)(2,1)} %select_convert_fusion), channel_id=1, source_target_pairs={{0,8},{8,0},{16,24},{24,16},{1,9},{9,1},{17,25},{25,17},{2,10},{10... | collective-permute-start | bytes 1179656 | tf_op jit(solution)/shard_map/ppermute | solution.py:808
  461.4 36.7 %all-to-all-start.4 = ((bf16[8,64,1536]{2,1,0:T(8,128)(2,1)}), bf16[8,64,1536]{2,1,0:T(8,128)(2,1)}, u32[]{:S(2)}, u32[]{:S(2)}) async-start(bf16[8,64,1536]{2,1,0:T(8,128)(2,1)} %bitcast.47), calls=%async_computation.6 | async-start | bytes 3145728 | tf_op jit(solution)/shard_map/all_to_all | solution.py:807
  465.8 32.3 %collective-permute-start.32 = (bf16[192,1536]{1,0:T(8,128)(2,1)}, bf16[192,1536]{1,0:T(8,128)(2,1)}, u32[]{:S(2)}, u32[]{:S(2)}) collective-permute-start(bf16[192,1536]{1,0:T(8,128)(2,1)} %maximum_select_fusion.3), channel_id=1, source_target_pairs={{0,8},{8,0},{16,24},{24,16},{1,9},{9,1},{17,25},{25,17},{2,10},{10... | collective-permute-start | bytes 1769480 | tf_op jit(solution)/shard_map/ppermute | solution.py:808
  467.2 30.8 %collective-permute-start.34 = (bf16[48,3072]{1,0:T(8,128)(2,1)}, bf16[48,3072]{1,0:T(8,128)(2,1)}, u32[]{:S(2)}, u32[]{:S(2)}) collective-permute-start(bf16[48,3072]{1,0:T(8,128)(2,1)} %select_convert_fusion.1), channel_id=1, source_target_pairs={{0,16},{8,24},{16,0},{24,8},{1,17},{9,25},{17,1},{25,9},{2,18},{10... | collective-permute-start | bytes 884744 | tf_op jit(solution)/shard_map/ppermute | solution.py:808
  468.9 29.2 %collective-permute-start.33 = (bf16[96,1408]{1,0:T(8,128)(2,1)}, bf16[96,1408]{1,0:T(8,128)(2,1)}, u32[]{:S(2)}, u32[]{:S(2)}) collective-permute-start(bf16[96,1408]{1,0:T(8,128)(2,1)} %select_convert_fusion.3), channel_id=1, source_target_pairs={{0,8},{8,0},{16,24},{24,16},{1,9},{9,1},{17,25},{25,17},{2,10},{10... | collective-permute-start | bytes 811016 | tf_op jit(solution)/shard_map/ppermute | solution.py:808
  469.2 27.6 %collective-permute-start.31 = (bf16[48,2048]{1,0:T(8,128)(2,1)S(1)}, bf16[48,2048]{1,0:T(8,128)(2,1)S(1)}, u32[]{:S(2)}, u32[]{:S(2)}) collective-permute-start(bf16[48,2048]{1,0:T(8,128)(2,1)S(1)} %select_convert_fusion.4), channel_id=1, source_target_pairs={{0,16},{8,24},{16,0},{24,8},{1,17},{9,25},{17,1},{25,9},{2,18},{10... | collective-permute-start | bytes 589832 | tf_op jit(solution)/shard_map/ppermute | solution.py:808
  500.4 32.0 %collective-permute-start.37 = (bf16[48,3072]{1,0:T(8,128)(2,1)S(1)}, bf16[48,3072]{1,0:T(8,128)(2,1)S(1)}, u32[]{:S(2)}, u32[]{:S(2)}) collective-permute-start(bf16[48,3072]{1,0:T(8,128)(2,1)S(1)} %add_convert_fusion), channel_id=1, source_target_pairs={{0,16},{8,24},{16,0},{24,8},{1,17},{9,25},{17,1},{25,9},{2,18},{10... | collective-permute-start | bytes 884744 | tf_op jit(solution)/shard_map/ppermute | solution.py:808
  503.2 29.1 %collective-permute-start.35 = (bf16[48,2048]{1,0:T(8,128)(2,1)S(1)}, bf16[48,2048]{1,0:T(8,128)(2,1)S(1)}, u32[]{:S(2)}, u32[]{:S(2)}) collective-permute-start(bf16[48,2048]{1,0:T(8,128)(2,1)S(1)} %add_convert_fusion.2), channel_id=1, source_target_pairs={{0,16},{8,24},{16,0},{24,8},{1,17},{9,25},{17,1},{25,9},{2,18},{10... | collective-permute-start | bytes 589832 | tf_op jit(solution)/shard_map/ppermute | solution.py:808
  503.3 29.0 %collective-permute-start.36 = (bf16[48,1408]{1,0:T(8,128)(2,1)S(1)}, bf16[48,1408]{1,0:T(8,128)(2,1)S(1)}, u32[]{:S(2)}, u32[]{:S(2)}) collective-permute-start(bf16[48,1408]{1,0:T(8,128)(2,1)S(1)} %select_convert_fusion.5), channel_id=1, source_target_pairs={{0,16},{8,24},{16,0},{24,8},{1,17},{9,25},{17,1},{25,9},{2,18},{10... | collective-permute-start | bytes 405512 | tf_op jit(solution)/shard_map/ppermute | solution.py:808
  506.2 12.4 %collective-permute-start.38 = (f32[1,2688]{1,0:T(1,128)S(1)}, f32[1,2688]{1,0:T(1,128)S(1)}, u32[]{:S(2)}, u32[]{:S(2)}) collective-permute-start(f32[1,2688]{1,0:T(1,128)S(1)} %broadcast_in_dim.35), channel_id=1, source_target_pairs={{0,8},{8,16},{16,24},{24,0},{1,9},{9,17},{17,25},{25,1},{2,10},{10... | collective-permute-start | bytes 32264 | tf_op jit(solution)/shard_map/ppermute | solution.py:808
  506.4 24.9 %collective-permute-start.39 = (f32[1,2688]{1,0:T(1,128)S(1)}, f32[1,2688]{1,0:T(1,128)S(1)}, u32[]{:S(2)}, u32[]{:S(2)}) collective-permute-start(f32[1,2688]{1,0:T(1,128)S(1)} %broadcast_in_dim.35), channel_id=1, source_target_pairs={{0,16},{8,24},{16,0},{24,8},{1,17},{9,25},{17,1},{25,9},{2,18},{10... | collective-permute-start | bytes 32264 | tf_op jit(solution)/shard_map/ppermute | solution.py:808
  518.6 13.8 %collective-permute-start.40 = (f32[1,2688]{1,0:T(1,128)S(1)}, f32[1,2688]{1,0:T(1,128)S(1)}, u32[]{:S(2)}, u32[]{:S(2)}) collective-permute-start(f32[1,2688]{1,0:T(1,128)S(1)} %broadcast_in_dim.35), channel_id=1, source_target_pairs={{0,24},{8,0},{16,8},{24,16},{1,25},{9,1},{17,9},{25,17},{2,26},{10... | collective-permute-start | bytes 32264 | tf_op jit(solution)/shard_map/ppermute | solution.py:808
  532.6 25.5 %collective-permute-start.43 = (bf16[96,3072]{1,0:T(8,128)(2,1)S(1)}, bf16[96,3072]{1,0:T(8,128)(2,1)S(1)}, u32[]{:S(2)}, u32[]{:S(2)}) collective-permute-start(bf16[96,3072]{1,0:T(8,128)(2,1)S(1)} %maximum_select_fusion.4), channel_id=1, source_target_pairs={{0,8},{8,0},{16,24},{24,16},{1,9},{9,1},{17,25},{25,17},{2,10},{10... | collective-permute-start | bytes 1769480 | tf_op jit(solution)/shard_map/ppermute | solution.py:808
  541.4 16.7 %collective-permute-start.41 = (bf16[96,2048]{1,0:T(8,128)(2,1)S(1)}, bf16[96,2048]{1,0:T(8,128)(2,1)S(1)}, u32[]{:S(2)}, u32[]{:S(2)}) collective-permute-start(bf16[96,2048]{1,0:T(8,128)(2,1)S(1)} %maximum_select_fusion.5), channel_id=1, source_target_pairs={{0,8},{8,0},{16,24},{24,16},{1,9},{9,1},{17,25},{25,17},{2,10},{10... | collective-permute-start | bytes 1179656 | tf_op jit(solution)/shard_map/ppermute | solution.py:808
  544.0 12.9 %collective-permute-start.42 = (bf16[48,1408]{1,0:T(8,128)(2,1)S(1)}, bf16[48,1408]{1,0:T(8,128)(2,1)S(1)}, u32[]{:S(2)}, u32[]{:S(2)}) collective-permute-start(bf16[48,1408]{1,0:T(8,128)(2,1)S(1)} %add_convert_fusion.3), channel_id=1, source_target_pairs={{0,16},{8,24},{16,0},{24,8},{1,17},{9,25},{17,1},{25,9},{2,18},{10... | collective-permute-start | bytes 405512 | tf_op jit(solution)/shard_map/ppermute | solution.py:808
  558.2 7.6 %collective-permute-start.44 = (bf16[96,1408]{1,0:T(8,128)(2,1)S(1)}, bf16[96,1408]{1,0:T(8,128)(2,1)S(1)}, u32[]{:S(2)}, u32[]{:S(2)}) collective-permute-start(bf16[96,1408]{1,0:T(8,128)(2,1)S(1)} %maximum_select_fusion.6), channel_id=1, source_target_pairs={{0,8},{8,0},{16,24},{24,16},{1,9},{9,1},{17,25},{25,17},{2,10},{10... | collective-permute-start | bytes 811016 | tf_op jit(solution)/shard_map/ppermute | solution.py:808
  (51 other events, 390.9 us)
Sparse Core Ops, SparseCore 0:
  92.1 93.3 all-gather.1
  232.7 77.4 reduce-scatter.2
  313.7 101.2 reduce-scatter.4

commit v4 on v3

--- a/solution.py
+++ b/solution.py
@@ -22,7 +22,6 @@
 LANES = GROUP * HEAD_DIM
 NEG = -1e30
 VMEM = 56 * 1024 * 1024
-BIG = 56 * 1024 * 1024
 
 
 def dot32(a, b, dims=(((1,), (0,)), ((), ())), precision=None):
@@ -114,13 +113,27 @@
     return jnp.broadcast_to(values[:, k : k + 1], (Q, Q))
 
 
+def conv_act(x_ref, conv_ref, cols, c, first):
+    moved = shifted_down(x_ref, cols, c, first, Q)
+    mixed = conv_ref[4:5, cols] + conv_ref[3:4, cols] * moved[0]
+    for j in range(1, KW):
+        mixed = mixed + conv_ref[KW - 1 - j : KW - j, cols] * moved[j]
+    return moved, mixed
+
+
+def both_heads(left, right, half):
+    none = jnp.zeros_like(right)
+    stacked = jnp.concatenate([jnp.where(half, right, none), jnp.where(half, none, right)], axis=0)
+    return dot32(jnp.concatenate(left, axis=1), stacked)
+
+
 def forward_kernel(first_ref, x_ref, conv_ref, gain_ref, wide_ref, tall_ref, bc_ref, bct_ref, ssm_ref, states_ref, state):
     first = first_ref[0]
     group = pl.program_id(0)
     half = lax.broadcasted_iota(jnp.int32, (Q, Q), 1) < HEAD_DIM
     state[...] = jnp.zeros_like(state)
-
     shift = (Q - GROUP * group) % Q
+    pairs = range(GROUP // 2)
     for c in range(x_ref.shape[0] // Q):
         rows = slice(c * Q, c * Q + Q)
         inside, carry, last, through = chunk_masks(first, c, False)
@@ -128,40 +141,39 @@
         cp = pltpu.roll(wide_ref[rows, 3 * Q :], shift, 1)
         cpt = tall_ref[pl.ds(pl.multiple_of(128 + group * GROUP, GROUP), GROUP), rows]
         scores = wide_ref[rows, :Q]
-        c16 = bc_ref[rows, NSTATE:]
-        for p in range(GROUP // 2):
+        old16 = state[...].astype(jnp.bfloat16)
+        states_ref[c * NSTATE : (c + 1) * NSTATE, :] = old16
+        if c > 0:
+            carried = dot32(bc_ref[rows, NSTATE:], old16)
+        weighted, ends = [], []
+        for p in pairs:
             cols = slice(p * Q, p * Q + Q)
-            moved = shifted_down(x_ref, cols, c, first, Q)
-            mixed = conv_ref[4:5, cols] + conv_ref[3:4, cols] * moved[0]
-            for j in range(1, KW):
-                mixed = mixed + conv_ref[KW - 1 - j : KW - j, cols] * moved[j]
+            _, mixed = conv_act(x_ref, conv_ref, cols, c, first)
             xs = mixed * sigmoid(mixed)
-            x16 = xs.astype(jnp.bfloat16)
-            locals_, cums, cps = [], [], []
-            for e in range(2):
-                k = 2 * p + e
+            mixing, cums, cps = [], [], []
+            for k in (2 * p, 2 * p + 1):
                 cum_b = lane_column(cum, k)
                 decay = jnp.exp(jnp.where(inside, cum_b - cpt[k : k + 1, :], NEG))
-                locals_.append(dot32((scores * decay).astype(jnp.bfloat16), x16))
+                mixing.append((scores * decay).astype(jnp.bfloat16))
                 cums.append(cum_b)
                 cps.append(lane_column(cp, k))
             cum_pair = jnp.where(half, cums[0], cums[1])
             cp_pair = jnp.where(half, cps[0], cps[1])
-            y = jnp.where(half, locals_[0], locals_[1])
-            old = state[:, cols]
-            old16 = old.astype(jnp.bfloat16)
-            states_ref[c * NSTATE : (c + 1) * NSTATE, cols] = old16
+            y = both_heads(mixing, xs.astype(jnp.bfloat16), half)
             if c > 0:
-                y = y + jnp.where(carry, jnp.exp(cum_pair), 0.0) * dot32(c16, old16)
+                y = y + jnp.where(carry, jnp.exp(cum_pair), 0.0) * carried[:, cols]
             ssm_ref[rows, cols] = y + gain_ref[0:1, cols] * xs
             end = cum_pair[Q - 1 : Q, :]
-            weight = jnp.where(last, jnp.exp(end - cp_pair), 0.0)
-            fresh = dot32(bct_ref[:NSTATE, rows], (weight * xs).astype(jnp.bfloat16))
-            keep = jnp.where(through, jnp.exp(end), 0.0)
-            state[:, cols] = fresh if c == 0 else keep * old + fresh
-
-
-def gated_kernel(z_ref, ssm_ref, gain_ref, gated_ref, r_ref):
+            weighted.append((jnp.where(last, jnp.exp(end - cp_pair), 0.0) * xs).astype(jnp.bfloat16))
+            ends.append(end)
+        fresh = dot32(bct_ref[:NSTATE, rows], jnp.concatenate(weighted, axis=1))
+        for p in pairs:
+            cols = slice(p * Q, p * Q + Q)
+            kept = 0.0 if c == 0 else jnp.where(through, jnp.exp(ends[p]), 0.0) * state[:, cols]
+            state[:, cols] = kept + fresh[:, cols]
+
+
+def gated_kernel(order, me_ref, z_ref, ssm_ref, gain_ref, gated_ref, sent_ref, r_ref):
     squares = jnp.zeros((Q, Q), jnp.float32)
     for p in range(z_ref.shape[1] // Q):
         cols = slice(p * Q, p * Q + Q)
@@ -176,15 +188,18 @@
         zv = z_ref[:, cols]
         g = ssm_ref[:, cols] * (zv * sigmoid(zv))
         gated_ref[:, cols] = (g * wide * gain_ref[1:2, cols]).astype(gated_ref.dtype)
-
-
-def gate_kernel(z_ref, ssm_ref, cot_ref, weight_ref, rk_ref, gain_ref, dz_ref, ds_ref, grads_ref):
+    part = gated_ref.shape[1] // 8
+    for i, j in enumerate(order):
+        sent_ref[:, i * part : (i + 1) * part] = gated_ref[:, pl.ds(pl.multiple_of((me_ref[0] ^ j) * part, 128), part)]
+
+
+def gate_kernel(z_ref, ssm_ref, cot_ref, weight_ref, rk_ref, gain_ref, dz_ref, ds_ref, grads_ref, d_gated):
+    d_gated[...] = dot32(cot_ref[...], weight_ref[...], NT)
     grads_ref[...] = jnp.zeros_like(grads_ref)
     for c in range(z_ref.shape[0] // Q):
         rows = slice(c * Q, c * Q + Q)
         scale = lane_column(rk_ref[rows, :], 0)
         pull = lane_column(rk_ref[rows, :], 1)
-        d_gated = dot32(cot_ref[rows, :], weight_ref[...], NT)
         for p in range(z_ref.shape[1] // Q):
             cols = slice(p * Q, p * Q + Q)
             zv = z_ref[rows, cols]
@@ -192,28 +207,25 @@
             silu_z = zv * sz
             ssm = ssm_ref[rows, cols]
             g = ssm * silu_z
-            gs = d_gated[:, cols] * scale
+            gs = d_gated[rows, cols] * scale
             grads_ref[0:1, cols] += sum_rows(gs * g)
             d_g = gain_ref[1:2, cols] * gs - g * pull
             dz_ref[rows, cols] = (d_g * ssm * (sz + silu_z * (1.0 - sz))).astype(dz_ref.dtype)
             ds_ref[rows, cols] = (d_g * silu_z).astype(ds_ref.dtype)
 
 
-def split_dot(values, right):
-    high = values.astype(jnp.bfloat16)
-    low = (values - high.astype(jnp.float32)).astype(jnp.bfloat16)
-    return dot32(high, right) + dot32(low, right)
-
-
-def backward_kernel(base, first_ref, x_ref, ssm_ref, ds_ref, conv_ref, gain_ref, wide_ref, tall_ref, bc_ref, bct_ref, states_ref, d_ref, grads_ref, sums_ref, flow_ref, dstate, dconv):
+def eight_rows(v):
+    return functools.reduce(jnp.add, [v[i : i + 8, :] for i in range(0, v.shape[0], 8)])
+
+
+def backward_kernel(base, first_ref, x_ref, ssm_ref, ds_ref, conv_ref, gain_ref, wide_ref, tall_ref, bc_ref, bct_ref, states_ref, d_ref, grads_ref, sums_ref, flow_ref, dstate, dconv, acc):
     first = first_ref[0]
     group = base + pl.program_id(0)
-    lane = lax.broadcasted_iota(jnp.int32, (Q, Q), 1)
-    half = lane < HEAD_DIM
+    half = lax.broadcasted_iota(jnp.int32, (Q, Q), 1) < HEAD_DIM
     dstate[...] = jnp.zeros_like(dstate)
+    acc[...] = jnp.zeros_like(acc)
     rows_all = x_ref.shape[0]
     dconv[rows_all : rows_all + 8, :] = jnp.zeros((8, dconv.shape[1]), jnp.float32)
-    grads_ref[...] = jnp.zeros_like(grads_ref)
     flow_ref[...] = jnp.zeros_like(flow_ref)
 
     @pl.when(pl.program_id(0) == 0)
@@ -222,6 +234,8 @@
 
     shift = (Q - GROUP * group) % Q
     chunks = rows_all // Q
+    pairs = range(GROUP // 2)
+    pick = (lax.broadcasted_iota(jnp.int32, (LANES, Q), 1) == GROUP * group + row_ids(0, LANES, Q) // HEAD_DIM).astype(jnp.bfloat16)
     for c in range(chunks - 1, -1, -1):
         rows = slice(c * Q, c * Q + Q)
         inside, carry, last, through = chunk_masks(first, c, True)
@@ -231,69 +245,76 @@
         scores_t = wide_ref[rows, Q : 2 * Q]
         b16, c16t = bc_ref[rows, :NSTATE], bct_ref[NSTATE:, rows]
         dst = jnp.zeros((Q, Q), jnp.float32)
-        db = jnp.zeros((Q, NSTATE), jnp.float32)
-        dc = jnp.zeros((Q, NSTATE), jnp.float32)
-        us, vs, ws = (jnp.zeros((Q, Q), jnp.float32) for _ in range(3))
-        for p in range(GROUP // 2):
+        if c < chunks - 1:
+            later16 = dstate[...].astype(jnp.bfloat16)
+            carried = dot32(b16, later16)
+        high, low, local, weighted, carries, eys, ends = ([] for _ in range(7))
+        for p in pairs:
             cols = slice(p * Q, p * Q + Q)
-            moved = shifted_down(x_ref, cols, c, first, Q)
-            mixed = conv_ref[4:5, cols] + conv_ref[3:4, cols] * moved[0]
-            for j in range(1, KW):
-                mixed = mixed + conv_ref[KW - 1 - j : KW - j, cols] * moved[j]
+            moved, mixed = conv_act(x_ref, conv_ref, cols, c, first)
             sx = sigmoid(mixed)
             xs = mixed * sx
             x16 = xs.astype(jnp.bfloat16)
             skip = gain_ref[0:1, cols]
-            y = ssm_ref[rows, cols] - skip * xs
             dy16 = ds_ref[rows, cols]
             d_ssm = dy16.astype(jnp.float32)
-            grads_ref[5:6, cols] += sum_rows(d_ssm * xs)
-            locals_, cums, cps = [], [], []
-            for e in range(2):
-                k = 2 * p + e
+            acc[40:48, cols] += eight_rows(d_ssm * xs)
+            mixing, cums, cps = [], [], []
+            for k in (2 * p, 2 * p + 1):
                 cp_b = lane_column(cp, k)
                 decay = jnp.exp(jnp.where(inside, cumt[k : k + 1, :] - cp_b, NEG))
-                locals_.append(dot32((scores_t * decay).astype(jnp.bfloat16), dy16))
-                x_half = jnp.where(half == (e == 0), x16, jnp.zeros_like(x16))
+                mixing.append((scores_t * decay).astype(jnp.bfloat16))
+                x_half = jnp.where(half == (k == 2 * p), x16, jnp.zeros_like(x16))
                 dst = dst + decay * dot32(x_half, dy16, NT)
                 cums.append(lane_column(cum, k))
                 cps.append(cp_b)
             cum_pair = jnp.where(half, cums[0], cums[1])
             cp_pair = jnp.where(half, cps[0], cps[1])
-            dx = jnp.where(half, locals_[0], locals_[1])
-            x32 = x16.astype(jnp.float32)
-            pick = (lane == GROUP * group + 2 * p + (row_ids(0, Q, Q) >= HEAD_DIM).astype(jnp.int32)).astype(jnp.bfloat16)
-            in_dot = x32 * dx
-            us = us + split_dot(d_ssm * y - in_dot, pick)
-            vs = vs + split_dot(in_dot, pick)
+            dx = both_heads(mixing, dy16, half)
+            in_dot = x16.astype(jnp.float32) * dx
+            u = d_ssm * (ssm_ref[rows, cols] - skip * xs) - in_dot
+            high.append(u.astype(jnp.bfloat16))
+            low.append((u - high[-1].astype(jnp.float32)).astype(jnp.bfloat16))
+            local.append(in_dot.astype(jnp.bfloat16))
             end = cum_pair[Q - 1 : Q, :]
-            keep = jnp.where(through, jnp.exp(end), 0.0)
+            ends.append(end)
             if c < chunks - 1:
-                later = dstate[:, cols]
-                later16 = later.astype(jnp.bfloat16)
                 weight = jnp.where(last, jnp.exp(end - cp_pair), 0.0)
-                carried = weight * dot32(b16, later16)
-                dx = dx + carried
-                ws = ws + split_dot(xs * carried, pick)
-                db = db + dot32((weight * xs).astype(jnp.bfloat16), later16, NT)
+                moved_in = weight * carried[:, cols]
+                dx = dx + moved_in
+                carries.append((xs * moved_in).astype(jnp.bfloat16))
+                weighted.append((weight * xs).astype(jnp.bfloat16))
             if c > 0:
-                ey16 = (jnp.where(carry, jnp.exp(cum_pair), 0.0) * d_ssm).astype(jnp.bfloat16)
-                old16 = states_ref[c * NSTATE : (c + 1) * NSTATE, cols]
-                dc = dc + dot32(ey16, old16, NT)
-                fresh = dot32(c16t, ey16)
-                if c < chunks - 1:
-                    flow_ref[c : c + 1, cols] = keep * sum_rows(later * old16.astype(jnp.float32))
-                    fresh = keep * later + fresh
-                dstate[:, cols] = fresh
+                eys.append((jnp.where(carry, jnp.exp(cum_pair), 0.0) * d_ssm).astype(jnp.bfloat16))
             d_mixed = (dx + skip * d_ssm) * (sx + xs * (1.0 - sx))
             dconv[rows, cols] = d_mixed
-            grads_ref[4:5, cols] += sum_rows(d_mixed)
+            acc[32:40, cols] += eight_rows(d_mixed)
             for j in range(KW):
-                grads_ref[KW - 1 - j : KW - j, cols] += sum_rows(d_mixed * moved[j])
+                acc[8 * (KW - 1 - j) : 8 * (KW - j), cols] += eight_rows(d_mixed * moved[j])
             taps = [conv_ref[i : i + 1, cols] for i in range(KW)]
             d_ref[rows, cols] = conv_back(dconv, cols, c, first, Q, taps).astype(d_ref.dtype)
-        for i, term in enumerate((dst, db, dc, us, vs, ws)):
-            sums_ref[rows, i * Q : (i + 1) * Q] += term
+        join = functools.partial(jnp.concatenate, axis=1)
+        sums_ref[rows, :Q] += dst
+        sums_ref[rows, 3 * Q : 4 * Q] += dot32(join(high), pick) + dot32(join(low), pick)
+        sums_ref[rows, 4 * Q : 5 * Q] += dot32(join(local), pick)
+        if c < chunks - 1:
+            sums_ref[rows, Q : 2 * Q] += dot32(join(weighted), later16, NT)
+            sums_ref[rows, 5 * Q :] += dot32(join(carries), pick)
+        if c > 0:
+            ey16 = join(eys)
+            old16 = states_ref[c * NSTATE : (c + 1) * NSTATE, :]
+            sums_ref[rows, 2 * Q : 3 * Q] += dot32(ey16, old16, NT)
+            fresh = dot32(c16t, ey16)
+            for p in pairs:
+                cols = slice(p * Q, p * Q + Q)
+                if c < chunks - 1:
+                    kept = jnp.where(through, jnp.exp(ends[p]), 0.0) * dstate[:, cols]
+                    flow_ref[c : c + 1, cols] = sum_rows(kept * old16[:, cols].astype(jnp.float32))
+                    dstate[:, cols] = kept + fresh[:, cols]
+                else:
+                    dstate[:, cols] = fresh[:, cols]
+    for i in range(8):
+        grads_ref[i : i + 1, :] = sum_rows(acc[8 * i : 8 * i + 8, :]) if i < 6 else jnp.zeros((1, LANES), jnp.float32)
 
 
 def post_kernel(calls, first_ref, bcd_ref, conv_ref, head_ref, bc_ref, *refs):
@@ -398,19 +419,20 @@
     )(first, x, conv, gains, *prep)
 
 
-def run_gated(z, ssm, gains):
+def run_gated(order, me, z, ssm, gains):
     rows, width = z.shape
+    b16 = jnp.bfloat16
     block = pl.BlockSpec((Q, width), lambda g: (g, 0))
     thin = pl.BlockSpec((Q, Q), lambda g: (g, 0))
     return pl.pallas_call(
-        gated_kernel,
+        functools.partial(gated_kernel, order),
         grid=(rows // Q,),
-        in_specs=[block, block, whole(gains.shape)],
-        out_specs=[block, thin],
-        out_shape=[shaped((rows, width), jnp.bfloat16), shaped((rows, Q), jnp.float32)],
+        in_specs=[smem(), block, block, whole(gains.shape)],
+        out_specs=[block, block, thin],
+        out_shape=[shaped((rows, width), b16), shaped((rows, width), b16), shaped((rows, Q), jnp.float32)],
         compiler_params=params(),
         cost_estimate=cost(4000000000, 16000000),
-    )(z, ssm, gains)
+    )(me, z, ssm, gains)
 
 
 def run_gate(z, ssm, cot, weight, rk, gains):
@@ -424,6 +446,7 @@
         in_specs=[block, block, whole(cot.shape), pl.BlockSpec((LANES, width), lambda g: (g, 0)), whole(rk.shape), eight],
         out_specs=[block, block, eight],
         out_shape=[shaped((rows, DI), b16)] * 2 + [shaped((8, DI), jnp.float32)],
+        scratch_shapes=[pltpu.VMEM((rows, LANES), jnp.float32)],
         compiler_params=params(),
         cost_estimate=cost(12000000000, 36000000),
     )(z, ssm, cot, weight, rk, gains)
@@ -443,7 +466,7 @@
         in_specs=[smem(), block, block, block, eight, eight] + [whole(v.shape) for v in prep] + [pl.BlockSpec((chunks * NSTATE, LANES), at)],
         out_specs=[pl.BlockSpec((rows, LANES), here), own, whole((rows, 6 * Q)), own],
         out_shape=[shaped((rows, count * LANES), b16), shaped((8, count * LANES), f32), shaped((rows, 6 * Q), f32), shaped((8, count * LANES), f32)],
-        scratch_shapes=[pltpu.VMEM((NSTATE, LANES), f32), pltpu.VMEM((rows + 8, LANES), f32)],
+        scratch_shapes=[pltpu.VMEM((NSTATE, LANES), f32), pltpu.VMEM((rows + 8, LANES), f32), pltpu.VMEM((48, LANES), f32)],
         compiler_params=params(),
         cost_estimate=cost(count * 7000000000, count * 8000000),
     )(first, x, ssm, ds, conv, gains, *prep, states)
@@ -660,6 +683,30 @@
     )(*args)
 
 
+def terms_kernel(left_ref, right_ref, got_ref, *outs):
+    rows = outs[0].shape[0]
+    product = dot32(left_ref[...], right_ref[...]) + got_ref[...].astype(jnp.float32)
+    for i, ref in enumerate(outs):
+        ref[...] = product[i * rows : (i + 1) * rows, :].astype(ref.dtype)
+
+
+def run_terms(left, right, got):
+    rows, inner = left.shape
+    cols = right.shape[1]
+    step = 512 if cols % 512 == 0 else cols
+    here = lambda g: (0, g)
+    kinds = [jnp.bfloat16] * 3 + [jnp.float32]
+    return pl.pallas_call(
+        terms_kernel,
+        grid=(cols // step,),
+        in_specs=[whole(left.shape), pl.BlockSpec((inner, step), here), pl.BlockSpec((rows, step), here)],
+        out_specs=[pl.BlockSpec((rows // 4, step), here)] * 4,
+        out_shape=[shaped((rows // 4, cols), kind) for kind in kinds],
+        compiler_params=params(),
+        cost_estimate=cost(2 * rows * inner * cols, 6 * rows * cols),
+    )(left, right, got)
+
+
 def norm_kernel(order, me_ref, x_ref, gain_ref, out_ref, sent_ref, turned):
     rows, width = x_ref.shape
     for c in range(rows // Q):
@@ -689,6 +736,39 @@
     )(me, x, gain)
 
 
+def open_kernel(places, behind, widths, me_ref, first_ref, x_ref, *refs):
+    count = len(places)
+    tails, pieces, refs = refs[: len(behind)], refs[len(behind) : len(behind) + count], refs[len(behind) + count :]
+    gain_ref, conv_ref, heads_ref, gains_ref, out_ref, sent_ref, bcd_ref, full_ref, *prep_refs, found, turned = refs
+    unpack_kernel(behind, widths, me_ref, *tails, gain_ref, conv_ref, heads_ref, gains_ref, found)
+    norm_kernel(ORDER, me_ref, x_ref, gain_ref, out_ref, sent_ref, turned)
+    project_kernel(places, me_ref, out_ref, *pieces, bcd_ref, full_ref)
+    prep_kernel(first_ref, bcd_ref, conv_ref.at[:, pl.ds(DI, 2 * NSTATE)], heads_ref, *prep_refs)
+
+
+def run_open(me, first, x, pieces, rows, widths, skip):
+    f32, b16 = jnp.float32, jnp.bfloat16
+    toks, width = x.shape
+    wide, taps, few, long = widths
+    behind = [[p for p in pieces if p[1] == j][-1] for j in range(8)]
+    places = tuple((j, start, min(v.shape[0], width // 8 - start)) for v, j, start in pieces)
+    shapes = [((1, 8 * wide), f32), ((8, 8 * taps), f32), ((8, 128), f32), ((8, 8 * long), f32)]
+    shapes += [((toks, width), b16), ((width, toks), b16), ((toks, BCD), f32), ((width, BCD), b16)]
+    shapes += [((toks, 4 * Q), f32), ((256, toks), f32), ((toks, 2 * NSTATE), b16), ((2 * NSTATE, toks), b16)]
+    return pl.pallas_call(
+        functools.partial(open_kernel, places, tuple(j for _, j, _ in behind), widths),
+        grid=(1,),
+        in_specs=[smem(), smem(), whole(x.shape)]
+        + [pl.BlockSpec((SMALL, 512), lambda g, at=(rows - start) // SMALL: (at, 0)) for _, _, start in behind]
+        + [pl.BlockSpec((v.shape[0], BCD), lambda g: (0, skip // BCD)) for v, _, _ in pieces],
+        out_specs=[whole(s) for s, _ in shapes],
+        out_shape=[shaped(s, d) for s, d in shapes],
+        scratch_shapes=[pltpu.VMEM((8, SMALL, 512), f32), pltpu.VMEM((width, toks), b16)],
+        compiler_params=params(),
+        cost_estimate=cost(6000000000, 10000000),
+    )(me, first, x, *[v for v, _, _ in behind], *[v for v, _, _ in pieces])
+
+
 def norm_back_kernel(d_ref, x_ref, cot_ref, gain_ref, out_ref, grad_ref):
     @pl.when(pl.program_id(0) == 0)
     def _():
@@ -755,17 +835,37 @@
     return v.astype(jnp.float32)
 
 
-def group_sum(product, rows):
+def group_sum(left, right):
+    half = left.shape[0] // 2
+    odd = jnp.dot(left[:half], right, preferred_element_type=jnp.float32).astype(jnp.bfloat16)
+    (got,) = yield [(odd, "fsdp", partners(1))], 1
+    *terms, own = run_terms(left[half:], right, got)
+    others = yield [(v, "fsdp", partners(j)) for v, j in zip(terms, ORDER[4:7])], 1
+    return own + widen(others[0]) + widen(others[1]) + widen(others[2])
+
+
+def relayed_sum(left, right):
     b16 = jnp.bfloat16
+    rows = left.shape[1] // 8
+    half = rows // 2
+
+    def product(start, stop):
+        return contract_rows(left[:, start * rows : stop * rows], right)
+
     (got,) = yield [(product(0, 4).astype(b16), "fsdp", partners(1))], 1
-    terms = [product(4 + i, 5 + i) + widen(got[i * rows : (i + 1) * rows]) for i in range(4)]
-    others = yield [(v.astype(b16), "fsdp", partners(j)) for v, j in zip(terms, ORDER[4:7])], 1
-    return terms[3] + widen(others[0]) + widen(others[1]) + widen(others[2])
-
-
-def left_rows(left, right):
-    rows = left.shape[0] // 8
-    return lambda i, j: jnp.dot(left[i * rows : j * rows], right, preferred_element_type=jnp.float32)
+    far = (product(4, 5) + widen(got[:rows])).astype(b16)
+    from_x, from_y = yield [(far[:half], "fsdp", partners(2)), (far[half:], "fsdp", partners(4))], 1
+    low = jnp.pad(widen(from_y), ((half, 0), (0, 0)))
+    high = jnp.pad(widen(from_x), ((0, half), (0, 0)))
+    to_x = (product(5, 6) + widen(got[rows : 2 * rows]) + low).astype(b16)
+    to_y = (product(6, 7) + widen(got[2 * rows : 3 * rows]) + high).astype(b16)
+    got_x, got_y = yield [(to_x, "fsdp", partners(2)), (to_y, "fsdp", partners(4))], 1
+    return product(7, 8) + widen(got[3 * rows :]) + widen(got_x) + widen(got_y)
+
+
+def out_sum(left, right):
+    own = yield from relayed_sum(left, right)
+    return (yield from half_sum(own))
 
 
 def half_sum(own):
@@ -794,9 +894,12 @@
 
 
 def small_sum(rows):
-    place = lax.axis_index("rep")
-    (got,) = yield [(rows, "fsdp", None)], 1
-    row = jnp.sum(got, axis=0, keepdims=True)
+    me, place = lax.axis_index("fsdp"), lax.axis_index("rep")
+    rows = rows[me ^ jnp.array(ORDER, jnp.int32)]
+    (got,) = yield [(rows[:4], "fsdp", partners(1))], 1
+    rows = rows[4:] + got
+    others = yield [(rows[i : i + 1], "fsdp", partners(j)) for i, j in enumerate(ORDER[4:7])], 1
+    row = rows[3:] + others[0] + others[1] + others[2]
     got = yield [(row, "rep", rotated(k)) for k in (1, 2, 3)], 1
     stack = jnp.concatenate([row, *got])
     return jnp.sum(stack[(place - jnp.arange(4)) % 4], axis=0)
@@ -809,7 +912,7 @@
 
 
 def slice_sum(left, right):
-    own = yield from group_sum(left_rows(left, right), left.shape[0] // 8)
+    own = yield from group_sum(left, right)
     return (yield from half_sum(own))
 
 
@@ -881,19 +984,17 @@
     small = jnp.pad(small, ((0, SMALL - small.shape[0]), (0, 0)))
     if custom():
         rows, span = in_weight.shape[0], DI + BCD
-        w_xb = jnp.pad(in_weight[:, DI:], ((0, SMALL), (0, span + DI - in_weight.shape[1])))
+        w_xb = lax.pad(in_weight, jnp.zeros((), b16), ((0, SMALL, 0), (-DI, span + DI - in_weight.shape[1], 0)))
         e_xb = moves.add(gathered_rows(w_xb + jnp.pad(small, ((rows, 0), (0, span - small.shape[1])))))
         moves.turn()
         e_x = moves.add(dealt(blocks(tokens), 1))
-        moves.turn()
+        (cot_blocks,) = moves.turn(lambda v: (blocks(v),), cotangent)
         out_weight = moves.after(out_weight)
         w_out = lax.all_gather(out_weight, "fsdp", axis=0, tiled=True)
         moves.turn()
         pieces = e_xb["value"]
         x = e_x["value"].reshape(tok_rows, width)
-        behind = [[p for p in pieces if p[1] == j][-1] for j in range(8)]
         widths = (norm_gain.size, conv_bias.size, dt_bias.size, gated_gain.size)
-        gain, conv, heads, gains = run_unpack(me, behind, rows, widths)
     else:
         x = deal(tokens)
         w_z = lax.all_gather(in_weight[:, :DI], "fsdp", axis=0, tiled=True)
@@ -908,27 +1009,29 @@
         conv = jnp.concatenate([taps, bias, jnp.zeros((3, bias.shape[1]), f32)])
         heads = pad_lanes(jnp.concatenate([step_bias, rate, jnp.zeros((6, HEADS), f32)]), 128)
         gains = jnp.concatenate([jnp.repeat(skip, HEAD_DIM, axis=1), ggain, jnp.zeros((6, DI), f32)])
-    conv_x, conv_bc = conv[:, :DI], conv[:, DI:]
-
     if custom():
 
         def open_up(x):
-            normed, sent = run_norm(ORDER, me, x, gain)
-            bcd, w_b = run_project(me, normed, pieces, DI, BCD)
-            xr, w_x = run_project(me, normed, pieces, 0, DI)
-            return normed, sent, bcd, w_b, xr, w_x, run_prep(first, bcd, conv_bc, heads)
+            gain, conv, heads, gains, normed, sent, bcd, w_b, *prep = run_open(me, first, x, pieces, rows, widths, DI)
+            return gain, conv, heads, gains, normed, sent, bcd, w_b, prep, *run_project(me, normed, pieces, 0, DI)
 
         e_z = moves.add(gathered_rows(in_weight[:, :DI]))
-        normed, sent, bcd, w_b, xr, w_x, prep = moves.turn(open_up, x)
-        e_cot = moves.add(dealt(blocks(cotangent), 1))
+        gain, conv, heads, gains, normed, sent, bcd, w_b, prep, xr, w_x = moves.turn(open_up, x)
+        conv_x, conv_bc = conv[:, :DI], conv[:, DI:]
         ssm, states = moves.turn(lambda v: run_forward(first, v, conv_x, gains, prep), xr)
         moves.turn()
-        z, w_z = run_project(me, normed, e_z["value"], 0, DI)
-        gated, r = run_gated(z, ssm, gains)
+        e_cot = moves.add(dealt(cot_blocks, 1))
+
+        def close_up(ssm):
+            z, full = run_project(me, normed, e_z["value"], 0, DI)
+            return z, full, *run_gated(ORDER, me, z, ssm, gains)
+
+        z, w_z, gated, gated_sent, r = moves.turn(close_up, ssm)
         cot = e_cot["value"].reshape(tok_rows, width)
-        out_term, gated = tie(contract_rows(gated, cot, b16), gated)
-        result, rk = run_out(gated, w_out, x, cot, r)
+        e_rows = moves.add(out_sum(gated_sent, cot))
+        result, rk = moves.turn(lambda v: run_out(v, w_out, x, cot, r), gated)
     else:
+        conv_x, conv_bc = conv[:, :DI], conv[:, DI:]
         normed, sent = run_norm((0,), me * 0, x, gain)
         w_x, w_b = w_xb[:, :DI], w_xb[:, DI:]
         bcd = jnp.dot(normed, w_b, preferred_element_type=f32)
@@ -937,13 +1040,12 @@
         prep = run_prep(first, bcd, conv_bc, heads)
         ssm, states = run_forward(first, xr, conv_x, gains, prep)
         z = jnp.dot(normed, w_z, preferred_element_type=f32)
-        gated, r = run_gated(z, ssm, gains)
+        gated, _, r = run_gated(tuple(range(8)), me * 0, z, ssm, gains)
         result, rk = run_out(gated, w_out, x, cot, r)
-        out_term = contract_rows(gated, cot, b16)
-    s_out = lax.psum_scatter(out_term, "fsdp", scatter_dimension=0, tiled=True)
-    dz, ds, ggrads = run_gate(z, ssm, cot, w_out, rk, gains)
-    z_term, ds = tie(contract_rows(normed, dz, b16), ds)
-    s_z = lax.psum_scatter(z_term, "fsdp", scatter_dimension=0, tiled=True)
+        s_out = lax.psum_scatter(contract_rows(gated, cot, b16), "fsdp", scatter_dimension=0, tiled=True)
+
+    def gate(rk):
+        return run_gate(z, ssm, cot, w_out, rk, gains)
 
     def backward(base, count, ds):
         return run_backward(base, count, first, xr, ssm, ds, conv_x, gains, prep, states)
@@ -956,22 +1058,28 @@
         return run_back(pairs + [(d_b, 0, w_b, 0, BCD)])
 
     if custom():
-        backs = [backward(*CALLS[0], ds)]
+        dz, ds, ggrads = moves.turn(gate, rk)
+
+        def first_back(dz, ds):
+            z_term, ds = tie(contract_rows(normed, dz, b16), ds)
+            held.append(lax.psum_scatter(z_term, "fsdp", scatter_dimension=0, tiled=True))
+            return backward(*CALLS[0], ds)
+
+        held = []
+        backs = [moves.turn(first_back, dz, ds)]
+        (s_z,) = held
         e_first = moves.add(slice_sum(sent, backs[0][0]))
-        e_output = moves.add(dealt(result.reshape(groups, block_rows, width), 1))
 
         def middle(ds):
             both = backs + [backward(*CALLS[1], ds)]
             return both[1], *close(both)
 
-        s_out, ds = tie(s_out, ds)
-        e_rows = moves.add(half_sum(s_out))
         last, d_b, bgrads, hgrads = moves.turn(middle, ds)
         backs.append(last)
+        s_z, d_b = tie(s_z, d_b)
         e_last = moves.add(slice_sum(sent, jnp.concatenate([last[0], d_b], axis=1)))
+        e_z = moves.add(half_sum(s_z))
         (d_normed,) = moves.turn(lambda d: (back(backs, d),), d_b)
-        s_z, d_normed = tie(s_z, d_normed)
-        e_z = moves.add(half_sum(s_z))
 
         def finish(d_normed):
             d_input, ngrads = run_norm_back(d_normed, x, cot, gain)
@@ -979,6 +1087,8 @@
 
         d_input, packed = moves.turn(finish, d_normed)
     else:
+        dz, ds, ggrads = gate(rk)
+        s_z = lax.psum_scatter(contract_rows(normed, dz, b16), "fsdp", scatter_dimension=0, tiled=True)
         backs = [backward(*call, ds) for call in CALLS]
         d_b, bgrads, hgrads = close(backs)
         d_normed = back(backs, d_b)
@@ -1005,22 +1115,41 @@
         packed = pad_lanes(packed, packed.shape[1] + -packed.shape[1] % 128)
     sizes = [v.size for v in own_small]
     tail = in_weight.shape[1] - 2 * DI
+
+    def cut(row):
+        ends, outs = 0, []
+        for size in sizes:
+            outs.append(row[ends : ends + size])
+            ends += size
+        return outs
+
     if custom():
         e_small = moves.add(small_sum(packed))
         e_input = moves.add(dealt(d_input.reshape(groups, block_rows, width), 1))
+        moves.turn()
+        e_output = moves.add(dealt(result.reshape(groups, block_rows, width), 1))
+        moves.turn()
+
+        def restored(entry):
+            return entry["value"][targets].reshape(tok_rows, width)
+
+        input_grad, r_out = moves.turn(lambda: (restored(e_input), widen(e_rows["value"])))
+        (output,) = moves.turn(lambda: (restored(e_output),))
+        last = CALLS[-1][1] * LANES + tail
+
+        def gather_up():
+            known = jnp.concatenate([e_z["value"], e_first["value"], jnp.zeros((rows, last), b16)], axis=1)
+            return widen(known), *cut(e_small["value"])
+
+        r_in, *outs = moves.turn(gather_up)
         moves.finish()
-        output, input_grad = (e["value"][targets].reshape(tok_rows, width) for e in (e_output, e_input))
-        r_small, r_out = e_small["value"], e_rows["value"]
-        r_in = jnp.concatenate([e_z["value"], e_first["value"], e_last["value"][:, : CALLS[-1][1] * LANES + tail]], axis=1)
+        r_in = lax.dynamic_update_slice(r_in, widen(e_last["value"][:, :last]), (0, r_in.shape[1] - last))
     else:
         s_small = jnp.sum(lax.all_to_all(packed, "fsdp", split_axis=0, concat_axis=0, tiled=True), axis=0)
         r_small = jnp.sum(lax.all_gather(s_small, "rep", axis=0, tiled=False), axis=0)
         *r_in, r_out = lax.psum((s_z, *s_in, s_out), "rep")
         r_in = jnp.concatenate(r_in, axis=1)[:, : in_weight.shape[1]]
-    ends, outs = 0, []
-    for size in sizes:
-        outs.append(r_small[ends : ends + size])
-        ends += size
+        outs = cut(r_small)
     return (output, input_grad, outs[0], r_in.astype(f32), outs[1].reshape(conv_weight.shape), outs[2], outs[3], outs[4], outs[5], outs[6], r_out.astype(f32))
 
 

time: 582 us -> 540 us (0.928)
  waiting for transfers between devices: 186 us -> 163 us
  matrix products: 45.6 us -> 32.6 us
  other arithmetic: 18.9 us -> 29.5 us
  Pallas kernels: 189 us -> 179 us
  blocking collectives: 7.7 us -> 0 us
    ppermute x45 -> x54, waiting for transfers between devices: 186 us -> 159 us  [transfer(): return lax.ppermute(v, axis, pairs)]
    dot_general x10 -> x2, matrix products: 26.8 us -> 9.23 us  [group_sum(): jnp.dot(left[:half], right, preferred_element_type=jnp.float32)]
    pallas_call x4, Pallas kernels: 18.4 us -> 29 us  [the longest x2 11.4 us: run_terms(): pl.pallas_call(terms_kernel, grid=(cols // step,), in_specs=[whole(left.s...]
    pallas_call x2, Pallas kernels: 50.3 us -> 41.2 us  [run_backward(): pl.pallas_call(functools.partial(backward_kernel, base), grid=(count,), i...]
    all_to_all x1 -> x0, blocking collectives: 7.7 us -> none  [transfer(): return lax.all_to_all(v, axis, split_axis=0, concat_axis=0, tiled=True)]
    dot_general x2 -> x6, matrix products: 18.8 us -> 23.4 us  [contract_rows(): lax.dot_general(left, right, (((0,), (0,)), ((), ())), preferred_element_...]
    pallas_call x3 -> x2, Pallas kernels: 31.1 us -> 27.3 us  [run_project(): pl.pallas_call(functools.partial(project_kernel, places), grid=(cols // s...]
    ppermute x45 -> x54, starting transfers between devices: 54.3 us -> 54.2 us  [transfer(): return lax.ppermute(v, axis, pairs)]
  transfers between devices with their start and end apart: 52 -> 60, of which waited for: 22 -> 21; matrix products, arithmetic and copies ran while one was open for 13% -> 9% of each run, Pallas kernels for 33% -> 33%
where the time goes in v4:
time: 540 us; the launch traced here: 531 us
  Pallas kernels  179 us (33%)
  waiting for transfers between devices  163 us (30%)
  starting transfers between devices  69.9 us (13%)
  local copies, waits for them, and re-layouts  41.5 us (8%)
  matrix products  32.6 us (6%)
  other arithmetic  29.5 us (5%)
  between operations  15.3 us (3%)
    ppermute x54, waiting for transfers between devices, transfer(): return lax.ppermute(v, axis, pairs)  159 us
    ppermute x54, starting transfers between devices, transfer(): return lax.ppermute(v, axis, pairs)  54.2 us
    pallas_call x2, Pallas kernels, run_backward(): pl.pallas_call(functools.partial(backward_kernel, base), grid=(count,), i...  41.2 us
    pallas_call x2, Pallas kernels, run_project(): pl.pallas_call(functools.partial(project_kernel, places), grid=(cols // s...  27.3 us
    dot_general x6, matrix products, contract_rows(): lax.dot_general(left, right, (((0,), (0,)), ((), ())), preferred_element_...  23.4 us
    pallas_call x1, Pallas kernels, run_back(): pl.pallas_call(functools.partial(back_kernel, tuple(spans), int(base is n...  21.9 us
    pallas_call x1, Pallas kernels, run_forward(): pl.pallas_call(forward_kernel, grid=(width // LANES,), in_specs=[smem(),...  20.1 us
    pallas_call x1, Pallas kernels, run_gate(): pl.pallas_call(gate_kernel, grid=(DI // LANES,), in_specs=[block, block,...  15.2 us
  transfers between devices with their start and end apart: 60, of which 21 were waited for; matrix products, arithmetic and copies ran while one was open for 9% of the time, Pallas kernels for 33%

profile of v4, /device:TPU:0, one launch (start us, length us, event | category | flops | bytes accessed | tf_op | source)
XLA Modules:
  0.0 531.4 jit_solution(1848186749749223980)
XLA Ops:
  12.1 2.6 fusion.1.refs_0_.refs_8_
  14.6 2.9 collective-permute-start
  21.9 27.5 %collective-permute-done.refs_2_.refs_10_ = bf16[208,3456]{1,0:T(8,128)(2,1)} collective-permute-done((bf16[208,3456]{1,0:T(8,128)(2,1)}, bf16[208,3456]{1,0:T(8,128)(2,1)}, u32[]{:S(2)}, u32[]{:S(2)}) %collective-permute-start) | collective-permute-done | bytes 1437728 | tf_op jit(solution)/shard_map/ppermute | solution.py:911
  50.8 2.4 slice.112
  54.1 3.6 all-to-all-start
  61.1 3.3 gather_fusion.1
  64.5 27.6 %collective-permute-done.2.refs_14_.refs_6_ = bf16[96,3456]{1,0:T(8,128)(2,1)} collective-permute-done((bf16[96,3456]{1,0:T(8,128)(2,1)}, bf16[96,3456]{1,0:T(8,128)(2,1)}, u32[]{:S(2)}, u32[]{:S(2)}) %collective-permute-start.2) | collective-permute-done | bytes 663584 | tf_op jit(solution)/shard_map/ppermute | solution.py:911
  99.6 2.5 collective-permute-done.10.refs_7_.refs_17_.refs_9_
  103.0 8.3 %shard_map.221 = (f32[1,1536]{1,0:T(1,128)}, f32[8,3328]{1,0:T(8,128)}, f32[8,128]{1,0:T(8,128)}, f32[8,3072]{1,0:T(8,128)}, bf16[512,1536]{1,0:T(8,128)(2,1)}, ...) custom-call(s32[1]{0:T(128)} %bitcast.7.me_ref, ...), custom_call_target="tpu_custom_call" | custom-call | flops 2000000000 | bytes 3333333 | tf_op jit(solution)/shard_map/pallas_call | solution.py:758
  111.4 13.6 %shard_map.222 = (f32[512,3072]{1,0:T(8,128)}, bf16[1536,3072]{1,0:T(8,128)(2,1)}) custom-call(s32[1]{0:T(128)} %bitcast.7.me_ref, bf16[512,1536]{1,0:T(8,128)(2,1)} %get-tuple-element.300.left_ref, bf16[208,3456]{1,0:T(8,128)(2,1)} %fusion.1.refs_0_.refs_8_, bf16[208,3456]{1,0:T(8,128)(2,1)} %collective-permute-done.4.refs_1_.refs_9_, ...), custom_call_target="tpu_custom_call" | custom-call | flops 1610612736 | bytes 9437184 | tf_op jit(solution)/shard_map/pallas_call | solution.py:517
  125.0 13.8 %collective-permute-done.5.refs_2_ = bf16[192,3072]{1,0:T(8,128)(2,1)S(1)} collective-permute-done((bf16[192,3072]{1,0:T(8,128)(2,1)}, bf16[192,3072]{1,0:T(8,128)(2,1)S(1)}, u32[]{:S(2)}, u32[]{:S(2)}) %collective-permute-start.5) | collective-permute-done | bytes 1179680 | tf_op jit(solution)/shard_map/ppermute | solution.py:911
  141.0 2.5 collective-permute-start.11
  145.4 20.1 %shard_map.223 = (f32[512,3072]{1,0:T(8,128)}, bf16[512,3072]{1,0:T(8,128)(2,1)}) custom-call(s32[1]{0:T(128)} %bitcast.48, f32[512,3072]{1,0:T(8,128)} %get-tuple-element.289.x_ref, f32[8,3072]{1,0:T(8,128)} %slice.119.conv_ref, f32[8,3072]{1,0:T(8,128)} %get-tuple-element.291.gain_ref, f32[512,512]{1,0:T(8,128)} %get-tuple-element.292.wide_ref, ...), custom_call_target="tpu_custom_call" | custom-call | flops 6666666496 | bytes 6666666 | tf_op jit(solution)/shard_map/pallas_call | solution.py:410
  165.5 4.7 collective-permute-done.11.refs_6_
  173.3 3.6 all-to-all-start.1
  178.0 2.6 collective-permute-done.16.refs_8_
  181.7 13.7 %shard_map.224 = (f32[512,3072]{1,0:T(8,128)}, bf16[1536,3072]{1,0:T(8,128)(2,1)}) custom-call(s32[1]{0:T(128)} %bitcast.7.me_ref, bf16[512,1536]{1,0:T(8,128)(2,1)} %get-tuple-element.300.left_ref, bf16[192,3072]{1,0:T(8,128)(2,1)} %slice.111.refs_0_, bf16[192,3072]{1,0:T(8,128)(2,1)} %copy-done.17, bf16[192,3072]{1,0:T(8,128)(2,1)} %copy-done.14, ...), custom_call_target="tpu_custom_call" | custom-call | flops 1610612736 | bytes 9437184 | tf_op jit(solution)/shard_map/pallas_call | solution.py:517
  195.4 9.2 %shard_map.225 = (bf16[512,3072]{1,0:T(8,128)(2,1)}, bf16[512,3072]{1,0:T(8,128)(2,1)}, f32[512,128]{1,0:T(8,128)}) custom-call(s32[1]{0:T(128)} %bitcast.7.me_ref, f32[512,3072]{1,0:T(8,128)} %get-tuple-element.331.z_ref, f32[512,3072]{1,0:T(8,128)} %get-tuple-element.314.ssm_ref, f32[8,3072]{1,0:T(8,128)} %get-tuple-element.291.gain_ref), custom_call_target="tpu_custom_call" | custom-call | flops 1333333376 | bytes 5333333 | tf_op jit(solution)/shard_map/pallas_call | solution.py:427
  204.7 6.3 %convolution_convert_fusion = bf16[1536,1536]{1,0:T(8,128)(2,1)} fusion(bf16[512,1536]{1,0:T(8,128)(2,1)S(1)} %bitcast.31, bf16[512,3072]{1,0:T(8,128)(2,1)} %get-tuple-element.318), kind=kOutput, calls=%fused_computation.6 | convolution fusion | flops 2418278400 | bytes 7864320 | tf_op jit(solution)/shard_map/dot_general | solution.py:493
  211.3 10.6 %shard_map.226 = (bf16[512,1536]{1,0:T(8,128)(2,1)}, f32[512,128]{1,0:T(8,128)}) custom-call(bf16[512,3072]{1,0:T(8,128)(2,1)} %get-tuple-element.322.gated_ref, bf16[3072,1536]{1,0:T(8,128)(2,1)} %all-gather.2.cloned.1.call-done.weight_ref, bf16[512,1536]{1,0:T(8,128)(2,1)} %bitcast.40, bf16[512,1536]{1,0:T(8,128)(2,1)} %bitcast.32, ...), custom_call_target="tpu_custom_call" | custom-call | flops 3221225472 | bytes 8388608 | tf_op jit(solution)/shard_map/pallas_call | solution.py:591
  227.4 15.2 %shard_map.227 = (bf16[512,3072]{1,0:T(8,128)(2,1)}, bf16[512,3072]{1,0:T(8,128)(2,1)}, f32[8,3072]{1,0:T(8,128)}) custom-call(f32[512,3072]{1,0:T(8,128)} %get-tuple-element.331.z_ref, f32[512,3072]{1,0:T(8,128)} %get-tuple-element.314.ssm_ref, bf16[512,1536]{1,0:T(8,128)(2,1)} %bitcast.33, bf16[3072,1536]{1,0:T(8,128)(2,1)} %all-gather.2.cloned.1.call-done.weight_ref, ...), custom_call_target="tpu_custom_call" | custom-call | flops 4000000000 | bytes 12000000 | tf_op jit(solution)/shard_map/pallas_call | solution.py:443
  242.6 3.3 add_convert_fusion.1
  248.8 7.5 %fusion.28 = bf16[1536,3072]{1,0:T(8,128)(2,1)} fusion(bf16[512,1536]{1,0:T(8,128)(2,1)S(1)} %copy-done.10, bf16[512,3072]{1,0:T(8,128)(2,1)S(1)} %copy-done.13), kind=kOutput, calls=%fused_computation.81 | convolution fusion | flops 4831838208 | bytes 14155776 | tf_op jit(solution)/shard_map/dot_general | solution.py:493
  259.8 26.0 %shard_map.228 = (bf16[512,2048]{1,0:T(8,128)(2,1)}, f32[8,2048]{1,0:T(8,128)}, f32[512,768]{1,0:T(8,128)}, f32[8,2048]{1,0:T(8,128)}) custom-call(s32[1]{0:T(128)} %bitcast.49, f32[512,3072]{1,0:T(8,128)} %get-tuple-element.289.x_ref, f32[512,3072]{1,0:T(8,128)} %get-tuple-element.314.ssm_ref, bf16[512,3072]{1,0:T(8,128)(2,1)} %get-tuple-element.355.ds_ref, ...), custom_call_target="tpu_custom_call" | custom-call | flops 9333332992 | bytes 10666666 | tf_op jit(solution)/shard_map/pallas_call | solution.py:463
  285.9 5.0 convolution_convert_fusion.1
  297.4 15.1 %shard_map.229 = (bf16[512,1024]{1,0:T(8,128)(2,1)}, f32[8,1024]{1,0:T(8,128)}, f32[512,768]{1,0:T(8,128)}, f32[8,1024]{1,0:T(8,128)}) custom-call(s32[1]{0:T(128)} %bitcast.50, f32[512,3072]{1,0:T(8,128)} %get-tuple-element.289.x_ref, f32[512,3072]{1,0:T(8,128)} %get-tuple-element.314.ssm_ref, bf16[512,3072]{1,0:T(8,128)(2,1)} %get-tuple-element.355.ds_ref, ...), custom_call_target="tpu_custom_call" | custom-call | flops 4666666496 | bytes 5333333 | tf_op jit(solution)/shard_map/pallas_call | solution.py:463
  312.5 6.4 %shard_map.230 = (bf16[512,384]{1,0:T(8,128)(2,1)}, f32[8,256]{1,0:T(8,128)}, f32[8,128]{1,0:T(8,128)}) custom-call(s32[1]{0:T(128)} %bitcast.51, f32[512,384]{1,0:T(8,128)} %get-tuple-element.360.bcd_ref, f32[8,256]{1,0:T(8,128)} %slice.132.conv_ref, f32[8,128]{1,0:T(8,128)} %get-tuple-element.361.head_ref, bf16[512,256]{1,0:T(8,128)(2,1)} %get-tuple-element.294.bc_ref, ...), custom_call_target="tpu_custom_call" | custom-call | flops 1333333376 | bytes 2666666 | tf_op jit(solution)/shard_map/pallas_call | solution.py:480
  319.0 6.3 %shard_map.231 = (bf16[192,2048]{1,0:T(8,128)(2,1)}, bf16[192,2048]{1,0:T(8,128)(2,1)}, bf16[192,2048]{1,0:T(8,128)(2,1)}, f32[192,2048]{1,0:T(8,128)}) custom-call(bf16[768,512]{1,0:T(8,128)(2,1)} %slice.116.left_ref, bf16[512,2048]{1,0:T(8,128)(2,1)} %get-tuple-element.350.right_ref.refs_2_, bf16[768,2048]{1,0:T(8,128)(2,1)} %collective-permute-done.24.got_ref), custom_call_target="tpu_custom_call" | custom-call | flops 536870912 | bytes 3145728 | tf_op jit(solution)/shard_map/pallas_call | solution.py:699
  328.5 4.3 reduce-scatter.2.cloned.1.call-done
  334.6 4.2 convolution_convert_fusion.2
  345.6 11.0 %collective-permute-done.25 = bf16[96,1536]{1,0:T(8,128)(2,1)S(1)} collective-permute-done((bf16[96,1536]{1,0:T(8,128)(2,1)}, bf16[96,1536]{1,0:T(8,128)(2,1)S(1)}, u32[]{:S(2)}, u32[]{:S(2)}) %collective-permute-start.25) | collective-permute-done | bytes 294944 | tf_op jit(solution)/shard_map/ppermute | solution.py:911
  357.2 21.9 %shard_map.232.d_ref = f32[512,1536]{1,0:T(8,128)} custom-call(bf16[512,3072]{1,0:T(8,128)(2,1)} %get-tuple-element.342.refs_0_, bf16[1536,3072]{1,0:T(8,128)(2,1)} %get-tuple-element.384.refs_1_, bf16[512,2048]{1,0:T(8,128)(2,1)} %get-tuple-element.350.right_ref.refs_2_, bf16[1536,3072]{1,0:T(8,128)(2,1)} %get-tuple-element.385.refs_3_.refs_5_, ...), custom_call_target="tpu_custom_call" | custom-call | flops 1000 | bytes 1000 | tf_op jit(solution)/shard_map/pallas_call | solution.py:674
  383.6 5.1 shard_map.233
  389.0 2.7 collective-permute-start.31
  395.2 9.9 %collective-permute-done.31 = bf16[96,1536]{1,0:T(8,128)(2,1)S(1)} collective-permute-done((bf16[96,1536]{1,0:T(8,128)(2,1)S(1)}, bf16[96,1536]{1,0:T(8,128)(2,1)S(1)}, u32[]{:S(2)}, u32[]{:S(2)}) %collective-permute-start.31) | collective-permute-done | bytes 294944 | tf_op jit(solution)/shard_map/ppermute | solution.py:911
  405.1 5.1 shard_map.234
  410.1 2.5 shard_map.235
  412.6 7.7 %collective-permute-done.36 = bf16[48,3072]{1,0:T(8,128)(2,1)S(1)} collective-permute-done((bf16[48,3072]{1,0:T(8,128)(2,1)S(1)}, bf16[48,3072]{1,0:T(8,128)(2,1)S(1)}, u32[]{:S(2)}, u32[]{:S(2)}) %collective-permute-start.36) | collective-permute-done | bytes 294944 | tf_op jit(solution)/shard_map/ppermute | solution.py:911
  425.6 3.6 all-to-all-start.2
  429.2 2.7 collective-permute-start.40
  435.4 23.8 %collective-permute-done.38 = bf16[48,2048]{1,0:T(8,128)(2,1)S(1)} collective-permute-done((bf16[48,2048]{1,0:T(8,128)(2,1)}, bf16[48,2048]{1,0:T(8,128)(2,1)S(1)}, u32[]{:S(2)}, u32[]{:S(2)}) %collective-permute-start.38) | collective-permute-done | bytes 196640 | tf_op jit(solution)/shard_map/ppermute | solution.py:911
  465.8 4.4 all-to-all-start.3
  474.4 2.8 collective-permute-start.45
  477.7 13.8 %collective-permute-done.45 = f32[1,2688]{1,0:T(1,128)S(1)} collective-permute-done((f32[1,2688]{1,0:T(1,128)S(1)}, f32[1,2688]{1,0:T(1,128)S(1)}, u32[]{:S(2)}, u32[]{:S(2)}) %collective-permute-start.45) | collective-permute-done | bytes 10784 | tf_op jit(solution)/shard_map/ppermute | solution.py:911
  492.1 3.1 collective-permute-done.47
  499.2 3.4 fusion.2
  511.8 3.2 gather_fusion.4
  515.6 2.6 maximum_convert_fusion
  (273 shorter events, 111.9 us)
Async XLA Ops:
  14.6 34.7 %collective-permute-start = (bf16[208,3456]{1,0:T(8,128)(2,1)}, bf16[208,3456]{1,0:T(8,128)(2,1)}, u32[]{:S(2)}, u32[]{:S(2)}) collective-permute-start(bf16[208,3456]{1,0:T(8,128)(2,1)} %fusion.1.refs_0_.refs_8_), channel_id=1, source_target_pairs={{0,2},{1,3},{2,0},{3,1},{4,6},{5,7},{6,4},{7,5},{8,10},{9,11},{10,... | collective-permute-start | bytes 4313096 | tf_op jit(solution)/shard_map/ppermute | solution.py:911
  17.6 33.2 %collective-permute-start.1 = (bf16[208,3456]{1,0:T(8,128)(2,1)}, bf16[208,3456]{1,0:T(8,128)(2,1)S(1)}, u32[]{:S(2)}, u32[]{:S(2)}) collective-permute-start(bf16[208,3456]{1,0:T(8,128)(2,1)} %fusion.1.refs_0_.refs_8_), channel_id=1, source_target_pairs={{0,4},{1,5},{2,6},{3,7},{4,0},{5,1},{6,2},{7,3},{8,12},{9,13},{10,... | collective-permute-start | bytes 4313096 | tf_op jit(solution)/shard_map/ppermute | solution.py:911
  54.1 40.4 %collective-permute-start.4 = (bf16[208,3456]{1,0:T(8,128)(2,1)}, bf16[208,3456]{1,0:T(8,128)(2,1)}, u32[]{:S(2)}, u32[]{:S(2)}) collective-permute-start(bf16[208,3456]{1,0:T(8,128)(2,1)} %fusion.1.refs_0_.refs_8_), channel_id=1, source_target_pairs={{0,1},{1,0},{2,3},{3,2},{4,5},{5,4},{6,7},{7,6},{8,9},{9,8},{10,11... | collective-permute-start | bytes 4313096 | tf_op jit(solution)/shard_map/ppermute | solution.py:911
  54.1 40.4 %all-to-all-start = ((bf16[8,64,1536]{2,1,0:T(8,128)(2,1)}), bf16[8,64,1536]{2,1,0:T(8,128)(2,1)S(1)}, u32[]{:S(2)}, u32[]{:S(2)}) async-start(bf16[8,64,1536]{2,1,0:T(8,128)(2,1)} %gather_fusion), calls=%async_computation | async-start | bytes 3145728 | tf_op jit(solution)/shard_map/all_to_all | solution.py:910
  57.7 153.6 %all-gather.2.cloned.1.call-start = ((), (), s32[]{:S(2)}) async-start(), calls=%async_computation.5 | async-start | bytes 10616832 | tf_op jit(solution)/shard_map/all_gather | solution.py:993
  57.8 36.7 %collective-permute-start.3 = (bf16[112,3456]{1,0:T(8,128)(2,1)}, bf16[112,3456]{1,0:T(8,128)(2,1)}, u32[]{:S(2)}, u32[]{:S(2)}) collective-permute-start(bf16[112,3456]{1,0:T(8,128)(2,1)} %slice.113), channel_id=1, source_target_pairs={{0,2},{1,3},{2,0},{3,1},{4,6},{5,7},{6,4},{7,5},{8,10},{9,11},{10,... | collective-permute-start | bytes 2322440 | tf_op jit(solution)/shard_map/ppermute | solution.py:911
  59.7 32.4 %collective-permute-start.2 = (bf16[96,3456]{1,0:T(8,128)(2,1)}, bf16[96,3456]{1,0:T(8,128)(2,1)}, u32[]{:S(2)}, u32[]{:S(2)}) collective-permute-start(bf16[96,3456]{1,0:T(8,128)(2,1)} %slice.112), channel_id=1, source_target_pairs={{0,4},{1,5},{2,6},{3,7},{4,0},{5,1},{6,2},{7,3},{8,12},{9,13},{10,... | collective-permute-start | bytes 1990664 | tf_op jit(solution)/shard_map/ppermute | solution.py:911
  97.6 41.2 %collective-permute-start.5 = (bf16[192,3072]{1,0:T(8,128)(2,1)}, bf16[192,3072]{1,0:T(8,128)(2,1)S(1)}, u32[]{:S(2)}, u32[]{:S(2)}) collective-permute-start(bf16[192,3072]{1,0:T(8,128)(2,1)} %slice.111.refs_0_), channel_id=1, source_target_pairs={{0,2},{1,3},{2,0},{3,1},{4,6},{5,7},{6,4},{7,5},{8,10},{9,11},{10,... | collective-permute-start | bytes 3538952 | tf_op jit(solution)/shard_map/ppermute | solution.py:911
  97.9 41.8 %collective-permute-start.6 = (bf16[192,3072]{1,0:T(8,128)(2,1)}, bf16[192,3072]{1,0:T(8,128)(2,1)}, u32[]{:S(2)}, u32[]{:S(2)}) collective-permute-start(bf16[192,3072]{1,0:T(8,128)(2,1)} %slice.111.refs_0_), channel_id=1, source_target_pairs={{0,4},{1,5},{2,6},{3,7},{4,0},{5,1},{6,2},{7,3},{8,12},{9,13},{10,... | collective-permute-start | bytes 3538952 | tf_op jit(solution)/shard_map/ppermute | solution.py:911
  140.9 31.2 %collective-permute-start.13 = (bf16[192,3072]{1,0:T(8,128)(2,1)}, bf16[192,3072]{1,0:T(8,128)(2,1)S(1)}, u32[]{:S(2)}, u32[]{:S(2)}) collective-permute-start(bf16[192,3072]{1,0:T(8,128)(2,1)} %slice.111.refs_0_), channel_id=1, source_target_pairs={{0,1},{1,0},{2,3},{3,2},{4,5},{5,4},{6,7},{7,6},{8,9},{9,8},{10,11... | collective-permute-start | bytes 3538952 | tf_op jit(solution)/shard_map/ppermute | solution.py:911
  141.0 29.2 %collective-permute-start.11 = (bf16[96,3072]{1,0:T(8,128)(2,1)S(1)}, bf16[96,3072]{1,0:T(8,128)(2,1)S(1)}, u32[]{:S(2)}, u32[]{:S(2)}) collective-permute-start(bf16[96,3072]{1,0:T(8,128)(2,1)S(1)} %slice.117), channel_id=1, source_target_pairs={{0,4},{1,5},{2,6},{3,7},{4,0},{5,1},{6,2},{7,3},{8,12},{9,13},{10,... | collective-permute-start | bytes 1769480 | tf_op jit(solution)/shard_map/ppermute | solution.py:911
  143.5 28.5 %collective-permute-start.12 = (bf16[96,3072]{1,0:T(8,128)(2,1)S(1)}, bf16[96,3072]{1,0:T(8,128)(2,1)S(1)}, u32[]{:S(2)}, u32[]{:S(2)}) collective-permute-start(bf16[96,3072]{1,0:T(8,128)(2,1)S(1)} %slice.118), channel_id=1, source_target_pairs={{0,2},{1,3},{2,0},{3,1},{4,6},{5,7},{6,4},{7,5},{8,10},{9,11},{10,... | collective-permute-start | bytes 1769480 | tf_op jit(solution)/shard_map/ppermute | solution.py:911
  172.1 8.8 %collective-permute-start.14 = (bf16[192,3072]{1,0:T(8,128)(2,1)S(1)}, bf16[192,3072]{1,0:T(8,128)(2,1)}, u32[]{:S(2)}, u32[]{:S(2)}) collective-permute-start(bf16[192,3072]{1,0:T(8,128)(2,1)S(1)} %collective-permute-done.5.refs_2_), channel_id=1, source_target_pairs={{0,1},{1,0},{2,3},{3,2},{4,5},{5,4},{6,7},{7,6},{8,9},{9,8},{10,11... | collective-permute-start | bytes 3538952 | tf_op jit(solution)/shard_map/ppermute | solution.py:911
  173.3 31.4 %all-to-all-start.1 = ((bf16[8,64,1536]{2,1,0:T(8,128)(2,1)}), bf16[8,64,1536]{2,1,0:T(8,128)(2,1)S(1)}, u32[]{:S(2)}, u32[]{:S(2)}) async-start(bf16[8,64,1536]{2,1,0:T(8,128)(2,1)} %gather_fusion.1), calls=%async_computation.1 | async-start | bytes 3145728 | tf_op jit(solution)/shard_map/all_to_all | solution.py:910
  176.9 156.0 %reduce-scatter.2.cloned.1.call-start = ((), (), s32[]{:S(2)}) async-start(), calls=%async_computation.6 | async-start | bytes 10616832 | tf_op jit(solution)/shard_map/reduce_scatter | solution.py:1065
  211.0 11.0 %collective-permute-start.18 = (bf16[1536,1536]{1,0:T(8,128)(2,1)}, bf16[1536,1536]{1,0:T(8,128)(2,1)}, u32[]{:S(2)}, u32[]{:S(2)}) collective-permute-start(bf16[1536,1536]{1,0:T(8,128)(2,1)} %convolution_convert_fusion), channel_id=1, source_target_pairs={{0,1},{1,0},{2,3},{3,2},{4,5},{5,4},{6,7},{7,6},{8,9},{9,8},{10,11... | collective-permute-start | bytes 14155784 | tf_op jit(solution)/shard_map/ppermute | solution.py:911
  224.3 18.3 %collective-permute-start.19 = (bf16[192,1536]{1,0:T(8,128)(2,1)S(1)}, bf16[192,1536]{1,0:T(8,128)(2,1)S(1)}, u32[]{:S(2)}, u32[]{:S(2)}) collective-permute-start(bf16[192,1536]{1,0:T(8,128)(2,1)S(1)} %get-tuple-element.329), channel_id=1, source_target_pairs={{0,2},{1,3},{2,0},{3,1},{4,6},{5,7},{6,4},{7,5},{8,10},{9,11},{10,... | collective-permute-start | bytes 1769480 | tf_op jit(solution)/shard_map/ppermute | solution.py:911
  225.9 16.7 %collective-permute-start.20 = (bf16[192,1536]{1,0:T(8,128)(2,1)S(1)}, bf16[192,1536]{1,0:T(8,128)(2,1)S(1)}, u32[]{:S(2)}, u32[]{:S(2)}) collective-permute-start(bf16[192,1536]{1,0:T(8,128)(2,1)S(1)} %get-tuple-element.330), channel_id=1, source_target_pairs={{0,4},{1,5},{2,6},{3,7},{4,0},{5,1},{6,2},{7,3},{8,12},{9,13},{10,... | collective-permute-start | bytes 1769480 | tf_op jit(solution)/shard_map/ppermute | solution.py:911
  256.3 29.6 %collective-permute-start.21 = (bf16[384,1536]{1,0:T(8,128)(2,1)}, bf16[384,1536]{1,0:T(8,128)(2,1)S(1)}, u32[]{:S(2)}, u32[]{:S(2)}) collective-permute-start(bf16[384,1536]{1,0:T(8,128)(2,1)} %add_convert_fusion.1), channel_id=1, source_target_pairs={{0,2},{1,3},{2,0},{3,1},{4,6},{5,7},{6,4},{7,5},{8,10},{9,11},{10,... | collective-permute-start | bytes 3538952 | tf_op jit(solution)/shard_map/ppermute | solution.py:911
  256.9 29.0 %collective-permute-start.22 = (bf16[384,1536]{1,0:T(8,128)(2,1)S(1)}, bf16[384,1536]{1,0:T(8,128)(2,1)S(1)}, u32[]{:S(2)}, u32[]{:S(2)}) collective-permute-start(bf16[384,1536]{1,0:T(8,128)(2,1)S(1)} %add_convert_fusion), channel_id=1, source_target_pairs={{0,4},{1,5},{2,6},{3,7},{4,0},{5,1},{6,2},{7,3},{8,12},{9,13},{10,... | collective-permute-start | bytes 3538952 | tf_op jit(solution)/shard_map/ppermute | solution.py:911
  292.9 26.1 %collective-permute-start.24 = (bf16[768,2048]{1,0:T(8,128)(2,1)}, bf16[768,2048]{1,0:T(8,128)(2,1)}, u32[]{:S(2)}, u32[]{:S(2)}) collective-permute-start(bf16[768,2048]{1,0:T(8,128)(2,1)} %convolution_convert_fusion.1), channel_id=1, source_target_pairs={{0,1},{1,0},{2,3},{3,2},{4,5},{5,4},{6,7},{7,6},{8,9},{9,8},{10,11... | collective-permute-start | bytes 9437192 | tf_op jit(solution)/shard_map/ppermute | solution.py:911
  293.0 26.0 %collective-permute-start.23 = (bf16[192,1536]{1,0:T(8,128)(2,1)S(1)}, bf16[192,1536]{1,0:T(8,128)(2,1)S(1)}, u32[]{:S(2)}, u32[]{:S(2)}) collective-permute-start(bf16[192,1536]{1,0:T(8,128)(2,1)S(1)} %select_convert_fusion), channel_id=1, source_target_pairs={{0,8},{8,0},{16,24},{24,16},{1,9},{9,1},{17,25},{25,17},{2,10},{10... | collective-permute-start | bytes 1769480 | tf_op jit(solution)/shard_map/ppermute | solution.py:911
  339.7 40.9 %collective-permute-start.29 = (bf16[768,1408]{1,0:T(8,128)(2,1)}, bf16[768,1408]{1,0:T(8,128)(2,1)S(1)}, u32[]{:S(2)}, u32[]{:S(2)}) collective-permute-start(bf16[768,1408]{1,0:T(8,128)(2,1)} %convolution_convert_fusion.2), channel_id=1, source_target_pairs={{0,1},{1,0},{2,3},{3,2},{4,5},{5,4},{6,7},{7,6},{8,9},{9,8},{10,11... | collective-permute-start | bytes 6488072 | tf_op jit(solution)/shard_map/ppermute | solution.py:911
  339.7 16.9 %collective-permute-start.25 = (bf16[96,1536]{1,0:T(8,128)(2,1)}, bf16[96,1536]{1,0:T(8,128)(2,1)S(1)}, u32[]{:S(2)}, u32[]{:S(2)}) collective-permute-start(bf16[96,1536]{1,0:T(8,128)(2,1)} %select_convert_fusion.3), channel_id=1, source_target_pairs={{0,16},{8,24},{16,0},{24,8},{1,17},{9,25},{17,1},{25,9},{2,18},{10... | collective-permute-start | bytes 884744 | tf_op jit(solution)/shard_map/ppermute | solution.py:911
  342.1 36.9 %collective-permute-start.26 = (bf16[192,2048]{1,0:T(8,128)(2,1)}, bf16[192,2048]{1,0:T(8,128)(2,1)S(1)}, u32[]{:S(2)}, u32[]{:S(2)}) collective-permute-start(bf16[192,2048]{1,0:T(8,128)(2,1)} %get-tuple-element.379), channel_id=1, source_target_pairs={{0,6},{1,7},{2,4},{3,5},{4,2},{5,3},{6,0},{7,1},{8,14},{9,15},{10,... | collective-permute-start | bytes 2359304 | tf_op jit(solution)/shard_map/ppermute | solution.py:911
  343.6 36.1 %collective-permute-start.27 = (bf16[192,2048]{1,0:T(8,128)(2,1)}, bf16[192,2048]{1,0:T(8,128)(2,1)S(1)}, u32[]{:S(2)}, u32[]{:S(2)}) collective-permute-start(bf16[192,2048]{1,0:T(8,128)(2,1)} %get-tuple-element.380), channel_id=1, source_target_pairs={{0,2},{1,3},{2,0},{3,1},{4,6},{5,7},{6,4},{7,5},{8,10},{9,11},{10,... | collective-permute-start | bytes 2359304 | tf_op jit(solution)/shard_map/ppermute | solution.py:911
  345.0 34.8 %collective-permute-start.28 = (bf16[192,2048]{1,0:T(8,128)(2,1)}, bf16[192,2048]{1,0:T(8,128)(2,1)S(1)}, u32[]{:S(2)}, u32[]{:S(2)}) collective-permute-start(bf16[192,2048]{1,0:T(8,128)(2,1)} %get-tuple-element.381), channel_id=1, source_target_pairs={{0,4},{1,5},{2,6},{3,7},{4,0},{5,1},{6,2},{7,3},{8,12},{9,13},{10,... | collective-permute-start | bytes 2359304 | tf_op jit(solution)/shard_map/ppermute | solution.py:911
  356.6 22.5 %collective-permute-start.30 = (bf16[96,3072]{1,0:T(8,128)(2,1)}, bf16[96,3072]{1,0:T(8,128)(2,1)S(1)}, u32[]{:S(2)}, u32[]{:S(2)}) collective-permute-start(bf16[96,3072]{1,0:T(8,128)(2,1)} %broadcast_select_fusion), channel_id=1, source_target_pairs={{0,8},{8,0},{16,24},{24,16},{1,9},{9,1},{17,25},{25,17},{2,10},{10... | collective-permute-start | bytes 1769480 | tf_op jit(solution)/shard_map/ppermute | solution.py:911
  389.0 16.1 %collective-permute-start.31 = (bf16[96,1536]{1,0:T(8,128)(2,1)S(1)}, bf16[96,1536]{1,0:T(8,128)(2,1)S(1)}, u32[]{:S(2)}, u32[]{:S(2)}) collective-permute-start(bf16[96,1536]{1,0:T(8,128)(2,1)S(1)} %add_convert_fusion.4), channel_id=1, source_target_pairs={{0,16},{8,24},{16,0},{24,8},{1,17},{9,25},{17,1},{25,9},{2,18},{10... | collective-permute-start | bytes 884744 | tf_op jit(solution)/shard_map/ppermute | solution.py:911
  391.7 28.6 %collective-permute-start.32 = (bf16[96,2048]{1,0:T(8,128)(2,1)S(1)}, bf16[96,2048]{1,0:T(8,128)(2,1)S(1)}, u32[]{:S(2)}, u32[]{:S(2)}) collective-permute-start(bf16[96,2048]{1,0:T(8,128)(2,1)S(1)} %select_convert_fusion.1), channel_id=1, source_target_pairs={{0,8},{8,0},{16,24},{24,16},{1,9},{9,1},{17,25},{25,17},{2,10},{10... | collective-permute-start | bytes 1179656 | tf_op jit(solution)/shard_map/ppermute | solution.py:911
  391.7 28.6 %collective-permute-start.33 = (bf16[192,1408]{1,0:T(8,128)(2,1)}, bf16[192,1408]{1,0:T(8,128)(2,1)S(1)}, u32[]{:S(2)}, u32[]{:S(2)}) collective-permute-start(bf16[192,1408]{1,0:T(8,128)(2,1)} %get-tuple-element.400), channel_id=1, source_target_pairs={{0,6},{1,7},{2,4},{3,5},{4,2},{5,3},{6,0},{7,1},{8,14},{9,15},{10,... | collective-permute-start | bytes 1622024 | tf_op jit(solution)/shard_map/ppermute | solution.py:911
  393.2 27.1 %collective-permute-start.34 = (bf16[192,1408]{1,0:T(8,128)(2,1)S(1)}, bf16[192,1408]{1,0:T(8,128)(2,1)S(1)}, u32[]{:S(2)}, u32[]{:S(2)}) collective-permute-start(bf16[192,1408]{1,0:T(8,128)(2,1)S(1)} %copy-done.46), channel_id=1, source_target_pairs={{0,2},{1,3},{2,0},{3,1},{4,6},{5,7},{6,4},{7,5},{8,10},{9,11},{10,... | collective-permute-start | bytes 1622024 | tf_op jit(solution)/shard_map/ppermute | solution.py:911
  394.5 25.7 %collective-permute-start.35 = (bf16[192,1408]{1,0:T(8,128)(2,1)S(1)}, bf16[192,1408]{1,0:T(8,128)(2,1)S(1)}, u32[]{:S(2)}, u32[]{:S(2)}) collective-permute-start(bf16[192,1408]{1,0:T(8,128)(2,1)S(1)} %copy-done.45), channel_id=1, source_target_pairs={{0,4},{1,5},{2,6},{3,7},{4,0},{5,1},{6,2},{7,3},{8,12},{9,13},{10,... | collective-permute-start | bytes 1622024 | tf_op jit(solution)/shard_map/ppermute | solution.py:911
  405.0 15.2 %collective-permute-start.36 = (bf16[48,3072]{1,0:T(8,128)(2,1)S(1)}, bf16[48,3072]{1,0:T(8,128)(2,1)S(1)}, u32[]{:S(2)}, u32[]{:S(2)}) collective-permute-start(bf16[48,3072]{1,0:T(8,128)(2,1)S(1)} %select_convert_fusion.2), channel_id=1, source_target_pairs={{0,16},{8,24},{16,0},{24,8},{1,17},{9,25},{17,1},{25,9},{2,18},{10... | collective-permute-start | bytes 884744 | tf_op jit(solution)/shard_map/ppermute | solution.py:911
  425.6 37.2 %all-to-all-start.2 = ((bf16[8,64,1536]{2,1,0:T(8,128)(2,1)}), bf16[8,64,1536]{2,1,0:T(8,128)(2,1)S(1)}, u32[]{:S(2)}, u32[]{:S(2)}) async-start(bf16[8,64,1536]{2,1,0:T(8,128)(2,1)} %bitcast.43), calls=%async_computation.3 | async-start | bytes 3145728 | tf_op jit(solution)/shard_map/all_to_all | solution.py:910
  429.2 33.6 %collective-permute-start.37 = (bf16[192,1536]{1,0:T(8,128)(2,1)}, bf16[192,1536]{1,0:T(8,128)(2,1)}, u32[]{:S(2)}, u32[]{:S(2)}) collective-permute-start(bf16[192,1536]{1,0:T(8,128)(2,1)} %maximum_select_fusion.3), channel_id=1, source_target_pairs={{0,8},{8,0},{16,24},{24,16},{1,9},{9,1},{17,25},{25,17},{2,10},{10... | collective-permute-start | bytes 1769480 | tf_op jit(solution)/shard_map/ppermute | solution.py:911
  429.2 32.1 %collective-permute-start.40 = (bf16[48,3072]{1,0:T(8,128)(2,1)}, bf16[48,3072]{1,0:T(8,128)(2,1)S(1)}, u32[]{:S(2)}, u32[]{:S(2)}) collective-permute-start(bf16[48,3072]{1,0:T(8,128)(2,1)} %add_convert_fusion.3), channel_id=1, source_target_pairs={{0,16},{8,24},{16,0},{24,8},{1,17},{9,25},{17,1},{25,9},{2,18},{10... | collective-permute-start | bytes 884744 | tf_op jit(solution)/shard_map/ppermute | solution.py:911
  432.0 29.4 %collective-permute-start.39 = (bf16[96,1408]{1,0:T(8,128)(2,1)}, bf16[96,1408]{1,0:T(8,128)(2,1)S(1)}, u32[]{:S(2)}, u32[]{:S(2)}) collective-permute-start(bf16[96,1408]{1,0:T(8,128)(2,1)} %select_convert_fusion.4), channel_id=1, source_target_pairs={{0,8},{8,0},{16,24},{24,16},{1,9},{9,1},{17,25},{25,17},{2,10},{10... | collective-permute-start | bytes 811016 | tf_op jit(solution)/shard_map/ppermute | solution.py:911
  432.0 27.2 %collective-permute-start.38 = (bf16[48,2048]{1,0:T(8,128)(2,1)}, bf16[48,2048]{1,0:T(8,128)(2,1)S(1)}, u32[]{:S(2)}, u32[]{:S(2)}) collective-permute-start(bf16[48,2048]{1,0:T(8,128)(2,1)} %select_convert_fusion.5), channel_id=1, source_target_pairs={{0,16},{8,24},{16,0},{24,8},{1,17},{9,25},{17,1},{25,9},{2,18},{10... | collective-permute-start | bytes 589832 | tf_op jit(solution)/shard_map/ppermute | solution.py:911
  465.8 30.1 %all-to-all-start.3 = ((bf16[8,64,1536]{2,1,0:T(8,128)(2,1)}), bf16[8,64,1536]{2,1,0:T(8,128)(2,1)}, u32[]{:S(2)}, u32[]{:S(2)}) async-start(bf16[8,64,1536]{2,1,0:T(8,128)(2,1)} %bitcast.42), calls=%async_computation.4 | async-start | bytes 3145728 | tf_op jit(solution)/shard_map/all_to_all | solution.py:910
  470.3 25.0 %collective-permute-start.44 = (bf16[96,3072]{1,0:T(8,128)(2,1)S(1)}, bf16[96,3072]{1,0:T(8,128)(2,1)}, u32[]{:S(2)}, u32[]{:S(2)}) collective-permute-start(bf16[96,3072]{1,0:T(8,128)(2,1)S(1)} %maximum_select_fusion.4), channel_id=1, source_target_pairs={{0,8},{8,0},{16,24},{24,16},{1,9},{9,1},{17,25},{25,17},{2,10},{10... | collective-permute-start | bytes 1769480 | tf_op jit(solution)/shard_map/ppermute | solution.py:911
  471.4 23.8 %collective-permute-start.42 = (bf16[48,2048]{1,0:T(8,128)(2,1)S(1)}, bf16[48,2048]{1,0:T(8,128)(2,1)S(1)}, u32[]{:S(2)}, u32[]{:S(2)}) collective-permute-start(bf16[48,2048]{1,0:T(8,128)(2,1)S(1)} %copy-done.20), channel_id=1, source_target_pairs={{0,16},{8,24},{16,0},{24,8},{1,17},{9,25},{17,1},{25,9},{2,18},{10... | collective-permute-start | bytes 589832 | tf_op jit(solution)/shard_map/ppermute | solution.py:911
  473.1 22.1 %collective-permute-start.43 = (bf16[48,1408]{1,0:T(8,128)(2,1)S(1)}, bf16[48,1408]{1,0:T(8,128)(2,1)S(1)}, u32[]{:S(2)}, u32[]{:S(2)}) collective-permute-start(bf16[48,1408]{1,0:T(8,128)(2,1)S(1)} %select_convert_fusion.6), channel_id=1, source_target_pairs={{0,16},{8,24},{16,0},{24,8},{1,17},{9,25},{17,1},{25,9},{2,18},{10... | collective-permute-start | bytes 405512 | tf_op jit(solution)/shard_map/ppermute | solution.py:911
  474.4 17.2 %collective-permute-start.45 = (f32[1,2688]{1,0:T(1,128)S(1)}, f32[1,2688]{1,0:T(1,128)S(1)}, u32[]{:S(2)}, u32[]{:S(2)}) collective-permute-start(f32[1,2688]{1,0:T(1,128)S(1)} %get-tuple-element.436), channel_id=1, source_target_pairs={{0,6},{1,7},{2,4},{3,5},{4,2},{5,3},{6,0},{7,1},{8,14},{9,15},{10,... | collective-permute-start | bytes 32264 | tf_op jit(solution)/shard_map/ppermute | solution.py:911
  477.1 15.0 %collective-permute-start.46 = (f32[1,2688]{1,0:T(1,128)S(1)}, f32[1,2688]{1,0:T(1,128)S(1)}, u32[]{:S(2)}, u32[]{:S(2)}) collective-permute-start(f32[1,2688]{1,0:T(1,128)S(1)} %get-tuple-element.437), channel_id=1, source_target_pairs={{0,2},{1,3},{2,0},{3,1},{4,6},{5,7},{6,4},{7,5},{8,10},{9,11},{10,... | collective-permute-start | bytes 32264 | tf_op jit(solution)/shard_map/ppermute | solution.py:911
  498.1 16.9 %collective-permute-start.48 = (bf16[96,2048]{1,0:T(8,128)(2,1)S(1)}, bf16[96,2048]{1,0:T(8,128)(2,1)S(1)}, u32[]{:S(2)}, u32[]{:S(2)}) collective-permute-start(bf16[96,2048]{1,0:T(8,128)(2,1)S(1)} %maximum_select_fusion.5), channel_id=1, source_target_pairs={{0,8},{8,0},{16,24},{24,16},{1,9},{9,1},{17,25},{25,17},{2,10},{10... | collective-permute-start | bytes 1179656 | tf_op jit(solution)/shard_map/ppermute | solution.py:911
  504.4 10.6 %collective-permute-start.49 = (bf16[48,1408]{1,0:T(8,128)(2,1)S(1)}, bf16[48,1408]{1,0:T(8,128)(2,1)S(1)}, u32[]{:S(2)}, u32[]{:S(2)}) collective-permute-start(bf16[48,1408]{1,0:T(8,128)(2,1)S(1)} %add_convert_fusion.6), channel_id=1, source_target_pairs={{0,16},{8,24},{16,0},{24,8},{1,17},{9,25},{17,1},{25,9},{2,18},{10... | collective-permute-start | bytes 405512 | tf_op jit(solution)/shard_map/ppermute | solution.py:911
  506.1 8.9 %collective-permute-start.50 = (f32[1,2688]{1,0:T(1,128)S(1)}, f32[1,2688]{1,0:T(1,128)S(1)}, u32[]{:S(2)}, u32[]{:S(2)}) collective-permute-start(f32[1,2688]{1,0:T(1,128)S(1)} %fusion.21), channel_id=1, source_target_pairs={{0,8},{8,16},{16,24},{24,0},{1,9},{9,17},{17,25},{25,1},{2,10},{10... | collective-permute-start | bytes 32264 | tf_op jit(solution)/shard_map/ppermute | solution.py:911
  (61 other events, 381.8 us)
Sparse Core Ops, SparseCore 0:
  94.7 85.0 all-gather.1
  256.4 76.3 reduce-scatter.1

commit v5 on v4

--- a/solution.py
+++ b/solution.py
@@ -498,6 +498,7 @@
 
 
 ORDER = (7, 3, 5, 1, 6, 2, 4, 0)
+DOUBLED = (0, 2, 4, 6, 1, 3, 5, 7)
 WIDE = 512
 
 
@@ -525,11 +526,9 @@
     )(me, left, *[v for v, _, _ in pieces])
 
 
-def unpack_kernel(places, widths, me_ref, *refs):
-    pieces, (gain_ref, conv_ref, heads_ref, gains_ref, found) = refs[:-5], refs[-5:]
-    span = found.shape[2]
-    for j, ref in zip(places, pieces):
-        found[me_ref[0] ^ j] = ref[:, :span].astype(jnp.float32)
+def unpack_kernel(widths, me_ref, small_ref, gain_ref, conv_ref, heads_ref, gains_ref, found):
+    for k, j in enumerate(DOUBLED):
+        found[me_ref[0] ^ j] = small_ref[k * SMALL : (k + 1) * SMALL, :].astype(jnp.float32)
     for ref in (gain_ref, conv_ref, heads_ref, gains_ref):
         ref[...] = jnp.zeros_like(ref)
     wide, taps, few, long = widths
@@ -540,22 +539,6 @@
         gains_ref[1:2, i * long : (i + 1) * long] = found[i, 9:10, :long]
     spread = (row_ids(0, 128, DI) == lax.broadcasted_iota(jnp.int32, (128, DI), 1) // HEAD_DIM).astype(jnp.float32)
     gains_ref[0:1, :] = dot32(heads_ref[...], spread, precision=lax.Precision.HIGHEST)[2:3, :]
-
-
-def run_unpack(me, pieces, rows, widths):
-    f32 = jnp.float32
-    wide, taps, few, long = widths
-    shapes = [(1, 8 * wide), (8, 8 * taps), (8, 128), (8, 8 * long)]
-    return pl.pallas_call(
-        functools.partial(unpack_kernel, tuple(j for _, j, _ in pieces), widths),
-        grid=(1,),
-        in_specs=[smem()] + [pl.BlockSpec((SMALL, 512), lambda g, at=(rows - start) // SMALL: (at, 0)) for _, _, start in pieces],
-        out_specs=[whole(s) for s in shapes],
-        out_shape=[shaped(s, f32) for s in shapes],
-        scratch_shapes=[pltpu.VMEM((8, SMALL, 512), f32)],
-        compiler_params=params(),
-        cost_estimate=cost(1000000, 1000000),
-    )(me, *[v for v, _, _ in pieces])
 
 
 def out_kernel(gated_ref, weight_ref, x_ref, cot_ref, r_ref, result_ref, rk_ref, acc):
@@ -683,23 +666,31 @@
     )(*args)
 
 
-def terms_kernel(left_ref, right_ref, got_ref, *outs):
+TN = (((0,), (0,)), ((), ()))
+
+
+def terms_kernel(turned, left_ref, right_ref, got_ref, *outs):
     rows = outs[0].shape[0]
-    product = dot32(left_ref[...], right_ref[...]) + got_ref[...].astype(jnp.float32)
+    if turned:
+        product = dot32(left_ref[...], right_ref[...], TN)
+    else:
+        product = dot32(left_ref[...], right_ref[...])
+    product = product + got_ref[...].astype(jnp.float32)
     for i, ref in enumerate(outs):
         ref[...] = product[i * rows : (i + 1) * rows, :].astype(ref.dtype)
 
 
-def run_terms(left, right, got):
-    rows, inner = left.shape
-    cols = right.shape[1]
+def run_terms(left, right, got, turned=False):
+    rows, cols = got.shape
+    inner = right.shape[0]
     step = 512 if cols % 512 == 0 else cols
     here = lambda g: (0, g)
     kinds = [jnp.bfloat16] * 3 + [jnp.float32]
-    return pl.pallas_call(
-        terms_kernel,
+    half = pl.BlockSpec((inner, rows), lambda g: (0, 1)) if turned else pl.BlockSpec((rows, inner), lambda g: (1, 0))
+    return pl.pallas_call(
+        functools.partial(terms_kernel, turned),
         grid=(cols // step,),
-        in_specs=[whole(left.shape), pl.BlockSpec((inner, step), here), pl.BlockSpec((rows, step), here)],
+        in_specs=[half, pl.BlockSpec((inner, step), here), pl.BlockSpec((rows, step), here)],
         out_specs=[pl.BlockSpec((rows // 4, step), here)] * 4,
         out_shape=[shaped((rows // 4, cols), kind) for kind in kinds],
         compiler_params=params(),
@@ -736,37 +727,33 @@
     )(me, x, gain)
 
 
-def open_kernel(places, behind, widths, me_ref, first_ref, x_ref, *refs):
-    count = len(places)
-    tails, pieces, refs = refs[: len(behind)], refs[len(behind) : len(behind) + count], refs[len(behind) + count :]
+def open_kernel(places, widths, me_ref, first_ref, x_ref, small_ref, *refs):
+    pieces, refs = refs[: len(places)], refs[len(places) :]
     gain_ref, conv_ref, heads_ref, gains_ref, out_ref, sent_ref, bcd_ref, full_ref, *prep_refs, found, turned = refs
-    unpack_kernel(behind, widths, me_ref, *tails, gain_ref, conv_ref, heads_ref, gains_ref, found)
+    unpack_kernel(widths, me_ref, small_ref, gain_ref, conv_ref, heads_ref, gains_ref, found)
     norm_kernel(ORDER, me_ref, x_ref, gain_ref, out_ref, sent_ref, turned)
     project_kernel(places, me_ref, out_ref, *pieces, bcd_ref, full_ref)
     prep_kernel(first_ref, bcd_ref, conv_ref.at[:, pl.ds(DI, 2 * NSTATE)], heads_ref, *prep_refs)
 
 
-def run_open(me, first, x, pieces, rows, widths, skip):
+def run_open(me, first, x, small, pieces, widths, skip):
     f32, b16 = jnp.float32, jnp.bfloat16
     toks, width = x.shape
     wide, taps, few, long = widths
-    behind = [[p for p in pieces if p[1] == j][-1] for j in range(8)]
     places = tuple((j, start, min(v.shape[0], width // 8 - start)) for v, j, start in pieces)
     shapes = [((1, 8 * wide), f32), ((8, 8 * taps), f32), ((8, 128), f32), ((8, 8 * long), f32)]
     shapes += [((toks, width), b16), ((width, toks), b16), ((toks, BCD), f32), ((width, BCD), b16)]
     shapes += [((toks, 4 * Q), f32), ((256, toks), f32), ((toks, 2 * NSTATE), b16), ((2 * NSTATE, toks), b16)]
     return pl.pallas_call(
-        functools.partial(open_kernel, places, tuple(j for _, j, _ in behind), widths),
+        functools.partial(open_kernel, places, widths),
         grid=(1,),
-        in_specs=[smem(), smem(), whole(x.shape)]
-        + [pl.BlockSpec((SMALL, 512), lambda g, at=(rows - start) // SMALL: (at, 0)) for _, _, start in behind]
-        + [pl.BlockSpec((v.shape[0], BCD), lambda g: (0, skip // BCD)) for v, _, _ in pieces],
+        in_specs=[smem(), smem(), whole(x.shape), whole(small.shape)] + [pl.BlockSpec((v.shape[0], BCD), lambda g: (0, skip // BCD)) for v, _, _ in pieces],
         out_specs=[whole(s) for s, _ in shapes],
         out_shape=[shaped(s, d) for s, d in shapes],
-        scratch_shapes=[pltpu.VMEM((8, SMALL, 512), f32), pltpu.VMEM((width, toks), b16)],
+        scratch_shapes=[pltpu.VMEM((8, SMALL, small.shape[1]), f32), pltpu.VMEM((width, toks), b16)],
         compiler_params=params(),
         cost_estimate=cost(6000000000, 10000000),
-    )(me, first, x, *[v for v, _, _ in behind], *[v for v, _, _ in pieces])
+    )(me, first, x, small, *[v for v, _, _ in pieces])
 
 
 def norm_back_kernel(d_ref, x_ref, cot_ref, gain_ref, out_ref, grad_ref):
@@ -817,11 +804,16 @@
     return lax.axis_size("fsdp") == 8 and lax.axis_size("rep") == 4
 
 
-def gathered_rows(w):
+def gathered_rows(w, late=False):
     half = w.shape[0] // 32 * 16
     two, four = yield [(w, "fsdp", partners(j)) for j in (2, 4)], 1
-    top, bottom, one = yield [(two[:half], "fsdp", partners(4)), (four[half:], "fsdp", partners(2)), (w, "fsdp", partners(1))], 1
-    three, five, other_top, other_bottom = yield [(v, "fsdp", partners(1)) for v in (two, four, top, bottom)], 1
+    sent = [(two[:half], "fsdp", partners(4)), (four[half:], "fsdp", partners(2))]
+    if late:
+        top, bottom, one, three = yield sent + [(v, "fsdp", partners(1)) for v in (w, two)], 1
+        five, other_top, other_bottom = yield [(v, "fsdp", partners(1)) for v in (four, top, bottom)], 1
+    else:
+        top, bottom, one, three, five = yield sent + [(v, "fsdp", partners(1)) for v in (w, two, four)], 1
+        other_top, other_bottom = yield [(v, "fsdp", partners(1)) for v in (top, bottom)], 1
     near = [(w, 0, 0), (one, 1, 0), (two, 2, 0), (three, 3, 0), (four, 4, 0), (five, 5, 0)]
     return near + [(top, 6, 0), (bottom, 6, half), (other_top, 7, 0), (other_bottom, 7, half)]
 
@@ -839,7 +831,7 @@
     half = left.shape[0] // 2
     odd = jnp.dot(left[:half], right, preferred_element_type=jnp.float32).astype(jnp.bfloat16)
     (got,) = yield [(odd, "fsdp", partners(1))], 1
-    *terms, own = run_terms(left[half:], right, got)
+    *terms, own = run_terms(left, right, got)
     others = yield [(v, "fsdp", partners(j)) for v, j in zip(terms, ORDER[4:7])], 1
     return own + widen(others[0]) + widen(others[1]) + widen(others[2])
 
@@ -930,7 +922,18 @@
         fresh = [e for e in self.active if e["got"] is None]
         arrays, values = tie([[item[0] for item in e["want"]] for e in fresh], values)
         for e, some in zip(fresh, arrays):
-            e["got"] = [transfer(v, *item[1:]) for v, item in zip(some, e["want"])]
+            e["got"] = [None] * len(some)
+        alike = {}
+        for e, some in zip(fresh, arrays):
+            for i, (v, item) in enumerate(zip(some, e["want"])):
+                kind = (item[1], str(item[2]), v.shape[0], v.dtype.name) if item[1] == "rep" else (id(e), i)
+                alike.setdefault(kind, []).append((e, i, v, item))
+        for group in alike.values():
+            moved = transfer(jnp.concatenate([g[2] for g in group], axis=1) if len(group) > 1 else group[0][2], *group[0][3][1:])
+            start = 0
+            for e, i, v, _ in group:
+                e["got"][i] = moved[:, start : start + v.shape[1]] if len(group) > 1 else moved
+                start += v.shape[1]
         results = work(*values) if work else ()
         for e in self.active:
             e["turns"] -= 1
@@ -978,20 +981,27 @@
         blocks = lax.all_to_all(values.reshape(groups, block_rows, width), "fsdp", split_axis=0, concat_axis=0, tiled=True)
         return blocks[targets].reshape(tok_rows, width)
 
-    own_small = [norm_gain[None], conv_weight, conv_bias[None], dt_bias[None], a_log[None], d_skip[None], gated_gain[None]]
-    longest = max(v.shape[1] for v in own_small)
-    small = jnp.concatenate([pad_lanes(v, longest) for v in own_small])
-    small = jnp.pad(small, ((0, SMALL - small.shape[0]), (0, 0)))
+    own_small = [norm_gain, conv_weight, conv_bias, dt_bias, a_log, d_skip, gated_gain]
+
+    def rows_of(values):
+        values = [v if v.ndim == 2 else v[None] for v in values]
+        longest = max(v.shape[1] for v in values)
+        packed = jnp.concatenate([pad_lanes(v, longest) for v in values])
+        return jnp.pad(packed, ((0, SMALL - packed.shape[0]), (0, 0)))
+
+    def doubled(v, bit):
+        return (jnp.concatenate([v, lax.ppermute(v, "fsdp", partners(bit))]),)
+
     if custom():
         rows, span = in_weight.shape[0], DI + BCD
-        w_xb = lax.pad(in_weight, jnp.zeros((), b16), ((0, SMALL, 0), (-DI, span + DI - in_weight.shape[1], 0)))
-        e_xb = moves.add(gathered_rows(w_xb + jnp.pad(small, ((rows, 0), (0, span - small.shape[1])))))
-        moves.turn()
-        e_x = moves.add(dealt(blocks(tokens), 1))
-        (cot_blocks,) = moves.turn(lambda v: (blocks(v),), cotangent)
+        w_xb = lax.pad(in_weight, jnp.zeros((), b16), ((0, 0, 0), (-DI, span + DI - in_weight.shape[1], 0)))
+        e_xb = moves.add(gathered_rows(w_xb, True))
+        e_x = moves.add(dealt(blocks(tokens), 2))
+        (small,) = moves.turn(lambda *v: doubled(rows_of(v), 2), *own_small)
+        small, cot_blocks = moves.turn(lambda v, c: (*doubled(v, 4), blocks(c)), small, cotangent)
         out_weight = moves.after(out_weight)
         w_out = lax.all_gather(out_weight, "fsdp", axis=0, tiled=True)
-        moves.turn()
+        (small,) = moves.turn(lambda v: doubled(v, 1), small)
         pieces = e_xb["value"]
         x = e_x["value"].reshape(tok_rows, width)
         widths = (norm_gain.size, conv_bias.size, dt_bias.size, gated_gain.size)
@@ -999,10 +1009,10 @@
         x = deal(tokens)
         w_z = lax.all_gather(in_weight[:, :DI], "fsdp", axis=0, tiled=True)
         w_out = lax.all_gather(out_weight, "fsdp", axis=0, tiled=True)
-        small_all = lax.all_gather(small, "fsdp", axis=0, tiled=False).astype(f32)
+        small_all = lax.all_gather(rows_of(own_small), "fsdp", axis=0, tiled=False).astype(f32)
         w_xb = lax.all_gather(pad_lanes(in_weight[:, DI:], DI + BCD), "fsdp", axis=0, tiled=True)
         parts, row = [], 0
-        for v in own_small:
+        for v in (u if u.ndim == 2 else u[None] for u in own_small):
             parts.append(small_all[:, row : row + v.shape[0], : v.shape[1]].transpose(1, 0, 2).reshape(v.shape[0], -1))
             row += v.shape[0]
         gain, taps, bias, step_bias, rate, skip, ggain = parts
@@ -1012,7 +1022,7 @@
     if custom():
 
         def open_up(x):
-            gain, conv, heads, gains, normed, sent, bcd, w_b, *prep = run_open(me, first, x, pieces, rows, widths, DI)
+            gain, conv, heads, gains, normed, sent, bcd, w_b, *prep = run_open(me, first, x, small, pieces, widths, DI)
             return gain, conv, heads, gains, normed, sent, bcd, w_b, prep, *run_project(me, normed, pieces, 0, DI)
 
         e_z = moves.add(gathered_rows(in_weight[:, :DI]))

time: 540 us -> 520 us (0.963)
  waiting for transfers between devices: 163 us -> 147 us
    ppermute x54 -> x52, waiting for transfers between devices: 159 us -> 98.3 us  [transfer(): return lax.ppermute(v, axis, pairs)]
    ppermute x0 -> x3, waiting for transfers between devices: none -> 42.7 us  [doubled(): return (jnp.concatenate([v, lax.ppermute(v, 'fsdp', partners(bit))]),)]
    ppermute x54 -> x52, starting transfers between devices: 54.2 us -> 54.7 us  [transfer(): return lax.ppermute(v, axis, pairs)]
  transfers between devices with their start and end apart: 60 -> 61, of which waited for: 21 -> 23; matrix products, arithmetic and copies ran while one was open for 9% -> 10% of each run, Pallas kernels for 33% -> 34%
where the time goes in v5:
time: 520 us; the launch traced here: 511 us
  Pallas kernels  179 us (34%)
  waiting for transfers between devices  147 us (28%)
  starting transfers between devices  71 us (14%)
  local copies, waits for them, and re-layouts  38.1 us (7%)
  matrix products  33.6 us (6%)
  other arithmetic  27.1 us (5%)
  between operations  15.4 us (3%)
    ppermute x52, waiting for transfers between devices, transfer(): return lax.ppermute(v, axis, pairs)  98.3 us
    ppermute x52, starting transfers between devices, transfer(): return lax.ppermute(v, axis, pairs)  54.7 us
    ppermute x3, waiting for transfers between devices, doubled(): return (jnp.concatenate([v, lax.ppermute(v, 'fsdp', partners(bit))]),)  42.7 us
    pallas_call x2, Pallas kernels, run_backward(): pl.pallas_call(functools.partial(backward_kernel, base), grid=(count,), i...  41.5 us
    pallas_call x2, Pallas kernels, run_project(): pl.pallas_call(functools.partial(project_kernel, places), grid=(cols // s...  27 us
    dot_general x6, matrix products, contract_rows(): lax.dot_general(left, right, (((0,), (0,)), ((), ())), preferred_element_...  24.4 us
    pallas_call x1, Pallas kernels, run_back(): pl.pallas_call(functools.partial(back_kernel, tuple(spans), int(base is n...  21.9 us
    pallas_call x1, Pallas kernels, run_forward(): pl.pallas_call(forward_kernel, grid=(width // LANES,), in_specs=[smem(),...  20.2 us
  transfers between devices with their start and end apart: 61, of which 23 were waited for; matrix products, arithmetic and copies ran while one was open for 10% of the time, Pallas kernels for 34%

profile of v5, /device:TPU:0, one launch (start us, length us, event | category | flops | bytes accessed | tf_op | source)
XLA Modules:
  0.0 511.4 jit_solution(16917103161424320801)
XLA Ops:
  7.2 2.6 pad_slice_fusion.refs_0_
  12.7 2.9 collective-permute-start
  18.0 3.6 all-to-all-start
  21.6 24.5 %collective-permute-done.2 = bf16[16,416]{1,0:T(8,128)(2,1)S(1)} collective-permute-done((bf16[16,416]{1,0:T(8,128)(2,1)S(1)}, bf16[16,416]{1,0:T(8,128)(2,1)S(1)}, u32[]{:S(2)}, u32[]{:S(2)}) %collective-permute-start.2) | collective-permute-done | bytes 13344 | tf_op jit(solution)/shard_map/ppermute | solution.py:993
  52.9 4.7 collective-permute-start.4
  57.6 3.2 gather_fusion.1
  60.8 17.3 %collective-permute-done.7 = bf16[32,416]{1,0:T(8,128)(2,1)S(1)} collective-permute-done((bf16[32,416]{1,0:T(8,128)(2,1)S(1)}, bf16[32,416]{1,0:T(8,128)(2,1)S(1)}, u32[]{:S(2)}, u32[]{:S(2)}) %collective-permute-start.7) | collective-permute-done | bytes 26656 | tf_op jit(solution)/shard_map/ppermute | solution.py:993
  78.4 2.8 slice.119.refs_0_
  88.2 8.0 %shard_map.221 = (f32[1,1536]{1,0:T(1,128)}, f32[8,3328]{1,0:T(8,128)}, f32[8,128]{1,0:T(8,128)}, f32[8,3072]{1,0:T(8,128)}, bf16[512,1536]{1,0:T(8,128)(2,1)}, ...) custom-call(s32[1]{0:T(128)} %bitcast.7.me_ref, ...), custom_call_target="tpu_custom_call" | custom-call | flops 2000000000 | bytes 3333333 | tf_op jit(solution)/shard_map/pallas_call | solution.py:747
  96.2 13.2 %shard_map.222 = (f32[512,3072]{1,0:T(8,128)}, bf16[1536,3072]{1,0:T(8,128)(2,1)}) custom-call(s32[1]{0:T(128)} %bitcast.7.me_ref, bf16[512,1536]{1,0:T(8,128)(2,1)} %get-tuple-element.326.left_ref, bf16[192,3456]{1,0:T(8,128)(2,1)} %pad_slice_fusion.refs_0_, bf16[192,3456]{1,0:T(8,128)(2,1)} %collective-permute-done.5.refs_1_, bf16[192,3456]{1,0:T(8,128)(2,1)} %copy-done.6, ...), custom_call_target="tpu_custom_call" | custom-call | flops 1610612736 | bytes 9437184 | tf_op jit(solution)/shard_map/pallas_call | solution.py:518
  109.4 12.7 %collective-permute-done.8.refs_2_ = bf16[192,3072]{1,0:T(8,128)(2,1)} collective-permute-done((bf16[192,3072]{1,0:T(8,128)(2,1)}, bf16[192,3072]{1,0:T(8,128)(2,1)}, u32[]{:S(2)}, u32[]{:S(2)}) %collective-permute-start.8) | collective-permute-done | bytes 1179680 | tf_op jit(solution)/shard_map/ppermute | solution.py:903
  125.0 2.5 collective-permute-start.14
  129.0 20.2 %shard_map.223 = (f32[512,3072]{1,0:T(8,128)}, bf16[512,3072]{1,0:T(8,128)(2,1)}) custom-call(s32[1]{0:T(128)} %bitcast.48, f32[512,3072]{1,0:T(8,128)} %get-tuple-element.315.x_ref, f32[8,3072]{1,0:T(8,128)} %slice.126.conv_ref, f32[8,3072]{1,0:T(8,128)} %get-tuple-element.317.gain_ref, f32[512,512]{1,0:T(8,128)} %get-tuple-element.318.wide_ref, ...), custom_call_target="tpu_custom_call" | custom-call | flops 6666666496 | bytes 6666666 | tf_op jit(solution)/shard_map/pallas_call | solution.py:410
  149.2 5.0 collective-permute-done.14.refs_6_
  157.9 3.6 all-to-all-start.1
  165.9 13.7 %shard_map.224 = (f32[512,3072]{1,0:T(8,128)}, bf16[1536,3072]{1,0:T(8,128)(2,1)}) custom-call(s32[1]{0:T(128)} %bitcast.7.me_ref, bf16[512,1536]{1,0:T(8,128)(2,1)} %get-tuple-element.326.left_ref, bf16[192,3072]{1,0:T(8,128)(2,1)} %slice.119.refs_0_, bf16[192,3072]{1,0:T(8,128)(2,1)} %copy-done.22, bf16[192,3072]{1,0:T(8,128)(2,1)} %collective-permute-done.8.refs_2_, ...), custom_call_target="tpu_custom_call" | custom-call | flops 1610612736 | bytes 9437184 | tf_op jit(solution)/shard_map/pallas_call | solution.py:518
  179.7 9.3 %shard_map.225 = (bf16[512,3072]{1,0:T(8,128)(2,1)}, bf16[512,3072]{1,0:T(8,128)(2,1)}, f32[512,128]{1,0:T(8,128)}) custom-call(s32[1]{0:T(128)} %bitcast.7.me_ref, f32[512,3072]{1,0:T(8,128)} %get-tuple-element.355.z_ref, f32[512,3072]{1,0:T(8,128)} %get-tuple-element.338.ssm_ref, f32[8,3072]{1,0:T(8,128)} %get-tuple-element.317.gain_ref), custom_call_target="tpu_custom_call" | custom-call | flops 1333333376 | bytes 5333333 | tf_op jit(solution)/shard_map/pallas_call | solution.py:427
  189.0 6.3 %convolution_convert_fusion = bf16[1536,1536]{1,0:T(8,128)(2,1)} fusion(bf16[512,1536]{1,0:T(8,128)(2,1)S(1)} %bitcast.31, bf16[512,3072]{1,0:T(8,128)(2,1)} %get-tuple-element.342), kind=kOutput, calls=%fused_computation.6 | convolution fusion | flops 2418278400 | bytes 7864320 | tf_op jit(solution)/shard_map/dot_general | solution.py:493
  195.6 10.6 %shard_map.226 = (bf16[512,1536]{1,0:T(8,128)(2,1)}, f32[512,128]{1,0:T(8,128)}) custom-call(bf16[512,3072]{1,0:T(8,128)(2,1)} %get-tuple-element.346.gated_ref, bf16[3072,1536]{1,0:T(8,128)(2,1)} %all-gather.2.cloned.1.call-done.weight_ref, bf16[512,1536]{1,0:T(8,128)(2,1)} %bitcast.40, bf16[512,1536]{1,0:T(8,128)(2,1)} %bitcast.32, ...), custom_call_target="tpu_custom_call" | custom-call | flops 3221225472 | bytes 8388608 | tf_op jit(solution)/shard_map/pallas_call | solution.py:574
  211.7 15.2 %shard_map.227 = (bf16[512,3072]{1,0:T(8,128)(2,1)}, bf16[512,3072]{1,0:T(8,128)(2,1)}, f32[8,3072]{1,0:T(8,128)}) custom-call(f32[512,3072]{1,0:T(8,128)} %get-tuple-element.355.z_ref, f32[512,3072]{1,0:T(8,128)} %get-tuple-element.338.ssm_ref, bf16[512,1536]{1,0:T(8,128)(2,1)} %bitcast.33, bf16[3072,1536]{1,0:T(8,128)(2,1)} %all-gather.2.cloned.1.call-done.weight_ref, ...), custom_call_target="tpu_custom_call" | custom-call | flops 4000000000 | bytes 12000000 | tf_op jit(solution)/shard_map/pallas_call | solution.py:443
  227.0 3.2 add_convert_fusion.1
  230.2 3.4 add_convert_fusion
  233.6 7.5 %fusion.27 = bf16[1536,3072]{1,0:T(8,128)(2,1)} fusion(bf16[512,1536]{1,0:T(8,128)(2,1)S(1)} %copy-done.8, bf16[512,3072]{1,0:T(8,128)(2,1)S(1)} %copy-done.14), kind=kOutput, calls=%fused_computation.85 | convolution fusion | flops 4831838208 | bytes 14155776 | tf_op jit(solution)/shard_map/dot_general | solution.py:493
  244.5 26.2 %shard_map.228 = (bf16[512,2048]{1,0:T(8,128)(2,1)}, f32[8,2048]{1,0:T(8,128)}, f32[512,768]{1,0:T(8,128)}, f32[8,2048]{1,0:T(8,128)}) custom-call(s32[1]{0:T(128)} %bitcast.49, f32[512,3072]{1,0:T(8,128)} %get-tuple-element.315.x_ref, f32[512,3072]{1,0:T(8,128)} %get-tuple-element.338.ssm_ref, bf16[512,3072]{1,0:T(8,128)(2,1)} %get-tuple-element.379.ds_ref, ...), custom_call_target="tpu_custom_call" | custom-call | flops 9333332992 | bytes 10666666 | tf_op jit(solution)/shard_map/pallas_call | solution.py:463
  270.7 5.0 convolution_convert_fusion.1
  280.7 15.3 %shard_map.229 = (bf16[512,1024]{1,0:T(8,128)(2,1)}, f32[8,1024]{1,0:T(8,128)}, f32[512,768]{1,0:T(8,128)}, f32[8,1024]{1,0:T(8,128)}) custom-call(s32[1]{0:T(128)} %bitcast.50, f32[512,3072]{1,0:T(8,128)} %get-tuple-element.315.x_ref, f32[512,3072]{1,0:T(8,128)} %get-tuple-element.338.ssm_ref, bf16[512,3072]{1,0:T(8,128)(2,1)} %get-tuple-element.379.ds_ref, ...), custom_call_target="tpu_custom_call" | custom-call | flops 4666666496 | bytes 5333333 | tf_op jit(solution)/shard_map/pallas_call | solution.py:463
  296.1 6.4 %shard_map.230 = (bf16[512,384]{1,0:T(8,128)(2,1)}, f32[8,256]{1,0:T(8,128)}, f32[8,128]{1,0:T(8,128)}) custom-call(s32[1]{0:T(128)} %bitcast.51, f32[512,384]{1,0:T(8,128)} %get-tuple-element.384.bcd_ref, f32[8,256]{1,0:T(8,128)} %slice.139.conv_ref, f32[8,128]{1,0:T(8,128)} %get-tuple-element.385.head_ref, bf16[512,256]{1,0:T(8,128)(2,1)} %get-tuple-element.320.bc_ref, ...), custom_call_target="tpu_custom_call" | custom-call | flops 1333333376 | bytes 2666666 | tf_op jit(solution)/shard_map/pallas_call | solution.py:480
  302.6 6.2 %shard_map.231 = (bf16[192,2048]{1,0:T(8,128)(2,1)}, bf16[192,2048]{1,0:T(8,128)(2,1)}, bf16[192,2048]{1,0:T(8,128)(2,1)}, f32[192,2048]{1,0:T(8,128)}) custom-call(bf16[1536,512]{1,0:T(8,128)(2,1)} %get-tuple-element.305.left_ref, bf16[512,2048]{1,0:T(8,128)(2,1)} %get-tuple-element.374.right_ref.refs_2_, bf16[768,2048]{1,0:T(8,128)(2,1)} %collective-permute-done.27.got_ref), custom_call_target="tpu_custom_call" | custom-call | flops 536870912 | bytes 3145728 | tf_op jit(solution)/shard_map/pallas_call | solution.py:690
  311.9 6.3 %reduce-scatter.2.cloned.1.call-done = bf16[192,3072]{1,0:T(8,128)(2,1)} async-done(((bf16[1536,3072]{1,0:T(8,128)(2,1)}), bf16[192,3072]{1,0:T(8,128)(2,1)}) %reduce-scatter.2.cloned.1.call-update) | async-done | bytes 1179664 | tf_op jit(solution)/shard_map/reduce_scatter | solution.py:1075
  320.0 4.2 convolution_convert_fusion.2
  330.9 11.0 %collective-permute-done.28 = bf16[96,1536]{1,0:T(8,128)(2,1)S(1)} collective-permute-done((bf16[96,1536]{1,0:T(8,128)(2,1)}, bf16[96,1536]{1,0:T(8,128)(2,1)S(1)}, u32[]{:S(2)}, u32[]{:S(2)}) %collective-permute-start.28) | collective-permute-done | bytes 294944 | tf_op jit(solution)/shard_map/ppermute | solution.py:903
  342.5 21.9 %shard_map.232.d_ref = f32[512,1536]{1,0:T(8,128)} custom-call(bf16[512,3072]{1,0:T(8,128)(2,1)} %get-tuple-element.366.refs_0_, bf16[1536,3072]{1,0:T(8,128)(2,1)} %get-tuple-element.408.refs_1_, bf16[512,2048]{1,0:T(8,128)(2,1)} %get-tuple-element.374.right_ref.refs_2_, bf16[1536,3072]{1,0:T(8,128)(2,1)} %get-tuple-element.409.refs_3_.refs_5_, ...), custom_call_target="tpu_custom_call" | custom-call | flops 1000 | bytes 1000 | tf_op jit(solution)/shard_map/pallas_call | solution.py:657
  368.8 5.1 shard_map.233
  374.2 2.8 collective-permute-start.34
  380.5 9.9 %collective-permute-done.34 = bf16[96,1536]{1,0:T(8,128)(2,1)S(1)} collective-permute-done((bf16[96,1536]{1,0:T(8,128)(2,1)S(1)}, bf16[96,1536]{1,0:T(8,128)(2,1)S(1)}, u32[]{:S(2)}, u32[]{:S(2)}) %collective-permute-start.34) | collective-permute-done | bytes 294944 | tf_op jit(solution)/shard_map/ppermute | solution.py:903
  390.4 5.1 shard_map.234
  397.9 7.6 %collective-permute-done.39 = bf16[48,3072]{1,0:T(8,128)(2,1)S(1)} collective-permute-done((bf16[48,3072]{1,0:T(8,128)(2,1)S(1)}, bf16[48,3072]{1,0:T(8,128)(2,1)S(1)}, u32[]{:S(2)}, u32[]{:S(2)}) %collective-permute-start.39) | collective-permute-done | bytes 294944 | tf_op jit(solution)/shard_map/ppermute | solution.py:903
  410.8 3.6 all-to-all-start.2
  415.6 2.9 collective-permute-start.41
  418.5 20.4 %collective-permute-done.41 = bf16[48,5120]{1,0:T(8,128)(2,1)S(1)} collective-permute-done((bf16[48,5120]{1,0:T(8,128)(2,1)S(1)}, bf16[48,5120]{1,0:T(8,128)(2,1)S(1)}, u32[]{:S(2)}, u32[]{:S(2)}) %collective-permute-start.41) | collective-permute-done | bytes 491552 | tf_op jit(solution)/shard_map/ppermute | solution.py:903
  439.6 7.0 %collective-permute-done.42 = bf16[96,1408]{1,0:T(8,128)(2,1)S(1)} collective-permute-done((bf16[96,1408]{1,0:T(8,128)(2,1)}, bf16[96,1408]{1,0:T(8,128)(2,1)S(1)}, u32[]{:S(2)}, u32[]{:S(2)}) %collective-permute-start.42) | collective-permute-done | bytes 270368 | tf_op jit(solution)/shard_map/ppermute | solution.py:903
  450.4 4.5 all-to-all-start.3
  455.3 2.6 collective-permute-start.44
  457.9 2.8 collective-permute-start.46
  461.5 13.9 %collective-permute-done.44 = bf16[48,3456]{1,0:T(8,128)(2,1)S(1)} collective-permute-done((bf16[48,3456]{1,0:T(8,128)(2,1)S(1)}, bf16[48,3456]{1,0:T(8,128)(2,1)S(1)}, u32[]{:S(2)}, u32[]{:S(2)}) %collective-permute-start.44) | collective-permute-done | bytes 331808 | tf_op jit(solution)/shard_map/ppermute | solution.py:903
  479.0 3.4 fusion.1
  491.6 3.2 gather_fusion.4
  495.5 2.6 maximum_convert_fusion
  (291 shorter events, 100.1 us)
Async XLA Ops:
  12.7 33.5 %collective-permute-start = (bf16[192,3456]{1,0:T(8,128)(2,1)}, bf16[192,3456]{1,0:T(8,128)(2,1)S(1)}, u32[]{:S(2)}, u32[]{:S(2)}) collective-permute-start(bf16[192,3456]{1,0:T(8,128)(2,1)} %pad_slice_fusion.refs_0_), channel_id=1, source_target_pairs={{0,2},{1,3},{2,0},{3,1},{4,6},{5,7},{6,4},{7,5},{8,10},{9,11},{10,... | collective-permute-start | bytes 3981320 | tf_op jit(solution)/shard_map/ppermute | solution.py:903
  15.6 32.4 %collective-permute-start.1 = (bf16[192,3456]{1,0:T(8,128)(2,1)}, bf16[192,3456]{1,0:T(8,128)(2,1)}, u32[]{:S(2)}, u32[]{:S(2)}) collective-permute-start(bf16[192,3456]{1,0:T(8,128)(2,1)} %pad_slice_fusion.refs_0_), channel_id=1, source_target_pairs={{0,4},{1,5},{2,6},{3,7},{4,0},{5,1},{6,2},{7,3},{8,12},{9,13},{10,... | collective-permute-start | bytes 3981320 | tf_op jit(solution)/shard_map/ppermute | solution.py:903
  17.4 28.7 %collective-permute-start.2 = (bf16[16,416]{1,0:T(8,128)(2,1)S(1)}, bf16[16,416]{1,0:T(8,128)(2,1)S(1)}, u32[]{:S(2)}, u32[]{:S(2)}) collective-permute-start(bf16[16,416]{1,0:T(8,128)(2,1)S(1)} %pad.49), channel_id=1, source_target_pairs={{0,2},{1,3},{2,0},{3,1},{4,6},{5,7},{6,4},{7,5},{8,10},{9,11},{10,... | collective-permute-start | bytes 39944 | tf_op jit(solution)/shard_map/ppermute | solution.py:993
  18.0 60.2 %all-to-all-start = ((bf16[8,64,1536]{2,1,0:T(8,128)(2,1)}), bf16[8,64,1536]{2,1,0:T(8,128)(2,1)S(1)}, u32[]{:S(2)}, u32[]{:S(2)}) async-start(bf16[8,64,1536]{2,1,0:T(8,128)(2,1)} %gather_fusion), calls=%async_computation | async-start | bytes 3145728 | tf_op jit(solution)/shard_map/all_to_all | solution.py:902
  21.5 174.1 %all-gather.2.cloned.1.call-start = ((), (), s32[]{:S(2)}) async-start(), calls=%async_computation.5 | async-start | bytes 10616832 | tf_op jit(solution)/shard_map/all_gather | solution.py:1003
  50.8 27.4 %collective-permute-start.5 = (bf16[192,3456]{1,0:T(8,128)(2,1)}, bf16[192,3456]{1,0:T(8,128)(2,1)}, u32[]{:S(2)}, u32[]{:S(2)}) collective-permute-start(bf16[192,3456]{1,0:T(8,128)(2,1)} %pad_slice_fusion.refs_0_), channel_id=1, source_target_pairs={{0,1},{1,0},{2,3},{3,2},{4,5},{5,4},{6,7},{7,6},{8,9},{9,8},{10,11... | collective-permute-start | bytes 3981320 | tf_op jit(solution)/shard_map/ppermute | solution.py:903
  50.9 27.4 %collective-permute-start.6 = (bf16[192,3456]{1,0:T(8,128)(2,1)S(1)}, bf16[192,3456]{1,0:T(8,128)(2,1)}, u32[]{:S(2)}, u32[]{:S(2)}) collective-permute-start(bf16[192,3456]{1,0:T(8,128)(2,1)S(1)} %collective-permute-done.refs_2_), channel_id=1, source_target_pairs={{0,1},{1,0},{2,3},{3,2},{4,5},{5,4},{6,7},{7,6},{8,9},{9,8},{10,11... | collective-permute-start | bytes 3981320 | tf_op jit(solution)/shard_map/ppermute | solution.py:903
  51.4 26.9 %collective-permute-start.3 = (bf16[96,3456]{1,0:T(8,128)(2,1)}, bf16[96,3456]{1,0:T(8,128)(2,1)}, u32[]{:S(2)}, u32[]{:S(2)}) collective-permute-start(bf16[96,3456]{1,0:T(8,128)(2,1)} %slice.120), channel_id=1, source_target_pairs={{0,4},{1,5},{2,6},{3,7},{4,0},{5,1},{6,2},{7,3},{8,12},{9,13},{10,... | collective-permute-start | bytes 1990664 | tf_op jit(solution)/shard_map/ppermute | solution.py:903
  52.9 25.3 %collective-permute-start.4 = (bf16[96,3456]{1,0:T(8,128)(2,1)}, bf16[96,3456]{1,0:T(8,128)(2,1)}, u32[]{:S(2)}, u32[]{:S(2)}) collective-permute-start(bf16[96,3456]{1,0:T(8,128)(2,1)} %slice.121), channel_id=1, source_target_pairs={{0,2},{1,3},{2,0},{3,1},{4,6},{5,7},{6,4},{7,5},{8,10},{9,11},{10,... | collective-permute-start | bytes 1990664 | tf_op jit(solution)/shard_map/ppermute | solution.py:903
  57.6 20.6 %collective-permute-start.7 = (bf16[32,416]{1,0:T(8,128)(2,1)S(1)}, bf16[32,416]{1,0:T(8,128)(2,1)S(1)}, u32[]{:S(2)}, u32[]{:S(2)}) collective-permute-start(bf16[32,416]{1,0:T(8,128)(2,1)S(1)} %pad_maximum_fusion.7), channel_id=1, source_target_pairs={{0,4},{1,5},{2,6},{3,7},{4,0},{5,1},{6,2},{7,3},{8,12},{9,13},{10,... | collective-permute-start | bytes 79880 | tf_op jit(solution)/shard_map/ppermute | solution.py:993
  81.2 40.9 %collective-permute-start.8 = (bf16[192,3072]{1,0:T(8,128)(2,1)}, bf16[192,3072]{1,0:T(8,128)(2,1)}, u32[]{:S(2)}, u32[]{:S(2)}) collective-permute-start(bf16[192,3072]{1,0:T(8,128)(2,1)} %slice.119.refs_0_), channel_id=1, source_target_pairs={{0,2},{1,3},{2,0},{3,1},{4,6},{5,7},{6,4},{7,5},{8,10},{9,11},{10,... | collective-permute-start | bytes 3538952 | tf_op jit(solution)/shard_map/ppermute | solution.py:903
  81.5 40.6 %collective-permute-start.9 = (bf16[192,3072]{1,0:T(8,128)(2,1)}, bf16[192,3072]{1,0:T(8,128)(2,1)}, u32[]{:S(2)}, u32[]{:S(2)}) collective-permute-start(bf16[192,3072]{1,0:T(8,128)(2,1)} %slice.119.refs_0_), channel_id=1, source_target_pairs={{0,4},{1,5},{2,6},{3,7},{4,0},{5,1},{6,2},{7,3},{8,12},{9,13},{10,... | collective-permute-start | bytes 3538952 | tf_op jit(solution)/shard_map/ppermute | solution.py:903
  124.4 31.7 %collective-permute-start.16 = (bf16[192,3072]{1,0:T(8,128)(2,1)}, bf16[192,3072]{1,0:T(8,128)(2,1)S(1)}, u32[]{:S(2)}, u32[]{:S(2)}) collective-permute-start(bf16[192,3072]{1,0:T(8,128)(2,1)} %slice.119.refs_0_), channel_id=1, source_target_pairs={{0,1},{1,0},{2,3},{3,2},{4,5},{5,4},{6,7},{7,6},{8,9},{9,8},{10,11... | collective-permute-start | bytes 3538952 | tf_op jit(solution)/shard_map/ppermute | solution.py:903
  124.4 32.4 %collective-permute-start.17 = (bf16[192,3072]{1,0:T(8,128)(2,1)}, bf16[192,3072]{1,0:T(8,128)(2,1)}, u32[]{:S(2)}, u32[]{:S(2)}) collective-permute-start(bf16[192,3072]{1,0:T(8,128)(2,1)} %collective-permute-done.8.refs_2_), channel_id=1, source_target_pairs={{0,1},{1,0},{2,3},{3,2},{4,5},{5,4},{6,7},{7,6},{8,9},{9,8},{10,11... | collective-permute-start | bytes 3538952 | tf_op jit(solution)/shard_map/ppermute | solution.py:903
  124.9 31.9 %collective-permute-start.18 = (bf16[192,3072]{1,0:T(8,128)(2,1)}, bf16[192,3072]{1,0:T(8,128)(2,1)}, u32[]{:S(2)}, u32[]{:S(2)}) collective-permute-start(bf16[192,3072]{1,0:T(8,128)(2,1)} %collective-permute-done.9.refs_4_), channel_id=1, source_target_pairs={{0,1},{1,0},{2,3},{3,2},{4,5},{5,4},{6,7},{7,6},{8,9},{9,8},{10,11... | collective-permute-start | bytes 3538952 | tf_op jit(solution)/shard_map/ppermute | solution.py:903
  125.0 29.2 %collective-permute-start.14 = (bf16[96,3072]{1,0:T(8,128)(2,1)S(1)}, bf16[96,3072]{1,0:T(8,128)(2,1)S(1)}, u32[]{:S(2)}, u32[]{:S(2)}) collective-permute-start(bf16[96,3072]{1,0:T(8,128)(2,1)S(1)} %slice.124), channel_id=1, source_target_pairs={{0,4},{1,5},{2,6},{3,7},{4,0},{5,1},{6,2},{7,3},{8,12},{9,13},{10,... | collective-permute-start | bytes 1769480 | tf_op jit(solution)/shard_map/ppermute | solution.py:903
  127.5 28.5 %collective-permute-start.15 = (bf16[96,3072]{1,0:T(8,128)(2,1)S(1)}, bf16[96,3072]{1,0:T(8,128)(2,1)S(1)}, u32[]{:S(2)}, u32[]{:S(2)}) collective-permute-start(bf16[96,3072]{1,0:T(8,128)(2,1)S(1)} %slice.125), channel_id=1, source_target_pairs={{0,2},{1,3},{2,0},{3,1},{4,6},{5,7},{6,4},{7,5},{8,10},{9,11},{10,... | collective-permute-start | bytes 1769480 | tf_op jit(solution)/shard_map/ppermute | solution.py:903
  157.9 31.1 %all-to-all-start.1 = ((bf16[8,64,1536]{2,1,0:T(8,128)(2,1)}), bf16[8,64,1536]{2,1,0:T(8,128)(2,1)S(1)}, u32[]{:S(2)}, u32[]{:S(2)}) async-start(bf16[8,64,1536]{2,1,0:T(8,128)(2,1)} %gather_fusion.1), calls=%async_computation.1 | async-start | bytes 3145728 | tf_op jit(solution)/shard_map/all_to_all | solution.py:902
  161.5 156.7 %reduce-scatter.2.cloned.1.call-start = ((), (), s32[]{:S(2)}) async-start(), calls=%async_computation.6 | async-start | bytes 10616832 | tf_op jit(solution)/shard_map/reduce_scatter | solution.py:1075
  208.5 18.4 %collective-permute-start.22 = (bf16[192,1536]{1,0:T(8,128)(2,1)S(1)}, bf16[192,1536]{1,0:T(8,128)(2,1)S(1)}, u32[]{:S(2)}, u32[]{:S(2)}) collective-permute-start(bf16[192,1536]{1,0:T(8,128)(2,1)S(1)} %get-tuple-element.353), channel_id=1, source_target_pairs={{0,2},{1,3},{2,0},{3,1},{4,6},{5,7},{6,4},{7,5},{8,10},{9,11},{10,... | collective-permute-start | bytes 1769480 | tf_op jit(solution)/shard_map/ppermute | solution.py:903
  210.2 16.7 %collective-permute-start.23 = (bf16[192,1536]{1,0:T(8,128)(2,1)S(1)}, bf16[192,1536]{1,0:T(8,128)(2,1)S(1)}, u32[]{:S(2)}, u32[]{:S(2)}) collective-permute-start(bf16[192,1536]{1,0:T(8,128)(2,1)S(1)} %get-tuple-element.354), channel_id=1, source_target_pairs={{0,4},{1,5},{2,6},{3,7},{4,0},{5,1},{6,2},{7,3},{8,12},{9,13},{10,... | collective-permute-start | bytes 1769480 | tf_op jit(solution)/shard_map/ppermute | solution.py:903
  241.1 29.6 %collective-permute-start.24 = (bf16[384,1536]{1,0:T(8,128)(2,1)}, bf16[384,1536]{1,0:T(8,128)(2,1)S(1)}, u32[]{:S(2)}, u32[]{:S(2)}) collective-permute-start(bf16[384,1536]{1,0:T(8,128)(2,1)} %add_convert_fusion.1), channel_id=1, source_target_pairs={{0,2},{1,3},{2,0},{3,1},{4,6},{5,7},{6,4},{7,5},{8,10},{9,11},{10,... | collective-permute-start | bytes 3538952 | tf_op jit(solution)/shard_map/ppermute | solution.py:903
  241.7 29.0 %collective-permute-start.25 = (bf16[384,1536]{1,0:T(8,128)(2,1)}, bf16[384,1536]{1,0:T(8,128)(2,1)}, u32[]{:S(2)}, u32[]{:S(2)}) collective-permute-start(bf16[384,1536]{1,0:T(8,128)(2,1)} %add_convert_fusion), channel_id=1, source_target_pairs={{0,4},{1,5},{2,6},{3,7},{4,0},{5,1},{6,2},{7,3},{8,12},{9,13},{10,... | collective-permute-start | bytes 3538952 | tf_op jit(solution)/shard_map/ppermute | solution.py:903
  278.2 24.4 %collective-permute-start.27 = (bf16[768,2048]{1,0:T(8,128)(2,1)}, bf16[768,2048]{1,0:T(8,128)(2,1)}, u32[]{:S(2)}, u32[]{:S(2)}) collective-permute-start(bf16[768,2048]{1,0:T(8,128)(2,1)} %convolution_convert_fusion.1), channel_id=1, source_target_pairs={{0,1},{1,0},{2,3},{3,2},{4,5},{5,4},{6,7},{7,6},{8,9},{9,8},{10,11... | collective-permute-start | bytes 9437192 | tf_op jit(solution)/shard_map/ppermute | solution.py:903
  278.3 24.3 %collective-permute-start.26 = (bf16[192,1536]{1,0:T(8,128)(2,1)S(1)}, bf16[192,1536]{1,0:T(8,128)(2,1)S(1)}, u32[]{:S(2)}, u32[]{:S(2)}) collective-permute-start(bf16[192,1536]{1,0:T(8,128)(2,1)S(1)} %select_convert_fusion), channel_id=1, source_target_pairs={{0,8},{8,0},{16,24},{24,16},{1,9},{9,1},{17,25},{25,17},{2,10},{10... | collective-permute-start | bytes 1769480 | tf_op jit(solution)/shard_map/ppermute | solution.py:903
  325.0 40.8 %collective-permute-start.32 = (bf16[768,1408]{1,0:T(8,128)(2,1)}, bf16[768,1408]{1,0:T(8,128)(2,1)S(1)}, u32[]{:S(2)}, u32[]{:S(2)}) collective-permute-start(bf16[768,1408]{1,0:T(8,128)(2,1)} %convolution_convert_fusion.2), channel_id=1, source_target_pairs={{0,1},{1,0},{2,3},{3,2},{4,5},{5,4},{6,7},{7,6},{8,9},{9,8},{10,11... | collective-permute-start | bytes 6488072 | tf_op jit(solution)/shard_map/ppermute | solution.py:903
  325.0 16.9 %collective-permute-start.28 = (bf16[96,1536]{1,0:T(8,128)(2,1)}, bf16[96,1536]{1,0:T(8,128)(2,1)S(1)}, u32[]{:S(2)}, u32[]{:S(2)}) collective-permute-start(bf16[96,1536]{1,0:T(8,128)(2,1)} %select_convert_fusion.3), channel_id=1, source_target_pairs={{0,16},{8,24},{16,0},{24,8},{1,17},{9,25},{17,1},{25,9},{2,18},{10... | collective-permute-start | bytes 884744 | tf_op jit(solution)/shard_map/ppermute | solution.py:903
  327.4 36.9 %collective-permute-start.29 = (bf16[192,2048]{1,0:T(8,128)(2,1)}, bf16[192,2048]{1,0:T(8,128)(2,1)S(1)}, u32[]{:S(2)}, u32[]{:S(2)}) collective-permute-start(bf16[192,2048]{1,0:T(8,128)(2,1)} %get-tuple-element.403), channel_id=1, source_target_pairs={{0,6},{1,7},{2,4},{3,5},{4,2},{5,3},{6,0},{7,1},{8,14},{9,15},{10,... | collective-permute-start | bytes 2359304 | tf_op jit(solution)/shard_map/ppermute | solution.py:903
  328.9 36.1 %collective-permute-start.30 = (bf16[192,2048]{1,0:T(8,128)(2,1)}, bf16[192,2048]{1,0:T(8,128)(2,1)S(1)}, u32[]{:S(2)}, u32[]{:S(2)}) collective-permute-start(bf16[192,2048]{1,0:T(8,128)(2,1)} %get-tuple-element.404), channel_id=1, source_target_pairs={{0,2},{1,3},{2,0},{3,1},{4,6},{5,7},{6,4},{7,5},{8,10},{9,11},{10,... | collective-permute-start | bytes 2359304 | tf_op jit(solution)/shard_map/ppermute | solution.py:903
  330.2 34.8 %collective-permute-start.31 = (bf16[192,2048]{1,0:T(8,128)(2,1)}, bf16[192,2048]{1,0:T(8,128)(2,1)S(1)}, u32[]{:S(2)}, u32[]{:S(2)}) collective-permute-start(bf16[192,2048]{1,0:T(8,128)(2,1)} %get-tuple-element.405), channel_id=1, source_target_pairs={{0,4},{1,5},{2,6},{3,7},{4,0},{5,1},{6,2},{7,3},{8,12},{9,13},{10,... | collective-permute-start | bytes 2359304 | tf_op jit(solution)/shard_map/ppermute | solution.py:903
  341.9 22.4 %collective-permute-start.33 = (bf16[96,3072]{1,0:T(8,128)(2,1)}, bf16[96,3072]{1,0:T(8,128)(2,1)S(1)}, u32[]{:S(2)}, u32[]{:S(2)}) collective-permute-start(bf16[96,3072]{1,0:T(8,128)(2,1)} %broadcast_select_fusion), channel_id=1, source_target_pairs={{0,8},{8,0},{16,24},{24,16},{1,9},{9,1},{17,25},{25,17},{2,10},{10... | collective-permute-start | bytes 1769480 | tf_op jit(solution)/shard_map/ppermute | solution.py:903
  374.2 16.2 %collective-permute-start.34 = (bf16[96,1536]{1,0:T(8,128)(2,1)S(1)}, bf16[96,1536]{1,0:T(8,128)(2,1)S(1)}, u32[]{:S(2)}, u32[]{:S(2)}) collective-permute-start(bf16[96,1536]{1,0:T(8,128)(2,1)S(1)} %add_convert_fusion.4), channel_id=1, source_target_pairs={{0,16},{8,24},{16,0},{24,8},{1,17},{9,25},{17,1},{25,9},{2,18},{10... | collective-permute-start | bytes 884744 | tf_op jit(solution)/shard_map/ppermute | solution.py:903
  377.0 28.5 %collective-permute-start.35 = (bf16[96,2048]{1,0:T(8,128)(2,1)S(1)}, bf16[96,2048]{1,0:T(8,128)(2,1)S(1)}, u32[]{:S(2)}, u32[]{:S(2)}) collective-permute-start(bf16[96,2048]{1,0:T(8,128)(2,1)S(1)} %select_convert_fusion.1), channel_id=1, source_target_pairs={{0,8},{8,0},{16,24},{24,16},{1,9},{9,1},{17,25},{25,17},{2,10},{10... | collective-permute-start | bytes 1179656 | tf_op jit(solution)/shard_map/ppermute | solution.py:903
  377.0 28.5 %collective-permute-start.36 = (bf16[192,1408]{1,0:T(8,128)(2,1)}, bf16[192,1408]{1,0:T(8,128)(2,1)S(1)}, u32[]{:S(2)}, u32[]{:S(2)}) collective-permute-start(bf16[192,1408]{1,0:T(8,128)(2,1)} %get-tuple-element.424), channel_id=1, source_target_pairs={{0,6},{1,7},{2,4},{3,5},{4,2},{5,3},{6,0},{7,1},{8,14},{9,15},{10,... | collective-permute-start | bytes 1622024 | tf_op jit(solution)/shard_map/ppermute | solution.py:903
  378.5 27.1 %collective-permute-start.37 = (bf16[192,1408]{1,0:T(8,128)(2,1)S(1)}, bf16[192,1408]{1,0:T(8,128)(2,1)S(1)}, u32[]{:S(2)}, u32[]{:S(2)}) collective-permute-start(bf16[192,1408]{1,0:T(8,128)(2,1)S(1)} %copy-done.48), channel_id=1, source_target_pairs={{0,2},{1,3},{2,0},{3,1},{4,6},{5,7},{6,4},{7,5},{8,10},{9,11},{10,... | collective-permute-start | bytes 1622024 | tf_op jit(solution)/shard_map/ppermute | solution.py:903
  379.8 25.7 %collective-permute-start.38 = (bf16[192,1408]{1,0:T(8,128)(2,1)S(1)}, bf16[192,1408]{1,0:T(8,128)(2,1)S(1)}, u32[]{:S(2)}, u32[]{:S(2)}) collective-permute-start(bf16[192,1408]{1,0:T(8,128)(2,1)S(1)} %copy-done.47), channel_id=1, source_target_pairs={{0,4},{1,5},{2,6},{3,7},{4,0},{5,1},{6,2},{7,3},{8,12},{9,13},{10,... | collective-permute-start | bytes 1622024 | tf_op jit(solution)/shard_map/ppermute | solution.py:903
  390.4 15.1 %collective-permute-start.39 = (bf16[48,3072]{1,0:T(8,128)(2,1)S(1)}, bf16[48,3072]{1,0:T(8,128)(2,1)S(1)}, u32[]{:S(2)}, u32[]{:S(2)}) collective-permute-start(bf16[48,3072]{1,0:T(8,128)(2,1)S(1)} %select_convert_fusion.2), channel_id=1, source_target_pairs={{0,16},{8,24},{16,0},{24,8},{1,17},{9,25},{17,1},{25,9},{2,18},{10... | collective-permute-start | bytes 884744 | tf_op jit(solution)/shard_map/ppermute | solution.py:903
  410.8 36.5 %all-to-all-start.2 = ((bf16[8,64,1536]{2,1,0:T(8,128)(2,1)}), bf16[8,64,1536]{2,1,0:T(8,128)(2,1)S(1)}, u32[]{:S(2)}, u32[]{:S(2)}) async-start(bf16[8,64,1536]{2,1,0:T(8,128)(2,1)} %bitcast.43), calls=%async_computation.3 | async-start | bytes 3145728 | tf_op jit(solution)/shard_map/all_to_all | solution.py:902
  414.4 32.9 %collective-permute-start.40 = (bf16[192,1536]{1,0:T(8,128)(2,1)}, bf16[192,1536]{1,0:T(8,128)(2,1)}, u32[]{:S(2)}, u32[]{:S(2)}) collective-permute-start(bf16[192,1536]{1,0:T(8,128)(2,1)} %maximum_select_fusion.3), channel_id=1, source_target_pairs={{0,8},{8,0},{16,24},{24,16},{1,9},{9,1},{17,25},{25,17},{2,10},{10... | collective-permute-start | bytes 1769480 | tf_op jit(solution)/shard_map/ppermute | solution.py:903
  415.6 23.3 %collective-permute-start.41 = (bf16[48,5120]{1,0:T(8,128)(2,1)S(1)}, bf16[48,5120]{1,0:T(8,128)(2,1)S(1)}, u32[]{:S(2)}, u32[]{:S(2)}) collective-permute-start(bf16[48,5120]{1,0:T(8,128)(2,1)S(1)} %pad_maximum_fusion.2), channel_id=1, source_target_pairs={{0,16},{8,24},{16,0},{24,8},{1,17},{9,25},{17,1},{25,9},{2,18},{10... | collective-permute-start | bytes 1474568 | tf_op jit(solution)/shard_map/ppermute | solution.py:903
  418.4 28.2 %collective-permute-start.42 = (bf16[96,1408]{1,0:T(8,128)(2,1)}, bf16[96,1408]{1,0:T(8,128)(2,1)S(1)}, u32[]{:S(2)}, u32[]{:S(2)}) collective-permute-start(bf16[96,1408]{1,0:T(8,128)(2,1)} %select_convert_fusion.4), channel_id=1, source_target_pairs={{0,8},{8,0},{16,24},{24,16},{1,9},{9,1},{17,25},{25,17},{2,10},{10... | collective-permute-start | bytes 811016 | tf_op jit(solution)/shard_map/ppermute | solution.py:903
  418.5 21.1 %collective-permute-start.43 = (f32[4,2688]{1,0:T(4,128)S(1)}, f32[4,2688]{1,0:T(4,128)S(1)}, u32[]{:S(2)}, u32[]{:S(2)}) collective-permute-start(f32[4,2688]{1,0:T(4,128)S(1)} %slice.172), channel_id=1, source_target_pairs={{0,1},{1,0},{2,3},{3,2},{4,5},{5,4},{6,7},{7,6},{8,9},{9,8},{10,11... | collective-permute-start | bytes 129032 | tf_op jit(solution)/shard_map/ppermute | solution.py:903
  450.4 27.3 %all-to-all-start.3 = ((bf16[8,64,1536]{2,1,0:T(8,128)(2,1)}), bf16[8,64,1536]{2,1,0:T(8,128)(2,1)}, u32[]{:S(2)}, u32[]{:S(2)}) async-start(bf16[8,64,1536]{2,1,0:T(8,128)(2,1)} %bitcast.42), calls=%async_computation.4 | async-start | bytes 3145728 | tf_op jit(solution)/shard_map/all_to_all | solution.py:902
  454.9 22.8 %collective-permute-start.45 = (bf16[96,3072]{1,0:T(8,128)(2,1)S(1)}, bf16[96,3072]{1,0:T(8,128)(2,1)}, u32[]{:S(2)}, u32[]{:S(2)}) collective-permute-start(bf16[96,3072]{1,0:T(8,128)(2,1)S(1)} %maximum_select_fusion.4), channel_id=1, source_target_pairs={{0,8},{8,0},{16,24},{24,16},{1,9},{9,1},{17,25},{25,17},{2,10},{10... | collective-permute-start | bytes 1769480 | tf_op jit(solution)/shard_map/ppermute | solution.py:903
  455.3 20.1 %collective-permute-start.44 = (bf16[48,3456]{1,0:T(8,128)(2,1)S(1)}, bf16[48,3456]{1,0:T(8,128)(2,1)S(1)}, u32[]{:S(2)}, u32[]{:S(2)}) collective-permute-start(bf16[48,3456]{1,0:T(8,128)(2,1)S(1)} %pad_maximum_fusion.3), channel_id=1, source_target_pairs={{0,16},{8,24},{16,0},{24,8},{1,17},{9,25},{17,1},{25,9},{2,18},{10... | collective-permute-start | bytes 995336 | tf_op jit(solution)/shard_map/ppermute | solution.py:903
  457.9 18.3 %collective-permute-start.46 = (f32[1,2688]{1,0:T(1,128)S(1)}, f32[1,2688]{1,0:T(1,128)S(1)}, u32[]{:S(2)}, u32[]{:S(2)}) collective-permute-start(f32[1,2688]{1,0:T(1,128)S(1)} %get-tuple-element.460), channel_id=1, source_target_pairs={{0,6},{1,7},{2,4},{3,5},{4,2},{5,3},{6,0},{7,1},{8,14},{9,15},{10,... | collective-permute-start | bytes 32264 | tf_op jit(solution)/shard_map/ppermute | solution.py:903
  460.7 15.5 %collective-permute-start.47 = (f32[1,2688]{1,0:T(1,128)S(1)}, f32[1,2688]{1,0:T(1,128)S(1)}, u32[]{:S(2)}, u32[]{:S(2)}) collective-permute-start(f32[1,2688]{1,0:T(1,128)S(1)} %get-tuple-element.461), channel_id=1, source_target_pairs={{0,2},{1,3},{2,0},{3,1},{4,6},{5,7},{6,4},{7,5},{8,10},{9,11},{10,... | collective-permute-start | bytes 32264 | tf_op jit(solution)/shard_map/ppermute | solution.py:903
  477.9 17.0 %collective-permute-start.49 = (bf16[96,2048]{1,0:T(8,128)(2,1)S(1)}, bf16[96,2048]{1,0:T(8,128)(2,1)S(1)}, u32[]{:S(2)}, u32[]{:S(2)}) collective-permute-start(bf16[96,2048]{1,0:T(8,128)(2,1)S(1)} %maximum_select_fusion.5), channel_id=1, source_target_pairs={{0,8},{8,0},{16,24},{24,16},{1,9},{9,1},{17,25},{25,17},{2,10},{10... | collective-permute-start | bytes 1179656 | tf_op jit(solution)/shard_map/ppermute | solution.py:903
  (66 other events, 366.9 us)
Sparse Core Ops, SparseCore 0:
  78.4 84.8 all-gather.1
  241.2 76.8 reduce-scatter.1

commit v6 on v5

--- a/solution.py
+++ b/solution.py
@@ -669,6 +669,25 @@
 TN = (((0,), (0,)), ((), ()))
 
 
+def restore_kernel(targets_ref, blocks_ref, out_ref):
+    count, rows, _ = blocks_ref.shape
+    for i in range(count):
+        out_ref[i * rows : (i + 1) * rows, :] = blocks_ref[targets_ref[i]]
+
+
+def run_restore(targets, blocks):
+    count, rows, width = blocks.shape
+    return pl.pallas_call(
+        restore_kernel,
+        grid=(1,),
+        in_specs=[smem(), whole(blocks.shape)],
+        out_specs=whole((count * rows, width)),
+        out_shape=shaped((count * rows, width), blocks.dtype),
+        compiler_params=params(),
+        cost_estimate=cost(6000000000, 12000000),
+    )(targets, blocks)
+
+
 def terms_kernel(turned, left_ref, right_ref, got_ref, *outs):
     rows = outs[0].shape[0]
     if turned:
@@ -1086,7 +1105,6 @@
 
         last, d_b, bgrads, hgrads = moves.turn(middle, ds)
         backs.append(last)
-        s_z, d_b = tie(s_z, d_b)
         e_last = moves.add(slice_sum(sent, jnp.concatenate([last[0], d_b], axis=1)))
         e_z = moves.add(half_sum(s_z))
         (d_normed,) = moves.turn(lambda d: (back(backs, d),), d_b)
@@ -1141,7 +1159,7 @@
         moves.turn()
 
         def restored(entry):
-            return entry["value"][targets].reshape(tok_rows, width)
+            return run_restore(targets, entry["value"])
 
         input_grad, r_out = moves.turn(lambda: (restored(e_input), widen(e_rows["value"])))
         (output,) = moves.turn(lambda: (restored(e_output),))

time: 520 us -> 509 us (0.979)
  local copies, waits for them, and re-layouts: 38.1 us -> 30.3 us
    pallas_call x0 -> x2, Pallas kernels: none -> 5.33 us  [run_restore(): pl.pallas_call(restore_kernel, grid=(1,), in_specs=[smem(), whole(blocks....]
  transfers between devices with their start and end apart: 61 -> 61, of which waited for: 23 -> 24; matrix products, arithmetic and copies ran while one was open for 10% -> 9% of each run, Pallas kernels for 34% -> 36%
where the time goes in v6:
time: 509 us; the launch traced here: 501 us
  Pallas kernels  184 us (36%)
  waiting for transfers between devices  143 us (28%)
  starting transfers between devices  73.5 us (14%)
  matrix products  32.1 us (6%)
  local copies, waits for them, and re-layouts  30.3 us (6%)
  other arithmetic  22.1 us (4%)
  between operations  15.6 us (3%)
    ppermute x52, waiting for transfers between devices, transfer(): return lax.ppermute(v, axis, pairs)  97.9 us
    ppermute x52, starting transfers between devices, transfer(): return lax.ppermute(v, axis, pairs)  56.6 us
    ppermute x3, waiting for transfers between devices, doubled(): return (jnp.concatenate([v, lax.ppermute(v, 'fsdp', partners(bit))]),)  42.7 us
    pallas_call x2, Pallas kernels, run_backward(): pl.pallas_call(functools.partial(backward_kernel, base), grid=(count,), i...  41.3 us
    pallas_call x2, Pallas kernels, run_project(): pl.pallas_call(functools.partial(project_kernel, places), grid=(cols // s...  26.9 us
    dot_general x6, matrix products, contract_rows(): lax.dot_general(left, right, (((0,), (0,)), ((), ())), preferred_element_...  24.4 us
    pallas_call x1, Pallas kernels, run_back(): pl.pallas_call(functools.partial(back_kernel, tuple(spans), int(base is n...  21.9 us
    pallas_call x1, Pallas kernels, run_forward(): pl.pallas_call(forward_kernel, grid=(width // LANES,), in_specs=[smem(),...  20.1 us
  transfers between devices with their start and end apart: 61, of which 24 were waited for; matrix products, arithmetic and copies ran while one was open for 9% of the time, Pallas kernels for 36%

profile of v6, /device:TPU:0, one launch (start us, length us, event | category | flops | bytes accessed | tf_op | source)
XLA Modules:
  0.0 500.7 jit_solution(5168211614611796149)
XLA Ops:
  12.7 2.9 collective-permute-start
  18.0 3.6 all-to-all-start
  21.6 24.5 %collective-permute-done.2 = bf16[16,416]{1,0:T(8,128)(2,1)S(1)} collective-permute-done((bf16[16,416]{1,0:T(8,128)(2,1)S(1)}, bf16[16,416]{1,0:T(8,128)(2,1)S(1)}, u32[]{:S(2)}, u32[]{:S(2)}) %collective-permute-start.2) | collective-permute-done | bytes 13344 | tf_op jit(solution)/shard_map/ppermute | solution.py:1012
  52.9 4.7 collective-permute-start.4
  57.6 3.2 gather_fusion.1
  60.8 17.4 %collective-permute-done.7 = bf16[32,416]{1,0:T(8,128)(2,1)S(1)} collective-permute-done((bf16[32,416]{1,0:T(8,128)(2,1)S(1)}, bf16[32,416]{1,0:T(8,128)(2,1)S(1)}, u32[]{:S(2)}, u32[]{:S(2)}) %collective-permute-start.7) | collective-permute-done | bytes 26656 | tf_op jit(solution)/shard_map/ppermute | solution.py:1012
  87.2 8.1 %shard_map.221 = (f32[1,1536]{1,0:T(1,128)}, f32[8,3328]{1,0:T(8,128)}, f32[8,128]{1,0:T(8,128)}, f32[8,3072]{1,0:T(8,128)}, bf16[512,1536]{1,0:T(8,128)(2,1)}, ...) custom-call(s32[1]{0:T(128)} %bitcast.7.me_ref, ...), custom_call_target="tpu_custom_call" | custom-call | flops 2000000000 | bytes 3333333 | tf_op jit(solution)/shard_map/pallas_call | solution.py:766
  95.4 13.2 %shard_map.222 = (f32[512,3072]{1,0:T(8,128)}, bf16[1536,3072]{1,0:T(8,128)(2,1)}) custom-call(s32[1]{0:T(128)} %bitcast.7.me_ref, bf16[512,1536]{1,0:T(8,128)(2,1)} %get-tuple-element.324.left_ref, bf16[192,3456]{1,0:T(8,128)(2,1)} %pad_slice_fusion.refs_0_, bf16[192,3456]{1,0:T(8,128)(2,1)} %collective-permute-done.5.refs_1_, bf16[192,3456]{1,0:T(8,128)(2,1)} %copy-done.6, ...), custom_call_target="tpu_custom_call" | custom-call | flops 1610612736 | bytes 9437184 | tf_op jit(solution)/shard_map/pallas_call | solution.py:518
  108.6 12.3 %collective-permute-done.8.refs_2_ = bf16[192,3072]{1,0:T(8,128)(2,1)S(1)} collective-permute-done((bf16[192,3072]{1,0:T(8,128)(2,1)S(1)}, bf16[192,3072]{1,0:T(8,128)(2,1)S(1)}, u32[]{:S(2)}, u32[]{:S(2)}) %collective-permute-start.8) | collective-permute-done | bytes 1179680 | tf_op jit(solution)/shard_map/ppermute | solution.py:922
  127.1 20.1 %shard_map.223 = (f32[512,3072]{1,0:T(8,128)}, bf16[512,3072]{1,0:T(8,128)(2,1)}) custom-call(s32[1]{0:T(128)} %bitcast.40, f32[512,3072]{1,0:T(8,128)} %get-tuple-element.313.x_ref, f32[8,3072]{1,0:T(8,128)} %slice.126.conv_ref, f32[8,3072]{1,0:T(8,128)} %get-tuple-element.315.gain_ref, f32[512,512]{1,0:T(8,128)} %get-tuple-element.316.wide_ref, ...), custom_call_target="tpu_custom_call" | custom-call | flops 6666666496 | bytes 6666666 | tf_op jit(solution)/shard_map/pallas_call | solution.py:410
  147.2 5.0 %collective-permute-done.14.refs_6_ = bf16[96,3072]{1,0:T(8,128)(2,1)S(1)} collective-permute-done((bf16[96,3072]{1,0:T(8,128)(2,1)}, bf16[96,3072]{1,0:T(8,128)(2,1)S(1)}, u32[]{:S(2)}, u32[]{:S(2)}) %collective-permute-start.14) | collective-permute-done | bytes 589856 | tf_op jit(solution)/shard_map/ppermute | solution.py:922
  156.0 3.6 all-to-all-start.1
  164.7 13.7 %shard_map.224 = (f32[512,3072]{1,0:T(8,128)}, bf16[1536,3072]{1,0:T(8,128)(2,1)}) custom-call(s32[1]{0:T(128)} %bitcast.7.me_ref, bf16[512,1536]{1,0:T(8,128)(2,1)} %get-tuple-element.324.left_ref, bf16[192,3072]{1,0:T(8,128)(2,1)} %copy-done.13, bf16[192,3072]{1,0:T(8,128)(2,1)} %copy-done.24, bf16[192,3072]{1,0:T(8,128)(2,1)} %copy-done.19, ...), custom_call_target="tpu_custom_call" | custom-call | flops 1610612736 | bytes 9437184 | tf_op jit(solution)/shard_map/pallas_call | solution.py:518
  178.4 9.2 %shard_map.225 = (bf16[512,3072]{1,0:T(8,128)(2,1)}, bf16[512,3072]{1,0:T(8,128)(2,1)}, f32[512,128]{1,0:T(8,128)}) custom-call(s32[1]{0:T(128)} %bitcast.7.me_ref, f32[512,3072]{1,0:T(8,128)} %get-tuple-element.353.z_ref, f32[512,3072]{1,0:T(8,128)} %get-tuple-element.336.ssm_ref, f32[8,3072]{1,0:T(8,128)} %get-tuple-element.315.gain_ref), custom_call_target="tpu_custom_call" | custom-call | flops 1333333376 | bytes 5333333 | tf_op jit(solution)/shard_map/pallas_call | solution.py:427
  187.7 6.3 %convolution_convert_fusion = bf16[1536,1536]{1,0:T(8,128)(2,1)} fusion(bf16[512,1536]{1,0:T(8,128)(2,1)S(1)} %bitcast.25, bf16[512,3072]{1,0:T(8,128)(2,1)} %get-tuple-element.340), kind=kOutput, calls=%fused_computation.4 | convolution fusion | flops 2418278400 | bytes 7864320 | tf_op jit(solution)/shard_map/dot_general | solution.py:493
  194.3 10.6 %shard_map.226 = (bf16[512,1536]{1,0:T(8,128)(2,1)}, f32[512,128]{1,0:T(8,128)}) custom-call(bf16[512,3072]{1,0:T(8,128)(2,1)} %get-tuple-element.344.gated_ref, bf16[3072,1536]{1,0:T(8,128)(2,1)} %all-gather.2.cloned.1.call-done.weight_ref, bf16[512,1536]{1,0:T(8,128)(2,1)} %bitcast.34, bf16[512,1536]{1,0:T(8,128)(2,1)} %bitcast.26, ...), custom_call_target="tpu_custom_call" | custom-call | flops 3221225472 | bytes 8388608 | tf_op jit(solution)/shard_map/pallas_call | solution.py:574
  210.5 15.2 %shard_map.227 = (bf16[512,3072]{1,0:T(8,128)(2,1)}, bf16[512,3072]{1,0:T(8,128)(2,1)}, f32[8,3072]{1,0:T(8,128)}) custom-call(f32[512,3072]{1,0:T(8,128)} %get-tuple-element.353.z_ref, f32[512,3072]{1,0:T(8,128)} %get-tuple-element.336.ssm_ref, bf16[512,1536]{1,0:T(8,128)(2,1)} %bitcast.27, bf16[3072,1536]{1,0:T(8,128)(2,1)} %all-gather.2.cloned.1.call-done.weight_ref, ...), custom_call_target="tpu_custom_call" | custom-call | flops 4000000000 | bytes 12000000 | tf_op jit(solution)/shard_map/pallas_call | solution.py:443
  225.7 3.2 add_convert_fusion.1
  229.0 3.4 add_convert_fusion
  232.4 7.5 %fusion.26 = bf16[1536,3072]{1,0:T(8,128)(2,1)} fusion(bf16[512,1536]{1,0:T(8,128)(2,1)S(1)} %copy-done.8, bf16[512,3072]{1,0:T(8,128)(2,1)S(1)} %copy-done.16), kind=kOutput, calls=%fused_computation.80 | convolution fusion | flops 4831838208 | bytes 14155776 | tf_op jit(solution)/shard_map/dot_general | solution.py:493
  243.3 26.2 %shard_map.228 = (bf16[512,2048]{1,0:T(8,128)(2,1)}, f32[8,2048]{1,0:T(8,128)}, f32[512,768]{1,0:T(8,128)}, f32[8,2048]{1,0:T(8,128)}) custom-call(s32[1]{0:T(128)} %bitcast.41, f32[512,3072]{1,0:T(8,128)} %get-tuple-element.313.x_ref, f32[512,3072]{1,0:T(8,128)} %get-tuple-element.336.ssm_ref, bf16[512,3072]{1,0:T(8,128)(2,1)} %get-tuple-element.377.ds_ref, ...), custom_call_target="tpu_custom_call" | custom-call | flops 9333332992 | bytes 10666666 | tf_op jit(solution)/shard_map/pallas_call | solution.py:463
  269.5 5.0 %convolution_convert_fusion.1 = bf16[768,2048]{1,0:T(8,128)(2,1)} fusion(bf16[512,2048]{1,0:T(8,128)(2,1)} %get-tuple-element.372.right_ref.refs_2_, bf16[1536,512]{1,0:T(8,128)(2,1)S(1)} %copy-done.9), kind=kOutput, calls=%fused_computation.5 | convolution fusion | flops 1612185600 | bytes 6029312 | tf_op jit(solution)/shard_map/dot_general | solution.py:851
  277.0 2.9 collective-permute-start.26
  281.2 15.1 %shard_map.229 = (bf16[512,1024]{1,0:T(8,128)(2,1)}, f32[8,1024]{1,0:T(8,128)}, f32[512,768]{1,0:T(8,128)}, f32[8,1024]{1,0:T(8,128)}) custom-call(s32[1]{0:T(128)} %bitcast.42, f32[512,3072]{1,0:T(8,128)} %get-tuple-element.313.x_ref, f32[512,3072]{1,0:T(8,128)} %get-tuple-element.336.ssm_ref, bf16[512,3072]{1,0:T(8,128)(2,1)} %get-tuple-element.377.ds_ref, ...), custom_call_target="tpu_custom_call" | custom-call | flops 4666666496 | bytes 5333333 | tf_op jit(solution)/shard_map/pallas_call | solution.py:463
  296.3 6.4 %shard_map.230 = (bf16[512,384]{1,0:T(8,128)(2,1)}, f32[8,256]{1,0:T(8,128)}, f32[8,128]{1,0:T(8,128)}) custom-call(s32[1]{0:T(128)} %bitcast.43, f32[512,384]{1,0:T(8,128)} %get-tuple-element.382.bcd_ref, f32[8,256]{1,0:T(8,128)} %slice.139.conv_ref, f32[8,128]{1,0:T(8,128)} %get-tuple-element.383.head_ref, bf16[512,256]{1,0:T(8,128)(2,1)} %get-tuple-element.318.bc_ref, ...), custom_call_target="tpu_custom_call" | custom-call | flops 1333333376 | bytes 2666666 | tf_op jit(solution)/shard_map/pallas_call | solution.py:480
  302.8 6.2 %shard_map.231 = (bf16[192,2048]{1,0:T(8,128)(2,1)}, bf16[192,2048]{1,0:T(8,128)(2,1)}, bf16[192,2048]{1,0:T(8,128)(2,1)}, f32[192,2048]{1,0:T(8,128)}) custom-call(bf16[1536,512]{1,0:T(8,128)(2,1)} %get-tuple-element.303.left_ref, bf16[512,2048]{1,0:T(8,128)(2,1)} %get-tuple-element.372.right_ref.refs_2_, bf16[768,2048]{1,0:T(8,128)(2,1)} %collective-permute-done.27.got_ref), custom_call_target="tpu_custom_call" | custom-call | flops 536870912 | bytes 3145728 | tf_op jit(solution)/shard_map/pallas_call | solution.py:709
  310.5 2.7 convolution_convert_fusion.2
  314.3 2.7 reduce-scatter.2.cloned.1.call-done
  325.1 11.0 %collective-permute-done.28 = bf16[96,1536]{1,0:T(8,128)(2,1)} collective-permute-done((bf16[96,1536]{1,0:T(8,128)(2,1)}, bf16[96,1536]{1,0:T(8,128)(2,1)}, u32[]{:S(2)}, u32[]{:S(2)}) %collective-permute-start.28) | collective-permute-done | bytes 294944 | tf_op jit(solution)/shard_map/ppermute | solution.py:922
  336.6 21.9 %shard_map.232.d_ref = f32[512,1536]{1,0:T(8,128)} custom-call(bf16[512,3072]{1,0:T(8,128)(2,1)} %get-tuple-element.364.refs_0_, bf16[1536,3072]{1,0:T(8,128)(2,1)} %get-tuple-element.404.refs_1_, bf16[512,2048]{1,0:T(8,128)(2,1)} %get-tuple-element.372.right_ref.refs_2_, bf16[1536,3072]{1,0:T(8,128)(2,1)} %get-tuple-element.405.refs_3_.refs_5_, ...), custom_call_target="tpu_custom_call" | custom-call | flops 1000 | bytes 1000 | tf_op jit(solution)/shard_map/pallas_call | solution.py:657
  363.3 5.2 %shard_map.233 = (bf16[192,1408]{1,0:T(8,128)(2,1)}, bf16[192,1408]{1,0:T(8,128)(2,1)}, bf16[192,1408]{1,0:T(8,128)(2,1)}, f32[192,1408]{1,0:T(8,128)}) custom-call(bf16[1536,512]{1,0:T(8,128)(2,1)} %get-tuple-element.303.left_ref, bf16[512,1408]{1,0:T(8,128)(2,1)} %copy-done.14, bf16[768,1408]{1,0:T(8,128)(2,1)} %copy-done.21), custom_call_target="tpu_custom_call" | custom-call | flops 369098752 | bytes 2162688 | tf_op jit(solution)/shard_map/pallas_call | solution.py:709
  368.8 2.8 collective-permute-start.34
  375.1 9.9 %collective-permute-done.34 = bf16[96,1536]{1,0:T(8,128)(2,1)S(1)} collective-permute-done((bf16[96,1536]{1,0:T(8,128)(2,1)S(1)}, bf16[96,1536]{1,0:T(8,128)(2,1)S(1)}, u32[]{:S(2)}, u32[]{:S(2)}) %collective-permute-start.34) | collective-permute-done | bytes 294944 | tf_op jit(solution)/shard_map/ppermute | solution.py:922
  385.0 5.0 %shard_map.234 = (bf16[512,1536]{1,0:T(8,128)(2,1)}, f32[8,1536]{1,0:T(8,128)}) custom-call(f32[512,1536]{1,0:T(8,128)} %shard_map.232.d_ref, bf16[512,1536]{1,0:T(8,128)(2,1)} %bitcast.35, bf16[512,1536]{1,0:T(8,128)(2,1)} %bitcast.28, f32[1,1536]{1,0:T(1,128)} %get-tuple-element.425.gain_ref), custom_call_target="tpu_custom_call" | custom-call | flops 1000 | bytes 1000 | tf_op jit(solution)/shard_map/pallas_call | solution.py:795
  392.5 7.6 %collective-permute-done.39 = bf16[48,3072]{1,0:T(8,128)(2,1)S(1)} collective-permute-done((bf16[48,3072]{1,0:T(8,128)(2,1)S(1)}, bf16[48,3072]{1,0:T(8,128)(2,1)S(1)}, u32[]{:S(2)}, u32[]{:S(2)}) %collective-permute-start.39) | collective-permute-done | bytes 294944 | tf_op jit(solution)/shard_map/ppermute | solution.py:922
  405.1 4.3 all-to-all-start.2
  409.6 2.9 collective-permute-start.41
  412.5 21.2 %collective-permute-done.41 = bf16[48,5120]{1,0:T(8,128)(2,1)S(1)} collective-permute-done((bf16[48,5120]{1,0:T(8,128)(2,1)S(1)}, bf16[48,5120]{1,0:T(8,128)(2,1)S(1)}, u32[]{:S(2)}, u32[]{:S(2)}) %collective-permute-start.41) | collective-permute-done | bytes 491552 | tf_op jit(solution)/shard_map/ppermute | solution.py:922
  433.8 7.7 %collective-permute-done.42 = bf16[96,1408]{1,0:T(8,128)(2,1)} collective-permute-done((bf16[96,1408]{1,0:T(8,128)(2,1)}, bf16[96,1408]{1,0:T(8,128)(2,1)}, u32[]{:S(2)}, u32[]{:S(2)}) %collective-permute-start.42) | collective-permute-done | bytes 270368 | tf_op jit(solution)/shard_map/ppermute | solution.py:922
  442.9 4.3 all-to-all-start.3
  447.7 2.6 collective-permute-start.44
  450.3 2.8 collective-permute-start.46
  453.8 3.0 fusion.1
  456.8 2.7 shard_map.236
  459.4 8.4 %collective-permute-done.44 = bf16[48,3456]{1,0:T(8,128)(2,1)S(1)} collective-permute-done((bf16[48,3456]{1,0:T(8,128)(2,1)S(1)}, bf16[48,3456]{1,0:T(8,128)(2,1)S(1)}, u32[]{:S(2)}, u32[]{:S(2)}) %collective-permute-start.44) | collective-permute-done | bytes 331808 | tf_op jit(solution)/shard_map/ppermute | solution.py:922
  478.9 2.7 shard_map.237
  481.6 3.3 collective-permute-done.51
  485.9 2.6 maximum_convert_fusion
  (298 shorter events, 98.2 us)
Async XLA Ops:
  12.7 33.5 %collective-permute-start = (bf16[192,3456]{1,0:T(8,128)(2,1)}, bf16[192,3456]{1,0:T(8,128)(2,1)S(1)}, u32[]{:S(2)}, u32[]{:S(2)}) collective-permute-start(bf16[192,3456]{1,0:T(8,128)(2,1)} %pad_slice_fusion.refs_0_), channel_id=1, source_target_pairs={{0,2},{1,3},{2,0},{3,1},{4,6},{5,7},{6,4},{7,5},{8,10},{9,11},{10,... | collective-permute-start | bytes 3981320 | tf_op jit(solution)/shard_map/ppermute | solution.py:922
  15.6 32.4 %collective-permute-start.1 = (bf16[192,3456]{1,0:T(8,128)(2,1)}, bf16[192,3456]{1,0:T(8,128)(2,1)}, u32[]{:S(2)}, u32[]{:S(2)}) collective-permute-start(bf16[192,3456]{1,0:T(8,128)(2,1)} %pad_slice_fusion.refs_0_), channel_id=1, source_target_pairs={{0,4},{1,5},{2,6},{3,7},{4,0},{5,1},{6,2},{7,3},{8,12},{9,13},{10,... | collective-permute-start | bytes 3981320 | tf_op jit(solution)/shard_map/ppermute | solution.py:922
  17.4 28.7 %collective-permute-start.2 = (bf16[16,416]{1,0:T(8,128)(2,1)S(1)}, bf16[16,416]{1,0:T(8,128)(2,1)S(1)}, u32[]{:S(2)}, u32[]{:S(2)}) collective-permute-start(bf16[16,416]{1,0:T(8,128)(2,1)S(1)} %pad.49), channel_id=1, source_target_pairs={{0,2},{1,3},{2,0},{3,1},{4,6},{5,7},{6,4},{7,5},{8,10},{9,11},{10,... | collective-permute-start | bytes 39944 | tf_op jit(solution)/shard_map/ppermute | solution.py:1012
  18.0 60.2 %all-to-all-start = ((bf16[8,64,1536]{2,1,0:T(8,128)(2,1)}), bf16[8,64,1536]{2,1,0:T(8,128)(2,1)S(1)}, u32[]{:S(2)}, u32[]{:S(2)}) async-start(bf16[8,64,1536]{2,1,0:T(8,128)(2,1)} %gather_fusion), calls=%async_computation | async-start | bytes 3145728 | tf_op jit(solution)/shard_map/all_to_all | solution.py:921
  21.6 172.7 %all-gather.2.cloned.1.call-start = ((), (), s32[]{:S(2)}) async-start(), calls=%async_computation.5 | async-start | bytes 10616832 | tf_op jit(solution)/shard_map/all_gather | solution.py:1022
  50.9 27.4 %collective-permute-start.5 = (bf16[192,3456]{1,0:T(8,128)(2,1)}, bf16[192,3456]{1,0:T(8,128)(2,1)}, u32[]{:S(2)}, u32[]{:S(2)}) collective-permute-start(bf16[192,3456]{1,0:T(8,128)(2,1)} %pad_slice_fusion.refs_0_), channel_id=1, source_target_pairs={{0,1},{1,0},{2,3},{3,2},{4,5},{5,4},{6,7},{7,6},{8,9},{9,8},{10,11... | collective-permute-start | bytes 3981320 | tf_op jit(solution)/shard_map/ppermute | solution.py:922
  50.9 27.4 %collective-permute-start.6 = (bf16[192,3456]{1,0:T(8,128)(2,1)S(1)}, bf16[192,3456]{1,0:T(8,128)(2,1)}, u32[]{:S(2)}, u32[]{:S(2)}) collective-permute-start(bf16[192,3456]{1,0:T(8,128)(2,1)S(1)} %collective-permute-done.refs_2_), channel_id=1, source_target_pairs={{0,1},{1,0},{2,3},{3,2},{4,5},{5,4},{6,7},{7,6},{8,9},{9,8},{10,11... | collective-permute-start | bytes 3981320 | tf_op jit(solution)/shard_map/ppermute | solution.py:922
  51.4 26.9 %collective-permute-start.3 = (bf16[96,3456]{1,0:T(8,128)(2,1)}, bf16[96,3456]{1,0:T(8,128)(2,1)}, u32[]{:S(2)}, u32[]{:S(2)}) collective-permute-start(bf16[96,3456]{1,0:T(8,128)(2,1)} %slice.120), channel_id=1, source_target_pairs={{0,4},{1,5},{2,6},{3,7},{4,0},{5,1},{6,2},{7,3},{8,12},{9,13},{10,... | collective-permute-start | bytes 1990664 | tf_op jit(solution)/shard_map/ppermute | solution.py:922
  52.9 25.3 %collective-permute-start.4 = (bf16[96,3456]{1,0:T(8,128)(2,1)}, bf16[96,3456]{1,0:T(8,128)(2,1)}, u32[]{:S(2)}, u32[]{:S(2)}) collective-permute-start(bf16[96,3456]{1,0:T(8,128)(2,1)} %slice.121), channel_id=1, source_target_pairs={{0,2},{1,3},{2,0},{3,1},{4,6},{5,7},{6,4},{7,5},{8,10},{9,11},{10,... | collective-permute-start | bytes 1990664 | tf_op jit(solution)/shard_map/ppermute | solution.py:922
  57.6 20.6 %collective-permute-start.7 = (bf16[32,416]{1,0:T(8,128)(2,1)S(1)}, bf16[32,416]{1,0:T(8,128)(2,1)S(1)}, u32[]{:S(2)}, u32[]{:S(2)}) collective-permute-start(bf16[32,416]{1,0:T(8,128)(2,1)S(1)} %pad_maximum_fusion.7), channel_id=1, source_target_pairs={{0,4},{1,5},{2,6},{3,7},{4,0},{5,1},{6,2},{7,3},{8,12},{9,13},{10,... | collective-permute-start | bytes 79880 | tf_op jit(solution)/shard_map/ppermute | solution.py:1012
  80.2 40.7 %collective-permute-start.8 = (bf16[192,3072]{1,0:T(8,128)(2,1)S(1)}, bf16[192,3072]{1,0:T(8,128)(2,1)S(1)}, u32[]{:S(2)}, u32[]{:S(2)}) collective-permute-start(bf16[192,3072]{1,0:T(8,128)(2,1)S(1)} %slice.119.refs_0_), channel_id=1, source_target_pairs={{0,2},{1,3},{2,0},{3,1},{4,6},{5,7},{6,4},{7,5},{8,10},{9,11},{10,... | collective-permute-start | bytes 3538952 | tf_op jit(solution)/shard_map/ppermute | solution.py:922
  80.6 40.3 %collective-permute-start.9 = (bf16[192,3072]{1,0:T(8,128)(2,1)S(1)}, bf16[192,3072]{1,0:T(8,128)(2,1)S(1)}, u32[]{:S(2)}, u32[]{:S(2)}) collective-permute-start(bf16[192,3072]{1,0:T(8,128)(2,1)S(1)} %slice.119.refs_0_), channel_id=1, source_target_pairs={{0,4},{1,5},{2,6},{3,7},{4,0},{5,1},{6,2},{7,3},{8,12},{9,13},{10,... | collective-permute-start | bytes 3538952 | tf_op jit(solution)/shard_map/ppermute | solution.py:922
  122.8 31.2 %collective-permute-start.16 = (bf16[192,3072]{1,0:T(8,128)(2,1)S(1)}, bf16[192,3072]{1,0:T(8,128)(2,1)S(1)}, u32[]{:S(2)}, u32[]{:S(2)}) collective-permute-start(bf16[192,3072]{1,0:T(8,128)(2,1)S(1)} %slice.119.refs_0_), channel_id=1, source_target_pairs={{0,1},{1,0},{2,3},{3,2},{4,5},{5,4},{6,7},{7,6},{8,9},{9,8},{10,11... | collective-permute-start | bytes 3538952 | tf_op jit(solution)/shard_map/ppermute | solution.py:922
  122.8 31.2 %collective-permute-start.17 = (bf16[192,3072]{1,0:T(8,128)(2,1)S(1)}, bf16[192,3072]{1,0:T(8,128)(2,1)S(1)}, u32[]{:S(2)}, u32[]{:S(2)}) collective-permute-start(bf16[192,3072]{1,0:T(8,128)(2,1)S(1)} %collective-permute-done.8.refs_2_), channel_id=1, source_target_pairs={{0,1},{1,0},{2,3},{3,2},{4,5},{5,4},{6,7},{7,6},{8,9},{9,8},{10,11... | collective-permute-start | bytes 3538952 | tf_op jit(solution)/shard_map/ppermute | solution.py:922
  123.3 30.7 %collective-permute-start.18 = (bf16[192,3072]{1,0:T(8,128)(2,1)S(1)}, bf16[192,3072]{1,0:T(8,128)(2,1)S(1)}, u32[]{:S(2)}, u32[]{:S(2)}) collective-permute-start(bf16[192,3072]{1,0:T(8,128)(2,1)S(1)} %collective-permute-done.9.refs_4_), channel_id=1, source_target_pairs={{0,1},{1,0},{2,3},{3,2},{4,5},{5,4},{6,7},{7,6},{8,9},{9,8},{10,11... | collective-permute-start | bytes 3538952 | tf_op jit(solution)/shard_map/ppermute | solution.py:922
  123.3 28.9 %collective-permute-start.14 = (bf16[96,3072]{1,0:T(8,128)(2,1)}, bf16[96,3072]{1,0:T(8,128)(2,1)S(1)}, u32[]{:S(2)}, u32[]{:S(2)}) collective-permute-start(bf16[96,3072]{1,0:T(8,128)(2,1)} %slice.124), channel_id=1, source_target_pairs={{0,4},{1,5},{2,6},{3,7},{4,0},{5,1},{6,2},{7,3},{8,12},{9,13},{10,... | collective-permute-start | bytes 1769480 | tf_op jit(solution)/shard_map/ppermute | solution.py:922
  125.1 28.9 %collective-permute-start.15 = (bf16[96,3072]{1,0:T(8,128)(2,1)}, bf16[96,3072]{1,0:T(8,128)(2,1)}, u32[]{:S(2)}, u32[]{:S(2)}) collective-permute-start(bf16[96,3072]{1,0:T(8,128)(2,1)} %slice.125), channel_id=1, source_target_pairs={{0,2},{1,3},{2,0},{3,1},{4,6},{5,7},{6,4},{7,5},{8,10},{9,11},{10,... | collective-permute-start | bytes 1769480 | tf_op jit(solution)/shard_map/ppermute | solution.py:922
  156.0 31.7 %all-to-all-start.1 = ((bf16[8,64,1536]{2,1,0:T(8,128)(2,1)}), bf16[8,64,1536]{2,1,0:T(8,128)(2,1)S(1)}, u32[]{:S(2)}, u32[]{:S(2)}) async-start(bf16[8,64,1536]{2,1,0:T(8,128)(2,1)} %gather_fusion.1), calls=%async_computation.1 | async-start | bytes 3145728 | tf_op jit(solution)/shard_map/all_to_all | solution.py:921
  159.6 157.5 %reduce-scatter.2.cloned.1.call-start = ((), (), s32[]{:S(2)}) async-start(), calls=%async_computation.6 | async-start | bytes 10616832 | tf_op jit(solution)/shard_map/reduce_scatter | solution.py:1094
  207.2 18.5 %collective-permute-start.22 = (bf16[192,1536]{1,0:T(8,128)(2,1)S(1)}, bf16[192,1536]{1,0:T(8,128)(2,1)S(1)}, u32[]{:S(2)}, u32[]{:S(2)}) collective-permute-start(bf16[192,1536]{1,0:T(8,128)(2,1)S(1)} %get-tuple-element.351), channel_id=1, source_target_pairs={{0,2},{1,3},{2,0},{3,1},{4,6},{5,7},{6,4},{7,5},{8,10},{9,11},{10,... | collective-permute-start | bytes 1769480 | tf_op jit(solution)/shard_map/ppermute | solution.py:922
  208.9 16.8 %collective-permute-start.23 = (bf16[192,1536]{1,0:T(8,128)(2,1)S(1)}, bf16[192,1536]{1,0:T(8,128)(2,1)S(1)}, u32[]{:S(2)}, u32[]{:S(2)}) collective-permute-start(bf16[192,1536]{1,0:T(8,128)(2,1)S(1)} %get-tuple-element.352), channel_id=1, source_target_pairs={{0,4},{1,5},{2,6},{3,7},{4,0},{5,1},{6,2},{7,3},{8,12},{9,13},{10,... | collective-permute-start | bytes 1769480 | tf_op jit(solution)/shard_map/ppermute | solution.py:922
  239.9 29.6 %collective-permute-start.24 = (bf16[384,1536]{1,0:T(8,128)(2,1)}, bf16[384,1536]{1,0:T(8,128)(2,1)S(1)}, u32[]{:S(2)}, u32[]{:S(2)}) collective-permute-start(bf16[384,1536]{1,0:T(8,128)(2,1)} %add_convert_fusion.1), channel_id=1, source_target_pairs={{0,2},{1,3},{2,0},{3,1},{4,6},{5,7},{6,4},{7,5},{8,10},{9,11},{10,... | collective-permute-start | bytes 3538952 | tf_op jit(solution)/shard_map/ppermute | solution.py:922
  240.0 29.5 %collective-permute-start.25 = (bf16[384,1536]{1,0:T(8,128)(2,1)}, bf16[384,1536]{1,0:T(8,128)(2,1)}, u32[]{:S(2)}, u32[]{:S(2)}) collective-permute-start(bf16[384,1536]{1,0:T(8,128)(2,1)} %add_convert_fusion), channel_id=1, source_target_pairs={{0,4},{1,5},{2,6},{3,7},{4,0},{5,1},{6,2},{7,3},{8,12},{9,13},{10,... | collective-permute-start | bytes 3538952 | tf_op jit(solution)/shard_map/ppermute | solution.py:922
  276.9 25.8 %collective-permute-start.27 = (bf16[768,2048]{1,0:T(8,128)(2,1)}, bf16[768,2048]{1,0:T(8,128)(2,1)}, u32[]{:S(2)}, u32[]{:S(2)}) collective-permute-start(bf16[768,2048]{1,0:T(8,128)(2,1)} %convolution_convert_fusion.1), channel_id=1, source_target_pairs={{0,1},{1,0},{2,3},{3,2},{4,5},{5,4},{6,7},{7,6},{8,9},{9,8},{10,11... | collective-permute-start | bytes 9437192 | tf_op jit(solution)/shard_map/ppermute | solution.py:922
  277.0 25.7 %collective-permute-start.26 = (bf16[192,1536]{1,0:T(8,128)(2,1)S(1)}, bf16[192,1536]{1,0:T(8,128)(2,1)S(1)}, u32[]{:S(2)}, u32[]{:S(2)}) collective-permute-start(bf16[192,1536]{1,0:T(8,128)(2,1)S(1)} %select_convert_fusion), channel_id=1, source_target_pairs={{0,8},{8,0},{16,24},{24,16},{1,9},{9,1},{17,25},{25,17},{2,10},{10... | collective-permute-start | bytes 1769480 | tf_op jit(solution)/shard_map/ppermute | solution.py:922
  319.2 40.9 %collective-permute-start.32 = (bf16[768,1408]{1,0:T(8,128)(2,1)}, bf16[768,1408]{1,0:T(8,128)(2,1)S(1)}, u32[]{:S(2)}, u32[]{:S(2)}) collective-permute-start(bf16[768,1408]{1,0:T(8,128)(2,1)} %convolution_convert_fusion.2), channel_id=1, source_target_pairs={{0,1},{1,0},{2,3},{3,2},{4,5},{5,4},{6,7},{7,6},{8,9},{9,8},{10,11... | collective-permute-start | bytes 6488072 | tf_op jit(solution)/shard_map/ppermute | solution.py:922
  319.2 17.0 %collective-permute-start.28 = (bf16[96,1536]{1,0:T(8,128)(2,1)}, bf16[96,1536]{1,0:T(8,128)(2,1)}, u32[]{:S(2)}, u32[]{:S(2)}) collective-permute-start(bf16[96,1536]{1,0:T(8,128)(2,1)} %select_convert_fusion.3), channel_id=1, source_target_pairs={{0,16},{8,24},{16,0},{24,8},{1,17},{9,25},{17,1},{25,9},{2,18},{10... | collective-permute-start | bytes 884744 | tf_op jit(solution)/shard_map/ppermute | solution.py:922
  321.6 36.9 %collective-permute-start.29 = (bf16[192,2048]{1,0:T(8,128)(2,1)}, bf16[192,2048]{1,0:T(8,128)(2,1)S(1)}, u32[]{:S(2)}, u32[]{:S(2)}) collective-permute-start(bf16[192,2048]{1,0:T(8,128)(2,1)} %get-tuple-element.399), channel_id=1, source_target_pairs={{0,6},{1,7},{2,4},{3,5},{4,2},{5,3},{6,0},{7,1},{8,14},{9,15},{10,... | collective-permute-start | bytes 2359304 | tf_op jit(solution)/shard_map/ppermute | solution.py:922
  323.0 36.1 %collective-permute-start.30 = (bf16[192,2048]{1,0:T(8,128)(2,1)}, bf16[192,2048]{1,0:T(8,128)(2,1)S(1)}, u32[]{:S(2)}, u32[]{:S(2)}) collective-permute-start(bf16[192,2048]{1,0:T(8,128)(2,1)} %get-tuple-element.400), channel_id=1, source_target_pairs={{0,2},{1,3},{2,0},{3,1},{4,6},{5,7},{6,4},{7,5},{8,10},{9,11},{10,... | collective-permute-start | bytes 2359304 | tf_op jit(solution)/shard_map/ppermute | solution.py:922
  324.4 34.8 %collective-permute-start.31 = (bf16[192,2048]{1,0:T(8,128)(2,1)}, bf16[192,2048]{1,0:T(8,128)(2,1)S(1)}, u32[]{:S(2)}, u32[]{:S(2)}) collective-permute-start(bf16[192,2048]{1,0:T(8,128)(2,1)} %get-tuple-element.401), channel_id=1, source_target_pairs={{0,4},{1,5},{2,6},{3,7},{4,0},{5,1},{6,2},{7,3},{8,12},{9,13},{10,... | collective-permute-start | bytes 2359304 | tf_op jit(solution)/shard_map/ppermute | solution.py:922
  336.1 22.4 %collective-permute-start.33 = (bf16[96,3072]{1,0:T(8,128)(2,1)}, bf16[96,3072]{1,0:T(8,128)(2,1)S(1)}, u32[]{:S(2)}, u32[]{:S(2)}) collective-permute-start(bf16[96,3072]{1,0:T(8,128)(2,1)} %broadcast_select_fusion), channel_id=1, source_target_pairs={{0,8},{8,0},{16,24},{24,16},{1,9},{9,1},{17,25},{25,17},{2,10},{10... | collective-permute-start | bytes 1769480 | tf_op jit(solution)/shard_map/ppermute | solution.py:922
  368.8 16.2 %collective-permute-start.34 = (bf16[96,1536]{1,0:T(8,128)(2,1)S(1)}, bf16[96,1536]{1,0:T(8,128)(2,1)S(1)}, u32[]{:S(2)}, u32[]{:S(2)}) collective-permute-start(bf16[96,1536]{1,0:T(8,128)(2,1)S(1)} %add_convert_fusion.4), channel_id=1, source_target_pairs={{0,16},{8,24},{16,0},{24,8},{1,17},{9,25},{17,1},{25,9},{2,18},{10... | collective-permute-start | bytes 884744 | tf_op jit(solution)/shard_map/ppermute | solution.py:922
  371.6 28.5 %collective-permute-start.36 = (bf16[192,1408]{1,0:T(8,128)(2,1)}, bf16[192,1408]{1,0:T(8,128)(2,1)S(1)}, u32[]{:S(2)}, u32[]{:S(2)}) collective-permute-start(bf16[192,1408]{1,0:T(8,128)(2,1)} %get-tuple-element.420), channel_id=1, source_target_pairs={{0,6},{1,7},{2,4},{3,5},{4,2},{5,3},{6,0},{7,1},{8,14},{9,15},{10,... | collective-permute-start | bytes 1622024 | tf_op jit(solution)/shard_map/ppermute | solution.py:922
  373.1 27.0 %collective-permute-start.37 = (bf16[192,1408]{1,0:T(8,128)(2,1)S(1)}, bf16[192,1408]{1,0:T(8,128)(2,1)S(1)}, u32[]{:S(2)}, u32[]{:S(2)}) collective-permute-start(bf16[192,1408]{1,0:T(8,128)(2,1)S(1)} %copy-done.53), channel_id=1, source_target_pairs={{0,2},{1,3},{2,0},{3,1},{4,6},{5,7},{6,4},{7,5},{8,10},{9,11},{10,... | collective-permute-start | bytes 1622024 | tf_op jit(solution)/shard_map/ppermute | solution.py:922
  374.4 25.7 %collective-permute-start.38 = (bf16[192,1408]{1,0:T(8,128)(2,1)S(1)}, bf16[192,1408]{1,0:T(8,128)(2,1)S(1)}, u32[]{:S(2)}, u32[]{:S(2)}) collective-permute-start(bf16[192,1408]{1,0:T(8,128)(2,1)S(1)} %copy-done.52), channel_id=1, source_target_pairs={{0,4},{1,5},{2,6},{3,7},{4,0},{5,1},{6,2},{7,3},{8,12},{9,13},{10,... | collective-permute-start | bytes 1622024 | tf_op jit(solution)/shard_map/ppermute | solution.py:922
  375.1 25.0 %collective-permute-start.35 = (bf16[96,2048]{1,0:T(8,128)(2,1)S(1)}, bf16[96,2048]{1,0:T(8,128)(2,1)S(1)}, u32[]{:S(2)}, u32[]{:S(2)}) collective-permute-start(bf16[96,2048]{1,0:T(8,128)(2,1)S(1)} %select_convert_fusion.1), channel_id=1, source_target_pairs={{0,8},{8,0},{16,24},{24,16},{1,9},{9,1},{17,25},{25,17},{2,10},{10... | collective-permute-start | bytes 1179656 | tf_op jit(solution)/shard_map/ppermute | solution.py:922
  385.0 15.1 %collective-permute-start.39 = (bf16[48,3072]{1,0:T(8,128)(2,1)S(1)}, bf16[48,3072]{1,0:T(8,128)(2,1)S(1)}, u32[]{:S(2)}, u32[]{:S(2)}) collective-permute-start(bf16[48,3072]{1,0:T(8,128)(2,1)S(1)} %select_convert_fusion.2), channel_id=1, source_target_pairs={{0,16},{8,24},{16,0},{24,8},{1,17},{9,25},{17,1},{25,9},{2,18},{10... | collective-permute-start | bytes 884744 | tf_op jit(solution)/shard_map/ppermute | solution.py:922
  405.1 36.4 %all-to-all-start.2 = ((bf16[8,64,1536]{2,1,0:T(8,128)(2,1)}), bf16[8,64,1536]{2,1,0:T(8,128)(2,1)}, u32[]{:S(2)}, u32[]{:S(2)}) async-start(bf16[8,64,1536]{2,1,0:T(8,128)(2,1)} %bitcast.37), calls=%async_computation.3 | async-start | bytes 3145728 | tf_op jit(solution)/shard_map/all_to_all | solution.py:921
  409.4 32.0 %collective-permute-start.40 = (bf16[192,1536]{1,0:T(8,128)(2,1)S(1)}, bf16[192,1536]{1,0:T(8,128)(2,1)}, u32[]{:S(2)}, u32[]{:S(2)}) collective-permute-start(bf16[192,1536]{1,0:T(8,128)(2,1)S(1)} %maximum_select_fusion.3), channel_id=1, source_target_pairs={{0,8},{8,0},{16,24},{24,16},{1,9},{9,1},{17,25},{25,17},{2,10},{10... | collective-permute-start | bytes 1769480 | tf_op jit(solution)/shard_map/ppermute | solution.py:922
  409.6 24.1 %collective-permute-start.41 = (bf16[48,5120]{1,0:T(8,128)(2,1)S(1)}, bf16[48,5120]{1,0:T(8,128)(2,1)S(1)}, u32[]{:S(2)}, u32[]{:S(2)}) collective-permute-start(bf16[48,5120]{1,0:T(8,128)(2,1)S(1)} %pad_maximum_fusion.2), channel_id=1, source_target_pairs={{0,16},{8,24},{16,0},{24,8},{1,17},{9,25},{17,1},{25,9},{2,18},{10... | collective-permute-start | bytes 1474568 | tf_op jit(solution)/shard_map/ppermute | solution.py:922
  412.5 29.0 %collective-permute-start.42 = (bf16[96,1408]{1,0:T(8,128)(2,1)}, bf16[96,1408]{1,0:T(8,128)(2,1)}, u32[]{:S(2)}, u32[]{:S(2)}) collective-permute-start(bf16[96,1408]{1,0:T(8,128)(2,1)} %select_convert_fusion.4), channel_id=1, source_target_pairs={{0,8},{8,0},{16,24},{24,16},{1,9},{9,1},{17,25},{25,17},{2,10},{10... | collective-permute-start | bytes 811016 | tf_op jit(solution)/shard_map/ppermute | solution.py:922
  412.5 21.2 %collective-permute-start.43 = (f32[4,2688]{1,0:T(4,128)S(1)}, f32[4,2688]{1,0:T(4,128)S(1)}, u32[]{:S(2)}, u32[]{:S(2)}) collective-permute-start(f32[4,2688]{1,0:T(4,128)S(1)} %slice.168), channel_id=1, source_target_pairs={{0,1},{1,0},{2,3},{3,2},{4,5},{5,4},{6,7},{7,6},{8,9},{9,8},{10,11... | collective-permute-start | bytes 129032 | tf_op jit(solution)/shard_map/ppermute | solution.py:922
  442.9 27.2 %all-to-all-start.3 = ((bf16[8,64,1536]{2,1,0:T(8,128)(2,1)}), bf16[8,64,1536]{2,1,0:T(8,128)(2,1)}, u32[]{:S(2)}, u32[]{:S(2)}) async-start(bf16[8,64,1536]{2,1,0:T(8,128)(2,1)} %bitcast.36), calls=%async_computation.4 | async-start | bytes 3145728 | tf_op jit(solution)/shard_map/all_to_all | solution.py:921
  447.3 22.9 %collective-permute-start.45 = (bf16[96,3072]{1,0:T(8,128)(2,1)S(1)}, bf16[96,3072]{1,0:T(8,128)(2,1)}, u32[]{:S(2)}, u32[]{:S(2)}) collective-permute-start(bf16[96,3072]{1,0:T(8,128)(2,1)S(1)} %maximum_select_fusion.4), channel_id=1, source_target_pairs={{0,8},{8,0},{16,24},{24,16},{1,9},{9,1},{17,25},{25,17},{2,10},{10... | collective-permute-start | bytes 1769480 | tf_op jit(solution)/shard_map/ppermute | solution.py:922
  447.7 20.2 %collective-permute-start.44 = (bf16[48,3456]{1,0:T(8,128)(2,1)S(1)}, bf16[48,3456]{1,0:T(8,128)(2,1)S(1)}, u32[]{:S(2)}, u32[]{:S(2)}) collective-permute-start(bf16[48,3456]{1,0:T(8,128)(2,1)S(1)} %pad_maximum_fusion.3), channel_id=1, source_target_pairs={{0,16},{8,24},{16,0},{24,8},{1,17},{9,25},{17,1},{25,9},{2,18},{10... | collective-permute-start | bytes 995336 | tf_op jit(solution)/shard_map/ppermute | solution.py:922
  450.3 18.2 %collective-permute-start.46 = (f32[1,2688]{1,0:T(1,128)S(1)}, f32[1,2688]{1,0:T(1,128)S(1)}, u32[]{:S(2)}, u32[]{:S(2)}) collective-permute-start(f32[1,2688]{1,0:T(1,128)S(1)} %get-tuple-element.456), channel_id=1, source_target_pairs={{0,6},{1,7},{2,4},{3,5},{4,2},{5,3},{6,0},{7,1},{8,14},{9,15},{10,... | collective-permute-start | bytes 32264 | tf_op jit(solution)/shard_map/ppermute | solution.py:922
  453.1 15.4 %collective-permute-start.47 = (f32[1,2688]{1,0:T(1,128)S(1)}, f32[1,2688]{1,0:T(1,128)S(1)}, u32[]{:S(2)}, u32[]{:S(2)}) collective-permute-start(f32[1,2688]{1,0:T(1,128)S(1)} %get-tuple-element.457), channel_id=1, source_target_pairs={{0,2},{1,3},{2,0},{3,1},{4,6},{5,7},{6,4},{7,5},{8,10},{9,11},{10,... | collective-permute-start | bytes 32264 | tf_op jit(solution)/shard_map/ppermute | solution.py:922
  453.6 14.8 %collective-permute-start.48 = (f32[1,2688]{1,0:T(1,128)S(1)}, f32[1,2688]{1,0:T(1,128)S(1)}, u32[]{:S(2)}, u32[]{:S(2)}) collective-permute-start(f32[1,2688]{1,0:T(1,128)S(1)} %get-tuple-element.458), channel_id=1, source_target_pairs={{0,4},{1,5},{2,6},{3,7},{4,0},{5,1},{6,2},{7,3},{8,12},{9,13},{10,... | collective-permute-start | bytes 32264 | tf_op jit(solution)/shard_map/ppermute | solution.py:922
  (70 other events, 449.4 us)
Sparse Core Ops, SparseCore 0:
  78.4 85.1 all-gather.1
  240.0 76.9 reduce-scatter.1

commit v7 on v6

--- a/solution.py
+++ b/solution.py
@@ -1015,14 +1015,22 @@
         rows, span = in_weight.shape[0], DI + BCD
         w_xb = lax.pad(in_weight, jnp.zeros((), b16), ((0, 0, 0), (-DI, span + DI - in_weight.shape[1], 0)))
         e_xb = moves.add(gathered_rows(w_xb, True))
-        e_x = moves.add(dealt(blocks(tokens), 2))
-        (small,) = moves.turn(lambda *v: doubled(rows_of(v), 2), *own_small)
-        small, cot_blocks = moves.turn(lambda v, c: (*doubled(v, 4), blocks(c)), small, cotangent)
+
+        def deal_out(values):
+            return lax.all_to_all(values, "fsdp", split_axis=0, concat_axis=0, tiled=True)
+
+        def first_turn(tokens, *values):
+            ahead.append(deal_out(blocks(tokens)))
+            return doubled(rows_of(values), 2)
+
+        ahead = []
+        (small,) = moves.turn(first_turn, tokens, *own_small)
+        small, cot_blocks, x = moves.turn(lambda v, c: (*doubled(v, 4), blocks(c), ahead[0]), small, cotangent)
         out_weight = moves.after(out_weight)
         w_out = lax.all_gather(out_weight, "fsdp", axis=0, tiled=True)
         (small,) = moves.turn(lambda v: doubled(v, 1), small)
         pieces = e_xb["value"]
-        x = e_x["value"].reshape(tok_rows, width)
+        x = x.reshape(tok_rows, width)
         widths = (norm_gain.size, conv_bias.size, dt_bias.size, gated_gain.size)
     else:
         x = deal(tokens)
@@ -1111,9 +1119,10 @@
 
         def finish(d_normed):
             d_input, ngrads = run_norm_back(d_normed, x, cot, gain)
-            return d_input, run_pack(widths, [b[1] for b in backs], bgrads, hgrads, ggrads, ngrads)
-
-        d_input, packed = moves.turn(finish, d_normed)
+            ahead.append(deal_out(d_input.reshape(groups, block_rows, width)))
+            return (run_pack(widths, [b[1] for b in backs], bgrads, hgrads, ggrads, ngrads),)
+
+        (packed,) = moves.turn(finish, d_normed)
     else:
         dz, ds, ggrads = gate(rk)
         s_z = lax.psum_scatter(contract_rows(normed, dz, b16), "fsdp", scatter_dimension=0, tiled=True)
@@ -1153,16 +1162,12 @@
 
     if custom():
         e_small = moves.add(small_sum(packed))
-        e_input = moves.add(dealt(d_input.reshape(groups, block_rows, width), 1))
         moves.turn()
         e_output = moves.add(dealt(result.reshape(groups, block_rows, width), 1))
         moves.turn()
 
-        def restored(entry):
-            return run_restore(targets, entry["value"])
-
-        input_grad, r_out = moves.turn(lambda: (restored(e_input), widen(e_rows["value"])))
-        (output,) = moves.turn(lambda: (restored(e_output),))
+        input_grad, r_out = moves.turn(lambda: (run_restore(targets, ahead[1]), widen(e_rows["value"])))
+        (output,) = moves.turn(lambda: (run_restore(targets, e_output["value"]),))
         last = CALLS[-1][1] * LANES + tail
 
         def gather_up():

time: 509 us -> 503 us (0.988)
  waiting for transfers between devices: 143 us -> 137 us
    all_to_all x0 -> x2, starting transfers between devices: none -> 7.87 us  [deal_out(): lax.all_to_all(values, 'fsdp', split_axis=0, concat_axis=0, tiled=True)]
    all_to_all x4 -> x2, starting transfers between devices: 15.8 us -> 8.02 us  [transfer(): return lax.all_to_all(v, axis, split_axis=0, concat_axis=0, tiled=True)]
  transfers between devices with their start and end apart: 61 -> 61, of which waited for: 24 -> 24; matrix products, arithmetic and copies ran while one was open for 9% -> 10% of each run, Pallas kernels for 36% -> 36%
where the time goes in v7:
time: 503 us; the launch traced here: 494 us
  Pallas kernels  184 us (37%)
  waiting for transfers between devices  137 us (27%)
  starting transfers between devices  70.2 us (14%)
  local copies, waits for them, and re-layouts  32.9 us (7%)
  matrix products  32.1 us (6%)
  other arithmetic  22.8 us (5%)
  between operations  15.5 us (3%)
    ppermute x52, waiting for transfers between devices, transfer(): return lax.ppermute(v, axis, pairs)  94.1 us
    ppermute x52, starting transfers between devices, transfer(): return lax.ppermute(v, axis, pairs)  53.2 us
    pallas_call x2, Pallas kernels, run_backward(): pl.pallas_call(functools.partial(backward_kernel, base), grid=(count,), i...  41.5 us
    ppermute x3, waiting for transfers between devices, doubled(): return (jnp.concatenate([v, lax.ppermute(v, 'fsdp', partners(bit))]),)  38.8 us
    pallas_call x2, Pallas kernels, run_project(): pl.pallas_call(functools.partial(project_kernel, places), grid=(cols // s...  26.9 us
    dot_general x6, matrix products, contract_rows(): lax.dot_general(left, right, (((0,), (0,)), ((), ())), preferred_element_...  24.4 us
    pallas_call x1, Pallas kernels, run_back(): pl.pallas_call(functools.partial(back_kernel, tuple(spans), int(base is n...  21.8 us
    pallas_call x1, Pallas kernels, run_forward(): pl.pallas_call(forward_kernel, grid=(width // LANES,), in_specs=[smem(),...  20.1 us
  transfers between devices with their start and end apart: 61, of which 24 were waited for; matrix products, arithmetic and copies ran while one was open for 10% of the time, Pallas kernels for 36%

profile of v7, /device:TPU:0, one launch (start us, length us, event | category | flops | bytes accessed | tf_op | source)
XLA Modules:
  0.0 494.4 jit_solution(3374868978428827776)
XLA Ops:
  7.3 2.6 pad_slice_fusion.refs_0_
  9.9 2.9 collective-permute-start
  17.9 3.6 all-to-all-start
  21.6 21.8 %collective-permute-done.2 = bf16[16,416]{1,0:T(8,128)(2,1)S(1)} collective-permute-done((bf16[16,416]{1,0:T(8,128)(2,1)S(1)}, bf16[16,416]{1,0:T(8,128)(2,1)S(1)}, u32[]{:S(2)}, u32[]{:S(2)}) %collective-permute-start.2) | collective-permute-done | bytes 13344 | tf_op jit(solution)/shard_map/ppermute | solution.py:1012
  51.2 4.7 collective-permute-start.4
  55.9 3.2 gather_fusion
  59.1 16.3 %collective-permute-done.7 = bf16[32,416]{1,0:T(8,128)(2,1)S(1)} collective-permute-done((bf16[32,416]{1,0:T(8,128)(2,1)S(1)}, bf16[32,416]{1,0:T(8,128)(2,1)S(1)}, u32[]{:S(2)}, u32[]{:S(2)}) %collective-permute-start.7) | collective-permute-done | bytes 26656 | tf_op jit(solution)/shard_map/ppermute | solution.py:1012
  75.6 3.3 slice.119.refs_0_
  85.4 8.0 %shard_map.221 = (f32[1,1536]{1,0:T(1,128)}, f32[8,3328]{1,0:T(8,128)}, f32[8,128]{1,0:T(8,128)}, f32[8,3072]{1,0:T(8,128)}, bf16[512,1536]{1,0:T(8,128)(2,1)}, ...) custom-call(s32[1]{0:T(128)} %bitcast.7.me_ref, ...), custom_call_target="tpu_custom_call" | custom-call | flops 2000000000 | bytes 3333333 | tf_op jit(solution)/shard_map/pallas_call | solution.py:766
  93.3 13.2 %shard_map.222 = (f32[512,3072]{1,0:T(8,128)}, bf16[1536,3072]{1,0:T(8,128)(2,1)}) custom-call(s32[1]{0:T(128)} %bitcast.7.me_ref, bf16[512,1536]{1,0:T(8,128)(2,1)} %get-tuple-element.321.left_ref, bf16[192,3456]{1,0:T(8,128)(2,1)} %pad_slice_fusion.refs_0_, bf16[192,3456]{1,0:T(8,128)(2,1)} %copy-done.10, bf16[192,3456]{1,0:T(8,128)(2,1)} %collective-permute-done.refs_2_, ...), custom_call_target="tpu_custom_call" | custom-call | flops 1610612736 | bytes 9437184 | tf_op jit(solution)/shard_map/pallas_call | solution.py:518
  106.5 12.7 %collective-permute-done.8.refs_2_ = bf16[192,3072]{1,0:T(8,128)(2,1)S(1)} collective-permute-done((bf16[192,3072]{1,0:T(8,128)(2,1)}, bf16[192,3072]{1,0:T(8,128)(2,1)S(1)}, u32[]{:S(2)}, u32[]{:S(2)}) %collective-permute-start.8) | collective-permute-done | bytes 1179680 | tf_op jit(solution)/shard_map/ppermute | solution.py:922
  125.4 20.1 %shard_map.223 = (f32[512,3072]{1,0:T(8,128)}, bf16[512,3072]{1,0:T(8,128)(2,1)}) custom-call(s32[1]{0:T(128)} %bitcast.40, f32[512,3072]{1,0:T(8,128)} %get-tuple-element.310.x_ref, f32[8,3072]{1,0:T(8,128)} %slice.126.conv_ref, f32[8,3072]{1,0:T(8,128)} %get-tuple-element.312.gain_ref, f32[512,512]{1,0:T(8,128)} %get-tuple-element.313.wide_ref, ...), custom_call_target="tpu_custom_call" | custom-call | flops 6666666496 | bytes 6666666 | tf_op jit(solution)/shard_map/pallas_call | solution.py:410
  145.5 4.9 collective-permute-done.14.refs_6_
  155.3 3.7 all-to-all-start.1
  163.3 13.7 %shard_map.224 = (f32[512,3072]{1,0:T(8,128)}, bf16[1536,3072]{1,0:T(8,128)(2,1)}) custom-call(s32[1]{0:T(128)} %bitcast.7.me_ref, bf16[512,1536]{1,0:T(8,128)(2,1)} %get-tuple-element.321.left_ref, bf16[192,3072]{1,0:T(8,128)(2,1)} %slice.119.refs_0_, bf16[192,3072]{1,0:T(8,128)(2,1)} %copy-done.21, bf16[192,3072]{1,0:T(8,128)(2,1)} %copy-done.17, ...), custom_call_target="tpu_custom_call" | custom-call | flops 1610612736 | bytes 9437184 | tf_op jit(solution)/shard_map/pallas_call | solution.py:518
  177.0 9.2 %shard_map.225 = (bf16[512,3072]{1,0:T(8,128)(2,1)}, bf16[512,3072]{1,0:T(8,128)(2,1)}, f32[512,128]{1,0:T(8,128)}) custom-call(s32[1]{0:T(128)} %bitcast.7.me_ref, f32[512,3072]{1,0:T(8,128)} %get-tuple-element.350.z_ref, f32[512,3072]{1,0:T(8,128)} %get-tuple-element.333.ssm_ref, f32[8,3072]{1,0:T(8,128)} %get-tuple-element.312.gain_ref), custom_call_target="tpu_custom_call" | custom-call | flops 1333333376 | bytes 5333333 | tf_op jit(solution)/shard_map/pallas_call | solution.py:427
  186.3 6.3 %convolution_convert_fusion = bf16[1536,1536]{1,0:T(8,128)(2,1)} fusion(bf16[512,1536]{1,0:T(8,128)(2,1)S(1)} %bitcast.25, bf16[512,3072]{1,0:T(8,128)(2,1)} %get-tuple-element.337), kind=kOutput, calls=%fused_computation.4 | convolution fusion | flops 2418278400 | bytes 7864320 | tf_op jit(solution)/shard_map/dot_general | solution.py:493
  192.9 10.6 %shard_map.226 = (bf16[512,1536]{1,0:T(8,128)(2,1)}, f32[512,128]{1,0:T(8,128)}) custom-call(bf16[512,3072]{1,0:T(8,128)(2,1)} %get-tuple-element.341.gated_ref, bf16[3072,1536]{1,0:T(8,128)(2,1)} %all-gather.2.cloned.1.call-done.weight_ref, bf16[512,1536]{1,0:T(8,128)(2,1)} %bitcast.34, bf16[512,1536]{1,0:T(8,128)(2,1)} %bitcast.26, ...), custom_call_target="tpu_custom_call" | custom-call | flops 3221225472 | bytes 8388608 | tf_op jit(solution)/shard_map/pallas_call | solution.py:574
  209.0 15.2 %shard_map.227 = (bf16[512,3072]{1,0:T(8,128)(2,1)}, bf16[512,3072]{1,0:T(8,128)(2,1)}, f32[8,3072]{1,0:T(8,128)}) custom-call(f32[512,3072]{1,0:T(8,128)} %get-tuple-element.350.z_ref, f32[512,3072]{1,0:T(8,128)} %get-tuple-element.333.ssm_ref, bf16[512,1536]{1,0:T(8,128)(2,1)} %bitcast.27, bf16[3072,1536]{1,0:T(8,128)(2,1)} %all-gather.2.cloned.1.call-done.weight_ref, ...), custom_call_target="tpu_custom_call" | custom-call | flops 4000000000 | bytes 12000000 | tf_op jit(solution)/shard_map/pallas_call | solution.py:443
  224.3 3.2 add_convert_fusion.1
  227.5 3.4 add_convert_fusion
  230.9 7.5 %fusion.26 = bf16[1536,3072]{1,0:T(8,128)(2,1)} fusion(bf16[512,1536]{1,0:T(8,128)(2,1)S(1)} %copy-done.7, bf16[512,3072]{1,0:T(8,128)(2,1)S(1)} %copy-done.14), kind=kOutput, calls=%fused_computation.80 | convolution fusion | flops 4831838208 | bytes 14155776 | tf_op jit(solution)/shard_map/dot_general | solution.py:493
  241.9 26.2 %shard_map.228 = (bf16[512,2048]{1,0:T(8,128)(2,1)}, f32[8,2048]{1,0:T(8,128)}, f32[512,768]{1,0:T(8,128)}, f32[8,2048]{1,0:T(8,128)}) custom-call(s32[1]{0:T(128)} %bitcast.41, f32[512,3072]{1,0:T(8,128)} %get-tuple-element.310.x_ref, f32[512,3072]{1,0:T(8,128)} %get-tuple-element.333.ssm_ref, bf16[512,3072]{1,0:T(8,128)(2,1)} %get-tuple-element.374.ds_ref, ...), custom_call_target="tpu_custom_call" | custom-call | flops 9333332992 | bytes 10666666 | tf_op jit(solution)/shard_map/pallas_call | solution.py:463
  268.1 5.0 %convolution_convert_fusion.1 = bf16[768,2048]{1,0:T(8,128)(2,1)} fusion(bf16[512,2048]{1,0:T(8,128)(2,1)} %get-tuple-element.369.right_ref.refs_2_, bf16[1536,512]{1,0:T(8,128)(2,1)S(1)} %copy-done.8), kind=kOutput, calls=%fused_computation.5 | convolution fusion | flops 1612185600 | bytes 6029312 | tf_op jit(solution)/shard_map/dot_general | solution.py:851
  278.1 15.3 %shard_map.229 = (bf16[512,1024]{1,0:T(8,128)(2,1)}, f32[8,1024]{1,0:T(8,128)}, f32[512,768]{1,0:T(8,128)}, f32[8,1024]{1,0:T(8,128)}) custom-call(s32[1]{0:T(128)} %bitcast.42, f32[512,3072]{1,0:T(8,128)} %get-tuple-element.310.x_ref, f32[512,3072]{1,0:T(8,128)} %get-tuple-element.333.ssm_ref, bf16[512,3072]{1,0:T(8,128)(2,1)} %get-tuple-element.374.ds_ref, ...), custom_call_target="tpu_custom_call" | custom-call | flops 4666666496 | bytes 5333333 | tf_op jit(solution)/shard_map/pallas_call | solution.py:463
  293.5 6.4 %shard_map.230 = (bf16[512,384]{1,0:T(8,128)(2,1)}, f32[8,256]{1,0:T(8,128)}, f32[8,128]{1,0:T(8,128)}) custom-call(s32[1]{0:T(128)} %bitcast.43, f32[512,384]{1,0:T(8,128)} %get-tuple-element.379.bcd_ref, f32[8,256]{1,0:T(8,128)} %slice.139.conv_ref, f32[8,128]{1,0:T(8,128)} %get-tuple-element.380.head_ref, bf16[512,256]{1,0:T(8,128)(2,1)} %get-tuple-element.315.bc_ref, ...), custom_call_target="tpu_custom_call" | custom-call | flops 1333333376 | bytes 2666666 | tf_op jit(solution)/shard_map/pallas_call | solution.py:480
  300.0 6.2 %shard_map.231 = (bf16[192,2048]{1,0:T(8,128)(2,1)}, bf16[192,2048]{1,0:T(8,128)(2,1)}, bf16[192,2048]{1,0:T(8,128)(2,1)}, f32[192,2048]{1,0:T(8,128)}) custom-call(bf16[1536,512]{1,0:T(8,128)(2,1)} %get-tuple-element.300.left_ref, bf16[512,2048]{1,0:T(8,128)(2,1)} %get-tuple-element.369.right_ref.refs_2_, bf16[768,2048]{1,0:T(8,128)(2,1)} %collective-permute-done.27.got_ref), custom_call_target="tpu_custom_call" | custom-call | flops 536870912 | bytes 3145728 | tf_op jit(solution)/shard_map/pallas_call | solution.py:709
  307.7 2.7 convolution_convert_fusion.2
  311.5 4.0 reduce-scatter.2.cloned.1.call-done
  323.4 11.1 %collective-permute-done.28 = bf16[96,1536]{1,0:T(8,128)(2,1)} collective-permute-done((bf16[96,1536]{1,0:T(8,128)(2,1)}, bf16[96,1536]{1,0:T(8,128)(2,1)}, u32[]{:S(2)}, u32[]{:S(2)}) %collective-permute-start.28) | collective-permute-done | bytes 294944 | tf_op jit(solution)/shard_map/ppermute | solution.py:922
  335.0 21.8 %shard_map.232.d_ref = f32[512,1536]{1,0:T(8,128)} custom-call(bf16[512,3072]{1,0:T(8,128)(2,1)} %get-tuple-element.361.refs_0_, bf16[1536,3072]{1,0:T(8,128)(2,1)} %get-tuple-element.401.refs_1_, bf16[512,2048]{1,0:T(8,128)(2,1)} %get-tuple-element.369.right_ref.refs_2_, bf16[1536,3072]{1,0:T(8,128)(2,1)} %get-tuple-element.402.refs_3_.refs_5_, ...), custom_call_target="tpu_custom_call" | custom-call | flops 1000 | bytes 1000 | tf_op jit(solution)/shard_map/pallas_call | solution.py:657
  361.7 5.2 %shard_map.233 = (bf16[192,1408]{1,0:T(8,128)(2,1)}, bf16[192,1408]{1,0:T(8,128)(2,1)}, bf16[192,1408]{1,0:T(8,128)(2,1)}, f32[192,1408]{1,0:T(8,128)}) custom-call(bf16[1536,512]{1,0:T(8,128)(2,1)} %get-tuple-element.300.left_ref, bf16[512,1408]{1,0:T(8,128)(2,1)} %copy-done.12, bf16[768,1408]{1,0:T(8,128)(2,1)} %copy-done.18), custom_call_target="tpu_custom_call" | custom-call | flops 369098752 | bytes 2162688 | tf_op jit(solution)/shard_map/pallas_call | solution.py:709
  367.2 2.8 collective-permute-start.34
  373.5 9.9 %collective-permute-done.34 = bf16[96,1536]{1,0:T(8,128)(2,1)S(1)} collective-permute-done((bf16[96,1536]{1,0:T(8,128)(2,1)S(1)}, bf16[96,1536]{1,0:T(8,128)(2,1)S(1)}, u32[]{:S(2)}, u32[]{:S(2)}) %collective-permute-start.34) | collective-permute-done | bytes 294944 | tf_op jit(solution)/shard_map/ppermute | solution.py:922
  383.4 5.1 %shard_map.234 = (bf16[512,1536]{1,0:T(8,128)(2,1)}, f32[8,1536]{1,0:T(8,128)}) custom-call(f32[512,1536]{1,0:T(8,128)} %shard_map.232.d_ref, bf16[512,1536]{1,0:T(8,128)(2,1)} %bitcast.35, bf16[512,1536]{1,0:T(8,128)(2,1)} %bitcast.28, f32[1,1536]{1,0:T(1,128)} %get-tuple-element.427.gain_ref), custom_call_target="tpu_custom_call" | custom-call | flops 1000 | bytes 1000 | tf_op jit(solution)/shard_map/pallas_call | solution.py:795
  390.9 7.5 %collective-permute-done.39 = bf16[48,3072]{1,0:T(8,128)(2,1)S(1)} collective-permute-done((bf16[48,3072]{1,0:T(8,128)(2,1)S(1)}, bf16[48,3072]{1,0:T(8,128)(2,1)S(1)}, u32[]{:S(2)}, u32[]{:S(2)}) %collective-permute-start.39) | collective-permute-done | bytes 294944 | tf_op jit(solution)/shard_map/ppermute | solution.py:922
  404.4 2.8 collective-permute-start.41
  407.2 4.3 all-to-all-start.3
  411.5 16.4 %collective-permute-done.41 = bf16[48,5120]{1,0:T(8,128)(2,1)S(1)} collective-permute-done((bf16[48,5120]{1,0:T(8,128)(2,1)}, bf16[48,5120]{1,0:T(8,128)(2,1)S(1)}, u32[]{:S(2)}, u32[]{:S(2)}) %collective-permute-start.41) | collective-permute-done | bytes 491552 | tf_op jit(solution)/shard_map/ppermute | solution.py:922
  427.9 7.3 %collective-permute-done.42 = bf16[96,1408]{1,0:T(8,128)(2,1)} collective-permute-done((bf16[96,1408]{1,0:T(8,128)(2,1)}, bf16[96,1408]{1,0:T(8,128)(2,1)}, u32[]{:S(2)}, u32[]{:S(2)}) %collective-permute-start.42) | collective-permute-done | bytes 270368 | tf_op jit(solution)/shard_map/ppermute | solution.py:922
  436.6 4.3 all-to-all-start.2
  443.0 2.8 collective-permute-start.46
  446.5 3.0 fusion.1
  449.5 2.7 shard_map.236
  452.2 9.3 %collective-permute-done.44 = bf16[48,3456]{1,0:T(8,128)(2,1)S(1)} collective-permute-done((bf16[48,3456]{1,0:T(8,128)(2,1)S(1)}, bf16[48,3456]{1,0:T(8,128)(2,1)S(1)}, u32[]{:S(2)}, u32[]{:S(2)}) %collective-permute-start.44) | collective-permute-done | bytes 331808 | tf_op jit(solution)/shard_map/ppermute | solution.py:922
  471.7 2.7 shard_map.237
  474.4 4.2 collective-permute-done.51
  479.6 2.6 maximum_convert_fusion
  (289 shorter events, 97.4 us)
Async XLA Ops:
  9.9 33.5 %collective-permute-start = (bf16[192,3456]{1,0:T(8,128)(2,1)}, bf16[192,3456]{1,0:T(8,128)(2,1)}, u32[]{:S(2)}, u32[]{:S(2)}) collective-permute-start(bf16[192,3456]{1,0:T(8,128)(2,1)} %pad_slice_fusion.refs_0_), channel_id=1, source_target_pairs={{0,2},{1,3},{2,0},{3,1},{4,6},{5,7},{6,4},{7,5},{8,10},{9,11},{10,... | collective-permute-start | bytes 3981320 | tf_op jit(solution)/shard_map/ppermute | solution.py:922
  12.8 32.4 %collective-permute-start.1 = (bf16[192,3456]{1,0:T(8,128)(2,1)}, bf16[192,3456]{1,0:T(8,128)(2,1)}, u32[]{:S(2)}, u32[]{:S(2)}) collective-permute-start(bf16[192,3456]{1,0:T(8,128)(2,1)} %pad_slice_fusion.refs_0_), channel_id=1, source_target_pairs={{0,4},{1,5},{2,6},{3,7},{4,0},{5,1},{6,2},{7,3},{8,12},{9,13},{10,... | collective-permute-start | bytes 3981320 | tf_op jit(solution)/shard_map/ppermute | solution.py:922
  14.6 28.7 %collective-permute-start.2 = (bf16[16,416]{1,0:T(8,128)(2,1)S(1)}, bf16[16,416]{1,0:T(8,128)(2,1)S(1)}, u32[]{:S(2)}, u32[]{:S(2)}) collective-permute-start(bf16[16,416]{1,0:T(8,128)(2,1)S(1)} %pad.49), channel_id=1, source_target_pairs={{0,2},{1,3},{2,0},{3,1},{4,6},{5,7},{6,4},{7,5},{8,10},{9,11},{10,... | collective-permute-start | bytes 39944 | tf_op jit(solution)/shard_map/ppermute | solution.py:1012
  17.9 57.5 %all-to-all-start = ((bf16[8,64,1536]{2,1,0:T(8,128)(2,1)}), bf16[8,64,1536]{2,1,0:T(8,128)(2,1)S(1)}, u32[]{:S(2)}, u32[]{:S(2)}) async-start(bf16[8,64,1536]{2,1,0:T(8,128)(2,1)} %gather_fusion.1), calls=%async_computation | async-start | bytes 3145728 | tf_op jit(solution)/shard_map/all_to_all | solution.py:1020
  21.5 171.4 %all-gather.2.cloned.1.call-start = ((), (), s32[]{:S(2)}) async-start(), calls=%async_computation.5 | async-start | bytes 10616832 | tf_op jit(solution)/shard_map/all_gather | solution.py:1030
  49.1 26.3 %collective-permute-start.5 = (bf16[192,3456]{1,0:T(8,128)(2,1)}, bf16[192,3456]{1,0:T(8,128)(2,1)S(1)}, u32[]{:S(2)}, u32[]{:S(2)}) collective-permute-start(bf16[192,3456]{1,0:T(8,128)(2,1)} %pad_slice_fusion.refs_0_), channel_id=1, source_target_pairs={{0,1},{1,0},{2,3},{3,2},{4,5},{5,4},{6,7},{7,6},{8,9},{9,8},{10,11... | collective-permute-start | bytes 3981320 | tf_op jit(solution)/shard_map/ppermute | solution.py:922
  49.1 26.3 %collective-permute-start.6 = (bf16[192,3456]{1,0:T(8,128)(2,1)}, bf16[192,3456]{1,0:T(8,128)(2,1)}, u32[]{:S(2)}, u32[]{:S(2)}) collective-permute-start(bf16[192,3456]{1,0:T(8,128)(2,1)} %collective-permute-done.refs_2_), channel_id=1, source_target_pairs={{0,1},{1,0},{2,3},{3,2},{4,5},{5,4},{6,7},{7,6},{8,9},{9,8},{10,11... | collective-permute-start | bytes 3981320 | tf_op jit(solution)/shard_map/ppermute | solution.py:922
  49.6 25.8 %collective-permute-start.3 = (bf16[96,3456]{1,0:T(8,128)(2,1)}, bf16[96,3456]{1,0:T(8,128)(2,1)}, u32[]{:S(2)}, u32[]{:S(2)}) collective-permute-start(bf16[96,3456]{1,0:T(8,128)(2,1)} %slice.120), channel_id=1, source_target_pairs={{0,4},{1,5},{2,6},{3,7},{4,0},{5,1},{6,2},{7,3},{8,12},{9,13},{10,... | collective-permute-start | bytes 1990664 | tf_op jit(solution)/shard_map/ppermute | solution.py:922
  51.2 24.2 %collective-permute-start.4 = (bf16[96,3456]{1,0:T(8,128)(2,1)}, bf16[96,3456]{1,0:T(8,128)(2,1)}, u32[]{:S(2)}, u32[]{:S(2)}) collective-permute-start(bf16[96,3456]{1,0:T(8,128)(2,1)} %slice.121), channel_id=1, source_target_pairs={{0,2},{1,3},{2,0},{3,1},{4,6},{5,7},{6,4},{7,5},{8,10},{9,11},{10,... | collective-permute-start | bytes 1990664 | tf_op jit(solution)/shard_map/ppermute | solution.py:922
  55.9 19.5 %collective-permute-start.7 = (bf16[32,416]{1,0:T(8,128)(2,1)S(1)}, bf16[32,416]{1,0:T(8,128)(2,1)S(1)}, u32[]{:S(2)}, u32[]{:S(2)}) collective-permute-start(bf16[32,416]{1,0:T(8,128)(2,1)S(1)} %pad_maximum_fusion.7), channel_id=1, source_target_pairs={{0,4},{1,5},{2,6},{3,7},{4,0},{5,1},{6,2},{7,3},{8,12},{9,13},{10,... | collective-permute-start | bytes 79880 | tf_op jit(solution)/shard_map/ppermute | solution.py:1012
  78.9 40.3 %collective-permute-start.8 = (bf16[192,3072]{1,0:T(8,128)(2,1)}, bf16[192,3072]{1,0:T(8,128)(2,1)S(1)}, u32[]{:S(2)}, u32[]{:S(2)}) collective-permute-start(bf16[192,3072]{1,0:T(8,128)(2,1)} %slice.119.refs_0_), channel_id=1, source_target_pairs={{0,2},{1,3},{2,0},{3,1},{4,6},{5,7},{6,4},{7,5},{8,10},{9,11},{10,... | collective-permute-start | bytes 3538952 | tf_op jit(solution)/shard_map/ppermute | solution.py:922
  79.2 40.2 %collective-permute-start.9 = (bf16[192,3072]{1,0:T(8,128)(2,1)}, bf16[192,3072]{1,0:T(8,128)(2,1)}, u32[]{:S(2)}, u32[]{:S(2)}) collective-permute-start(bf16[192,3072]{1,0:T(8,128)(2,1)} %slice.119.refs_0_), channel_id=1, source_target_pairs={{0,4},{1,5},{2,6},{3,7},{4,0},{5,1},{6,2},{7,3},{8,12},{9,13},{10,... | collective-permute-start | bytes 3538952 | tf_op jit(solution)/shard_map/ppermute | solution.py:922
  120.7 31.5 %collective-permute-start.16 = (bf16[192,3072]{1,0:T(8,128)(2,1)}, bf16[192,3072]{1,0:T(8,128)(2,1)S(1)}, u32[]{:S(2)}, u32[]{:S(2)}) collective-permute-start(bf16[192,3072]{1,0:T(8,128)(2,1)} %slice.119.refs_0_), channel_id=1, source_target_pairs={{0,1},{1,0},{2,3},{3,2},{4,5},{5,4},{6,7},{7,6},{8,9},{9,8},{10,11... | collective-permute-start | bytes 3538952 | tf_op jit(solution)/shard_map/ppermute | solution.py:922
  120.8 31.4 %collective-permute-start.17 = (bf16[192,3072]{1,0:T(8,128)(2,1)S(1)}, bf16[192,3072]{1,0:T(8,128)(2,1)S(1)}, u32[]{:S(2)}, u32[]{:S(2)}) collective-permute-start(bf16[192,3072]{1,0:T(8,128)(2,1)S(1)} %collective-permute-done.8.refs_2_), channel_id=1, source_target_pairs={{0,1},{1,0},{2,3},{3,2},{4,5},{5,4},{6,7},{7,6},{8,9},{9,8},{10,11... | collective-permute-start | bytes 3538952 | tf_op jit(solution)/shard_map/ppermute | solution.py:922
  121.3 32.0 %collective-permute-start.18 = (bf16[192,3072]{1,0:T(8,128)(2,1)}, bf16[192,3072]{1,0:T(8,128)(2,1)S(1)}, u32[]{:S(2)}, u32[]{:S(2)}) collective-permute-start(bf16[192,3072]{1,0:T(8,128)(2,1)} %collective-permute-done.9.refs_4_), channel_id=1, source_target_pairs={{0,1},{1,0},{2,3},{3,2},{4,5},{5,4},{6,7},{7,6},{8,9},{9,8},{10,11... | collective-permute-start | bytes 3538952 | tf_op jit(solution)/shard_map/ppermute | solution.py:922
  121.4 29.0 %collective-permute-start.14 = (bf16[96,3072]{1,0:T(8,128)(2,1)S(1)}, bf16[96,3072]{1,0:T(8,128)(2,1)S(1)}, u32[]{:S(2)}, u32[]{:S(2)}) collective-permute-start(bf16[96,3072]{1,0:T(8,128)(2,1)S(1)} %slice.124), channel_id=1, source_target_pairs={{0,4},{1,5},{2,6},{3,7},{4,0},{5,1},{6,2},{7,3},{8,12},{9,13},{10,... | collective-permute-start | bytes 1769480 | tf_op jit(solution)/shard_map/ppermute | solution.py:922
  123.7 28.5 %collective-permute-start.15 = (bf16[96,3072]{1,0:T(8,128)(2,1)S(1)}, bf16[96,3072]{1,0:T(8,128)(2,1)S(1)}, u32[]{:S(2)}, u32[]{:S(2)}) collective-permute-start(bf16[96,3072]{1,0:T(8,128)(2,1)S(1)} %slice.125), channel_id=1, source_target_pairs={{0,2},{1,3},{2,0},{3,1},{4,6},{5,7},{6,4},{7,5},{8,10},{9,11},{10,... | collective-permute-start | bytes 1769480 | tf_op jit(solution)/shard_map/ppermute | solution.py:922
  155.3 30.9 %all-to-all-start.1 = ((bf16[8,64,1536]{2,1,0:T(8,128)(2,1)}), bf16[8,64,1536]{2,1,0:T(8,128)(2,1)S(1)}, u32[]{:S(2)}, u32[]{:S(2)}) async-start(bf16[8,64,1536]{2,1,0:T(8,128)(2,1)} %gather_fusion), calls=%async_computation.1 | async-start | bytes 3145728 | tf_op jit(solution)/shard_map/all_to_all | solution.py:921
  159.1 156.4 %reduce-scatter.2.cloned.1.call-start = ((), (), s32[]{:S(2)}) async-start(), calls=%async_computation.6 | async-start | bytes 10616832 | tf_op jit(solution)/shard_map/reduce_scatter | solution.py:1102
  205.8 18.5 %collective-permute-start.22 = (bf16[192,1536]{1,0:T(8,128)(2,1)S(1)}, bf16[192,1536]{1,0:T(8,128)(2,1)S(1)}, u32[]{:S(2)}, u32[]{:S(2)}) collective-permute-start(bf16[192,1536]{1,0:T(8,128)(2,1)S(1)} %get-tuple-element.348), channel_id=1, source_target_pairs={{0,2},{1,3},{2,0},{3,1},{4,6},{5,7},{6,4},{7,5},{8,10},{9,11},{10,... | collective-permute-start | bytes 1769480 | tf_op jit(solution)/shard_map/ppermute | solution.py:922
  207.5 16.7 %collective-permute-start.23 = (bf16[192,1536]{1,0:T(8,128)(2,1)S(1)}, bf16[192,1536]{1,0:T(8,128)(2,1)S(1)}, u32[]{:S(2)}, u32[]{:S(2)}) collective-permute-start(bf16[192,1536]{1,0:T(8,128)(2,1)S(1)} %get-tuple-element.349), channel_id=1, source_target_pairs={{0,4},{1,5},{2,6},{3,7},{4,0},{5,1},{6,2},{7,3},{8,12},{9,13},{10,... | collective-permute-start | bytes 1769480 | tf_op jit(solution)/shard_map/ppermute | solution.py:922
  238.5 29.6 %collective-permute-start.24 = (bf16[384,1536]{1,0:T(8,128)(2,1)}, bf16[384,1536]{1,0:T(8,128)(2,1)S(1)}, u32[]{:S(2)}, u32[]{:S(2)}) collective-permute-start(bf16[384,1536]{1,0:T(8,128)(2,1)} %add_convert_fusion.1), channel_id=1, source_target_pairs={{0,2},{1,3},{2,0},{3,1},{4,6},{5,7},{6,4},{7,5},{8,10},{9,11},{10,... | collective-permute-start | bytes 3538952 | tf_op jit(solution)/shard_map/ppermute | solution.py:922
  239.1 29.0 %collective-permute-start.25 = (bf16[384,1536]{1,0:T(8,128)(2,1)}, bf16[384,1536]{1,0:T(8,128)(2,1)}, u32[]{:S(2)}, u32[]{:S(2)}) collective-permute-start(bf16[384,1536]{1,0:T(8,128)(2,1)} %add_convert_fusion), channel_id=1, source_target_pairs={{0,4},{1,5},{2,6},{3,7},{4,0},{5,1},{6,2},{7,3},{8,12},{9,13},{10,... | collective-permute-start | bytes 3538952 | tf_op jit(solution)/shard_map/ppermute | solution.py:922
  275.6 24.4 %collective-permute-start.27 = (bf16[768,2048]{1,0:T(8,128)(2,1)}, bf16[768,2048]{1,0:T(8,128)(2,1)}, u32[]{:S(2)}, u32[]{:S(2)}) collective-permute-start(bf16[768,2048]{1,0:T(8,128)(2,1)} %convolution_convert_fusion.1), channel_id=1, source_target_pairs={{0,1},{1,0},{2,3},{3,2},{4,5},{5,4},{6,7},{7,6},{8,9},{9,8},{10,11... | collective-permute-start | bytes 9437192 | tf_op jit(solution)/shard_map/ppermute | solution.py:922
  275.6 24.3 %collective-permute-start.26 = (bf16[192,1536]{1,0:T(8,128)(2,1)S(1)}, bf16[192,1536]{1,0:T(8,128)(2,1)S(1)}, u32[]{:S(2)}, u32[]{:S(2)}) collective-permute-start(bf16[192,1536]{1,0:T(8,128)(2,1)S(1)} %select_convert_fusion), channel_id=1, source_target_pairs={{0,8},{8,0},{16,24},{24,16},{1,9},{9,1},{17,25},{25,17},{2,10},{10... | collective-permute-start | bytes 1769480 | tf_op jit(solution)/shard_map/ppermute | solution.py:922
  317.5 40.9 %collective-permute-start.32 = (bf16[768,1408]{1,0:T(8,128)(2,1)}, bf16[768,1408]{1,0:T(8,128)(2,1)S(1)}, u32[]{:S(2)}, u32[]{:S(2)}) collective-permute-start(bf16[768,1408]{1,0:T(8,128)(2,1)} %convolution_convert_fusion.2), channel_id=1, source_target_pairs={{0,1},{1,0},{2,3},{3,2},{4,5},{5,4},{6,7},{7,6},{8,9},{9,8},{10,11... | collective-permute-start | bytes 6488072 | tf_op jit(solution)/shard_map/ppermute | solution.py:922
  317.6 17.0 %collective-permute-start.28 = (bf16[96,1536]{1,0:T(8,128)(2,1)}, bf16[96,1536]{1,0:T(8,128)(2,1)}, u32[]{:S(2)}, u32[]{:S(2)}) collective-permute-start(bf16[96,1536]{1,0:T(8,128)(2,1)} %select_convert_fusion.3), channel_id=1, source_target_pairs={{0,16},{8,24},{16,0},{24,8},{1,17},{9,25},{17,1},{25,9},{2,18},{10... | collective-permute-start | bytes 884744 | tf_op jit(solution)/shard_map/ppermute | solution.py:922
  320.0 36.9 %collective-permute-start.29 = (bf16[192,2048]{1,0:T(8,128)(2,1)}, bf16[192,2048]{1,0:T(8,128)(2,1)S(1)}, u32[]{:S(2)}, u32[]{:S(2)}) collective-permute-start(bf16[192,2048]{1,0:T(8,128)(2,1)} %get-tuple-element.396), channel_id=1, source_target_pairs={{0,6},{1,7},{2,4},{3,5},{4,2},{5,3},{6,0},{7,1},{8,14},{9,15},{10,... | collective-permute-start | bytes 2359304 | tf_op jit(solution)/shard_map/ppermute | solution.py:922
  321.4 36.1 %collective-permute-start.30 = (bf16[192,2048]{1,0:T(8,128)(2,1)}, bf16[192,2048]{1,0:T(8,128)(2,1)S(1)}, u32[]{:S(2)}, u32[]{:S(2)}) collective-permute-start(bf16[192,2048]{1,0:T(8,128)(2,1)} %get-tuple-element.397), channel_id=1, source_target_pairs={{0,2},{1,3},{2,0},{3,1},{4,6},{5,7},{6,4},{7,5},{8,10},{9,11},{10,... | collective-permute-start | bytes 2359304 | tf_op jit(solution)/shard_map/ppermute | solution.py:922
  322.8 34.8 %collective-permute-start.31 = (bf16[192,2048]{1,0:T(8,128)(2,1)}, bf16[192,2048]{1,0:T(8,128)(2,1)S(1)}, u32[]{:S(2)}, u32[]{:S(2)}) collective-permute-start(bf16[192,2048]{1,0:T(8,128)(2,1)} %get-tuple-element.398), channel_id=1, source_target_pairs={{0,4},{1,5},{2,6},{3,7},{4,0},{5,1},{6,2},{7,3},{8,12},{9,13},{10,... | collective-permute-start | bytes 2359304 | tf_op jit(solution)/shard_map/ppermute | solution.py:922
  334.5 22.3 %collective-permute-start.33 = (bf16[96,3072]{1,0:T(8,128)(2,1)}, bf16[96,3072]{1,0:T(8,128)(2,1)S(1)}, u32[]{:S(2)}, u32[]{:S(2)}) collective-permute-start(bf16[96,3072]{1,0:T(8,128)(2,1)} %broadcast_select_fusion), channel_id=1, source_target_pairs={{0,8},{8,0},{16,24},{24,16},{1,9},{9,1},{17,25},{25,17},{2,10},{10... | collective-permute-start | bytes 1769480 | tf_op jit(solution)/shard_map/ppermute | solution.py:922
  367.2 16.2 %collective-permute-start.34 = (bf16[96,1536]{1,0:T(8,128)(2,1)S(1)}, bf16[96,1536]{1,0:T(8,128)(2,1)S(1)}, u32[]{:S(2)}, u32[]{:S(2)}) collective-permute-start(bf16[96,1536]{1,0:T(8,128)(2,1)S(1)} %add_convert_fusion.4), channel_id=1, source_target_pairs={{0,16},{8,24},{16,0},{24,8},{1,17},{9,25},{17,1},{25,9},{2,18},{10... | collective-permute-start | bytes 884744 | tf_op jit(solution)/shard_map/ppermute | solution.py:922
  370.0 28.5 %collective-permute-start.36 = (bf16[192,1408]{1,0:T(8,128)(2,1)}, bf16[192,1408]{1,0:T(8,128)(2,1)S(1)}, u32[]{:S(2)}, u32[]{:S(2)}) collective-permute-start(bf16[192,1408]{1,0:T(8,128)(2,1)} %get-tuple-element.417), channel_id=1, source_target_pairs={{0,6},{1,7},{2,4},{3,5},{4,2},{5,3},{6,0},{7,1},{8,14},{9,15},{10,... | collective-permute-start | bytes 1622024 | tf_op jit(solution)/shard_map/ppermute | solution.py:922
  371.4 27.0 %collective-permute-start.37 = (bf16[192,1408]{1,0:T(8,128)(2,1)S(1)}, bf16[192,1408]{1,0:T(8,128)(2,1)S(1)}, u32[]{:S(2)}, u32[]{:S(2)}) collective-permute-start(bf16[192,1408]{1,0:T(8,128)(2,1)S(1)} %copy-done.48), channel_id=1, source_target_pairs={{0,2},{1,3},{2,0},{3,1},{4,6},{5,7},{6,4},{7,5},{8,10},{9,11},{10,... | collective-permute-start | bytes 1622024 | tf_op jit(solution)/shard_map/ppermute | solution.py:922
  372.8 25.7 %collective-permute-start.38 = (bf16[192,1408]{1,0:T(8,128)(2,1)S(1)}, bf16[192,1408]{1,0:T(8,128)(2,1)S(1)}, u32[]{:S(2)}, u32[]{:S(2)}) collective-permute-start(bf16[192,1408]{1,0:T(8,128)(2,1)S(1)} %copy-done.47), channel_id=1, source_target_pairs={{0,4},{1,5},{2,6},{3,7},{4,0},{5,1},{6,2},{7,3},{8,12},{9,13},{10,... | collective-permute-start | bytes 1622024 | tf_op jit(solution)/shard_map/ppermute | solution.py:922
  373.5 25.0 %collective-permute-start.35 = (bf16[96,2048]{1,0:T(8,128)(2,1)S(1)}, bf16[96,2048]{1,0:T(8,128)(2,1)S(1)}, u32[]{:S(2)}, u32[]{:S(2)}) collective-permute-start(bf16[96,2048]{1,0:T(8,128)(2,1)S(1)} %select_convert_fusion.1), channel_id=1, source_target_pairs={{0,8},{8,0},{16,24},{24,16},{1,9},{9,1},{17,25},{25,17},{2,10},{10... | collective-permute-start | bytes 1179656 | tf_op jit(solution)/shard_map/ppermute | solution.py:922
  383.4 15.1 %collective-permute-start.39 = (bf16[48,3072]{1,0:T(8,128)(2,1)S(1)}, bf16[48,3072]{1,0:T(8,128)(2,1)S(1)}, u32[]{:S(2)}, u32[]{:S(2)}) collective-permute-start(bf16[48,3072]{1,0:T(8,128)(2,1)S(1)} %select_convert_fusion.2), channel_id=1, source_target_pairs={{0,16},{8,24},{16,0},{24,8},{1,17},{9,25},{17,1},{25,9},{2,18},{10... | collective-permute-start | bytes 884744 | tf_op jit(solution)/shard_map/ppermute | solution.py:922
  403.5 31.7 %collective-permute-start.40 = (bf16[192,1536]{1,0:T(8,128)(2,1)S(1)}, bf16[192,1536]{1,0:T(8,128)(2,1)}, u32[]{:S(2)}, u32[]{:S(2)}) collective-permute-start(bf16[192,1536]{1,0:T(8,128)(2,1)S(1)} %maximum_select_fusion.3), channel_id=1, source_target_pairs={{0,8},{8,0},{16,24},{24,16},{1,9},{9,1},{17,25},{25,17},{2,10},{10... | collective-permute-start | bytes 1769480 | tf_op jit(solution)/shard_map/ppermute | solution.py:922
  404.4 23.5 %collective-permute-start.41 = (bf16[48,5120]{1,0:T(8,128)(2,1)}, bf16[48,5120]{1,0:T(8,128)(2,1)S(1)}, u32[]{:S(2)}, u32[]{:S(2)}) collective-permute-start(bf16[48,5120]{1,0:T(8,128)(2,1)} %pad_maximum_fusion.2), channel_id=1, source_target_pairs={{0,16},{8,24},{16,0},{24,8},{1,17},{9,25},{17,1},{25,9},{2,18},{10... | collective-permute-start | bytes 1474568 | tf_op jit(solution)/shard_map/ppermute | solution.py:922
  407.2 28.0 %collective-permute-start.42 = (bf16[96,1408]{1,0:T(8,128)(2,1)}, bf16[96,1408]{1,0:T(8,128)(2,1)}, u32[]{:S(2)}, u32[]{:S(2)}) collective-permute-start(bf16[96,1408]{1,0:T(8,128)(2,1)} %select_convert_fusion.4), channel_id=1, source_target_pairs={{0,8},{8,0},{16,24},{24,16},{1,9},{9,1},{17,25},{25,17},{2,10},{10... | collective-permute-start | bytes 811016 | tf_op jit(solution)/shard_map/ppermute | solution.py:922
  407.2 20.7 %collective-permute-start.43 = (f32[4,2688]{1,0:T(4,128)S(1)}, f32[4,2688]{1,0:T(4,128)S(1)}, u32[]{:S(2)}, u32[]{:S(2)}) collective-permute-start(f32[4,2688]{1,0:T(4,128)S(1)} %slice.168), channel_id=1, source_target_pairs={{0,1},{1,0},{2,3},{3,2},{4,5},{5,4},{6,7},{7,6},{8,9},{9,8},{10,11... | collective-permute-start | bytes 129032 | tf_op jit(solution)/shard_map/ppermute | solution.py:922
  407.2 29.3 %all-to-all-start.3 = ((bf16[8,64,1536]{2,1,0:T(8,128)(2,1)}), bf16[8,64,1536]{2,1,0:T(8,128)(2,1)}, u32[]{:S(2)}, u32[]{:S(2)}) async-start(bf16[8,64,1536]{2,1,0:T(8,128)(2,1)} %bitcast.37), calls=%async_computation.4 | async-start | bytes 3145728 | tf_op jit(solution)/shard_map/all_to_all | solution.py:1020
  436.6 27.3 %all-to-all-start.2 = ((bf16[8,64,1536]{2,1,0:T(8,128)(2,1)}), bf16[8,64,1536]{2,1,0:T(8,128)(2,1)}, u32[]{:S(2)}, u32[]{:S(2)}) async-start(bf16[8,64,1536]{2,1,0:T(8,128)(2,1)} %bitcast.36), calls=%async_computation.3 | async-start | bytes 3145728 | tf_op jit(solution)/shard_map/all_to_all | solution.py:921
  441.0 22.9 %collective-permute-start.45 = (bf16[96,3072]{1,0:T(8,128)(2,1)S(1)}, bf16[96,3072]{1,0:T(8,128)(2,1)}, u32[]{:S(2)}, u32[]{:S(2)}) collective-permute-start(bf16[96,3072]{1,0:T(8,128)(2,1)S(1)} %maximum_select_fusion.4), channel_id=1, source_target_pairs={{0,8},{8,0},{16,24},{24,16},{1,9},{9,1},{17,25},{25,17},{2,10},{10... | collective-permute-start | bytes 1769480 | tf_op jit(solution)/shard_map/ppermute | solution.py:922
  441.3 20.2 %collective-permute-start.44 = (bf16[48,3456]{1,0:T(8,128)(2,1)S(1)}, bf16[48,3456]{1,0:T(8,128)(2,1)S(1)}, u32[]{:S(2)}, u32[]{:S(2)}) collective-permute-start(bf16[48,3456]{1,0:T(8,128)(2,1)S(1)} %pad_maximum_fusion.3), channel_id=1, source_target_pairs={{0,16},{8,24},{16,0},{24,8},{1,17},{9,25},{17,1},{25,9},{2,18},{10... | collective-permute-start | bytes 995336 | tf_op jit(solution)/shard_map/ppermute | solution.py:922
  443.0 19.1 %collective-permute-start.46 = (f32[1,2688]{1,0:T(1,128)S(1)}, f32[1,2688]{1,0:T(1,128)S(1)}, u32[]{:S(2)}, u32[]{:S(2)}) collective-permute-start(f32[1,2688]{1,0:T(1,128)S(1)} %get-tuple-element.450), channel_id=1, source_target_pairs={{0,6},{1,7},{2,4},{3,5},{4,2},{5,3},{6,0},{7,1},{8,14},{9,15},{10,... | collective-permute-start | bytes 32264 | tf_op jit(solution)/shard_map/ppermute | solution.py:922
  445.8 16.3 %collective-permute-start.47 = (f32[1,2688]{1,0:T(1,128)S(1)}, f32[1,2688]{1,0:T(1,128)S(1)}, u32[]{:S(2)}, u32[]{:S(2)}) collective-permute-start(f32[1,2688]{1,0:T(1,128)S(1)} %get-tuple-element.451), channel_id=1, source_target_pairs={{0,2},{1,3},{2,0},{3,1},{4,6},{5,7},{6,4},{7,5},{8,10},{9,11},{10,... | collective-permute-start | bytes 32264 | tf_op jit(solution)/shard_map/ppermute | solution.py:922
  446.4 15.8 %collective-permute-start.48 = (f32[1,2688]{1,0:T(1,128)S(1)}, f32[1,2688]{1,0:T(1,128)S(1)}, u32[]{:S(2)}, u32[]{:S(2)}) collective-permute-start(f32[1,2688]{1,0:T(1,128)S(1)} %get-tuple-element.452), channel_id=1, source_target_pairs={{0,4},{1,5},{2,6},{3,7},{4,0},{5,1},{6,2},{7,3},{8,12},{9,13},{10,... | collective-permute-start | bytes 32264 | tf_op jit(solution)/shard_map/ppermute | solution.py:922
  (65 other events, 396.1 us)
Sparse Core Ops, SparseCore 0:
  75.6 84.6 all-gather.1
  238.6 76.8 reduce-scatter.1
